TPU v7x, 256 devices: a whole 4x4x8 slice. The times are simulated.
256 devices in a mesh: cuts: 8 (over x, y_lo), zero: 32 (over z, y_hi, core).
Axes of the slice: x: 4, y: 4 (y_hi: 2, y_lo: 2; y = y_hi * 2 + y_lo), z: 8, core: 2. Of those that a mesh axis runs over, the one named last changes fastest.
Arguments:
- inputs: bfloat16 [32768, 5632], P(('cuts', 'zero')), may hold values from -6 to 6
- cotangent: bfloat16 [32768, 5632], P(('cuts', 'zero')), may hold values from -6 to 6
- gate_a_weight: bfloat16 [5632, 176], P('zero'), may hold values from -0.4375 to 0.4375
- gate_x_weight: bfloat16 [5632, 176], P('zero'), may hold values from -0.4375 to 0.4375
- gate_a_bias: bfloat16 [5632], P('zero'), may hold values from -3 to 3
- gate_x_bias: bfloat16 [5632], P('zero'), may hold values from -3 to 3
- decay_param: bfloat16 [5632], P('zero'), may hold values from -9 to -4.28125
Outputs:
- input_grad: bfloat16 [32768, 5632], P(('cuts', 'zero'))
- gate_a_grad: float32 [5632, 176], P('zero')
- gate_x_grad: float32 [5632, 176], P('zero')
- bias_a_grad: float32 [5632], P('zero')
- bias_x_grad: float32 [5632], P('zero')
- decay_grad: float32 [5632], P('zero')
All inputs are finite; a program needn't handle non-finite values.
Results may differ from a plain program's by a relative error of at most 0.008.
Values may be sent and summed in bfloat16 or wider, within the bound.
No kernel may reach another device: no remote copies, remote signals or barrier semaphores. Data moves between devices by JAX's collectives and lax.ppermute only.
A program may use at most 128 MiB of HBM per device.

v0:
```python
import jax
import jax.numpy as jnp
from jax import lax
from jax.sharding import PartitionSpec as P


def state_history(coefficients, addend_terms):
    length, hidden_width = coefficients.shape
    block_groups = length // 8
    coef_blocks = coefficients.reshape(block_groups, 8, hidden_width)
    addend_block_list = addend_terms.reshape(block_groups, 8, hidden_width)

    def advance(carry, pair):
        coef_rows, add_rows = pair
        outputs = []
        for index in range(8):
            carry = coef_rows[index] * carry + add_rows[index]
            outputs.append(carry)
        return (carry, jnp.stack(outputs))

    _, result = lax.scan(
        advance, jnp.zeros((hidden_width,), jnp.float32), (coef_blocks, addend_block_list)
    )
    return result.reshape(length, hidden_width)


def reverse_state_history(coefficients, addend_terms):
    length, hidden_width = coefficients.shape
    block_groups = length // 8
    coef_blocks = coefficients.reshape(block_groups, 8, hidden_width)
    addend_block_list = addend_terms.reshape(block_groups, 8, hidden_width)

    def retreat(carry, pair):
        coef_rows, add_rows = pair
        outputs = [None] * 8
        for index in range(7, -1, -1):
            carry = add_rows[index] + coef_rows[index] * carry
            outputs[index] = carry
        return (carry, jnp.stack(outputs))

    _, result = lax.scan(
        retreat,
        jnp.zeros((hidden_width,), jnp.float32),
        (coef_blocks, addend_block_list),
        reverse=True,
    )
    return result.reshape(length, hidden_width)


def per_device(
    inputs, cotangent, gate_a_weight, gate_x_weight, gate_a_bias, gate_x_bias, decay_param
):
    weight_a, weight_x, bias_a, bias_x, decay_raw = (
        lax.all_gather(gate_a_weight, "zero", axis=0, tiled=True),
        lax.all_gather(gate_x_weight, "zero", axis=0, tiled=True),
        lax.all_gather(gate_a_bias, "zero", axis=0, tiled=True),
        lax.all_gather(gate_x_bias, "zero", axis=0, tiled=True),
        lax.all_gather(decay_param, "zero", axis=0, tiled=True),
    )
    length, hidden_width = inputs.shape
    block = weight_a.shape[1]
    heads = hidden_width // block
    blocks_in = inputs.reshape(length, heads, block)
    cube_a = weight_a.reshape(heads, block, block)
    cube_x = weight_x.reshape(heads, block, block)
    pre_gate = jnp.einsum(
        "thb,hbk->thk", blocks_in, cube_a, preferred_element_type=jnp.float32
    ).reshape(length, hidden_width) + bias_a.astype(jnp.float32)
    pre_input = jnp.einsum(
        "thb,hbk->thk", blocks_in, cube_x, preferred_element_type=jnp.float32
    ).reshape(length, hidden_width) + bias_x.astype(jnp.float32)
    recur_gate = jax.nn.sigmoid(pre_gate)
    input_gate = jax.nn.sigmoid(pre_input)
    softened = jax.nn.softplus(decay_raw.astype(jnp.float32))
    log_decay = -8.0 * softened * recur_gate
    decay = jnp.exp(log_decay)
    scaled = jnp.sqrt(-jnp.expm1(2.0 * log_decay))
    values_f = inputs.astype(jnp.float32)
    drive = scaled * input_gate * values_f
    states = state_history(decay, drive)
    zero_row = jnp.zeros((1, hidden_width), jnp.float32)
    earlier = jnp.concatenate([zero_row, states[:-1]], axis=0)
    coeffs = jnp.concatenate([decay[1:], zero_row], axis=0)
    adjoint = reverse_state_history(coeffs, cotangent.astype(jnp.float32))
    grad_log = adjoint * earlier * decay - adjoint * input_gate * values_f * decay * decay / scaled
    delta_gate = (grad_log * (-8.0 * softened) * recur_gate * (1.0 - recur_gate)).astype(
        jnp.bfloat16
    )
    delta_input = (adjoint * scaled * values_f * input_gate * (1.0 - input_gate)).astype(
        jnp.bfloat16
    )
    delta_gate3 = delta_gate.reshape(length, heads, block)
    delta_input3 = delta_input.reshape(length, heads, block)
    factor = 1.0 / jnp.sqrt(jnp.float32(length * lax.axis_size("cuts") * lax.axis_size("zero")))
    grad_wa = (
        jnp.einsum(
            "thb,thk->hbk", blocks_in, delta_gate3, preferred_element_type=jnp.float32
        ).reshape(hidden_width, block)
        * factor
    )
    grad_wx = (
        jnp.einsum(
            "thb,thk->hbk", blocks_in, delta_input3, preferred_element_type=jnp.float32
        ).reshape(hidden_width, block)
        * factor
    )
    grad_ba = jnp.sum(delta_gate.astype(jnp.float32), axis=0) * factor
    grad_bx = jnp.sum(delta_input.astype(jnp.float32), axis=0) * factor
    grad_soft = jnp.sum(grad_log * (-8.0 * recur_gate), axis=0) * factor
    back = jnp.einsum(
        "thk,hbk->thb", delta_gate3, cube_a, preferred_element_type=jnp.float32
    ) + jnp.einsum("thk,hbk->thb", delta_input3, cube_x, preferred_element_type=jnp.float32)
    input_grad = (adjoint * scaled * input_gate + back.reshape(length, hidden_width)).astype(
        jnp.bfloat16
    )
    shares = (
        lax.psum_scatter(grad_wa, "zero", scatter_dimension=0, tiled=True),
        lax.psum_scatter(grad_wx, "zero", scatter_dimension=0, tiled=True),
        lax.psum_scatter(grad_ba, "zero", scatter_dimension=0, tiled=True),
        lax.psum_scatter(grad_bx, "zero", scatter_dimension=0, tiled=True),
        lax.psum_scatter(grad_soft, "zero", scatter_dimension=0, tiled=True),
    )
    totals = lax.psum((shares[0], shares[1], shares[2], shares[3], shares[4]), "cuts")
    own_decay = jax.nn.sigmoid(decay_param.astype(jnp.float32))
    return (input_grad, totals[0], totals[1], totals[2], totals[3], totals[4] * own_decay)


def solution(mesh):
    placed = (
        P(("cuts", "zero"), None),
        P(("cuts", "zero"), None),
        P("zero", None),
        P("zero", None),
        P("zero"),
        P("zero"),
        P("zero"),
    )
    return jax.shard_map(
        per_device,
        mesh=mesh,
        in_specs=placed,
        out_specs=(
            P(("cuts", "zero"), None),
            P("zero", None),
            P("zero", None),
            P("zero"),
            P("zero"),
            P("zero"),
        ),
        check_vma=False,
    )
```

profile of v0, /device:TPU:1, one launch (start us, length us, event | category | flops | bytes accessed | tf_op | source)
XLA Modules:
  0.0 970.3 jit_solution(5774004185267001362)
XLA Ops:
  13.3 132.4 %all-reduce.11 = (bf16[5632]{0:T(1024)(128)(2,1)S(1)}, bf16[5632]{0:T(1024)(128)(2,1)S(1)}, bf16[5632]{0:T(1024)(128)(2,1)S(1)}) all-reduce(bf16[5632]{0:T(1024)(128)(2,1)S(1)} %dynamic-update-slice, bf16[5632]{0:T(1024)(128)(2,1)S(1)} %dynamic-update-slice.1, ...), channel_id=1, replica_groups=mesh['cuts'=8,'zero'=32] {'zero'}, use_global_device_ids=true, to_apply=%add.2 | all-reduce | flops 16896 | bytes 67584
  149.8 4.7 fusion.19
  156.8 22.9 %all-gather.5.cloned.1.call-done = bf16[5632,176]{1,0:T(8,128)(2,1)} async-done(((bf16[176,176]{1,0:T(8,128)(2,1)}), bf16[5632,176]{1,0:T(8,128)(2,1)}) %all-gather.5.cloned.1.call-update) | async-done | bytes 1982480 | tf_op jit(solution)/shard_map/all_gather | solution.py:55
  179.6 5.1 fusion.20
  184.7 3.5 copy.60
  188.2 5.2 copy.61
  193.4 5.5 reshape.148
  198.9 4.7 multiply_exponential_fusion
  203.6 5.6 multiply_exponential_fusion.1
  211.1 74.5 %while.31 = (s32[]{:T(128)}, f32[5632]{0:T(1024)S(1)}, f32[16,8,5632]{2,1,0:T(8,128)}, f32[16,8,5632]{2,1,0:T(8,128)}, f32[16,8,5632]{2,1,0:T(8,128)}, /*index=5...) while((s32[]{:T(128)}, f32[5632]{0:T(1024)S(1)}, ...), condition=%wide.region_3.4_spmd.clone, body=%wide.region_2.3_spmd.clone.sunk | while | flops 95754 | bytes 2366211 | solution.py:21
  211.1 3.4 dynamic-slice_reduce_fusion.35
  215.8 3.1 dynamic-slice_reduce_fusion.35
  220.1 3.3 dynamic-slice_reduce_fusion.35
  224.7 3.4 dynamic-slice_reduce_fusion.35
  229.2 3.7 dynamic-slice_reduce_fusion.35
  234.1 3.5 dynamic-slice_reduce_fusion.35
  238.9 3.3 dynamic-slice_reduce_fusion.35
  243.4 3.5 dynamic-slice_reduce_fusion.35
  248.2 3.5 dynamic-slice_reduce_fusion.35
  252.9 3.2 dynamic-slice_reduce_fusion.35
  257.3 3.6 dynamic-slice_reduce_fusion.35
  262.1 3.4 dynamic-slice_reduce_fusion.35
  266.7 3.8 dynamic-slice_reduce_fusion.35
  271.7 3.3 dynamic-slice_reduce_fusion.35
  276.3 3.6 dynamic-slice_reduce_fusion.35
  281.0 3.4 dynamic-slice_reduce_fusion.35
  291.5 70.5 %while.30 = (s32[]{:T(128)}, f32[5632]{0:T(1024)S(1)}, f32[16,8,5632]{2,1,0:T(8,128)}, f32[16,8,5632]{2,1,0:T(8,128)}, f32[16,8,5632]{2,1,0:T(8,128)}, /*index=5...) while((s32[]{:T(128)}, f32[5632]{0:T(1024)S(1)}, ...), condition=%wide.region_1.2_spmd.clone, body=%wide.region_0.1_spmd.clone.sunk | while | flops 95755 | bytes 2365723 | solution.py:41
  300.1 3.3 dynamic-slice_reduce_fusion.34
  309.0 3.3 dynamic-slice_reduce_fusion.34
  317.9 3.3 dynamic-slice_reduce_fusion.34
  322.5 3.3 dynamic-slice_reduce_fusion.34
  335.6 3.1 dynamic-slice_reduce_fusion.34
  340.0 3.3 dynamic-slice_reduce_fusion.34
  344.5 3.1 dynamic-slice_reduce_fusion.34
  348.8 3.2 dynamic-slice_reduce_fusion.34
  357.5 3.2 dynamic-slice_reduce_fusion.34
  361.9 8.4 convert_reduce_fusion
  375.0 5.2 broadcast_multiply_fusion.1
  382.8 5.3 broadcast_multiply_fusion
  390.0 4.9 fusion.21
  395.0 5.9 convolution_add_fusion
  400.9 3.4 copy.66
  404.3 102.9 %reduce-scatter.3.cloned.1.call-done = f32[176,176]{1,0:T(8,128)} async-done(((f32[5632,176]{1,0:T(8,128)}), f32[176,176]{1,0:T(8,128)}) %reduce-scatter.3.cloned.1.call-update) | async-done | bytes 123920 | tf_op jit(solution)/shard_map/reduce_scatter | solution.py:117
  507.2 137.2 %reduce-scatter.5.cloned.1.call-done = f32[176,176]{1,0:T(8,128)} async-done(((f32[5632,176]{1,0:T(8,128)}), f32[176,176]{1,0:T(8,128)}) %reduce-scatter.5.cloned.1.call-update) | async-done | bytes 123920 | tf_op jit(solution)/shard_map/reduce_scatter | solution.py:118
  644.4 7.6 add_convert_fusion
  652.1 233.5 %all-reduce.15.cloned.1.call-done = (f32[5632]{0:T(1024)}, f32[5632]{0:T(1024)}, f32[5632]{0:T(1024)}) async-done(((f32[5632]{0:T(1024)}, f32[5632]{0:T(1024)}, f32[5632]{0:T(1024)}), (f32[5632]{0:T(1024)}, f32[5632]{0:T(1024)}, f32[5632]{0:T(1024)})) %all-reduce.15.cloned.1.call-update) | async-done | bytes 67600
  887.9 15.4 %all-reduce.9 = (f32[176]{0:T(256)}, f32[176]{0:T(256)}, f32[176]{0:T(256)S(1)}) all-reduce(f32[176]{0:T(256)S(1)} %dynamic-slice.4, f32[176]{0:T(256)S(1)} %dynamic-slice.6, f32[176]{0:T(256)S(1)} %dynamic-slice.8), channel_id=1, replica_groups=mesh['cuts'=8,'zero'=32] {'cuts'}, use_global_device_ids=true, to_apply=%region_10.11 | all-reduce | flops 528 | bytes 4224 | tf_op jit(solution)/shard_map/psum | solution.py:123
  903.9 56.3 %all-reduce.17.cloned.1.call-done = (f32[176,176]{1,0:T(8,128)}, f32[176,176]{1,0:T(8,128)}) async-done(((f32[176,176]{1,0:T(8,128)}, f32[176,176]{1,0:T(8,128)}), (f32[176,176]{1,0:T(8,128)}, f32[176,176]{1,0:T(8,128)})) %all-reduce.17.cloned.1.call-update) | async-done | bytes 247824 | tf_op jit(solution)/shard_map/psum | solution.py:123
  (412 shorter events, 92.2 us)
Async XLA Ops:
  7.2 140.6 %copy-start.3 = (bf16[128,5632]{1,0:T(8,128)(2,1)S(1)}, bf16[128,5632]{1,0:T(8,128)(2,1)}, u32[]{:S(2)}) copy-start(bf16[128,5632]{1,0:T(8,128)(2,1)} %param.12) | copy-start | bytes 4325380
  7.2 142.6 %all-gather.3.cloned.1.call-start = ((), (), s32[]{:S(2)}) async-start(), calls=%async_computation.2 | async-start | bytes 2973696 | tf_op jit(solution)/shard_map/all_gather | solution.py:54
  7.9 171.7 %all-gather.5.cloned.1.call-start = ((), (), s32[]{:S(2)}) async-start(), calls=%async_computation.3 | async-start | bytes 2973696 | tf_op jit(solution)/shard_map/all_gather | solution.py:55
  8.7 498.5 %reduce-scatter.3.cloned.1.call-start = ((), (), s32[]{:S(2)}) async-start(), calls=%async_computation.4 | async-start | bytes 5947392 | tf_op jit(solution)/shard_map/reduce_scatter | solution.py:117
  147.7 6.8 copy-start.1
  198.9 4.7 copy-start
  198.9 4.7 copy-start.2
  380.2 264.2 %reduce-scatter.5.cloned.1.call-start = ((), (), s32[]{:S(2)}) async-start(), calls=%async_computation.5 | async-start | bytes 5947392 | tf_op jit(solution)/shard_map/reduce_scatter | solution.py:118
  388.1 497.5 %all-reduce.15.cloned.1.call-start = ((), (), s32[]{:S(2)}) async-start(), calls=%async_computation.6 | async-start | bytes 147456
  394.9 565.3 %all-reduce.17.cloned.1.call-start = ((), (), s32[]{:S(2)}) async-start(), calls=%async_computation.7 | async-start | bytes 720896 | tf_op jit(solution)/shard_map/psum | solution.py:123
  644.4 258.9 %copy-start.4 = (bf16[176]{0:T(256)(128)(2,1)S(1)}, bf16[176]{0:T(256)(128)(2,1)}, u32[]{:S(2)}) copy-start(bf16[176]{0:T(256)(128)(2,1)} %param.17) | copy-start | bytes 1060
Sparse Core Ops, SparseCore 0:
  10.8 86.8 all-gather.2
  100.4 79.1 all-gather.4
  380.3 126.8 reduce-scatter.2
  511.9 132.4 reduce-scatter.4
  647.7 237.8 all-reduce.14
  888.4 71.8 all-reduce.16
where the time goes:
time: 976 us; the launch traced here: 970 us
  waiting for transfers between devices  554 us (57%)
  local copies, waits for them, and re-layouts  185 us (19%)
  blocking collectives  148 us (15%)
  other arithmetic  33.8 us (3%)
  matrix products  31.1 us (3%)
  between operations  15.6 us (2%)
    unnamed x7, waiting for transfers between devices  235 us
    reduce_scatter x1, waiting for transfers between devices, per_device(): lax.psum_scatter(grad_wx, 'zero', scatter_dimension=0, tiled=True)  137 us
    unnamed x1, blocking collectives  132 us
    reduce_scatter x1, waiting for transfers between devices, per_device(): lax.psum_scatter(grad_wa, 'zero', scatter_dimension=0, tiled=True)  103 us
    psum x1, waiting for transfers between devices, per_device(): lax.psum((shares[0], shares[1], shares[2], shares[3], shares[4]), 'cuts')  56.3 us
    slice x16, local copies, waits for them, and re-layouts, advance(): carry = coef_rows[index] * carry + add_rows[index]  55 us
    slice x16, local copies, waits for them, and re-layouts, retreat(): carry = add_rows[index] + coef_rows[index] * carry  50.8 us
    all_gather x1, waiting for transfers between devices, per_device(): lax.all_gather(gate_x_weight, 'zero', axis=0, tiled=True)  22.9 us
  transfers between devices with their start and end apart: 6, of which 5 were waited for; matrix products, arithmetic and copies ran while one was open for 5% of the time, Pallas kernels for 0%

commit v1 on v0

v1 whole, which is shorter than its diff:
```python
import jax
import jax.numpy as jnp
from jax import lax
from jax.experimental import pallas as pl
from jax.experimental.pallas import tpu as pltpu
from jax.sharding import Mesh
from jax.sharding import PartitionSpec as P

BLK = 176
PAIR = 384
WROWS = 192
NZ, NY, NC = 8, 2, 2
NQ = NY * NC
NPAIR = NZ // 2
SEQ = 128
ROWS = NQ * SEQ
VMEM_LIMIT = 56 * 1024 * 1024


def lanes_of(shape):
    return lax.broadcasted_iota(jnp.int32, shape, len(shape) - 1)


def pack_kernel(ones_lane, who_ref, x_ref, *outs):
    who = who_ref[0]
    width = x_ref.shape[1]
    lane = lanes_of((SEQ, PAIR))

    def head_at(head, target):
        start = head * BLK
        base = min(start // 128 * 128, width - PAIR)
        window = x_ref[:, base : base + PAIR].astype(jnp.float32)
        return pltpu.roll(window, (target - (start - base)) % PAIR, 1)

    for p in range(NPAIR):
        for q in range(NQ):
            first = head_at(2 * NQ * p + q, 0)
            second = head_at(2 * NQ * p + NQ + q, BLK)
            fill = jnp.where(lane == 2 * BLK, ones_lane, 0.0)
            both = jnp.where(lane < BLK, first, jnp.where(lane < 2 * BLK, second, fill))
            both = both.astype(jnp.bfloat16)
            for k in range(NQ):

                @pl.when((who ^ k) == q)
                def _():
                    outs[k][:, p * PAIR : (p + 1) * PAIR] = both


def unpack_kernel(who_ref, *refs):
    who = who_ref[0]
    ins, out = refs[:NQ], refs[NQ]
    lane = lanes_of((SEQ, PAIR))
    for p in range(NPAIR):
        acc = [None] * (2 * NQ * BLK // 128)
        for q in range(NQ):
            slot = who ^ q
            val = ins[0][:, p * PAIR : (p + 1) * PAIR].astype(jnp.float32)
            for k in range(1, NQ):
                other = ins[k][:, p * PAIR : (p + 1) * PAIR].astype(jnp.float32)
                val = jnp.where(slot == k, other, val)
            for i in range(2):
                start = (i * NQ + q) * BLK
                base = min(start // 128 * 128, 2 * NQ * BLK - PAIR)
                off = start - base
                moved = pltpu.roll(val, (off - i * BLK) % PAIR, 1)
                moved = jnp.where((lane >= off) & (lane < off + BLK), moved, 0.0)
                for j in range(PAIR // 128):
                    if base + j * 128 < start + BLK and base + (j + 1) * 128 > start:
                        b = base // 128 + j
                        piece = moved[:, j * 128 : (j + 1) * 128]
                        acc[b] = piece if acc[b] is None else acc[b] + piece
        for b, block in enumerate(acc):
            at = p * 2 * NQ * BLK + b * 128
            out[:, at : at + 128] = block.astype(jnp.bfloat16)


def sigmoid(pre):
    base = 1.0 + jnp.exp(jnp.minimum(-pre, 80.0))
    rough = pl.reciprocal(base, approx=True)
    return rough * (2.0 - base * rough)


def one_minus_exp(log_a):
    series = -1.0 / 720.0
    for c in (-1.0 / 120.0, -1.0 / 24.0, -1.0 / 6.0, -0.5, -1.0):
        series = series * log_a + c
    return jnp.where(log_a > -0.25, series * log_a, 1.0 - jnp.exp(log_a))


CHUNK = 32


def main_kernel(factor, *refs):
    xs, cots = refs[:NQ], refs[NQ : 2 * NQ]
    w_ref = refs[2 * NQ]
    outs = refs[2 * NQ + 1 : 3 * NQ + 1]
    g_ref = refs[3 * NQ + 1]
    (wa, wx, x_all, da, dx, rg_s, e1_s, f1_s, g_s, a_s, d_s, c_s, dec_s, acc_s) = refs[3 * NQ + 2 :]
    nblk = PAIR // 128

    lane = lanes_of((WROWS, PAIR))
    w0 = w_ref[0].astype(jnp.float32)
    w1 = w_ref[1].astype(jnp.float32)
    low, high = lane < BLK, (lane >= BLK) & (lane < 2 * BLK)
    tail = jnp.zeros((2 * PAIR - 4 * BLK - 2 * (WROWS - BLK), PAIR), jnp.float32)[: PAIR - BLK - WROWS]
    parts = (
        (wa, jnp.where(low, w0, 0.0), jnp.where(high, pltpu.roll(w1, BLK, 1), 0.0)),
        (wx, jnp.where(low, pltpu.roll(w0, PAIR - BLK, 1), 0.0), jnp.where(high, w1, 0.0)),
    )
    for dst, a0, a1 in parts:
        dst[0:BLK, :] = a0[:BLK].astype(jnp.bfloat16)
        dst[BLK : 2 * BLK, :] = a1[:BLK].astype(jnp.bfloat16)
        dst[2 * BLK : BLK + WROWS, :] = (a0[BLK:] + a1[BLK:]).astype(jnp.bfloat16)
        dst[BLK + WROWS :, :] = tail.astype(jnp.bfloat16)
    dec = parts[0][1][BLK + 1 : BLK + 2] + parts[0][2][BLK + 1 : BLK + 2]
    soft = jnp.maximum(dec, 0.0) + jnp.log1p(jnp.exp(-jnp.abs(dec)))
    dec_s[...] = -8.0 * jnp.broadcast_to(soft, (8, PAIR))

    for s in range(NQ):
        rows = slice(s * SEQ, (s + 1) * SEQ)
        x_all[rows, :] = xs[s][...]
        pre_a = jnp.dot(xs[s][...], wa[...], preferred_element_type=jnp.float32)
        pre_x = jnp.dot(xs[s][...], wx[...], preferred_element_type=jnp.float32)
        for k in range(nblk):
            rg_s[k, rows, :] = pre_a[:, k * 128 : (k + 1) * 128]
            e1_s[k, rows, :] = pre_x[:, k * 128 : (k + 1) * 128]

    for k in range(nblk):
        coef = dec_s[0:1, k * 128 : (k + 1) * 128]
        for s in range(NQ):

            def gates(i, _, k=k, s=s, coef=coef):
                off = pl.multiple_of(i * CHUNK, CHUNK)
                rows = pl.ds(s * SEQ + off, CHUNK)
                x = xs[s][pl.ds(off, CHUNK), k * 128 : (k + 1) * 128].astype(jnp.float32)
                cot = cots[s][pl.ds(off, CHUNK), k * 128 : (k + 1) * 128].astype(jnp.float32)
                rgate = sigmoid(rg_s[k, rows, :])
                igate = sigmoid(e1_s[k, rows, :])
                less = one_minus_exp(coef * rgate)
                a = 1.0 - less
                var = less * (1.0 + a)
                inv = lax.rsqrt(var)
                scale = var * inv
                ix = igate * x
                drive = scale * ix
                c_s[k, rows, :] = cot
                rg_s[k, rows, :] = rgate
                a_s[k, rows, :] = a
                d_s[k, rows, :] = drive
                e1_s[k, rows, :] = ix * (a * inv)
                f1_s[k, rows, :] = drive * (1.0 - igate)
                g_s[k, rows, :] = scale * igate
                return 0

            lax.fori_loop(0, SEQ // CHUNK, gates, 0)

    def scan(t, carry):
        state, back = carry
        state, back = list(state), list(back)
        u = SEQ - 1 - t
        for k in range(nblk):
            here = pl.ds(t, NQ, stride=SEQ)
            a, d = a_s[k, here, :], d_s[k, here, :]
            d_s[k, here, :] = state[k]
            state[k] = a * state[k] + d
        for k in range(nblk):
            here = pl.ds(u, NQ, stride=SEQ)
            adj = c_s[k, here, :] + back[k]
            c_s[k, here, :] = adj
            back[k] = a_s[k, here, :] * adj
        return tuple(state), tuple(back)

    zero = tuple(jnp.zeros((NQ, 128), jnp.float32) for _ in range(nblk))
    lax.fori_loop(0, SEQ, scan, (zero, zero), unroll=8)

    for k in range(nblk):
        coef = dec_s[0:1, k * 128 : (k + 1) * 128]
        acc_s[:, k * 128 : (k + 1) * 128] = jnp.zeros((8, 128), jnp.float32)

        def deltas(i, _, k=k, coef=coef):
            rows = pl.ds(pl.multiple_of(i * CHUNK, CHUNK), CHUNK)
            adj, rgate = c_s[k, rows, :], rg_s[k, rows, :]
            q = adj * a_s[k, rows, :] * (d_s[k, rows, :] - e1_s[k, rows, :]) * rgate
            part = q[0:8]
            for j in range(1, CHUNK // 8):
                part = part + q[j * 8 : (j + 1) * 8]
            acc_s[:, k * 128 : (k + 1) * 128] += part
            da[rows, k * 128 : (k + 1) * 128] = (q * (coef - coef * rgate)).astype(jnp.bfloat16)
            dx[rows, k * 128 : (k + 1) * 128] = (adj * f1_s[k, rows, :]).astype(jnp.bfloat16)
            g_s[k, rows, :] = adj * g_s[k, rows, :]
            return 0

        lax.fori_loop(0, ROWS // CHUNK, deltas, 0)

    nt = (((1,), (1,)), ((), ()))
    tn = (((0,), (0,)), ((), ()))
    for s in range(NQ):
        rows = slice(s * SEQ, (s + 1) * SEQ)
        back = lax.dot_general(da[rows, :], wa[...], nt, preferred_element_type=jnp.float32)
        back += lax.dot_general(dx[rows, :], wx[...], nt, preferred_element_type=jnp.float32)
        for k in range(nblk):
            cols = slice(k * 128, (k + 1) * 128)
            outs[s][:, cols] = (back[:, cols] + g_s[k, rows, :]).astype(jnp.bfloat16)

    grad_a = lax.dot_general(x_all[...], da[...], tn, preferred_element_type=jnp.float32) * factor
    grad_x = lax.dot_general(x_all[...], dx[...], tn, preferred_element_type=jnp.float32) * factor
    dec_row = jnp.sum(acc_s[...], axis=0, keepdims=True) * (-8.0 * factor)
    extra = WROWS - BLK
    row16 = lax.broadcasted_iota(jnp.int32, (extra, PAIR), 0)
    low_a = jnp.where(row16 == 1, dec_row, grad_a[2 * BLK : 2 * BLK + extra])
    low_x = grad_x[2 * BLK : 2 * BLK + extra]
    head0_a = jnp.concatenate([grad_a[:BLK], low_a], axis=0)
    head0_x = jnp.concatenate([grad_x[:BLK], low_x], axis=0)
    head1_a = jnp.concatenate([grad_a[BLK : 2 * BLK], low_a], axis=0)
    head1_x = jnp.concatenate([grad_x[BLK : 2 * BLK], low_x], axis=0)
    first = jnp.where(low, head0_a, jnp.where(high, pltpu.roll(head0_x, BLK, 1), 0.0))
    second = jnp.where(low, pltpu.roll(head1_a, PAIR - BLK, 1), jnp.where(high, head1_x, 0.0))
    g_ref[0] = first.astype(g_ref.dtype)
    g_ref[1] = second.astype(g_ref.dtype)


def params():
    return pltpu.CompilerParams(vmem_limit_bytes=VMEM_LIMIT)


def pack(ones_lane, who, x, interpret=False):
    import functools

    return pl.pallas_call(
        functools.partial(pack_kernel, ones_lane),
        out_shape=[jax.ShapeDtypeStruct((SEQ, NPAIR * PAIR), jnp.bfloat16)] * NQ,
        in_specs=[pl.BlockSpec(memory_space=pltpu.SMEM), pl.BlockSpec(memory_space=pltpu.VMEM)],
        out_specs=[pl.BlockSpec(memory_space=pltpu.VMEM)] * NQ,
        compiler_params=params(),
        interpret=interpret,
    )(who, x)


def unpack(who, pieces, interpret=False):
    return pl.pallas_call(
        unpack_kernel,
        out_shape=jax.ShapeDtypeStruct((SEQ, NZ * NQ * BLK), jnp.bfloat16),
        in_specs=[pl.BlockSpec(memory_space=pltpu.SMEM)] + [pl.BlockSpec(memory_space=pltpu.VMEM)] * NQ,
        out_specs=pl.BlockSpec(memory_space=pltpu.VMEM),
        compiler_params=params(),
        interpret=interpret,
    )(who, *pieces)


def main_call(factor, xs, cots, w, grad_dtype=jnp.bfloat16, interpret=False):
    import functools

    npair = w.shape[0] // 2
    f32, bf16 = jnp.float32, jnp.bfloat16
    big = pltpu.VMEM((PAIR // 128, ROWS, 128), f32)
    tok = pl.BlockSpec((SEQ, PAIR), lambda p: (0, p))
    par = pl.BlockSpec((2, WROWS, PAIR), lambda p: (p, 0, 0))
    return pl.pallas_call(
        functools.partial(main_kernel, factor),
        grid=(npair,),
        out_shape=[jax.ShapeDtypeStruct((SEQ, npair * PAIR), bf16)] * NQ
        + [jax.ShapeDtypeStruct((2 * npair, WROWS, PAIR), grad_dtype)],
        in_specs=[tok] * (2 * NQ) + [par],
        out_specs=[tok] * NQ + [par],
        scratch_shapes=[
            pltpu.VMEM((PAIR, PAIR), bf16),
            pltpu.VMEM((PAIR, PAIR), bf16),
            pltpu.VMEM((ROWS, PAIR), bf16),
            pltpu.VMEM((ROWS, PAIR), bf16),
            pltpu.VMEM((ROWS, PAIR), bf16),
            big, big, big, big, big, big, big,
            pltpu.VMEM((8, PAIR), f32),
            pltpu.VMEM((8, PAIR), f32),
        ],
        compiler_params=params(),
        interpret=interpret,
    )(*xs, *cots, w)


def ring(n, k):
    return [(i, (i + k) % n) for i in range(n)]


def exchange(pieces):
    got = [pieces[0]]
    for k in range(1, NQ):
        perm = [(q, q ^ k) for q in range(NQ)]
        got.append(lax.ppermute(pieces[k], ("yh", "core"), perm))
    return got


def per_device(inputs, cotangent, wa, wx, ba, bx, decay):
    bf16, f32 = jnp.bfloat16, jnp.float32
    who = (lax.axis_index("yh") * NC + lax.axis_index("core")).astype(jnp.int32).reshape(1)
    zero = jnp.zeros((BLK,), bf16)
    tail = jnp.zeros((WROWS - BLK - 2, 2 * BLK), bf16)
    body = jnp.concatenate(
        [
            jnp.concatenate([wa, wx], axis=1),
            jnp.concatenate([ba, bx])[None],
            jnp.concatenate([decay, zero])[None],
            tail,
        ],
        axis=0,
    )
    mine = jnp.pad(body, ((0, 0), (0, PAIR - 2 * BLK)))
    weights = lax.all_gather(mine, "z")
    xs = exchange(pack(1.0, who, inputs))
    cots = exchange(pack(0.0, who, cotangent))
    total = SEQ * lax.axis_size("cuts") * lax.axis_size("z") * NQ
    res = main_call(float(total) ** -0.5, xs, cots, weights, f32)
    input_grad = unpack(who, exchange(res[:NQ]))
    share = lax.psum_scatter(res[NQ], "z", scatter_dimension=0, tiled=True)[0].astype(bf16)
    n = lax.axis_size("cuts")
    got = [share] + [lax.ppermute(share, "cuts", ring(n, k)) for k in range(1, n)]
    full = sum(g.astype(f32) for g in got)
    own = jax.nn.sigmoid(decay.astype(f32))
    return (
        input_grad,
        full[:BLK, :BLK],
        full[:BLK, BLK : 2 * BLK],
        full[BLK, :BLK],
        full[BLK, BLK : 2 * BLK],
        full[BLK + 1, :BLK] * own,
    )


def solution(mesh):
    sizes = dict(mesh.shape)
    fine = Mesh(mesh.devices.reshape(sizes["cuts"], NZ, NY, NC), ("cuts", "z", "yh", "core"))
    zero = ("z", "yh", "core")
    rows = P(("cuts",) + zero, None)
    return jax.shard_map(
        per_device,
        mesh=fine,
        in_specs=(rows, rows, P(zero, None), P(zero, None), P(zero), P(zero), P(zero)),
        out_specs=(rows, P(zero, None), P(zero, None), P(zero), P(zero), P(zero)),
        check_vma=False,
    )
```

time: 976 us -> 163 us (0.17)
  the two profiles are of different devices: /device:TPU:1 before, /device:TPU:22 now
where the time goes in v1:
time: 163 us; the launch traced here: 162 us
  waiting for transfers between devices  73.2 us (45%)
  Pallas kernels  46.8 us (29%)
  starting transfers between devices  20 us (12%)
  between operations  14.2 us (9%)
  local copies, waits for them, and re-layouts  4.6 us (3%)
  other arithmetic  3.5 us (2%)
    reduce_scatter x1, waiting for transfers between devices, per_device(): lax.psum_scatter(res[NQ], 'z', scatter_dimension=0, tiled=True)[0]  41.5 us
    pallas_call x1, Pallas kernels, main_call(): pl.pallas_call(functools.partial(main_kernel, factor), grid=(npair,), out...  33.8 us
    ppermute x9, waiting for transfers between devices, exchange(): got.append(lax.ppermute(pieces[k], ('yh', 'core'), perm))  26.8 us
    ppermute x9, starting transfers between devices, exchange(): got.append(lax.ppermute(pieces[k], ('yh', 'core'), perm))  10.1 us
    ppermute x7, starting transfers between devices, per_device(): lax.ppermute(share, 'cuts', ring(n, k))  9.86 us
    pallas_call x2, Pallas kernels, pack(): pl.pallas_call(functools.partial(pack_kernel, ones_lane), out_shape=[jax....  9.23 us
    ppermute x7, waiting for transfers between devices, per_device(): lax.ppermute(share, 'cuts', ring(n, k))  4.79 us
    pallas_call x1, Pallas kernels, unpack(): pl.pallas_call(unpack_kernel, out_shape=jax.ShapeDtypeStruct((SEQ, NZ * N...  3.82 us
  transfers between devices with their start and end apart: 18, of which 7 were waited for; matrix products, arithmetic and copies ran while one was open for 1% of the time, Pallas kernels for 8%

profile of v1, /device:TPU:22, one launch (start us, length us, event | category | flops | bytes accessed | tf_op | source)
XLA Modules:
  0.0 162.3 jit_solution(1023886577128606439)
XLA Ops:
  7.2 0.0 all-gather.3.cloned.1.call-start
  7.2 0.7 pad_maximum_fusion
  8.0 0.7 concatenate.14
  8.6 0.1 pad.10.clone
  8.7 1.1 maximum_maximum_fusion
  9.8 0.7 pad.5
  10.5 0.0 all-gather.3.cloned.1.call-update
  10.5 0.0 reduce-scatter.2.cloned.1.call-start
  10.5 4.6 %shard_map.118 = (bf16[128,1536]{1,0:T(8,128)(2,1)}, bf16[128,1536]{1,0:T(8,128)(2,1)}, bf16[128,1536]{1,0:T(8,128)(2,1)}, bf16[128,1536]{1,0:T(8,128)(2,1)}) custom-call(s32[1]{0:T(128)} %bitcast.who_ref, bf16[128,5632]{1,0:T(8,128)(2,1)} %x_ref.2), custom_call_target="tpu_custom_call" | custom-call | tf_op jit(solution)/shard_map/pallas_call | solution.py:229
  15.2 0.0 collective-permute-start
  15.2 0.3 collective-permute-start.1
  15.5 3.0 %collective-permute-start.2 = (bf16[128,1536]{1,0:T(8,128)(2,1)}, bf16[128,1536]{1,0:T(8,128)(2,1)S(1)}, u32[]{:S(2)}, u32[]{:S(2)}) collective-permute-start(bf16[128,1536]{1,0:T(8,128)(2,1)} %get-tuple-element.22), channel_id=1, source_target_pairs={{0,3},{1,2},{2,1},{3,0},{4,7},{5,6},{6,5},{7,4},{8,11},{9,10},{10,... | collective-permute-start | bytes 1179656 | tf_op jit(solution)/shard_map/ppermute | solution.py:288
  18.5 4.6 %shard_map.119 = (bf16[128,1536]{1,0:T(8,128)(2,1)}, bf16[128,1536]{1,0:T(8,128)(2,1)}, bf16[128,1536]{1,0:T(8,128)(2,1)}, bf16[128,1536]{1,0:T(8,128)(2,1)}) custom-call(s32[1]{0:T(128)} %bitcast.who_ref, bf16[128,5632]{1,0:T(8,128)(2,1)} %x_ref.3), custom_call_target="tpu_custom_call" | custom-call | tf_op jit(solution)/shard_map/pallas_call | solution.py:229
  23.1 0.3 collective-permute-start.3
  23.4 0.3 collective-permute-start.4
  23.8 0.0 collective-permute-done.refs_1_
  23.8 2.7 %collective-permute-start.5 = (bf16[128,1536]{1,0:T(8,128)(2,1)}, bf16[128,1536]{1,0:T(8,128)(2,1)S(1)}, u32[]{:S(2)}, u32[]{:S(2)}) collective-permute-start(bf16[128,1536]{1,0:T(8,128)(2,1)} %get-tuple-element.26), channel_id=1, source_target_pairs={{0,3},{1,2},{2,1},{3,0},{4,7},{5,6},{6,5},{7,4},{8,11},{9,10},{10,... | collective-permute-start | bytes 1179656 | tf_op jit(solution)/shard_map/ppermute | solution.py:288
  26.5 2.3 %collective-permute-done.1.refs_2_ = bf16[128,1536]{1,0:T(8,128)(2,1)S(1)} collective-permute-done((bf16[128,1536]{1,0:T(8,128)(2,1)}, bf16[128,1536]{1,0:T(8,128)(2,1)S(1)}, u32[]{:S(2)}, u32[]{:S(2)}) %collective-permute-start.1) | collective-permute-done | bytes 393248 | tf_op jit(solution)/shard_map/ppermute | solution.py:288
  28.8 7.7 %collective-permute-done.2.refs_3_ = bf16[128,1536]{1,0:T(8,128)(2,1)S(1)} collective-permute-done((bf16[128,1536]{1,0:T(8,128)(2,1)}, bf16[128,1536]{1,0:T(8,128)(2,1)S(1)}, u32[]{:S(2)}, u32[]{:S(2)}) %collective-permute-start.2) | collective-permute-done | bytes 393248 | tf_op jit(solution)/shard_map/ppermute | solution.py:288
  36.4 0.0 collective-permute-done.3.refs_5_
  36.4 9.2 %collective-permute-done.4.refs_6_ = bf16[128,1536]{1,0:T(8,128)(2,1)S(1)} collective-permute-done((bf16[128,1536]{1,0:T(8,128)(2,1)}, bf16[128,1536]{1,0:T(8,128)(2,1)S(1)}, u32[]{:S(2)}, u32[]{:S(2)}) %collective-permute-start.4) | collective-permute-done | bytes 393248 | tf_op jit(solution)/shard_map/ppermute | solution.py:288
  45.6 7.7 %collective-permute-done.5.refs_7_ = bf16[128,1536]{1,0:T(8,128)(2,1)S(1)} collective-permute-done((bf16[128,1536]{1,0:T(8,128)(2,1)}, bf16[128,1536]{1,0:T(8,128)(2,1)S(1)}, u32[]{:S(2)}, u32[]{:S(2)}) %collective-permute-start.5) | collective-permute-done | bytes 393248 | tf_op jit(solution)/shard_map/ppermute | solution.py:288
  53.3 0.7 copy-done.9
  54.1 33.8 %shard_map.120 = (bf16[128,1536]{1,0:T(8,128)(2,1)}, bf16[128,1536]{1,0:T(8,128)(2,1)}, bf16[128,1536]{1,0:T(8,128)(2,1)}, bf16[128,1536]{1,0:T(8,128)(2,1)}, f32[8,192,384]{2,1,0:T(8,128)}) custom-call(bf16[128,1536]{1,0:T(8,128)(2,1)} %get-tuple-element.19.refs_0_, bf16[128,1536]{1,0:T(8,128)(2,1)} %copy-done.1, bf16[128,1536]{1,0:T(8,128)(2,1)} %copy-done.3, ...), custom_call_target="tpu_custom_call" | custom-call | tf_op jit(solution)/shard_map/pallas_call | solution.py:258
  87.9 0.0 reduce-scatter.2.cloned.1.call-update
  87.9 0.9 copy-done.13
  88.9 0.2 collective-permute-start.6
  89.1 0.4 collective-permute-start.7
  89.4 2.8 %collective-permute-start.8 = (bf16[128,1536]{1,0:T(8,128)(2,1)S(1)}, bf16[128,1536]{1,0:T(8,128)(2,1)S(1)}, u32[]{:S(2)}, u32[]{:S(2)}) collective-permute-start(bf16[128,1536]{1,0:T(8,128)(2,1)S(1)} %copy-done.11), channel_id=1, source_target_pairs={{0,3},{1,2},{2,1},{3,0},{4,7},{5,6},{6,5},{7,4},{8,11},{9,10},{10,... | collective-permute-start | bytes 1179656 | tf_op jit(solution)/shard_map/ppermute | solution.py:288
  92.2 41.5 %reduce-scatter.2.cloned.1.call-done = f32[1,192,384]{2,1,0:T(8,128)} async-done(((f32[8,192,384]{2,1,0:T(8,128)}), f32[1,192,384]{2,1,0:T(8,128)}) %reduce-scatter.2.cloned.1.call-update) | async-done | bytes 294928 | tf_op jit(solution)/shard_map/reduce_scatter | solution.py:313
  133.8 1.0 convert_bitcast_fusion
  134.8 1.1 collective-permute-start.14
  135.9 1.7 %collective-permute-start.13 = (bf16[192,384]{1,0:T(8,128)(2,1)S(1)}, bf16[192,384]{1,0:T(8,128)(2,1)S(1)}, u32[]{:S(2)}, u32[]{:S(2)}) collective-permute-start(bf16[192,384]{1,0:T(8,128)(2,1)S(1)} %convert_bitcast_fusion), channel_id=1, source_target_pairs={{0,160},{32,192},{64,224},{96,0},{128,32},{160,64},{192,96},{224,1... | collective-permute-start | bytes 442376 | tf_op jit(solution)/shard_map/ppermute | solution.py:315
  137.6 2.3 %collective-permute-start.12 = (bf16[192,384]{1,0:T(8,128)(2,1)S(1)}, bf16[192,384]{1,0:T(8,128)(2,1)S(1)}, u32[]{:S(2)}, u32[]{:S(2)}) collective-permute-start(bf16[192,384]{1,0:T(8,128)(2,1)S(1)} %convert_bitcast_fusion), channel_id=1, source_target_pairs={{0,128},{32,160},{64,192},{96,224},{128,0},{160,32},{192,64},{224,... | collective-permute-start | bytes 442376 | tf_op jit(solution)/shard_map/ppermute | solution.py:315
  139.9 0.4 collective-permute-start.11
  140.4 2.1 %collective-permute-start.10 = (bf16[192,384]{1,0:T(8,128)(2,1)S(1)}, bf16[192,384]{1,0:T(8,128)(2,1)S(1)}, u32[]{:S(2)}, u32[]{:S(2)}) collective-permute-start(bf16[192,384]{1,0:T(8,128)(2,1)S(1)} %convert_bitcast_fusion), channel_id=1, source_target_pairs={{0,64},{32,96},{64,128},{96,160},{128,192},{160,224},{192,0},{224,... | collective-permute-start | bytes 442376 | tf_op jit(solution)/shard_map/ppermute | solution.py:315
  142.5 0.0 collective-permute-done.14
  142.5 2.2 %collective-permute-start.9 = (bf16[192,384]{1,0:T(8,128)(2,1)S(1)}, bf16[192,384]{1,0:T(8,128)(2,1)S(1)}, u32[]{:S(2)}, u32[]{:S(2)}) collective-permute-start(bf16[192,384]{1,0:T(8,128)(2,1)S(1)} %convert_bitcast_fusion), channel_id=1, source_target_pairs={{0,32},{32,64},{64,96},{96,128},{128,160},{160,192},{192,224},{224... | collective-permute-start | bytes 442376 | tf_op jit(solution)/shard_map/ppermute | solution.py:315
  144.6 3.5 %collective-permute-done.13 = bf16[192,384]{1,0:T(8,128)(2,1)S(1)} collective-permute-done((bf16[192,384]{1,0:T(8,128)(2,1)S(1)}, bf16[192,384]{1,0:T(8,128)(2,1)S(1)}, u32[]{:S(2)}, u32[]{:S(2)}) %collective-permute-start.13) | collective-permute-done | bytes 147488 | tf_op jit(solution)/shard_map/ppermute | solution.py:315
  148.2 0.0 collective-permute-start.15
  148.2 3.8 %shard_map.121 = bf16[128,5632]{1,0:T(8,128)(2,1)} custom-call(s32[1]{0:T(128)} %bitcast.who_ref, bf16[128,1536]{1,0:T(8,128)(2,1)} %get-tuple-element.27.refs_0_, bf16[128,1536]{1,0:T(8,128)(2,1)} %copy-done.2, bf16[128,1536]{1,0:T(8,128)(2,1)} %copy-done.4, bf16[128,1536]{1,0:T(8,128)(2,1)} %copy-done.6), custom_call_target="tpu_custom_call" | custom-call | tf_op jit(solution)/shard_map/pallas_call | solution.py:240
  152.0 0.0 collective-permute-done.10
  152.0 0.0 collective-permute-done.9
  152.0 1.3 collective-permute-done.15
  153.3 0.1 convert_add_fusion
  153.4 0.6 fusion
  154.1 0.8 fusion.1
  154.9 0.6 divide_multiply_fusion
  (35 shorter events, 0.1 us)
Async XLA Ops:
  7.2 46.1 %all-gather.3.cloned.1.call-start = ((), (), s32[]{:S(2)}) async-start(), calls=%async_computation.2 | async-start | bytes 1327104 | tf_op jit(solution)/shard_map/all_gather | solution.py:307
  10.5 123.3 %reduce-scatter.2.cloned.1.call-start = ((), (), s32[]{:S(2)}) async-start(), calls=%async_computation.1 | async-start | bytes 2654208 | tf_op jit(solution)/shard_map/reduce_scatter | solution.py:313
  15.2 8.6 %collective-permute-start = (bf16[128,1536]{1,0:T(8,128)(2,1)}, bf16[128,1536]{1,0:T(8,128)(2,1)S(1)}, u32[]{:S(2)}, u32[]{:S(2)}) collective-permute-start(bf16[128,1536]{1,0:T(8,128)(2,1)} %get-tuple-element.20), channel_id=1, source_target_pairs={{0,1},{1,0},{2,3},{3,2},{4,5},{5,4},{6,7},{7,6},{8,9},{9,8},{10,11... | collective-permute-start | bytes 1179656 | tf_op jit(solution)/shard_map/ppermute | solution.py:288
  15.2 13.6 %collective-permute-start.1 = (bf16[128,1536]{1,0:T(8,128)(2,1)}, bf16[128,1536]{1,0:T(8,128)(2,1)S(1)}, u32[]{:S(2)}, u32[]{:S(2)}) collective-permute-start(bf16[128,1536]{1,0:T(8,128)(2,1)} %get-tuple-element.21), channel_id=1, source_target_pairs={{0,2},{1,3},{2,0},{3,1},{4,6},{5,7},{6,4},{7,5},{8,10},{9,11},{10,... | collective-permute-start | bytes 1179656 | tf_op jit(solution)/shard_map/ppermute | solution.py:288
  15.5 20.9 %collective-permute-start.2 = (bf16[128,1536]{1,0:T(8,128)(2,1)}, bf16[128,1536]{1,0:T(8,128)(2,1)S(1)}, u32[]{:S(2)}, u32[]{:S(2)}) collective-permute-start(bf16[128,1536]{1,0:T(8,128)(2,1)} %get-tuple-element.22), channel_id=1, source_target_pairs={{0,3},{1,2},{2,1},{3,0},{4,7},{5,6},{6,5},{7,4},{8,11},{9,10},{10,... | collective-permute-start | bytes 1179656 | tf_op jit(solution)/shard_map/ppermute | solution.py:288
  23.1 13.3 %collective-permute-start.3 = (bf16[128,1536]{1,0:T(8,128)(2,1)}, bf16[128,1536]{1,0:T(8,128)(2,1)S(1)}, u32[]{:S(2)}, u32[]{:S(2)}) collective-permute-start(bf16[128,1536]{1,0:T(8,128)(2,1)} %get-tuple-element.24), channel_id=1, source_target_pairs={{0,1},{1,0},{2,3},{3,2},{4,5},{5,4},{6,7},{7,6},{8,9},{9,8},{10,11... | collective-permute-start | bytes 1179656 | tf_op jit(solution)/shard_map/ppermute | solution.py:288
  23.4 22.2 %collective-permute-start.4 = (bf16[128,1536]{1,0:T(8,128)(2,1)}, bf16[128,1536]{1,0:T(8,128)(2,1)S(1)}, u32[]{:S(2)}, u32[]{:S(2)}) collective-permute-start(bf16[128,1536]{1,0:T(8,128)(2,1)} %get-tuple-element.25), channel_id=1, source_target_pairs={{0,2},{1,3},{2,0},{3,1},{4,6},{5,7},{6,4},{7,5},{8,10},{9,11},{10,... | collective-permute-start | bytes 1179656 | tf_op jit(solution)/shard_map/ppermute | solution.py:288
  23.8 29.5 %copy-start.1 = (bf16[128,1536]{1,0:T(8,128)(2,1)}, bf16[128,1536]{1,0:T(8,128)(2,1)S(1)}, u32[]{:S(2)}) copy-start(bf16[128,1536]{1,0:T(8,128)(2,1)S(1)} %collective-permute-done.refs_1_) | copy-start | bytes 1179652
  23.8 29.5 %collective-permute-start.5 = (bf16[128,1536]{1,0:T(8,128)(2,1)}, bf16[128,1536]{1,0:T(8,128)(2,1)S(1)}, u32[]{:S(2)}, u32[]{:S(2)}) collective-permute-start(bf16[128,1536]{1,0:T(8,128)(2,1)} %get-tuple-element.26), channel_id=1, source_target_pairs={{0,3},{1,2},{2,1},{3,0},{4,7},{5,6},{6,5},{7,4},{8,11},{9,10},{10,... | collective-permute-start | bytes 1179656 | tf_op jit(solution)/shard_map/ppermute | solution.py:288
  28.8 24.5 %copy-start.3 = (bf16[128,1536]{1,0:T(8,128)(2,1)}, bf16[128,1536]{1,0:T(8,128)(2,1)S(1)}, u32[]{:S(2)}) copy-start(bf16[128,1536]{1,0:T(8,128)(2,1)S(1)} %collective-permute-done.1.refs_2_) | copy-start | bytes 1179652
  36.4 16.9 %copy-start.5 = (bf16[128,1536]{1,0:T(8,128)(2,1)}, bf16[128,1536]{1,0:T(8,128)(2,1)S(1)}, u32[]{:S(2)}) copy-start(bf16[128,1536]{1,0:T(8,128)(2,1)S(1)} %collective-permute-done.2.refs_3_) | copy-start | bytes 1179652
  36.4 16.9 %copy-start.7 = (bf16[128,1536]{1,0:T(8,128)(2,1)}, bf16[128,1536]{1,0:T(8,128)(2,1)S(1)}, u32[]{:S(2)}) copy-start(bf16[128,1536]{1,0:T(8,128)(2,1)S(1)} %collective-permute-done.3.refs_5_) | copy-start | bytes 1179652
  45.6 7.7 %copy-start.8 = (bf16[128,1536]{1,0:T(8,128)(2,1)}, bf16[128,1536]{1,0:T(8,128)(2,1)S(1)}, u32[]{:S(2)}) copy-start(bf16[128,1536]{1,0:T(8,128)(2,1)S(1)} %collective-permute-done.4.refs_6_) | copy-start | bytes 1179652
  53.3 0.8 copy-start.9
  87.9 1.0 copy-start.13
  87.9 1.2 copy-start.12
  87.9 1.6 copy-start.11
  88.9 48.7 %collective-permute-start.6 = (bf16[128,1536]{1,0:T(8,128)(2,1)S(1)}, bf16[128,1536]{1,0:T(8,128)(2,1)S(1)}, u32[]{:S(2)}, u32[]{:S(2)}) collective-permute-start(bf16[128,1536]{1,0:T(8,128)(2,1)S(1)} %copy-done.13), channel_id=1, source_target_pairs={{0,1},{1,0},{2,3},{3,2},{4,5},{5,4},{6,7},{7,6},{8,9},{9,8},{10,11... | collective-permute-start | bytes 1179656 | tf_op jit(solution)/shard_map/ppermute | solution.py:288
  89.1 50.8 %collective-permute-start.7 = (bf16[128,1536]{1,0:T(8,128)(2,1)S(1)}, bf16[128,1536]{1,0:T(8,128)(2,1)S(1)}, u32[]{:S(2)}, u32[]{:S(2)}) collective-permute-start(bf16[128,1536]{1,0:T(8,128)(2,1)S(1)} %copy-done.12), channel_id=1, source_target_pairs={{0,2},{1,3},{2,0},{3,1},{4,6},{5,7},{6,4},{7,5},{8,10},{9,11},{10,... | collective-permute-start | bytes 1179656 | tf_op jit(solution)/shard_map/ppermute | solution.py:288
  89.4 50.9 %collective-permute-start.8 = (bf16[128,1536]{1,0:T(8,128)(2,1)S(1)}, bf16[128,1536]{1,0:T(8,128)(2,1)S(1)}, u32[]{:S(2)}, u32[]{:S(2)}) collective-permute-start(bf16[128,1536]{1,0:T(8,128)(2,1)S(1)} %copy-done.11), channel_id=1, source_target_pairs={{0,3},{1,2},{2,1},{3,0},{4,7},{5,6},{6,5},{7,4},{8,11},{9,10},{10,... | collective-permute-start | bytes 1179656 | tf_op jit(solution)/shard_map/ppermute | solution.py:288
  134.8 7.7 %collective-permute-start.14 = (bf16[192,384]{1,0:T(8,128)(2,1)S(1)}, bf16[192,384]{1,0:T(8,128)(2,1)S(1)}, u32[]{:S(2)}, u32[]{:S(2)}) collective-permute-start(bf16[192,384]{1,0:T(8,128)(2,1)S(1)} %convert_bitcast_fusion), channel_id=1, source_target_pairs={{0,192},{32,224},{64,0},{96,32},{128,64},{160,96},{192,128},{224,1... | collective-permute-start | bytes 442376 | tf_op jit(solution)/shard_map/ppermute | solution.py:315
  135.9 12.3 %collective-permute-start.13 = (bf16[192,384]{1,0:T(8,128)(2,1)S(1)}, bf16[192,384]{1,0:T(8,128)(2,1)S(1)}, u32[]{:S(2)}, u32[]{:S(2)}) collective-permute-start(bf16[192,384]{1,0:T(8,128)(2,1)S(1)} %convert_bitcast_fusion), channel_id=1, source_target_pairs={{0,160},{32,192},{64,224},{96,0},{128,32},{160,64},{192,96},{224,1... | collective-permute-start | bytes 442376 | tf_op jit(solution)/shard_map/ppermute | solution.py:315
  137.6 10.6 %copy-start.2 = (bf16[128,1536]{1,0:T(8,128)(2,1)}, bf16[128,1536]{1,0:T(8,128)(2,1)S(1)}, u32[]{:S(2)}) copy-start(bf16[128,1536]{1,0:T(8,128)(2,1)S(1)} %collective-permute-done.6.refs_1_) | copy-start | bytes 1179652
  137.6 14.4 %collective-permute-start.12 = (bf16[192,384]{1,0:T(8,128)(2,1)S(1)}, bf16[192,384]{1,0:T(8,128)(2,1)S(1)}, u32[]{:S(2)}, u32[]{:S(2)}) collective-permute-start(bf16[192,384]{1,0:T(8,128)(2,1)S(1)} %convert_bitcast_fusion), channel_id=1, source_target_pairs={{0,128},{32,160},{64,192},{96,224},{128,0},{160,32},{192,64},{224,... | collective-permute-start | bytes 442376 | tf_op jit(solution)/shard_map/ppermute | solution.py:315
  139.9 8.3 %copy-start.4 = (bf16[128,1536]{1,0:T(8,128)(2,1)}, bf16[128,1536]{1,0:T(8,128)(2,1)S(1)}, u32[]{:S(2)}) copy-start(bf16[128,1536]{1,0:T(8,128)(2,1)S(1)} %collective-permute-done.7.refs_2_) | copy-start | bytes 1179652
  139.9 12.1 %collective-permute-start.11 = (bf16[192,384]{1,0:T(8,128)(2,1)S(1)}, bf16[192,384]{1,0:T(8,128)(2,1)S(1)}, u32[]{:S(2)}, u32[]{:S(2)}) collective-permute-start(bf16[192,384]{1,0:T(8,128)(2,1)S(1)} %convert_bitcast_fusion), channel_id=1, source_target_pairs={{0,96},{32,128},{64,160},{96,192},{128,224},{160,0},{192,32},{224,... | collective-permute-start | bytes 442376 | tf_op jit(solution)/shard_map/ppermute | solution.py:315
  140.4 7.8 %copy-start.6 = (bf16[128,1536]{1,0:T(8,128)(2,1)}, bf16[128,1536]{1,0:T(8,128)(2,1)S(1)}, u32[]{:S(2)}) copy-start(bf16[128,1536]{1,0:T(8,128)(2,1)S(1)} %collective-permute-done.8.refs_3_) | copy-start | bytes 1179652
  140.4 11.7 %collective-permute-start.10 = (bf16[192,384]{1,0:T(8,128)(2,1)S(1)}, bf16[192,384]{1,0:T(8,128)(2,1)S(1)}, u32[]{:S(2)}, u32[]{:S(2)}) collective-permute-start(bf16[192,384]{1,0:T(8,128)(2,1)S(1)} %convert_bitcast_fusion), channel_id=1, source_target_pairs={{0,64},{32,96},{64,128},{96,160},{128,192},{160,224},{192,0},{224,... | collective-permute-start | bytes 442376 | tf_op jit(solution)/shard_map/ppermute | solution.py:315
  142.5 9.6 %collective-permute-start.9 = (bf16[192,384]{1,0:T(8,128)(2,1)S(1)}, bf16[192,384]{1,0:T(8,128)(2,1)S(1)}, u32[]{:S(2)}, u32[]{:S(2)}) collective-permute-start(bf16[192,384]{1,0:T(8,128)(2,1)S(1)} %convert_bitcast_fusion), channel_id=1, source_target_pairs={{0,32},{32,64},{64,96},{96,128},{128,160},{160,192},{192,224},{224... | collective-permute-start | bytes 442376 | tf_op jit(solution)/shard_map/ppermute | solution.py:315
  148.2 5.1 %collective-permute-start.15 = (bf16[192,384]{1,0:T(8,128)(2,1)S(1)}, bf16[192,384]{1,0:T(8,128)(2,1)S(1)}, u32[]{:S(2)}, u32[]{:S(2)}) collective-permute-start(bf16[192,384]{1,0:T(8,128)(2,1)S(1)} %convert_bitcast_fusion), channel_id=1, source_target_pairs={{0,224},{32,0},{64,32},{96,64},{128,96},{160,128},{192,160},{224,1... | collective-permute-start | bytes 442376 | tf_op jit(solution)/shard_map/ppermute | solution.py:315
  148.2 5.1 %copy-start = (f32[1,192,384]{2,1,0:T(8,128)S(1)}, f32[1,192,384]{2,1,0:T(8,128)}, u32[]{:S(2)}) copy-start(f32[1,192,384]{2,1,0:T(8,128)} %reduce-scatter.2.cloned.1.call-done) | copy-start | bytes 884740
  152.0 2.9 %copy-start.10 = (bf16[176]{0:T(256)(128)(2,1)S(1)}, bf16[176]{0:T(256)(128)(2,1)}, u32[]{:S(2)}) copy-start(bf16[176]{0:T(256)(128)(2,1)} %param.13) | copy-start | bytes 1060
Sparse Core Ops, SparseCore 0:
  10.6 41.8 all-gather.2
  88.0 45.6 reduce-scatter.1

commit v2 on v0

v2 whole, which is shorter than its diff:
```python
import functools

import jax
import jax.numpy as jnp
from jax import lax
from jax.experimental import pallas as pl
from jax.experimental.pallas import tpu as pltpu
from jax.sharding import Mesh
from jax.sharding import PartitionSpec as P

BLK = 176
TWO = 2 * BLK
WROWS = 192
WCOLS = 384
NZ, NY, NC = 8, 2, 2
NQ = NY * NC
NI = 8
SEQ = 128
NSEQ = NI * NQ
STEP = 8
VMEM_LIMIT = 56 * 1024 * 1024


def pack_kernel(z_ref, x_ref, out_ref, turned):
    half = pl.program_id(1)

    @pl.when(half == 0)
    def _():
        turned[...] = x_ref[...].T

    rows = pl.ds(pl.multiple_of(half * NQ * BLK, 16), NQ * BLK)
    out_ref[...] = turned[rows, :].reshape(NQ, BLK, SEQ)


def unpack_kernel(z_ref, in_ref, out_ref, turned):
    half = pl.program_id(1)
    rows = pl.ds(pl.multiple_of(half * NQ * BLK, 16), NQ * BLK)
    turned[rows, :] = in_ref[...].reshape(NQ * BLK, SEQ)

    @pl.when(half == 1)
    def _():
        out_ref[...] = turned[...].T


def params():
    return pltpu.CompilerParams(vmem_limit_bytes=VMEM_LIMIT)


def turn_specs():
    wide = pl.BlockSpec((SEQ, 2 * NQ * BLK), lambda p, j, z: (0, p))
    tall = pl.BlockSpec((NQ, BLK, SEQ), lambda p, j, z: (lax.rem(2 * p + j + NZ - z[0], NZ), 0, 0))
    return wide, tall


def pack(z, x, interpret=False):
    wide, tall = turn_specs()
    return pl.pallas_call(
        pack_kernel,
        grid_spec=pltpu.PrefetchScalarGridSpec(
            num_scalar_prefetch=1,
            grid=(NZ // 2, 2),
            in_specs=[wide],
            out_specs=tall,
            scratch_shapes=[pltpu.VMEM((2 * NQ * BLK, SEQ), x.dtype)],
        ),
        out_shape=jax.ShapeDtypeStruct((NSEQ, BLK, SEQ), x.dtype),
        compiler_params=params(),
        interpret=interpret,
    )(z, x)


def unpack(z, y, interpret=False):
    wide, tall = turn_specs()
    return pl.pallas_call(
        unpack_kernel,
        grid_spec=pltpu.PrefetchScalarGridSpec(
            num_scalar_prefetch=1,
            grid=(NZ // 2, 2),
            in_specs=[tall],
            out_specs=wide,
            scratch_shapes=[pltpu.VMEM((2 * NQ * BLK, SEQ), y.dtype)],
        ),
        out_shape=jax.ShapeDtypeStruct((SEQ, NSEQ * BLK), y.dtype),
        compiler_params=params(),
        interpret=interpret,
    )(z, y)


def sigmoid(pre):
    base = 1.0 + jnp.exp(jnp.minimum(-pre, 80.0))
    rough = pl.reciprocal(base, approx=True)
    return rough * (2.0 - base * rough)


def one_minus_exp(log_a):
    series = -1.0 / 720.0
    for c in (-1.0 / 120.0, -1.0 / 24.0, -1.0 / 6.0, -0.5, -1.0):
        series = series * log_a + c
    return jnp.where(log_a > -0.25, series * log_a, 1.0 - jnp.exp(log_a))


CH = 16


def main_kernel(factor, x_ref, c_ref, w_ref, wt_ref, coef_ref, out_ref, g_ref, x_s, pre_s, d_s, q_s, g_s):
    step = pl.program_id(0)

    @pl.when(step == 0)
    def _():
        row = lax.broadcasted_iota(jnp.int32, (WROWS - BLK, STEP * SEQ), 0)
        x_s[BLK:, :] = jnp.where(row == 0, 1.0, 0.0).astype(x_s.dtype)
        q_s[...] = jnp.zeros_like(q_s)
        g_s[...] = jnp.zeros_like(g_s)

    for s in range(STEP):
        x_s[:BLK, s * SEQ : (s + 1) * SEQ] = x_ref[s]
    pre_s[...] = jnp.dot(wt_ref[...], x_s[...], preferred_element_type=jnp.float32)

    def one(s, _):
        cols = pl.ds(pl.multiple_of(s * SEQ, SEQ), SEQ)
        lane = lax.broadcasted_iota(jnp.int32, (CH, SEQ), 1)
        for r in range(0, BLK, CH):
            rows, more = slice(r, r + CH), slice(BLK + r, BLK + r + CH)
            coef = coef_ref[rows, :]
            x = x_ref[s, rows, :].astype(jnp.float32)
            adj = c_ref[s, rows, :].astype(jnp.float32)
            rgate = sigmoid(pre_s[rows, cols])
            igate = sigmoid(pre_s[more, cols])
            less = one_minus_exp(coef * rgate)
            a = 1.0 - less
            var = less * (1.0 + a)
            inv = lax.rsqrt(var)
            scale = var * inv
            ix = igate * x
            drive = scale * ix
            own = ix * (a * a * inv)
            a_first = jnp.where(lane == 0, 0.0, a)
            prod, state = a_first, drive
            for k in range(7):
                d = 1 << k
                adj = adj + pltpu.roll(prod * adj, SEQ - d, 1)
                state = state + prod * pltpu.roll(state, d, 1)
                if k < 6:
                    prod = prod * pltpu.roll(prod, d, 1)
            q = adj * (a_first * pltpu.roll(state, 1, 1) - own) * rgate
            q_s[rows, :] += q
            d_s[rows, cols] = (q * (coef - coef * rgate)).astype(jnp.bfloat16)
            d_s[more, cols] = (adj * (drive * (1.0 - igate))).astype(jnp.bfloat16)
            pre_s[rows, cols] = adj * (scale * igate)
        return 0

    lax.fori_loop(0, STEP, one, 0)

    back = jnp.dot(w_ref[:BLK, :TWO], d_s[...], preferred_element_type=jnp.float32)
    for s in range(STEP):
        cols = slice(s * SEQ, (s + 1) * SEQ)
        out_ref[s] = (back[:, cols] + pre_s[:BLK, cols]).astype(out_ref.dtype)
    nt = (((1,), (1,)), ((), ()))
    g_s[:, :TWO] += lax.dot_general(x_s[...], d_s[...], nt, preferred_element_type=jnp.float32)

    @pl.when(step == pl.num_programs(0) - 1)
    def _():
        g_ref[...] = (g_s[...] * factor).astype(g_ref.dtype)
        decay = jnp.sum(q_s[...].T, axis=0, keepdims=True) * (-8.0 * factor)
        tail = g_s[BLK:, :BLK] * factor
        row = lax.broadcasted_iota(jnp.int32, tail.shape, 0)
        g_ref[BLK:, :BLK] = jnp.where(row == 1, decay, tail).astype(g_ref.dtype)


def main_call(factor, x, c, w, wt, coef, grad_dtype=jnp.bfloat16, interpret=False):
    f32, bf16 = jnp.float32, jnp.bfloat16
    n = x.shape[0]
    tok = pl.BlockSpec((STEP, BLK, SEQ), lambda p: (p, 0, 0))
    full = lambda shape: pl.BlockSpec(shape, lambda p: (0, 0))
    return pl.pallas_call(
        functools.partial(main_kernel, factor),
        grid=(n // STEP,),
        out_shape=[
            jax.ShapeDtypeStruct((n, BLK, SEQ), bf16),
            jax.ShapeDtypeStruct((WROWS, WCOLS), grad_dtype),
        ],
        in_specs=[tok, tok, full((WROWS, WCOLS)), full((TWO, WROWS)), full((BLK, SEQ))],
        out_specs=[tok, full((WROWS, WCOLS))],
        scratch_shapes=[
            pltpu.VMEM((WROWS, STEP * SEQ), bf16),
            pltpu.VMEM((TWO, STEP * SEQ), f32),
            pltpu.VMEM((TWO, STEP * SEQ), bf16),
            pltpu.VMEM((BLK, SEQ), f32),
            pltpu.VMEM((WROWS, WCOLS), f32),
        ],
        compiler_params=params(),
        interpret=interpret,
    )(x, c, w, wt, coef)


def wire(wa, wx, ba, bx, decay):
    bf16 = jnp.bfloat16
    tail = jnp.zeros((WROWS - BLK - 2, TWO), bf16)
    body = jnp.concatenate(
        [
            jnp.concatenate([wa, wx], axis=1),
            jnp.concatenate([ba, bx])[None],
            jnp.concatenate([decay, jnp.zeros((BLK,), bf16)])[None],
            tail,
        ],
        axis=0,
    )
    return jnp.pad(body, ((0, 0), (0, WCOLS - TWO)))


def unwire(w):
    wt = w[:, :TWO].T
    coef = -8.0 * jax.nn.softplus(w[BLK + 1, :BLK].astype(jnp.float32))
    return wt, jnp.broadcast_to(coef[:, None], (BLK, SEQ))


def per_device(inputs, cotangent, wa, wx, ba, bx, decay):
    bf16, f32 = jnp.bfloat16, jnp.float32
    plane, line = ("cuts", "yh", "core"), ("cuts", "z")
    z = lax.axis_index("z").astype(jnp.int32).reshape(1)
    pairs = [(i, k, (k + i) % NZ) for i in range(NI) for k in range(NZ)]
    fetch = [(i * NZ + src, i * NZ + k) for i, k, src in pairs]
    home = [(b, a) for a, b in fetch]

    x = lax.all_to_all(pack(z, inputs), plane, 0, 0, tiled=True)
    w = lax.ppermute(wire(wa, wx, ba, bx, decay), line, fetch)
    c = lax.all_to_all(pack(z, cotangent), plane, 0, 0, tiled=True)
    wt, coef = unwire(w)
    total = SEQ * NSEQ * NZ
    out, grads = main_call(float(total) ** -0.5, x, c, w, wt, coef)
    input_grad = unpack(z, lax.all_to_all(out, plane, 0, 0, tiled=True))
    share = lax.ppermute(grads, line, home)
    parts = lax.all_to_all(jnp.broadcast_to(share, (NI, WROWS, WCOLS)), "cuts", 0, 0, tiled=True)
    full = jnp.sum(parts.astype(f32), axis=0)
    own = jax.nn.sigmoid(decay.astype(f32))
    return (
        input_grad,
        full[:BLK, :BLK],
        full[:BLK, BLK:TWO],
        full[BLK, :BLK],
        full[BLK, BLK:TWO],
        full[BLK + 1, :BLK] * own,
    )


def solution(mesh):
    fine = Mesh(mesh.devices.reshape(NI, NZ, NY, NC), ("cuts", "z", "yh", "core"))
    zero = ("z", "yh", "core")
    rows = P(("cuts",) + zero, None)
    return jax.shard_map(
        per_device,
        mesh=fine,
        in_specs=(rows, rows, P(zero, None), P(zero, None), P(zero), P(zero), P(zero)),
        out_specs=(rows, P(zero, None), P(zero, None), P(zero), P(zero), P(zero)),
        check_vma=False,
    )
```

time: 976 us -> 167 us (0.17)
  waiting for transfers between devices: 554 us -> 51.4 us
  local copies, waits for them, and re-layouts: 185 us -> 6.94 us
  blocking collectives: 148 us -> 34.7 us
  Pallas kernels: 0 us -> 46.8 us
  other arithmetic: 33.8 us -> 1.13 us
  matrix products: 31.1 us -> 0 us
  starting transfers between devices: 0.24 us -> 23.6 us
  between operations: 15.6 us -> 0.82 us
    reduce_scatter x2 -> x0, waiting for transfers between devices: 240 us -> none  [the longest x1 137 us: per_device(): lax.psum_scatter(grad_wx, 'zero', scatter_dimension=0, tiled=True)]
    unnamed x7 -> x0, waiting for transfers between devices: 235 us -> none
    unnamed x1 -> x0, blocking collectives: 132 us -> none
    slice x33 -> x2, local copies, waits for them, and re-layouts: 108 us -> 1.42 us  [the longest x1 0.79 us: per_device(): full[:BLK, BLK:TWO]]
    psum x1 -> x0, waiting for transfers between devices: 56.3 us -> none  [per_device(): lax.psum((shares[0], shares[1], shares[2], shares[3], shares[4]), 'cuts')]
    all_to_all x0 -> x3, waiting for transfers between devices: none -> 51.4 us  [the longest x1 18.7 us: per_device(): input_grad = unpack(z, lax.all_to_all(out, plane, 0, 0, tiled=True))]
    pallas_call x0 -> x4, Pallas kernels: none -> 46.8 us  [the longest x1 29.5 us: main_call(): pl.pallas_call(functools.partial(main_kernel, factor), grid=(n // STEP,),...]
    all_to_all x0 -> x1, blocking collectives: none -> 34.7 us  [per_device(): lax.all_to_all(jnp.broadcast_to(share, (NI, WROWS, WCOLS)), 'cuts', 0, 0,...]
  transfers between devices with their start and end apart: 6 -> 5, of which waited for: 5 -> 3; matrix products, arithmetic and copies ran while one was open for 5% -> 3% of each run, Pallas kernels for 0% -> 4%
where the time goes in v2:
time: 167 us; the launch traced here: 165 us
  waiting for transfers between devices  51.4 us (31%)
  Pallas kernels  46.8 us (28%)
  blocking collectives  34.7 us (21%)
  starting transfers between devices  23.6 us (14%)
  local copies, waits for them, and re-layouts  6.94 us (4%)
    all_to_all x1, blocking collectives, per_device(): lax.all_to_all(jnp.broadcast_to(share, (NI, WROWS, WCOLS)), 'cuts', 0, 0,...  34.7 us
    pallas_call x1, Pallas kernels, main_call(): pl.pallas_call(functools.partial(main_kernel, factor), grid=(n // STEP,),...  29.5 us
    all_to_all x1, waiting for transfers between devices, per_device(): input_grad = unpack(z, lax.all_to_all(out, plane, 0, 0, tiled=True))  18.7 us
    all_to_all x1, waiting for transfers between devices, per_device(): c = lax.all_to_all(pack(z, cotangent), plane, 0, 0, tiled=True)  17.7 us
    all_to_all x1, waiting for transfers between devices, per_device(): x = lax.all_to_all(pack(z, inputs), plane, 0, 0, tiled=True)  15 us
    pallas_call x2, Pallas kernels, pack(): pl.pallas_call(pack_kernel, grid_spec=pltpu.PrefetchScalarGridSpec(num_sc...  11.6 us
    all_to_all x1, starting transfers between devices, per_device(): input_grad = unpack(z, lax.all_to_all(out, plane, 0, 0, tiled=True))  8.61 us
    all_to_all x1, starting transfers between devices, per_device(): x = lax.all_to_all(pack(z, inputs), plane, 0, 0, tiled=True)  8.59 us
  transfers between devices with their start and end apart: 5, of which 3 were waited for; matrix products, arithmetic and copies ran while one was open for 3% of the time, Pallas kernels for 4%

profile of v2, /device:TPU:1, one launch (start us, length us, event | category | flops | bytes accessed | tf_op | source)
XLA Modules:
  0.0 165.5 jit_solution(11302460376509727626)
XLA Ops:
  0.6 5.8 %shard_map.118 = bf16[32,176,128]{2,1,0:T(8,128)(2,1)} custom-call(s32[1]{0:T(128)} %bitcast.z_ref, bf16[128,5632]{1,0:T(8,128)(2,1)} %x_ref.2), custom_call_target="tpu_custom_call" | custom-call | tf_op jit(solution)/shard_map/pallas_call | solution.py:57
  6.4 8.6 %all-to-all-start = ((bf16[32,176,128]{2,1,0:T(8,128)(2,1)}), bf16[32,176,128]{2,1,0:T(8,128)(2,1)S(1)}, u32[]{:S(2)}, u32[]{:S(2)}) async-start(bf16[32,176,128]{2,1,0:T(8,128)(2,1)} %shard_map.118), calls=%async_computation | async-start | bytes 2883584 | tf_op jit(solution)/shard_map/all_to_all | solution.py:225
  15.0 5.8 %shard_map.119 = bf16[32,176,128]{2,1,0:T(8,128)(2,1)} custom-call(s32[1]{0:T(128)} %bitcast.z_ref, bf16[128,5632]{1,0:T(8,128)(2,1)} %x_ref.3), custom_call_target="tpu_custom_call" | custom-call | tf_op jit(solution)/shard_map/pallas_call | solution.py:57
  20.9 0.0 copy-start.5
  20.9 0.0 copy-start.6
  20.9 0.0 copy-start.7
  20.9 0.0 copy-start.3
  20.9 0.0 copy-start.4
  20.9 15.0 %all-to-all-done.x_ref = bf16[32,176,128]{2,1,0:T(8,128)(2,1)S(1)} async-done(((bf16[32,176,128]{2,1,0:T(8,128)(2,1)}), bf16[32,176,128]{2,1,0:T(8,128)(2,1)S(1)}, u32[]{:S(2)}, u32[]{:S(2)}) %all-to-all-start) | async-done | bytes 1441824 | tf_op jit(solution)/shard_map/all_to_all | solution.py:225
  35.9 0.0 copy-start
  35.9 1.1 copy-done
  37.0 4.2 %all-to-all-start.1 = ((bf16[32,176,128]{2,1,0:T(8,128)(2,1)}), bf16[32,176,128]{2,1,0:T(8,128)(2,1)S(1)}, u32[]{:S(2)}, u32[]{:S(2)}) async-start(bf16[32,176,128]{2,1,0:T(8,128)(2,1)} %shard_map.119), calls=%async_computation.1 | async-start | bytes 2883584 | tf_op jit(solution)/shard_map/all_to_all | solution.py:227
  41.2 0.0 copy-done.5
  41.3 0.1 broadcast_in_dim.25
  41.4 0.0 copy-done.6
  41.4 0.0 copy-done.7
  41.4 0.1 pad_maximum_fusion
  41.5 0.1 broadcast_in_dim.24
  41.6 0.0 copy-done.3
  41.6 0.1 copy.21
  41.7 0.0 copy-done.4
  41.7 0.1 copy.22
  41.8 0.1 pad.10.clone
  41.9 0.1 maximum_maximum_fusion
  42.1 0.7 collective-permute-start
  42.8 0.0 collective-permute-done
  42.8 0.8 copy.25.w_ref
  43.5 0.2 convert_reduce_fusion.1
  43.7 0.7 slice_bitcast_fusion.wt_ref
  44.4 17.7 %all-to-all-done.1.c_ref = bf16[32,176,128]{2,1,0:T(8,128)(2,1)S(1)} async-done(((bf16[32,176,128]{2,1,0:T(8,128)(2,1)}), bf16[32,176,128]{2,1,0:T(8,128)(2,1)S(1)}, u32[]{:S(2)}, u32[]{:S(2)}) %all-to-all-start.1) | async-done | bytes 1441824 | tf_op jit(solution)/shard_map/all_to_all | solution.py:227
  62.1 0.0 copy-start.1
  62.1 0.8 broadcast_in_dim.22.coef_ref
  63.0 0.3 copy-done.1
  63.3 29.5 %shard_map.120 = (bf16[32,176,128]{2,1,0:T(8,128)(2,1)}, bf16[192,384]{1,0:T(8,128)(2,1)}) custom-call(bf16[32,176,128]{2,1,0:T(8,128)(2,1)} %copy-done, bf16[32,176,128]{2,1,0:T(8,128)(2,1)} %copy-done.1, bf16[192,384]{1,0:T(8,128)(2,1)} %copy.25.w_ref, bf16[352,192]{1,0:T(8,128)(2,1)} %slice_bitcast_fusion.wt_ref, f32[176,128]{1,0:T(8,128)} %broadcast_in_dim.22.coef_ref), custom_call_target="tpu_custom_call" | custom-call | tf_op jit(solution)/shard_map/pallas_call | solution.py:175
  92.7 1.6 collective-permute-start.1
  94.3 0.0 collective-permute-done.1
  94.3 0.1 broadcast_in_dim.23
  94.4 34.7 %all_to_all.20 = bf16[8,192,384]{2,1,0:T(8,128)(2,1)S(1)} all-to-all(bf16[8,192,384]{2,1,0:T(8,128)(2,1)S(1)} %broadcast_in_dim.23), channel_id=1, replica_groups=mesh['cuts'=8,'z'=8,'yh'=2,'core'=2] {'cuts'}, dimensions={0} | all-to-all | bytes 2359296 | tf_op jit(solution)/shard_map/all_to_all | solution.py:233
  129.1 8.6 %all-to-all-start.2 = ((bf16[32,176,128]{2,1,0:T(8,128)(2,1)}), bf16[32,176,128]{2,1,0:T(8,128)(2,1)S(1)}, u32[]{:S(2)}, u32[]{:S(2)}) async-start(bf16[32,176,128]{2,1,0:T(8,128)(2,1)} %get-tuple-element.8), calls=%async_computation.2 | async-start | bytes 2883584 | tf_op jit(solution)/shard_map/all_to_all | solution.py:231
  137.8 0.2 convert_reduce_fusion
  137.9 0.6 fusion.1
  138.6 0.6 divide_multiply_fusion
  139.1 0.8 fusion.2
  139.9 18.7 %all-to-all-done.2.in_ref = bf16[32,176,128]{2,1,0:T(8,128)(2,1)S(1)} async-done(((bf16[32,176,128]{2,1,0:T(8,128)(2,1)}), bf16[32,176,128]{2,1,0:T(8,128)(2,1)S(1)}, u32[]{:S(2)}, u32[]{:S(2)}) %all-to-all-start.2) | async-done | bytes 1441824 | tf_op jit(solution)/shard_map/all_to_all | solution.py:231
  158.6 0.0 copy-start.2
  158.6 1.1 copy-done.2
  159.8 5.7 %shard_map.121 = bf16[128,5632]{1,0:T(8,128)(2,1)} custom-call(s32[1]{0:T(128)} %bitcast.z_ref, bf16[32,176,128]{2,1,0:T(8,128)(2,1)} %copy-done.2), custom_call_target="tpu_custom_call" | custom-call | tf_op jit(solution)/shard_map/pallas_call | solution.py:74
  (4 shorter events, 0.1 us)
Async XLA Ops:
  6.4 29.5 %all-to-all-start = ((bf16[32,176,128]{2,1,0:T(8,128)(2,1)}), bf16[32,176,128]{2,1,0:T(8,128)(2,1)S(1)}, u32[]{:S(2)}, u32[]{:S(2)}) async-start(bf16[32,176,128]{2,1,0:T(8,128)(2,1)} %shard_map.118), calls=%async_computation | async-start | bytes 2883584 | tf_op jit(solution)/shard_map/all_to_all | solution.py:225
  20.9 20.4 %copy-start.5 = (bf16[176]{0:T(256)(128)(2,1)S(1)}, bf16[176]{0:T(256)(128)(2,1)}, u32[]{:S(2)}) copy-start(bf16[176]{0:T(256)(128)(2,1)} %param.13) | copy-start | bytes 1060
  20.9 20.5 %copy-start.6 = (bf16[176]{0:T(256)(128)(2,1)S(1)}, bf16[176]{0:T(256)(128)(2,1)}, u32[]{:S(2)}) copy-start(bf16[176]{0:T(256)(128)(2,1)} %param.12) | copy-start | bytes 1060
  20.9 20.5 %copy-start.7 = (bf16[176]{0:T(256)(128)(2,1)S(1)}, bf16[176]{0:T(256)(128)(2,1)}, u32[]{:S(2)}) copy-start(bf16[176]{0:T(256)(128)(2,1)} %param.11) | copy-start | bytes 1060
  20.9 20.7 %copy-start.3 = (bf16[176,176]{1,0:T(8,128)(2,1)S(1)}, bf16[176,176]{1,0:T(8,128)(2,1)}, u32[]{:S(2)}) copy-start(bf16[176,176]{1,0:T(8,128)(2,1)} %param.9) | copy-start | bytes 185860
  20.9 20.8 %copy-start.4 = (bf16[176,176]{1,0:T(8,128)(2,1)S(1)}, bf16[176,176]{1,0:T(8,128)(2,1)}, u32[]{:S(2)}) copy-start(bf16[176,176]{1,0:T(8,128)(2,1)} %param.10) | copy-start | bytes 185860
  35.9 1.1 copy-start
  37.0 25.1 %all-to-all-start.1 = ((bf16[32,176,128]{2,1,0:T(8,128)(2,1)}), bf16[32,176,128]{2,1,0:T(8,128)(2,1)S(1)}, u32[]{:S(2)}, u32[]{:S(2)}) async-start(bf16[32,176,128]{2,1,0:T(8,128)(2,1)} %shard_map.119), calls=%async_computation.1 | async-start | bytes 2883584 | tf_op jit(solution)/shard_map/all_to_all | solution.py:227
  42.1 0.7 collective-permute-start
  62.1 1.2 copy-start.1
  92.7 1.6 collective-permute-start.1
  129.1 29.5 %all-to-all-start.2 = ((bf16[32,176,128]{2,1,0:T(8,128)(2,1)}), bf16[32,176,128]{2,1,0:T(8,128)(2,1)S(1)}, u32[]{:S(2)}, u32[]{:S(2)}) async-start(bf16[32,176,128]{2,1,0:T(8,128)(2,1)} %get-tuple-element.8), calls=%async_computation.2 | async-start | bytes 2883584 | tf_op jit(solution)/shard_map/all_to_all | solution.py:231
  158.6 1.1 copy-start.2

commit v3 on v2

v3 whole, which is shorter than its diff:
```python
import functools

import jax
import jax.numpy as jnp
from jax import lax
from jax.experimental import pallas as pl
from jax.experimental.pallas import tpu as pltpu
from jax.sharding import Mesh
from jax.sharding import PartitionSpec as P

BLK = 176
TWO = 2 * BLK
WROWS = 192
WCOLS = 384
NZ, NY, NC = 8, 2, 2
NQ = NY * NC
NI = 8
SEQ = 128
NSEQ = NI * NQ
STEP = 8
VMEM_LIMIT = 56 * 1024 * 1024


def pack_kernel(z_ref, x_ref, c_ref, out_ref):
    first = z_ref[0] * NQ
    for k, ref in enumerate((x_ref, c_ref)):
        for p in range(NZ // 2):
            turned = ref[:, p * 2 * NQ * BLK : (p + 1) * 2 * NQ * BLK].T
            for h in range(2 * NQ):
                slot = lax.rem(2 * NQ * p + h + NSEQ - first, NSEQ)
                out_ref[slot, k * BLK : (k + 1) * BLK, :] = turned[h * BLK : (h + 1) * BLK, :]


def unpack_kernel(z_ref, in_ref, out_ref):
    first = z_ref[0] * NQ
    for p in range(NZ // 2):
        heads = [in_ref[lax.rem(2 * NQ * p + h + NSEQ - first, NSEQ)] for h in range(2 * NQ)]
        out_ref[:, p * 2 * NQ * BLK : (p + 1) * 2 * NQ * BLK] = jnp.concatenate(heads, axis=0).T


def params():
    return pltpu.CompilerParams(vmem_limit_bytes=VMEM_LIMIT)


SMEM = pl.BlockSpec(memory_space=pltpu.SMEM)
VMEM = pl.BlockSpec(memory_space=pltpu.VMEM)


def pack(z, x, c, interpret=False):
    return pl.pallas_call(
        pack_kernel,
        in_specs=[SMEM, VMEM, VMEM],
        out_specs=VMEM,
        out_shape=jax.ShapeDtypeStruct((NSEQ, TWO, SEQ), x.dtype),
        compiler_params=params(),
        interpret=interpret,
    )(z, x, c)


def unpack(z, y, interpret=False):
    return pl.pallas_call(
        unpack_kernel,
        in_specs=[SMEM, VMEM],
        out_specs=VMEM,
        out_shape=jax.ShapeDtypeStruct((SEQ, NSEQ * BLK), y.dtype),
        compiler_params=params(),
        interpret=interpret,
    )(z, y)


LN2 = 0.6931471805599453
LOG2E = 1.4426950408889634


def sigmoid(pre):
    base = 1.0 + jnp.exp2(jnp.minimum(pre * -LOG2E, 115.0))
    rough = pl.reciprocal(base, approx=True)
    return rough * (2.0 - base * rough)


def one_minus_square(u):
    series, power = 0.0, 1.0
    terms = []
    for k in range(1, 8):
        power = power * (2.0 * LN2) / k
        terms.append(-power)
    series = terms[-1]
    for t in terms[-2::-1]:
        series = series * u + t
    return series * u


def split(v):
    high = v.astype(jnp.bfloat16)
    return high, (v - high.astype(jnp.float32)).astype(jnp.bfloat16)


CH = 16


def main_kernel(
    factor, m_ref, w_ref, wt_ref, coef_ref, out_ref, g_ref,
    tri, x_s, pre_s, d_s, u_s, rest_s, own_s, f1_s, gain_s, drive_s, lh_s, log_s, fh_s, rh_s, fwd_s, rev_s, q_s, g_s,
):
    step = pl.program_id(0)
    f32, bf16 = jnp.float32, jnp.bfloat16

    @pl.when(step == 0)
    def _():
        row = lax.broadcasted_iota(jnp.int32, (WROWS - BLK, STEP * SEQ), 0)
        x_s[BLK:, :] = jnp.where(row == 0, 1.0, 0.0).astype(x_s.dtype)
        q_s[...] = jnp.zeros_like(q_s)
        g_s[...] = jnp.zeros_like(g_s)
        src = lax.broadcasted_iota(jnp.int32, (SEQ, SEQ), 0)
        dst = lax.broadcasted_iota(jnp.int32, (SEQ, SEQ), 1)
        for k, seen in enumerate((src <= dst, src < dst, src >= dst)):
            one = jnp.where(seen, 1.0, 0.0).astype(bf16)
            tri[k, :SEQ, :] = one
            tri[k, SEQ:, :] = one

    for s in range(STEP):
        x_s[:BLK, s * SEQ : (s + 1) * SEQ] = m_ref[s, :BLK, :]
    pre_s[...] = jnp.dot(wt_ref[...], x_s[...], preferred_element_type=f32)

    def each(body):
        def one(s, _):
            cols = pl.ds(pl.multiple_of(s * SEQ, SEQ), SEQ)
            for r in range(0, BLK, CH):
                body(s, r, cols, pl.ds(pl.multiple_of(s * BLK + r, 16), CH))
            return 0

        lax.fori_loop(0, STEP, one, 0)

    def gates(s, r, cols, at):
        x = m_ref[s, r : r + CH, :].astype(f32)
        rgate = sigmoid(pre_s[r : r + CH, cols])
        igate = sigmoid(pre_s[BLK + r : BLK + r + CH, cols])
        u = coef_ref[r : r + CH, :] * rgate
        var = one_minus_square(u)
        inv = lax.rsqrt(var)
        scale = var * inv
        ix = igate * x
        drive = scale * ix
        u_s[at, :] = u
        rest_s[at, :] = LN2 - LN2 * rgate
        own_s[at, :] = ix * (inv - scale)
        f1_s[at, :] = drive - drive * igate
        gain_s[at, :] = scale * igate
        drive_s[at, :] = drive
        lh_s[at, :SEQ], lh_s[at, SEQ:] = split(u)

    each(gates)
    log_s[...] = jnp.dot(lh_s[...], tri[0], preferred_element_type=f32)

    def weigh(s, r, cols, at):
        total = log_s[at, :]
        cot = m_ref[s, BLK + r : BLK + r + CH, :].astype(f32)
        fh_s[at, :SEQ], fh_s[at, SEQ:] = split(drive_s[at, :] * jnp.exp2(-total))
        rh_s[at, :SEQ], rh_s[at, SEQ:] = split(cot * jnp.exp2(total))

    each(weigh)
    fwd_s[...] = jnp.dot(fh_s[...], tri[1], preferred_element_type=f32)
    rev_s[...] = jnp.dot(rh_s[...], tri[2], preferred_element_type=f32)

    def deltas(s, r, cols, at):
        total = log_s[at, :]
        adj = rev_s[at, :] * jnp.exp2(-total)
        dlog = adj * (fwd_s[at, :] * jnp.exp2(total) - own_s[at, :])
        v = dlog * u_s[at, :]
        q_s[r : r + CH, :] += v
        d_s[r : r + CH, cols] = (v * rest_s[at, :]).astype(bf16)
        d_s[BLK + r : BLK + r + CH, cols] = (adj * f1_s[at, :]).astype(bf16)
        pre_s[r : r + CH, cols] = adj * gain_s[at, :]

    each(deltas)

    back = jnp.dot(w_ref[:BLK, :TWO], d_s[...], preferred_element_type=f32)
    for s in range(STEP):
        cols = slice(s * SEQ, (s + 1) * SEQ)
        out_ref[s] = (back[:, cols] + pre_s[:BLK, cols]).astype(out_ref.dtype)
    nt = (((1,), (1,)), ((), ()))
    g_s[:, :TWO] += lax.dot_general(x_s[...], d_s[...], nt, preferred_element_type=f32)

    @pl.when(step == pl.num_programs(0) - 1)
    def _():
        g_ref[...] = (g_s[...] * factor).astype(g_ref.dtype)
        decay = jnp.sum((q_s[...] / coef_ref[...]).T, axis=0, keepdims=True) * (-8.0 * factor)
        tail = g_s[BLK:, :BLK] * factor
        row = lax.broadcasted_iota(jnp.int32, tail.shape, 0)
        g_ref[BLK:, :BLK] = jnp.where(row == 1, decay, tail).astype(g_ref.dtype)


def main_call(factor, m, w, wt, coef, grad_dtype=jnp.bfloat16, interpret=False):
    f32, bf16 = jnp.float32, jnp.bfloat16
    n = m.shape[0]
    tok = lambda rows: pl.BlockSpec((STEP, rows, SEQ), lambda p: (p, 0, 0))
    full = lambda shape: pl.BlockSpec(shape, lambda p: (0, 0))
    wide = lambda kind: pltpu.VMEM((STEP * BLK, 2 * SEQ), kind)
    flat = pltpu.VMEM((STEP * BLK, SEQ), f32)
    return pl.pallas_call(
        functools.partial(main_kernel, factor),
        grid=(n // STEP,),
        out_shape=[
            jax.ShapeDtypeStruct((n, BLK, SEQ), bf16),
            jax.ShapeDtypeStruct((WROWS, WCOLS), grad_dtype),
        ],
        in_specs=[tok(TWO), full((WROWS, WCOLS)), full((TWO, WROWS)), full((BLK, SEQ))],
        out_specs=[tok(BLK), full((WROWS, WCOLS))],
        scratch_shapes=[
            pltpu.VMEM((3, 2 * SEQ, SEQ), bf16),
            pltpu.VMEM((WROWS, STEP * SEQ), bf16),
            pltpu.VMEM((TWO, STEP * SEQ), f32),
            pltpu.VMEM((TWO, STEP * SEQ), bf16),
            flat, flat, flat, flat, flat, flat,
            wide(bf16), flat, wide(bf16), wide(bf16), flat, flat,
            pltpu.VMEM((BLK, SEQ), f32),
            pltpu.VMEM((WROWS, WCOLS), f32),
        ],
        compiler_params=params(),
        interpret=interpret,
    )(m, w, wt, coef)


def wire(wa, wx, ba, bx, decay):
    bf16 = jnp.bfloat16
    tail = jnp.zeros((WROWS - BLK - 2, TWO), bf16)
    body = jnp.concatenate(
        [
            jnp.concatenate([wa, wx], axis=1),
            jnp.concatenate([ba, bx])[None],
            jnp.concatenate([decay, jnp.zeros((BLK,), bf16)])[None],
            tail,
        ],
        axis=0,
    )
    return jnp.pad(body, ((0, 0), (0, WCOLS - TWO)))


def unwire(w):
    wt = w[:, :TWO].T
    coef = (-8.0 * LOG2E) * jax.nn.softplus(w[BLK + 1, :BLK].astype(jnp.float32))
    return wt, jnp.broadcast_to(coef[:, None], (BLK, SEQ))


def per_device(inputs, cotangent, wa, wx, ba, bx, decay):
    bf16, f32 = jnp.bfloat16, jnp.float32
    plane, line = ("cuts", "yh", "core"), ("cuts", "z")
    z = lax.axis_index("z").astype(jnp.int32).reshape(1)
    pairs = [(i, k, (k + i) % NZ) for i in range(NI) for k in range(NZ)]
    fetch = [(i * NZ + src, i * NZ + k) for i, k, src in pairs]
    home = [(b, a) for a, b in fetch]

    sent = pack(z, inputs, cotangent)
    got = lax.all_to_all(sent, plane, 0, 0, tiled=True)
    w = lax.ppermute(wire(wa, wx, ba, bx, decay), line, fetch)
    wt, coef = unwire(w)
    total = SEQ * NSEQ * NZ
    out, grads = main_call(float(total) ** -0.5, got, w, wt, coef)
    input_grad = unpack(z, lax.all_to_all(out, plane, 0, 0, tiled=True))
    share = lax.ppermute(grads, line, home)
    parts = [share]
    for k in range(1, NI):
        parts.append(lax.ppermute(share, "cuts", [(i, (i + k) % NI) for i in range(NI)]))
    full = sum(p.astype(f32) for p in parts)
    own = jax.nn.sigmoid(decay.astype(f32))
    return (
        input_grad,
        full[:BLK, :BLK],
        full[:BLK, BLK:TWO],
        full[BLK, :BLK],
        full[BLK, BLK:TWO],
        full[BLK + 1, :BLK] * own,
    )


def solution(mesh):
    fine = Mesh(mesh.devices.reshape(NI, NZ, NY, NC), ("cuts", "z", "yh", "core"))
    zero = ("z", "yh", "core")
    rows = P(("cuts",) + zero, None)
    return jax.shard_map(
        per_device,
        mesh=fine,
        in_specs=(rows, rows, P(zero, None), P(zero, None), P(zero), P(zero), P(zero)),
        out_specs=(rows, P(zero, None), P(zero, None), P(zero), P(zero), P(zero)),
        check_vma=False,
    )
```

time: 167 us -> 123 us (0.74)
  blocking collectives: 34.7 us -> 0 us
  Pallas kernels: 46.8 us -> 26.6 us
  starting transfers between devices: 23.6 us -> 41.8 us
  waiting for transfers between devices: 51.4 us -> 45.9 us
    all_to_all x1 -> x0, blocking collectives: 34.7 us -> none  [per_device(): lax.all_to_all(jnp.broadcast_to(share, (NI, WROWS, WCOLS)), 'cuts', 0, 0,...]
    ppermute x0 -> x7, starting transfers between devices: none -> 24.8 us  [per_device(): lax.ppermute(share, 'cuts', [(i, (i + k) % NI) for i in range(NI)])]
    all_to_all x1, waiting for transfers between devices: 18.7 us -> 0.01 us  [per_device(): input_grad = unpack(z, lax.all_to_all(out, plane, 0, 0, tiled=True))]
    ppermute x0 -> x7, waiting for transfers between devices: none -> 13.1 us  [per_device(): lax.ppermute(share, 'cuts', [(i, (i + k) % NI) for i in range(NI)])]
    pallas_call x3 -> x2, Pallas kernels: 17.3 us -> 7.06 us  [the longest x1 4.17 us: pack(): pl.pallas_call(pack_kernel, in_specs=[SMEM, VMEM, VMEM], out_specs=VMEM,...]
    pallas_call x1, Pallas kernels: 29.5 us -> 19.5 us  [main_call(): pl.pallas_call(functools.partial(main_kernel, factor), grid=(n // STEP,),...]
    all_to_all x2 -> x1, starting transfers between devices: 12.8 us -> 8.73 us  [per_device(): got = lax.all_to_all(sent, plane, 0, 0, tiled=True)]
    all_to_all x1, starting transfers between devices: 8.61 us -> 6.92 us  [per_device(): input_grad = unpack(z, lax.all_to_all(out, plane, 0, 0, tiled=True))]
  transfers between devices with their start and end apart: 5 -> 11, of which waited for: 3 -> 5; matrix products, arithmetic and copies ran while one was open for 3% -> 4% of each run, Pallas kernels for 4% -> 0%
where the time goes in v3:
time: 123 us; the launch traced here: 122 us
  waiting for transfers between devices  45.9 us (37%)
  starting transfers between devices  41.8 us (34%)
  Pallas kernels  26.6 us (22%)
  local copies, waits for them, and re-layouts  6.18 us (5%)
    all_to_all x1, waiting for transfers between devices, per_device(): got = lax.all_to_all(sent, plane, 0, 0, tiled=True)  32.8 us
    ppermute x7, starting transfers between devices, per_device(): lax.ppermute(share, 'cuts', [(i, (i + k) % NI) for i in range(NI)])  24.8 us
    pallas_call x1, Pallas kernels, main_call(): pl.pallas_call(functools.partial(main_kernel, factor), grid=(n // STEP,),...  19.5 us
    ppermute x7, waiting for transfers between devices, per_device(): lax.ppermute(share, 'cuts', [(i, (i + k) % NI) for i in range(NI)])  13.1 us
    all_to_all x1, starting transfers between devices, per_device(): got = lax.all_to_all(sent, plane, 0, 0, tiled=True)  8.73 us
    all_to_all x1, starting transfers between devices, per_device(): input_grad = unpack(z, lax.all_to_all(out, plane, 0, 0, tiled=True))  6.92 us
    pallas_call x1, Pallas kernels, pack(): pl.pallas_call(pack_kernel, in_specs=[SMEM, VMEM, VMEM], out_specs=VMEM,...  4.17 us
    pallas_call x1, Pallas kernels, unpack(): pl.pallas_call(unpack_kernel, in_specs=[SMEM, VMEM], out_specs=VMEM, out_...  2.89 us
  transfers between devices with their start and end apart: 11, of which 5 were waited for; matrix products, arithmetic and copies ran while one was open for 4% of the time, Pallas kernels for 0%

profile of v3, /device:TPU:1, one launch (start us, length us, event | category | flops | bytes accessed | tf_op | source)
XLA Modules:
  0.0 122.3 jit_solution(9127696236859689777)
XLA Ops:
  0.6 4.2 %shard_map.118 = bf16[32,352,128]{2,1,0:T(8,128)(2,1)} custom-call(s32[1]{0:T(128)} %bitcast.z_ref, bf16[128,5632]{1,0:T(8,128)(2,1)} %x_ref.1, bf16[128,5632]{1,0:T(8,128)(2,1)} %c_ref.1), custom_call_target="tpu_custom_call" | custom-call | tf_op jit(solution)/shard_map/pallas_call | solution.py:50
  4.8 0.0 copy-start.3
  4.8 8.7 %all-to-all-start = ((bf16[32,352,128]{2,1,0:T(8,128)(2,1)}), bf16[32,352,128]{2,1,0:T(8,128)(2,1)S(1)}, u32[]{:S(2)}, u32[]{:S(2)}) async-start(bf16[32,352,128]{2,1,0:T(8,128)(2,1)} %shard_map.118), calls=%async_computation | async-start | bytes 5767168 | tf_op jit(solution)/shard_map/all_to_all | solution.py:254
  13.6 0.0 copy-done.4
  13.6 0.1 broadcast_in_dim.21
  13.7 0.0 copy-done.5
  13.7 0.0 copy-done.6
  13.7 0.1 pad_maximum_fusion
  13.8 0.1 broadcast_in_dim.20
  13.9 0.0 copy-done.2
  13.9 0.1 copy.17
  14.0 0.0 copy-done.3
  14.1 0.1 copy.16
  14.2 0.1 pad.10.clone
  14.2 0.1 maximum_maximum_fusion
  14.4 0.7 collective-permute-start
  15.1 0.0 collective-permute-done
  15.1 0.8 copy.20.w_ref
  15.9 0.2 convert_reduce_fusion
  16.1 0.7 slice_bitcast_fusion.wt_ref
  16.8 32.8 %all-to-all-done.m_ref = bf16[32,352,128]{2,1,0:T(8,128)(2,1)S(1)} async-done(((bf16[32,352,128]{2,1,0:T(8,128)(2,1)}), bf16[32,352,128]{2,1,0:T(8,128)(2,1)S(1)}, u32[]{:S(2)}, u32[]{:S(2)}) %all-to-all-start) | async-done | bytes 2883616 | tf_op jit(solution)/shard_map/all_to_all | solution.py:254
  49.6 0.8 broadcast_in_dim.19.coef_ref
  50.4 0.8 copy-done
  51.2 19.5 %shard_map.119 = (bf16[32,176,128]{2,1,0:T(8,128)(2,1)}, bf16[192,384]{1,0:T(8,128)(2,1)}) custom-call(bf16[32,352,128]{2,1,0:T(8,128)(2,1)} %copy-done, bf16[192,384]{1,0:T(8,128)(2,1)} %copy.20.w_ref, bf16[352,192]{1,0:T(8,128)(2,1)} %slice_bitcast_fusion.wt_ref, f32[176,128]{1,0:T(8,128)} %broadcast_in_dim.19.coef_ref), custom_call_target="tpu_custom_call" | custom-call | tf_op jit(solution)/shard_map/pallas_call | solution.py:200
  70.7 6.9 %all-to-all-start.1 = ((bf16[32,176,128]{2,1,0:T(8,128)(2,1)}), bf16[32,176,128]{2,1,0:T(8,128)(2,1)S(1)}, u32[]{:S(2)}, u32[]{:S(2)}) async-start(bf16[32,176,128]{2,1,0:T(8,128)(2,1)} %get-tuple-element.8), calls=%async_computation.1 | async-start | bytes 2883584 | tf_op jit(solution)/shard_map/all_to_all | solution.py:259
  77.6 0.7 collective-permute-start.1
  78.3 0.0 collective-permute-done.1
  78.3 13.2 %collective-permute-start.8 = (bf16[192,384]{1,0:T(8,128)(2,1)S(1)}, bf16[192,384]{1,0:T(8,128)(2,1)S(1)}, u32[]{:S(2)}, u32[]{:S(2)}) collective-permute-start(bf16[192,384]{1,0:T(8,128)(2,1)S(1)} %collective-permute-done.1), channel_id=1, source_target_pairs={{0,224},{32,0},{64,32},{96,64},{128,96},{160,128},{192,160},{224,1... | collective-permute-start | bytes 442376 | tf_op jit(solution)/shard_map/ppermute | solution.py:263
  91.5 8.0 %collective-permute-start.7 = (bf16[192,384]{1,0:T(8,128)(2,1)S(1)}, bf16[192,384]{1,0:T(8,128)(2,1)S(1)}, u32[]{:S(2)}, u32[]{:S(2)}) collective-permute-start(bf16[192,384]{1,0:T(8,128)(2,1)S(1)} %collective-permute-done.1), channel_id=1, source_target_pairs={{0,192},{32,224},{64,0},{96,32},{128,64},{160,96},{192,128},{224,1... | collective-permute-start | bytes 442376 | tf_op jit(solution)/shard_map/ppermute | solution.py:263
  99.5 0.0 collective-permute-start.6
  99.5 0.0 collective-permute-start.5
  99.5 2.4 %collective-permute-start.4 = (bf16[192,384]{1,0:T(8,128)(2,1)S(1)}, bf16[192,384]{1,0:T(8,128)(2,1)S(1)}, u32[]{:S(2)}, u32[]{:S(2)}) collective-permute-start(bf16[192,384]{1,0:T(8,128)(2,1)S(1)} %collective-permute-done.1), channel_id=1, source_target_pairs={{0,96},{32,128},{64,160},{96,192},{128,224},{160,0},{192,32},{224,... | collective-permute-start | bytes 442376 | tf_op jit(solution)/shard_map/ppermute | solution.py:263
  101.9 0.0 collective-permute-done.8
  101.9 1.2 collective-permute-start.3
  103.1 5.0 %collective-permute-done.7 = bf16[192,384]{1,0:T(8,128)(2,1)S(1)} collective-permute-done((bf16[192,384]{1,0:T(8,128)(2,1)S(1)}, bf16[192,384]{1,0:T(8,128)(2,1)S(1)}, u32[]{:S(2)}, u32[]{:S(2)}) %collective-permute-start.7) | collective-permute-done | bytes 147488 | tf_op jit(solution)/shard_map/ppermute | solution.py:263
  108.1 0.0 collective-permute-start.2
  108.1 0.0 collective-permute-done.6
  108.1 0.0 collective-permute-done.5
  108.1 0.5 collective-permute-done.4
  108.6 4.2 %collective-permute-done.3 = bf16[192,384]{1,0:T(8,128)(2,1)S(1)} collective-permute-done((bf16[192,384]{1,0:T(8,128)(2,1)S(1)}, bf16[192,384]{1,0:T(8,128)(2,1)S(1)}, u32[]{:S(2)}, u32[]{:S(2)}) %collective-permute-start.3) | collective-permute-done | bytes 147488 | tf_op jit(solution)/shard_map/ppermute | solution.py:263
  112.8 3.4 %collective-permute-done.2 = bf16[192,384]{1,0:T(8,128)(2,1)S(1)} collective-permute-done((bf16[192,384]{1,0:T(8,128)(2,1)S(1)}, bf16[192,384]{1,0:T(8,128)(2,1)S(1)}, u32[]{:S(2)}, u32[]{:S(2)}) %collective-permute-start.2) | collective-permute-done | bytes 147488 | tf_op jit(solution)/shard_map/ppermute | solution.py:263
  116.2 0.1 convert_add_fusion
  116.3 0.6 fusion.1
  116.9 0.6 divide_multiply_fusion
  117.5 0.8 fusion.2
  118.3 0.0 all-to-all-done.1.in_ref
  118.3 1.1 copy-done.1
  119.4 2.9 %shard_map.120 = bf16[128,5632]{1,0:T(8,128)(2,1)} custom-call(s32[1]{0:T(128)} %bitcast.z_ref, bf16[32,176,128]{2,1,0:T(8,128)(2,1)} %copy-done.1), custom_call_target="tpu_custom_call" | custom-call | tf_op jit(solution)/shard_map/pallas_call | solution.py:61
  (12 shorter events, 0.1 us)
Async XLA Ops:
  4.8 8.8 %copy-start.4 = (bf16[176]{0:T(256)(128)(2,1)S(1)}, bf16[176]{0:T(256)(128)(2,1)}, u32[]{:S(2)}) copy-start(bf16[176]{0:T(256)(128)(2,1)} %param.13) | copy-start | bytes 1060
  4.8 8.9 %copy-start.5 = (bf16[176]{0:T(256)(128)(2,1)S(1)}, bf16[176]{0:T(256)(128)(2,1)}, u32[]{:S(2)}) copy-start(bf16[176]{0:T(256)(128)(2,1)} %param.12) | copy-start | bytes 1060
  4.8 8.9 %copy-start.6 = (bf16[176]{0:T(256)(128)(2,1)S(1)}, bf16[176]{0:T(256)(128)(2,1)}, u32[]{:S(2)}) copy-start(bf16[176]{0:T(256)(128)(2,1)} %param.11) | copy-start | bytes 1060
  4.8 9.1 %copy-start.2 = (bf16[176,176]{1,0:T(8,128)(2,1)S(1)}, bf16[176,176]{1,0:T(8,128)(2,1)}, u32[]{:S(2)}) copy-start(bf16[176,176]{1,0:T(8,128)(2,1)} %param.10) | copy-start | bytes 185860
  4.8 9.2 %copy-start.3 = (bf16[176,176]{1,0:T(8,128)(2,1)S(1)}, bf16[176,176]{1,0:T(8,128)(2,1)}, u32[]{:S(2)}) copy-start(bf16[176,176]{1,0:T(8,128)(2,1)} %param.9) | copy-start | bytes 185860
  4.8 44.7 %all-to-all-start = ((bf16[32,352,128]{2,1,0:T(8,128)(2,1)}), bf16[32,352,128]{2,1,0:T(8,128)(2,1)S(1)}, u32[]{:S(2)}, u32[]{:S(2)}) async-start(bf16[32,352,128]{2,1,0:T(8,128)(2,1)} %shard_map.118), calls=%async_computation | async-start | bytes 5767168 | tf_op jit(solution)/shard_map/all_to_all | solution.py:254
  14.4 0.7 collective-permute-start
  49.6 1.6 %copy-start = (bf16[32,352,128]{2,1,0:T(8,128)(2,1)}, bf16[32,352,128]{2,1,0:T(8,128)(2,1)S(1)}, u32[]{:S(2)}) copy-start(bf16[32,352,128]{2,1,0:T(8,128)(2,1)S(1)} %all-to-all-done.m_ref) | copy-start | bytes 8650756
  70.7 6.9 %copy-start.7 = (bf16[192,384]{1,0:T(8,128)(2,1)S(1)}, bf16[192,384]{1,0:T(8,128)(2,1)}, u32[]{:S(2)}) copy-start(bf16[192,384]{1,0:T(8,128)(2,1)} %get-tuple-element.9) | copy-start | bytes 442372
  70.7 47.6 %all-to-all-start.1 = ((bf16[32,176,128]{2,1,0:T(8,128)(2,1)}), bf16[32,176,128]{2,1,0:T(8,128)(2,1)S(1)}, u32[]{:S(2)}, u32[]{:S(2)}) async-start(bf16[32,176,128]{2,1,0:T(8,128)(2,1)} %get-tuple-element.8), calls=%async_computation.1 | async-start | bytes 2883584 | tf_op jit(solution)/shard_map/all_to_all | solution.py:259
  77.6 0.7 collective-permute-start.1
  78.3 23.6 %collective-permute-start.8 = (bf16[192,384]{1,0:T(8,128)(2,1)S(1)}, bf16[192,384]{1,0:T(8,128)(2,1)S(1)}, u32[]{:S(2)}, u32[]{:S(2)}) collective-permute-start(bf16[192,384]{1,0:T(8,128)(2,1)S(1)} %collective-permute-done.1), channel_id=1, source_target_pairs={{0,224},{32,0},{64,32},{96,64},{128,96},{160,128},{192,160},{224,1... | collective-permute-start | bytes 442376 | tf_op jit(solution)/shard_map/ppermute | solution.py:263
  91.5 16.6 %collective-permute-start.7 = (bf16[192,384]{1,0:T(8,128)(2,1)S(1)}, bf16[192,384]{1,0:T(8,128)(2,1)S(1)}, u32[]{:S(2)}, u32[]{:S(2)}) collective-permute-start(bf16[192,384]{1,0:T(8,128)(2,1)S(1)} %collective-permute-done.1), channel_id=1, source_target_pairs={{0,192},{32,224},{64,0},{96,32},{128,64},{160,96},{192,128},{224,1... | collective-permute-start | bytes 442376 | tf_op jit(solution)/shard_map/ppermute | solution.py:263
  99.5 8.6 %collective-permute-start.6 = (bf16[192,384]{1,0:T(8,128)(2,1)S(1)}, bf16[192,384]{1,0:T(8,128)(2,1)S(1)}, u32[]{:S(2)}, u32[]{:S(2)}) collective-permute-start(bf16[192,384]{1,0:T(8,128)(2,1)S(1)} %collective-permute-done.1), channel_id=1, source_target_pairs={{0,160},{32,192},{64,224},{96,0},{128,32},{160,64},{192,96},{224,1... | collective-permute-start | bytes 442376 | tf_op jit(solution)/shard_map/ppermute | solution.py:263
  99.5 8.6 %collective-permute-start.5 = (bf16[192,384]{1,0:T(8,128)(2,1)S(1)}, bf16[192,384]{1,0:T(8,128)(2,1)S(1)}, u32[]{:S(2)}, u32[]{:S(2)}) collective-permute-start(bf16[192,384]{1,0:T(8,128)(2,1)S(1)} %collective-permute-done.1), channel_id=1, source_target_pairs={{0,128},{32,160},{64,192},{96,224},{128,0},{160,32},{192,64},{224,... | collective-permute-start | bytes 442376 | tf_op jit(solution)/shard_map/ppermute | solution.py:263
  99.5 9.1 %collective-permute-start.4 = (bf16[192,384]{1,0:T(8,128)(2,1)S(1)}, bf16[192,384]{1,0:T(8,128)(2,1)S(1)}, u32[]{:S(2)}, u32[]{:S(2)}) collective-permute-start(bf16[192,384]{1,0:T(8,128)(2,1)S(1)} %collective-permute-done.1), channel_id=1, source_target_pairs={{0,96},{32,128},{64,160},{96,192},{128,224},{160,0},{192,32},{224,... | collective-permute-start | bytes 442376 | tf_op jit(solution)/shard_map/ppermute | solution.py:263
  101.9 10.9 %collective-permute-start.3 = (bf16[192,384]{1,0:T(8,128)(2,1)S(1)}, bf16[192,384]{1,0:T(8,128)(2,1)S(1)}, u32[]{:S(2)}, u32[]{:S(2)}) collective-permute-start(bf16[192,384]{1,0:T(8,128)(2,1)S(1)} %collective-permute-done.1), channel_id=1, source_target_pairs={{0,64},{32,96},{64,128},{96,160},{128,192},{160,224},{192,0},{224,... | collective-permute-start | bytes 442376 | tf_op jit(solution)/shard_map/ppermute | solution.py:263
  108.1 8.1 %collective-permute-start.2 = (bf16[192,384]{1,0:T(8,128)(2,1)S(1)}, bf16[192,384]{1,0:T(8,128)(2,1)S(1)}, u32[]{:S(2)}, u32[]{:S(2)}) collective-permute-start(bf16[192,384]{1,0:T(8,128)(2,1)S(1)} %collective-permute-done.1), channel_id=1, source_target_pairs={{0,32},{32,64},{64,96},{96,128},{128,160},{160,192},{192,224},{224... | collective-permute-start | bytes 442376 | tf_op jit(solution)/shard_map/ppermute | solution.py:263
  118.3 1.1 copy-start.1

commit v4 on v3

v4 whole, which is shorter than its diff:
```python
import functools

import jax
import jax.numpy as jnp
from jax import lax
from jax.experimental import pallas as pl
from jax.experimental.pallas import tpu as pltpu
from jax.sharding import Mesh
from jax.sharding import PartitionSpec as P

BLK = 176
TWO = 2 * BLK
WROWS = 192
WCOLS = 384
NZ, NY, NC = 8, 2, 2
NQ = NY * NC
NI = 8
SEQ = 128
NSEQ = NI * NQ
STEP = 8
VMEM_LIMIT = 56 * 1024 * 1024


def pack_kernel(z_ref, x_ref, after_ref, out_ref):
    first = z_ref[0] * NQ
    for p in range(NZ // 2):
        turned = x_ref[:, p * 2 * NQ * BLK : (p + 1) * 2 * NQ * BLK].T
        for h in range(2 * NQ):
            slot = lax.rem(2 * NQ * p + h + NSEQ - first, NSEQ)
            out_ref[slot] = turned[h * BLK : (h + 1) * BLK, :]


def unpack_kernel(z_ref, in_ref, out_ref):
    first = z_ref[0] * NQ
    for p in range(NZ // 2):
        heads = [in_ref[lax.rem(2 * NQ * p + h + NSEQ - first, NSEQ)] for h in range(2 * NQ)]
        out_ref[:, p * 2 * NQ * BLK : (p + 1) * 2 * NQ * BLK] = jnp.concatenate(heads, axis=0).T


def params():
    return pltpu.CompilerParams(vmem_limit_bytes=VMEM_LIMIT)


SMEM = pl.BlockSpec(memory_space=pltpu.SMEM)
VMEM = pl.BlockSpec(memory_space=pltpu.VMEM)


def pack(z, x, after, interpret=False):
    return pl.pallas_call(
        pack_kernel,
        in_specs=[SMEM, VMEM, pl.BlockSpec(memory_space=pl.ANY)],
        out_specs=VMEM,
        out_shape=jax.ShapeDtypeStruct((NSEQ, BLK, SEQ), x.dtype),
        compiler_params=params(),
        interpret=interpret,
    )(z, x, after)


def unpack(z, y, interpret=False):
    return pl.pallas_call(
        unpack_kernel,
        in_specs=[SMEM, VMEM],
        out_specs=VMEM,
        out_shape=jax.ShapeDtypeStruct((SEQ, NSEQ * BLK), y.dtype),
        compiler_params=params(),
        interpret=interpret,
    )(z, y)


LN2 = 0.6931471805599453
LOG2E = 1.4426950408889634


def sigmoid(pre):
    base = 1.0 + jnp.exp2(jnp.minimum(pre * -LOG2E, 115.0))
    rough = pl.reciprocal(base, approx=True)
    return rough * (2.0 - base * rough)


def one_minus_square(u):
    series, power = 0.0, 1.0
    terms = []
    for k in range(1, 8):
        power = power * (2.0 * LN2) / k
        terms.append(-power)
    series = terms[-1]
    for t in terms[-2::-1]:
        series = series * u + t
    return series * u


def split(v):
    high = v.astype(jnp.bfloat16)
    return high, (v - high.astype(jnp.float32)).astype(jnp.bfloat16)


CH = 16


def each(body):
    def one(s, _):
        cols = pl.ds(pl.multiple_of(s * SEQ, SEQ), SEQ)
        for r in range(0, BLK, CH):
            body(s, r, cols, pl.ds(pl.multiple_of(s * BLK + r, 16), CH))
        return 0

    lax.fori_loop(0, STEP, one, 0)


def fill_triangle(tri, seen):
    src = lax.broadcasted_iota(jnp.int32, (SEQ, SEQ), 0)
    dst = lax.broadcasted_iota(jnp.int32, (SEQ, SEQ), 1)
    one = jnp.where(seen(src, dst), 1.0, 0.0).astype(jnp.bfloat16)
    tri[:SEQ, :] = one
    tri[SEQ:, :] = one


def fill_ones_row(x_s):
    row = lax.broadcasted_iota(jnp.int32, (WROWS - BLK, STEP * SEQ), 0)
    x_s[BLK:, :] = jnp.where(row == 0, 1.0, 0.0).astype(x_s.dtype)


def forward_kernel(
    x_ref, wt_ref, coef_ref, log_ref, a1_ref, v1_ref, f1_ref, gain_ref,
    upto, before, x_s, pre_s, u_s, rest_s, own_s, drive_s, lh_s, log_s, fh_s, fwd_s,
):
    f32, bf16 = jnp.float32, jnp.bfloat16

    @pl.when(pl.program_id(0) == 0)
    def _():
        fill_ones_row(x_s)
        fill_triangle(upto, lambda src, dst: src <= dst)
        fill_triangle(before, lambda src, dst: src < dst)

    for s in range(STEP):
        x_s[:BLK, s * SEQ : (s + 1) * SEQ] = x_ref[s]
    pre_s[...] = jnp.dot(wt_ref[...], x_s[...], preferred_element_type=f32)

    def gates(s, r, cols, at):
        x = x_ref[s, r : r + CH, :].astype(f32)
        rgate = sigmoid(pre_s[r : r + CH, cols])
        igate = sigmoid(pre_s[BLK + r : BLK + r + CH, cols])
        u = coef_ref[r : r + CH, :] * rgate
        var = one_minus_square(u)
        inv = lax.rsqrt(var)
        scale = var * inv
        ix = igate * x
        drive = scale * ix
        u_s[at, :] = u
        rest_s[at, :] = LN2 - LN2 * rgate
        own_s[at, :] = ix * (inv - scale)
        drive_s[at, :] = drive
        f1_ref[s, r : r + CH, :] = drive - drive * igate
        gain_ref[s, r : r + CH, :] = scale * igate
        lh_s[at, :SEQ], lh_s[at, SEQ:] = split(u)

    each(gates)
    log_s[...] = jnp.dot(lh_s[...], upto[...], preferred_element_type=f32)

    def weigh(s, r, cols, at):
        total = log_s[at, :]
        log_ref[s, r : r + CH, :] = total
        fh_s[at, :SEQ], fh_s[at, SEQ:] = split(drive_s[at, :] * jnp.exp2(-total))

    each(weigh)
    fwd_s[...] = jnp.dot(fh_s[...], before[...], preferred_element_type=f32)

    def factors(s, r, cols, at):
        v1 = (fwd_s[at, :] * jnp.exp2(log_s[at, :]) - own_s[at, :]) * u_s[at, :]
        v1_ref[s, r : r + CH, :] = v1
        a1_ref[s, r : r + CH, :] = v1 * rest_s[at, :]

    each(factors)


def backward_kernel(
    factor, x_ref, c_ref, log_ref, a1_ref, v1_ref, f1_ref, gain_ref, w_ref, coef_ref, out_ref, g_ref,
    after, x_s, d_s, rh_s, rev_s, term_s, q_s, g_s,
):
    step = pl.program_id(0)
    f32, bf16 = jnp.float32, jnp.bfloat16

    @pl.when(step == 0)
    def _():
        fill_ones_row(x_s)
        fill_triangle(after, lambda src, dst: src >= dst)
        q_s[...] = jnp.zeros_like(q_s)
        g_s[...] = jnp.zeros_like(g_s)

    for s in range(STEP):
        x_s[:BLK, s * SEQ : (s + 1) * SEQ] = x_ref[s]

    def weigh(s, r, cols, at):
        cot = c_ref[s, r : r + CH, :].astype(f32)
        rh_s[at, :SEQ], rh_s[at, SEQ:] = split(cot * jnp.exp2(log_ref[s, r : r + CH, :]))

    each(weigh)
    rev_s[...] = jnp.dot(rh_s[...], after[...], preferred_element_type=f32)

    def deltas(s, r, cols, at):
        adj = rev_s[at, :] * jnp.exp2(-log_ref[s, r : r + CH, :])
        q_s[r : r + CH, :] += adj * v1_ref[s, r : r + CH, :]
        d_s[r : r + CH, cols] = (adj * a1_ref[s, r : r + CH, :]).astype(bf16)
        d_s[BLK + r : BLK + r + CH, cols] = (adj * f1_ref[s, r : r + CH, :]).astype(bf16)
        term_s[r : r + CH, cols] = adj * gain_ref[s, r : r + CH, :]

    each(deltas)

    back = jnp.dot(w_ref[:BLK, :TWO], d_s[...], preferred_element_type=f32)
    for s in range(STEP):
        cols = slice(s * SEQ, (s + 1) * SEQ)
        out_ref[s] = (back[:, cols] + term_s[:, cols]).astype(out_ref.dtype)
    nt = (((1,), (1,)), ((), ()))
    g_s[:, :TWO] += lax.dot_general(x_s[...], d_s[...], nt, preferred_element_type=f32)

    @pl.when(step == pl.num_programs(0) - 1)
    def _():
        g_ref[...] = (g_s[...] * factor).astype(g_ref.dtype)
        decay = jnp.sum((q_s[...] / coef_ref[...]).T, axis=0, keepdims=True) * (-8.0 * factor)
        tail = g_s[BLK:, :BLK] * factor
        row = lax.broadcasted_iota(jnp.int32, tail.shape, 0)
        g_ref[BLK:, :BLK] = jnp.where(row == 1, decay, tail).astype(g_ref.dtype)


TOK = pl.BlockSpec((STEP, BLK, SEQ), lambda p: (p, 0, 0))


def full(*shape):
    return pl.BlockSpec(shape, lambda p: (0, 0))


def flat(kind=jnp.float32, times=1):
    return pltpu.VMEM((STEP * BLK, times * SEQ), kind)


def forward_call(x, wt, coef, interpret=False):
    f32, bf16 = jnp.float32, jnp.bfloat16
    n = x.shape[0]
    return pl.pallas_call(
        forward_kernel,
        grid=(n // STEP,),
        out_shape=[jax.ShapeDtypeStruct((n, BLK, SEQ), f32) for _ in range(5)],
        in_specs=[TOK, full(TWO, WROWS), full(BLK, SEQ)],
        out_specs=[TOK] * 5,
        scratch_shapes=[
            pltpu.VMEM((2 * SEQ, SEQ), bf16),
            pltpu.VMEM((2 * SEQ, SEQ), bf16),
            pltpu.VMEM((WROWS, STEP * SEQ), bf16),
            pltpu.VMEM((TWO, STEP * SEQ), f32),
            flat(), flat(), flat(), flat(), flat(bf16, 2), flat(), flat(bf16, 2), flat(),
        ],
        compiler_params=params(),
        interpret=interpret,
    )(x, wt, coef)


def backward_call(factor, x, c, made, w, coef, grad_dtype=jnp.bfloat16, interpret=False):
    f32, bf16 = jnp.float32, jnp.bfloat16
    n = x.shape[0]
    return pl.pallas_call(
        functools.partial(backward_kernel, factor),
        grid=(n // STEP,),
        out_shape=[
            jax.ShapeDtypeStruct((n, BLK, SEQ), bf16),
            jax.ShapeDtypeStruct((WROWS, WCOLS), grad_dtype),
        ],
        in_specs=[TOK] * 7 + [full(WROWS, WCOLS), full(BLK, SEQ)],
        out_specs=[TOK, full(WROWS, WCOLS)],
        scratch_shapes=[
            pltpu.VMEM((2 * SEQ, SEQ), bf16),
            pltpu.VMEM((WROWS, STEP * SEQ), bf16),
            pltpu.VMEM((TWO, STEP * SEQ), bf16),
            flat(bf16, 2),
            flat(),
            pltpu.VMEM((BLK, STEP * SEQ), f32),
            pltpu.VMEM((BLK, SEQ), f32),
            pltpu.VMEM((WROWS, WCOLS), f32),
        ],
        compiler_params=params(),
        interpret=interpret,
    )(x, c, *made, w, coef)


def wire(wa, wx, ba, bx, decay):
    bf16 = jnp.bfloat16
    tail = jnp.zeros((WROWS - BLK - 2, TWO), bf16)
    body = jnp.concatenate(
        [
            jnp.concatenate([wa, wx], axis=1),
            jnp.concatenate([ba, bx])[None],
            jnp.concatenate([decay, jnp.zeros((BLK,), bf16)])[None],
            tail,
        ],
        axis=0,
    )
    return jnp.pad(body, ((0, 0), (0, WCOLS - TWO)))


def unwire(w):
    wt = w[:, :TWO].T
    coef = (-8.0 * LOG2E) * jax.nn.softplus(w[BLK + 1, :BLK].astype(jnp.float32))
    return wt, jnp.broadcast_to(coef[:, None], (BLK, SEQ))


def per_device(inputs, cotangent, wa, wx, ba, bx, decay):
    bf16, f32 = jnp.bfloat16, jnp.float32
    plane, line = ("cuts", "yh", "core"), ("cuts", "z")
    z = lax.axis_index("z").astype(jnp.int32).reshape(1)
    pairs = [(i, k, (k + i) % NZ) for i in range(NI) for k in range(NZ)]
    fetch = [(i * NZ + src, i * NZ + k) for i, k, src in pairs]
    home = [(b, a) for a, b in fetch]

    x = lax.all_to_all(pack(z, inputs, z), plane, 0, 0, tiled=True)
    w = lax.ppermute(wire(wa, wx, ba, bx, decay), line, fetch)
    c = lax.all_to_all(pack(z, cotangent, w), plane, 0, 0, tiled=True)
    wt, coef = unwire(w)
    made = forward_call(x, wt, coef)
    total = SEQ * NSEQ * NZ
    out, grads = backward_call(float(total) ** -0.5, x, c, made, w, coef)
    share = lax.ppermute(grads, line, home)
    input_grad = unpack(z, lax.all_to_all(out, plane, 0, 0, tiled=True))
    parts = [share] + [lax.ppermute(share, "cuts", [(i, (i + 2 * k) % NI) for i in range(NI)]) for k in (1, 2, 3)]
    half = sum(p.astype(f32) for p in parts).astype(bf16)
    other = lax.ppermute(half, "cuts", [(i, i ^ 1) for i in range(NI)])
    full_sum = half.astype(f32) + other.astype(f32)
    own = jax.nn.sigmoid(decay.astype(f32))
    return (
        input_grad,
        full_sum[:BLK, :BLK],
        full_sum[:BLK, BLK:TWO],
        full_sum[BLK, :BLK],
        full_sum[BLK, BLK:TWO],
        full_sum[BLK + 1, :BLK] * own,
    )


def solution(mesh):
    fine = Mesh(mesh.devices.reshape(NI, NZ, NY, NC), ("cuts", "z", "yh", "core"))
    zero = ("z", "yh", "core")
    rows = P(("cuts",) + zero, None)
    return jax.shard_map(
        per_device,
        mesh=fine,
        in_specs=(rows, rows, P(zero, None), P(zero, None), P(zero), P(zero), P(zero)),
        out_specs=(rows, P(zero, None), P(zero, None), P(zero), P(zero), P(zero)),
        check_vma=False,
    )
```

time: 123 us -> 130 us (1.057); the launches traced: 122 us -> 128 us
  Pallas kernels: 26.6 us -> 36.7 us
  waiting for transfers between devices: 45.9 us -> 39.1 us
    all_to_all x1 -> x2, waiting for transfers between devices: 32.8 us -> 19.7 us  [the longest x1 16.2 us: per_device(): x = lax.all_to_all(pack(z, inputs, z), plane, 0, 0, tiled=True)]
    pallas_call x2 -> x4, Pallas kernels: 23.7 us -> 33.9 us  [the longest x1 15.8 us: forward_call(): pl.pallas_call(forward_kernel, grid=(n // STEP,), out_shape=[jax.ShapeDty...]
    ppermute x7 -> x4, starting transfers between devices: 24.8 us -> 16 us  [the longest x3 14.5 us: per_device(): lax.ppermute(share, 'cuts', [(i, (i + 2 * k) % NI) for i in range(NI)])]
    all_to_all x1 -> x2, starting transfers between devices: 8.73 us -> 16.8 us  [the longest x1 8.73 us: per_device(): x = lax.all_to_all(pack(z, inputs, z), plane, 0, 0, tiled=True)]
    ppermute x7 -> x4, waiting for transfers between devices: 13.1 us -> 19.4 us  [the longest x1 19.4 us: per_device(): other = lax.ppermute(half, 'cuts', [(i, i ^ 1) for i in range(NI)])]
    unnamed x18 -> x20, local copies, waits for them, and re-layouts: 2.1 us -> 4.04 us
  transfers between devices with their start and end apart: 11 -> 9, of which waited for: 5 -> 3; matrix products, arithmetic and copies ran while one was open for 4% -> 3% of each run, Pallas kernels for 0% -> 15%
where the time goes in v4:
time: 130 us; the launch traced here: 128 us
  starting transfers between devices  43 us (33%)
  waiting for transfers between devices  39.1 us (30%)
  Pallas kernels  36.7 us (28%)
  local copies, waits for them, and re-layouts  7.15 us (6%)
    ppermute x1, waiting for transfers between devices, per_device(): other = lax.ppermute(half, 'cuts', [(i, i ^ 1) for i in range(NI)])  19.4 us
    all_to_all x1, waiting for transfers between devices, per_device(): x = lax.all_to_all(pack(z, inputs, z), plane, 0, 0, tiled=True)  16.2 us
    pallas_call x1, Pallas kernels, forward_call(): pl.pallas_call(forward_kernel, grid=(n // STEP,), out_shape=[jax.ShapeDty...  15.8 us
    ppermute x3, starting transfers between devices, per_device(): lax.ppermute(share, 'cuts', [(i, (i + 2 * k) % NI) for i in range(NI)])  14.5 us
    pallas_call x1, Pallas kernels, backward_call(): pl.pallas_call(functools.partial(backward_kernel, factor), grid=(n // STE...  12.2 us
    all_to_all x1, starting transfers between devices, per_device(): x = lax.all_to_all(pack(z, inputs, z), plane, 0, 0, tiled=True)  8.73 us
    all_to_all x1, starting transfers between devices, per_device(): c = lax.all_to_all(pack(z, cotangent, w), plane, 0, 0, tiled=True)  8.12 us
    all_to_all x1, starting transfers between devices, per_device(): input_grad = unpack(z, lax.all_to_all(out, plane, 0, 0, tiled=True))  7.91 us
  transfers between devices with their start and end apart: 9, of which 3 were waited for; matrix products, arithmetic and copies ran while one was open for 3% of the time, Pallas kernels for 15%

profile of v4, /device:TPU:1, one launch (start us, length us, event | category | flops | bytes accessed | tf_op | source)
XLA Modules:
  0.0 127.7 jit_solution(9543897044059873931)
XLA Ops:
  0.6 2.9 %shard_map.118 = bf16[32,176,128]{2,1,0:T(8,128)(2,1)} custom-call(s32[1]{0:T(128)} %bitcast.z_ref.after_ref, bf16[128,5632]{1,0:T(8,128)(2,1)} %x_ref.2, s32[1]{0:T(128)} %bitcast.z_ref.after_ref), custom_call_target="tpu_custom_call" | custom-call | tf_op jit(solution)/shard_map/pallas_call | solution.py:49
  3.5 0.0 copy-start.8
  3.5 0.0 copy-start.9
  3.5 0.0 copy-start.7
  3.5 0.0 copy-start.5
  3.5 0.0 copy-start.6
  3.5 8.7 %all-to-all-start = ((bf16[32,176,128]{2,1,0:T(8,128)(2,1)}), bf16[32,176,128]{2,1,0:T(8,128)(2,1)S(1)}, u32[]{:S(2)}, u32[]{:S(2)}) async-start(bf16[32,176,128]{2,1,0:T(8,128)(2,1)} %shard_map.118), calls=%async_computation | async-start | bytes 2883584 | tf_op jit(solution)/shard_map/all_to_all | solution.py:313
  12.3 0.0 copy-done.8
  12.3 0.0 copy-done.9
  12.3 0.1 pad_maximum_fusion
  12.4 0.0 copy-done.7
  12.4 0.1 pad.10.clone
  12.5 0.0 copy-done.5
  12.5 0.0 copy-done.6
  12.5 0.1 maximum_maximum_fusion
  12.7 0.7 collective-permute-start
  13.3 0.0 collective-permute-done.after_ref.w_ref
  13.3 0.0 copy-start.3
  13.4 0.7 copy-done.3
  14.0 2.9 %shard_map.119 = bf16[32,176,128]{2,1,0:T(8,128)(2,1)} custom-call(s32[1]{0:T(128)} %bitcast.z_ref.after_ref, bf16[128,5632]{1,0:T(8,128)(2,1)} %x_ref.3, bf16[192,384]{1,0:T(8,128)(2,1)} %copy-done.3), custom_call_target="tpu_custom_call" | custom-call | tf_op jit(solution)/shard_map/pallas_call | solution.py:49
  16.9 16.2 %all-to-all-done.x_ref = bf16[32,176,128]{2,1,0:T(8,128)(2,1)S(1)} async-done(((bf16[32,176,128]{2,1,0:T(8,128)(2,1)}), bf16[32,176,128]{2,1,0:T(8,128)(2,1)S(1)}, u32[]{:S(2)}, u32[]{:S(2)}) %all-to-all-start) | async-done | bytes 1441824 | tf_op jit(solution)/shard_map/all_to_all | solution.py:313
  33.2 1.1 copy-done
  34.3 8.1 %all-to-all-start.1 = ((bf16[32,176,128]{2,1,0:T(8,128)(2,1)}), bf16[32,176,128]{2,1,0:T(8,128)(2,1)S(1)}, u32[]{:S(2)}, u32[]{:S(2)}) async-start(bf16[32,176,128]{2,1,0:T(8,128)(2,1)} %shard_map.119), calls=%async_computation.1 | async-start | bytes 2883584 | tf_op jit(solution)/shard_map/all_to_all | solution.py:315
  42.4 0.0 copy-done.4
  42.4 0.8 copy.13.wt_ref
  43.3 0.7 broadcast_in_dim.19.coef_ref
  44.0 15.8 %shard_map.120 = (f32[32,176,128]{2,1,0:T(8,128)}, f32[32,176,128]{2,1,0:T(8,128)}, f32[32,176,128]{2,1,0:T(8,128)}, f32[32,176,128]{2,1,0:T(8,128)}, f32[32,176,128]{2,1,0:T(8,128)}) custom-call(bf16[32,176,128]{2,1,0:T(8,128)(2,1)} %copy-done, bf16[352,192]{1,0:T(8,128)(2,1)} %copy.13.wt_ref, f32[176,128]{1,0:T(8,128)} %broadcast_in_dim.19.coef_ref), custom_call_target="tpu_custom_call" | custom-call | tf_op jit(solution)/shard_map/pallas_call | solution.py:239
  59.8 3.5 %all-to-all-done.1.c_ref = bf16[32,176,128]{2,1,0:T(8,128)(2,1)S(1)} async-done(((bf16[32,176,128]{2,1,0:T(8,128)(2,1)}), bf16[32,176,128]{2,1,0:T(8,128)(2,1)S(1)}, u32[]{:S(2)}, u32[]{:S(2)}) %all-to-all-start.1) | async-done | bytes 1441824 | tf_op jit(solution)/shard_map/all_to_all | solution.py:315
  63.3 1.1 copy-done.2
  64.4 12.2 %shard_map.121 = (bf16[32,176,128]{2,1,0:T(8,128)(2,1)}, bf16[192,384]{1,0:T(8,128)(2,1)}) custom-call(bf16[32,176,128]{2,1,0:T(8,128)(2,1)} %copy-done, bf16[32,176,128]{2,1,0:T(8,128)(2,1)} %copy-done.2, f32[32,176,128]{2,1,0:T(8,128)} %get-tuple-element.13.log_ref, f32[32,176,128]{2,1,0:T(8,128)} %get-tuple-element.14.a1_ref, ...), custom_call_target="tpu_custom_call" | custom-call | tf_op jit(solution)/shard_map/pallas_call | solution.py:260
  76.6 1.6 %collective-permute-start.1 = (bf16[192,384]{1,0:T(8,128)(2,1)}, bf16[192,384]{1,0:T(8,128)(2,1)S(1)}, u32[]{:S(2)}, u32[]{:S(2)}) collective-permute-start(bf16[192,384]{1,0:T(8,128)(2,1)} %get-tuple-element.19), channel_id=1, source_target_pairs={{0,0},{4,4},{8,8},{12,12},{16,16},{20,20},{24,24},{28,28},{32,36},... | collective-permute-start | bytes 442376 | tf_op jit(solution)/shard_map/ppermute | solution.py:320
  78.2 0.0 collective-permute-done.1
  78.2 12.3 %collective-permute-start.4 = (bf16[192,384]{1,0:T(8,128)(2,1)S(1)}, bf16[192,384]{1,0:T(8,128)(2,1)S(1)}, u32[]{:S(2)}, u32[]{:S(2)}) collective-permute-start(bf16[192,384]{1,0:T(8,128)(2,1)S(1)} %collective-permute-done.1), channel_id=1, source_target_pairs={{0,192},{32,224},{64,0},{96,32},{128,64},{160,96},{192,128},{224,1... | collective-permute-start | bytes 442376 | tf_op jit(solution)/shard_map/ppermute | solution.py:322
  90.5 2.2 %collective-permute-start.3 = (bf16[192,384]{1,0:T(8,128)(2,1)S(1)}, bf16[192,384]{1,0:T(8,128)(2,1)S(1)}, u32[]{:S(2)}, u32[]{:S(2)}) collective-permute-start(bf16[192,384]{1,0:T(8,128)(2,1)S(1)} %collective-permute-done.1), channel_id=1, source_target_pairs={{0,128},{32,160},{64,192},{96,224},{128,0},{160,32},{192,64},{224,... | collective-permute-start | bytes 442376 | tf_op jit(solution)/shard_map/ppermute | solution.py:322
  92.7 0.0 collective-permute-start.2
  92.7 7.9 %all-to-all-start.2 = ((bf16[32,176,128]{2,1,0:T(8,128)(2,1)}), bf16[32,176,128]{2,1,0:T(8,128)(2,1)S(1)}, u32[]{:S(2)}, u32[]{:S(2)}) async-start(bf16[32,176,128]{2,1,0:T(8,128)(2,1)} %get-tuple-element.18), calls=%async_computation.2 | async-start | bytes 2883584 | tf_op jit(solution)/shard_map/all_to_all | solution.py:321
  100.6 0.0 collective-permute-done.4
  100.6 0.0 collective-permute-done.3
  100.6 0.0 collective-permute-done.2
  100.7 0.1 add_convert_fusion
  100.7 1.5 %collective-permute-start.5 = (bf16[192,384]{1,0:T(8,128)(2,1)S(1)}, bf16[192,384]{1,0:T(8,128)(2,1)S(1)}, u32[]{:S(2)}, u32[]{:S(2)}) collective-permute-start(bf16[192,384]{1,0:T(8,128)(2,1)S(1)} %add_convert_fusion), channel_id=1, source_target_pairs={{0,32},{32,0},{64,96},{96,64},{128,160},{160,128},{192,224},{224,1... | collective-permute-start | bytes 442376 | tf_op jit(solution)/shard_map/ppermute | solution.py:324
  102.2 19.4 %collective-permute-done.5 = bf16[192,384]{1,0:T(8,128)(2,1)S(1)} collective-permute-done((bf16[192,384]{1,0:T(8,128)(2,1)S(1)}, bf16[192,384]{1,0:T(8,128)(2,1)S(1)}, u32[]{:S(2)}, u32[]{:S(2)}) %collective-permute-start.5) | collective-permute-done | bytes 147488 | tf_op jit(solution)/shard_map/ppermute | solution.py:324
  121.6 0.6 fusion.1
  122.3 0.6 divide_multiply_fusion
  122.9 0.8 fusion.2
  123.7 0.0 all-to-all-done.2.in_ref
  123.7 1.1 copy-done.1
  124.8 2.9 %shard_map.122 = bf16[128,5632]{1,0:T(8,128)(2,1)} custom-call(s32[1]{0:T(128)} %bitcast.z_ref.after_ref, bf16[32,176,128]{2,1,0:T(8,128)(2,1)} %copy-done.1), custom_call_target="tpu_custom_call" | custom-call | tf_op jit(solution)/shard_map/pallas_call | solution.py:60
  (13 shorter events, 0.1 us)
Async XLA Ops:
  3.5 8.8 %copy-start.8 = (bf16[176]{0:T(256)(128)(2,1)S(1)}, bf16[176]{0:T(256)(128)(2,1)}, u32[]{:S(2)}) copy-start(bf16[176]{0:T(256)(128)(2,1)} %param.12) | copy-start | bytes 1060
  3.5 8.8 %copy-start.9 = (bf16[176]{0:T(256)(128)(2,1)S(1)}, bf16[176]{0:T(256)(128)(2,1)}, u32[]{:S(2)}) copy-start(bf16[176]{0:T(256)(128)(2,1)} %param.11) | copy-start | bytes 1060
  3.5 8.9 %copy-start.7 = (bf16[176]{0:T(256)(128)(2,1)S(1)}, bf16[176]{0:T(256)(128)(2,1)}, u32[]{:S(2)}) copy-start(bf16[176]{0:T(256)(128)(2,1)} %param.13) | copy-start | bytes 1060
  3.5 9.0 %copy-start.5 = (bf16[176,176]{1,0:T(8,128)(2,1)S(1)}, bf16[176,176]{1,0:T(8,128)(2,1)}, u32[]{:S(2)}) copy-start(bf16[176,176]{1,0:T(8,128)(2,1)} %param.10) | copy-start | bytes 185860
  3.5 9.0 %copy-start.6 = (bf16[176,176]{1,0:T(8,128)(2,1)S(1)}, bf16[176,176]{1,0:T(8,128)(2,1)}, u32[]{:S(2)}) copy-start(bf16[176,176]{1,0:T(8,128)(2,1)} %param.9) | copy-start | bytes 185860
  3.5 29.6 %all-to-all-start = ((bf16[32,176,128]{2,1,0:T(8,128)(2,1)}), bf16[32,176,128]{2,1,0:T(8,128)(2,1)S(1)}, u32[]{:S(2)}, u32[]{:S(2)}) async-start(bf16[32,176,128]{2,1,0:T(8,128)(2,1)} %shard_map.118), calls=%async_computation | async-start | bytes 2883584 | tf_op jit(solution)/shard_map/all_to_all | solution.py:313
  12.7 0.7 collective-permute-start
  13.3 0.7 copy-start.3
  16.9 25.5 %copy-start.4 = (bf16[192,384]{1,0:T(8,128)(2,1)S(1)}, bf16[192,384]{1,0:T(8,128)(2,1)}, u32[]{:S(2)}) copy-start(bf16[192,384]{1,0:T(8,128)(2,1)} %copy-done.3) | copy-start | bytes 442372
  33.2 1.1 copy-start
  34.3 29.0 %all-to-all-start.1 = ((bf16[32,176,128]{2,1,0:T(8,128)(2,1)}), bf16[32,176,128]{2,1,0:T(8,128)(2,1)S(1)}, u32[]{:S(2)}, u32[]{:S(2)}) async-start(bf16[32,176,128]{2,1,0:T(8,128)(2,1)} %shard_map.119), calls=%async_computation.1 | async-start | bytes 2883584 | tf_op jit(solution)/shard_map/all_to_all | solution.py:315
  63.3 1.1 copy-start.2
  76.6 1.6 %collective-permute-start.1 = (bf16[192,384]{1,0:T(8,128)(2,1)}, bf16[192,384]{1,0:T(8,128)(2,1)S(1)}, u32[]{:S(2)}, u32[]{:S(2)}) collective-permute-start(bf16[192,384]{1,0:T(8,128)(2,1)} %get-tuple-element.19), channel_id=1, source_target_pairs={{0,0},{4,4},{8,8},{12,12},{16,16},{20,20},{24,24},{28,28},{32,36},... | collective-permute-start | bytes 442376 | tf_op jit(solution)/shard_map/ppermute | solution.py:320
  78.2 22.4 %collective-permute-start.4 = (bf16[192,384]{1,0:T(8,128)(2,1)S(1)}, bf16[192,384]{1,0:T(8,128)(2,1)S(1)}, u32[]{:S(2)}, u32[]{:S(2)}) collective-permute-start(bf16[192,384]{1,0:T(8,128)(2,1)S(1)} %collective-permute-done.1), channel_id=1, source_target_pairs={{0,192},{32,224},{64,0},{96,32},{128,64},{160,96},{192,128},{224,1... | collective-permute-start | bytes 442376 | tf_op jit(solution)/shard_map/ppermute | solution.py:322
  90.5 10.1 %collective-permute-start.3 = (bf16[192,384]{1,0:T(8,128)(2,1)S(1)}, bf16[192,384]{1,0:T(8,128)(2,1)S(1)}, u32[]{:S(2)}, u32[]{:S(2)}) collective-permute-start(bf16[192,384]{1,0:T(8,128)(2,1)S(1)} %collective-permute-done.1), channel_id=1, source_target_pairs={{0,128},{32,160},{64,192},{96,224},{128,0},{160,32},{192,64},{224,... | collective-permute-start | bytes 442376 | tf_op jit(solution)/shard_map/ppermute | solution.py:322
  92.7 7.9 %collective-permute-start.2 = (bf16[192,384]{1,0:T(8,128)(2,1)S(1)}, bf16[192,384]{1,0:T(8,128)(2,1)S(1)}, u32[]{:S(2)}, u32[]{:S(2)}) collective-permute-start(bf16[192,384]{1,0:T(8,128)(2,1)S(1)} %collective-permute-done.1), channel_id=1, source_target_pairs={{0,64},{32,96},{64,128},{96,160},{128,192},{160,224},{192,0},{224,... | collective-permute-start | bytes 442376 | tf_op jit(solution)/shard_map/ppermute | solution.py:322
  92.7 31.0 %all-to-all-start.2 = ((bf16[32,176,128]{2,1,0:T(8,128)(2,1)}), bf16[32,176,128]{2,1,0:T(8,128)(2,1)S(1)}, u32[]{:S(2)}, u32[]{:S(2)}) async-start(bf16[32,176,128]{2,1,0:T(8,128)(2,1)} %get-tuple-element.18), calls=%async_computation.2 | async-start | bytes 2883584 | tf_op jit(solution)/shard_map/all_to_all | solution.py:321
  100.7 20.9 %collective-permute-start.5 = (bf16[192,384]{1,0:T(8,128)(2,1)S(1)}, bf16[192,384]{1,0:T(8,128)(2,1)S(1)}, u32[]{:S(2)}, u32[]{:S(2)}) collective-permute-start(bf16[192,384]{1,0:T(8,128)(2,1)S(1)} %add_convert_fusion), channel_id=1, source_target_pairs={{0,32},{32,0},{64,96},{96,64},{128,160},{160,128},{192,224},{224,1... | collective-permute-start | bytes 442376 | tf_op jit(solution)/shard_map/ppermute | solution.py:324
  123.7 1.1 copy-start.1

commit v5 on v3

v5 whole, which is shorter than its diff:
```python
import functools

import jax
import jax.numpy as jnp
from jax import lax
from jax.experimental import pallas as pl
from jax.experimental.pallas import tpu as pltpu
from jax.sharding import Mesh
from jax.sharding import PartitionSpec as P

BLK = 176
TWO = 2 * BLK
WROWS = 192
WCOLS = 384
NZ, NY, NC = 8, 2, 2
NQ = NY * NC
NI = 8
SEQ = 128
NSEQ = NI * NQ
STEP = 8
VMEM_LIMIT = 56 * 1024 * 1024


def pack_kernel(z_ref, x_ref, c_ref, out_ref):
    odd = z_ref[0] & 1
    for k, ref in enumerate((x_ref, c_ref)):
        turned = ref[...].T
        for h in range(2 * NQ):
            slot = (h // NQ ^ odd) * NQ + h % NQ
            out_ref[slot, k * BLK : (k + 1) * BLK, :] = turned[h * BLK : (h + 1) * BLK, :]


def unpack_kernel(z_ref, in_ref, out_ref):
    odd = z_ref[0] & 1
    heads = [in_ref[(h // NQ ^ odd) * NQ + h % NQ] for h in range(2 * NQ)]
    out_ref[...] = jnp.concatenate(heads, axis=0).T


def params():
    return pltpu.CompilerParams(vmem_limit_bytes=VMEM_LIMIT)


def turn_specs(rows):
    wide = pl.BlockSpec((SEQ, 2 * NQ * BLK), lambda p, z: (0, p))
    tall = pl.BlockSpec((2 * NQ, rows, SEQ), lambda p, z: (p ^ (z[0] >> 1), 0, 0))
    return wide, tall


def pack(z, x, c, interpret=False):
    wide, tall = turn_specs(TWO)
    return pl.pallas_call(
        pack_kernel,
        grid_spec=pltpu.PrefetchScalarGridSpec(
            num_scalar_prefetch=1, grid=(NZ // 2,), in_specs=[wide, wide], out_specs=tall
        ),
        out_shape=jax.ShapeDtypeStruct((NSEQ, TWO, SEQ), x.dtype),
        compiler_params=params(),
        interpret=interpret,
    )(z, x, c)


def unpack(z, y, interpret=False):
    wide, tall = turn_specs(BLK)
    return pl.pallas_call(
        unpack_kernel,
        grid_spec=pltpu.PrefetchScalarGridSpec(
            num_scalar_prefetch=1, grid=(NZ // 2,), in_specs=[tall], out_specs=wide
        ),
        out_shape=jax.ShapeDtypeStruct((SEQ, NSEQ * BLK), y.dtype),
        compiler_params=params(),
        interpret=interpret,
    )(z, y)


LN2 = 0.6931471805599453
LOG2E = 1.4426950408889634


def sigmoid(pre):
    base = 1.0 + jnp.exp2(jnp.minimum(pre * -LOG2E, 115.0))
    rough = pl.reciprocal(base, approx=True)
    return rough * (2.0 - base * rough)


def one_minus_square(u):
    series, power = 0.0, 1.0
    terms = []
    for k in range(1, 8):
        power = power * (2.0 * LN2) / k
        terms.append(-power)
    series = terms[-1]
    for t in terms[-2::-1]:
        series = series * u + t
    return series * u


CH = 16


def main_kernel(
    factor, m_ref, w_ref, wt_ref, coef_ref, out_ref, g_ref,
    tri, x_s, pre_s, d_s, u_s, rest_s, own_s, f1_s, gain_s, drive_s, ub_s, log_s, fwd_in, rev_in, fwd_s, rev_s, q_s, g_s,
):
    step = pl.program_id(0)
    f32, bf16 = jnp.float32, jnp.bfloat16

    @pl.when(step == 0)
    def _():
        row = lax.broadcasted_iota(jnp.int32, (WROWS - BLK, STEP * SEQ), 0)
        x_s[BLK:, :] = jnp.where(row == 0, 1.0, 0.0).astype(x_s.dtype)
        q_s[...] = jnp.zeros_like(q_s)
        g_s[...] = jnp.zeros_like(g_s)
        src = lax.broadcasted_iota(jnp.int32, (2 * SEQ, 2 * SEQ), 0)
        dst = lax.broadcasted_iota(jnp.int32, (2 * SEQ, 2 * SEQ), 1)
        same = (src < SEQ) == (dst < SEQ)
        for k, seen in enumerate((src <= dst, src < dst, src >= dst)):
            tri[k] = jnp.where(seen & same, 1.0, 0.0).astype(bf16)

    for s in range(STEP):
        x_s[:BLK, s * SEQ : (s + 1) * SEQ] = m_ref[s, :BLK, :]
    pre_s[...] = jnp.dot(wt_ref[...], x_s[...], preferred_element_type=f32)

    def each(body):
        def two(p, _):
            for half in range(2):
                s = 2 * p + half
                cols = pl.ds(pl.multiple_of(s * SEQ, SEQ), SEQ)
                for r in range(0, BLK, CH):
                    rows = pl.ds(pl.multiple_of(p * BLK + r, 16), CH)
                    body(s, r, cols, (rows, slice(half * SEQ, (half + 1) * SEQ)))
            return 0

        lax.fori_loop(0, STEP // 2, two, 0)

    def gates(s, r, cols, at):
        x = m_ref[s, r : r + CH, :].astype(f32)
        rgate = sigmoid(pre_s[r : r + CH, cols])
        igate = sigmoid(pre_s[BLK + r : BLK + r + CH, cols])
        u = coef_ref[r : r + CH, :] * rgate
        var = one_minus_square(u)
        inv = lax.rsqrt(var)
        scale = var * inv
        ix = igate * x
        drive = scale * ix
        u_s[at] = u
        rest_s[at] = LN2 - LN2 * rgate
        own_s[at] = ix * (inv - scale)
        f1_s[at] = drive - drive * igate
        gain_s[at] = scale * igate
        drive_s[at] = drive
        ub_s[at] = u.astype(bf16)

    each(gates)
    log_s[...] = jnp.dot(ub_s[...], tri[0], preferred_element_type=f32)

    def weigh(s, r, cols, at):
        total = log_s[at]
        cot = m_ref[s, BLK + r : BLK + r + CH, :].astype(f32)
        fwd_in[at] = (drive_s[at] * jnp.exp2(-total)).astype(bf16)
        rev_in[at] = (cot * jnp.exp2(total)).astype(bf16)

    each(weigh)
    fwd_s[...] = jnp.dot(fwd_in[...], tri[1], preferred_element_type=f32)
    rev_s[...] = jnp.dot(rev_in[...], tri[2], preferred_element_type=f32)

    def deltas(s, r, cols, at):
        total = log_s[at]
        adj = rev_s[at] * jnp.exp2(-total)
        dlog = adj * (fwd_s[at] * jnp.exp2(total) - own_s[at])
        v = dlog * u_s[at]
        q_s[r : r + CH, :] += v
        d_s[r : r + CH, cols] = (v * rest_s[at]).astype(bf16)
        d_s[BLK + r : BLK + r + CH, cols] = (adj * f1_s[at]).astype(bf16)
        pre_s[r : r + CH, cols] = adj * gain_s[at]

    each(deltas)

    back = jnp.dot(w_ref[:BLK, :TWO], d_s[...], preferred_element_type=f32)
    for s in range(STEP):
        cols = slice(s * SEQ, (s + 1) * SEQ)
        out_ref[s] = (back[:, cols] + pre_s[:BLK, cols]).astype(out_ref.dtype)
    nt = (((1,), (1,)), ((), ()))
    g_s[:, :TWO] += lax.dot_general(x_s[...], d_s[...], nt, preferred_element_type=f32)

    @pl.when(step == pl.num_programs(0) - 1)
    def _():
        g_ref[...] = (g_s[...] * factor).astype(g_ref.dtype)
        decay = jnp.sum((q_s[...] / coef_ref[...]).T, axis=0, keepdims=True) * (-8.0 * factor)
        tail = g_s[BLK:, :BLK] * factor
        row = lax.broadcasted_iota(jnp.int32, tail.shape, 0)
        g_ref[BLK:, :BLK] = jnp.where(row == 1, decay, tail).astype(g_ref.dtype)


def main_call(factor, m, w, wt, coef, grad_dtype=jnp.bfloat16, interpret=False):
    f32, bf16 = jnp.float32, jnp.bfloat16
    n = m.shape[0]
    tok = lambda rows: pl.BlockSpec((STEP, rows, SEQ), lambda p: (p, 0, 0))
    full = lambda shape: pl.BlockSpec(shape, lambda p: (0, 0))
    flat, half = (pltpu.VMEM((STEP // 2 * BLK, 2 * SEQ), kind) for kind in (f32, bf16))
    return pl.pallas_call(
        functools.partial(main_kernel, factor),
        grid=(n // STEP,),
        out_shape=[
            jax.ShapeDtypeStruct((n, BLK, SEQ), bf16),
            jax.ShapeDtypeStruct((WROWS, WCOLS), grad_dtype),
        ],
        in_specs=[tok(TWO), full((WROWS, WCOLS)), full((TWO, WROWS)), full((BLK, SEQ))],
        out_specs=[tok(BLK), full((WROWS, WCOLS))],
        scratch_shapes=[
            pltpu.VMEM((3, 2 * SEQ, 2 * SEQ), bf16),
            pltpu.VMEM((WROWS, STEP * SEQ), bf16),
            pltpu.VMEM((TWO, STEP * SEQ), f32),
            pltpu.VMEM((TWO, STEP * SEQ), bf16),
            flat, flat, flat, flat, flat, flat,
            half, flat, half, half, flat, flat,
            pltpu.VMEM((BLK, SEQ), f32),
            pltpu.VMEM((WROWS, WCOLS), f32),
        ],
        compiler_params=params(),
        interpret=interpret,
    )(m, w, wt, coef)


def wire(wa, wx, ba, bx, decay):
    bf16 = jnp.bfloat16
    tail = jnp.zeros((WROWS - BLK - 2, TWO), bf16)
    body = jnp.concatenate(
        [
            jnp.concatenate([wa, wx], axis=1),
            jnp.concatenate([ba, bx])[None],
            jnp.concatenate([decay, jnp.zeros((BLK,), bf16)])[None],
            tail,
        ],
        axis=0,
    )
    return jnp.pad(body, ((0, 0), (0, WCOLS - TWO)))


def unwire(w):
    wt = w[:, :TWO].T
    coef = (-8.0 * LOG2E) * jax.nn.softplus(w[BLK + 1, :BLK].astype(jnp.float32))
    return wt, jnp.broadcast_to(coef[:, None], (BLK, SEQ))


def per_device(inputs, cotangent, wa, wx, ba, bx, decay):
    bf16, f32 = jnp.bfloat16, jnp.float32
    plane, line = ("cuts", "yh", "core"), ("cuts", "z")
    z = lax.axis_index("z").astype(jnp.int32).reshape(1)
    everyone = [(i, k) for i in range(NI) for k in range(NZ)]
    fetch = [(i * NZ + (k ^ i), i * NZ + k) for i, k in everyone]
    across = [(i * NZ + (k ^ i), (i ^ 1) * NZ + k) for i, k in everyone]

    got = lax.all_to_all(pack(z, inputs, cotangent), plane, 0, 0, tiled=True)
    w = lax.ppermute(wire(wa, wx, ba, bx, decay), line, fetch)
    wt, coef = unwire(w)
    total = SEQ * NSEQ * NZ
    out, grads = main_call(float(total) ** -0.5, got, w, wt, coef)
    input_grad = unpack(z, lax.all_to_all(out, plane, 0, 0, tiled=True))
    pair = lax.ppermute(grads, line, fetch).astype(f32) + lax.ppermute(grads, line, across).astype(f32)
    pair = pair.astype(bf16)
    parts = [pair] + [lax.ppermute(pair, "cuts", [(i, (i + 2 * k) % NI) for i in range(NI)]) for k in (1, 2, 3)]
    parts, input_grad = lax.optimization_barrier((parts, input_grad))
    full = sum(p.astype(f32) for p in parts)
    own = jax.nn.sigmoid(decay.astype(f32))
    return (
        input_grad,
        full[:BLK, :BLK],
        full[:BLK, BLK:TWO],
        full[BLK, :BLK],
        full[BLK, BLK:TWO],
        full[BLK + 1, :BLK] * own,
    )


def solution(mesh):
    fine = Mesh(mesh.devices.reshape(NI, NZ, NY, NC), ("cuts", "z", "yh", "core"))
    zero = ("z", "yh", "core")
    rows = P(("cuts",) + zero, None)
    return jax.shard_map(
        per_device,
        mesh=fine,
        in_specs=(rows, rows, P(zero, None), P(zero, None), P(zero), P(zero), P(zero)),
        out_specs=(rows, P(zero, None), P(zero, None), P(zero), P(zero), P(zero)),
        check_vma=False,
    )
```

time: 123 us -> 112 us (0.911)
  the two profiles are of different devices: /device:TPU:1 before, /device:TPU:16 now
where the time goes in v5:
time: 112 us
  waiting for transfers between devices  51.6 us (46%)
  starting transfers between devices  27 us (24%)
  Pallas kernels  25.3 us (23%)
  local copies, waits for them, and re-layouts  6.18 us (6%)
    all_to_all x1, waiting for transfers between devices, per_device(): got = lax.all_to_all(pack(z, inputs, cotangent), plane, 0, 0, tiled=True)  33.1 us
    ppermute x1, waiting for transfers between devices, per_device(): lax.ppermute(grads, line, across).astype(f32)  18.5 us
    pallas_call x1, Pallas kernels, main_call(): pl.pallas_call(functools.partial(main_kernel, factor), grid=(n // STEP,),...  17 us
    ppermute x3, starting transfers between devices, per_device(): lax.ppermute(pair, 'cuts', [(i, (i + 2 * k) % NI) for i in range(NI)])  10.2 us
    all_to_all x1, starting transfers between devices, per_device(): got = lax.all_to_all(pack(z, inputs, cotangent), plane, 0, 0, tiled=True)  7.56 us
    all_to_all x1, starting transfers between devices, per_device(): input_grad = unpack(z, lax.all_to_all(out, plane, 0, 0, tiled=True))  6.62 us
    pallas_call x1, Pallas kernels, pack(): pl.pallas_call(pack_kernel, grid_spec=pltpu.PrefetchScalarGridSpec(num_sc...  4.5 us
    pallas_call x1, Pallas kernels, unpack(): pl.pallas_call(unpack_kernel, grid_spec=pltpu.PrefetchScalarGridSpec(num_...  3.77 us
  transfers between devices with their start and end apart: 8, of which 2 were waited for; matrix products, arithmetic and copies ran while one was open for 2% of the time, Pallas kernels for 3%

profile of v5, /device:TPU:16, one launch (start us, length us, event | category | flops | bytes accessed | tf_op | source)
XLA Modules:
  0.0 112.0 jit_solution(18134437945238990583)
XLA Ops:
  0.6 4.5 %shard_map.118 = bf16[32,352,128]{2,1,0:T(8,128)(2,1)} custom-call(s32[1]{0:T(128)} %bitcast.z_ref, bf16[128,5632]{1,0:T(8,128)(2,1)} %x_ref.1, bf16[128,5632]{1,0:T(8,128)(2,1)} %c_ref.1), custom_call_target="tpu_custom_call" | custom-call | tf_op jit(solution)/shard_map/pallas_call | solution.py:51
  5.1 0.0 copy-start.4
  5.1 0.0 copy-start.5
  5.1 0.0 copy-start.6
  5.1 0.0 copy-start.2
  5.2 0.0 copy-start.3
  5.2 7.6 %all-to-all-start = ((bf16[32,352,128]{2,1,0:T(8,128)(2,1)}), bf16[32,352,128]{2,1,0:T(8,128)(2,1)S(1)}, u32[]{:S(2)}, u32[]{:S(2)}) async-start(bf16[32,352,128]{2,1,0:T(8,128)(2,1)} %shard_map.118), calls=%async_computation | async-start | bytes 5767168 | tf_op jit(solution)/shard_map/all_to_all | solution.py:253
  12.7 0.0 copy-done.4
  12.8 0.1 broadcast_in_dim.21
  12.9 0.0 copy-done.5
  12.9 0.0 copy-done.6
  12.9 0.1 pad_maximum_fusion
  13.0 0.1 broadcast_in_dim.20
  13.1 0.0 copy-done.2
  13.1 0.1 copy.17
  13.2 0.0 copy-done.3
  13.2 0.1 copy.16
  13.3 0.1 pad.10.clone
  13.4 0.1 maximum_maximum_fusion
  13.6 0.7 collective-permute-start
  14.3 0.0 collective-permute-done
  14.3 0.8 copy.20.w_ref
  15.1 0.2 convert_reduce_fusion
  15.3 0.7 slice_bitcast_fusion.wt_ref
  16.0 33.1 %all-to-all-done.m_ref = bf16[32,352,128]{2,1,0:T(8,128)(2,1)S(1)} async-done(((bf16[32,352,128]{2,1,0:T(8,128)(2,1)}), bf16[32,352,128]{2,1,0:T(8,128)(2,1)S(1)}, u32[]{:S(2)}, u32[]{:S(2)}) %all-to-all-start) | async-done | bytes 2883616 | tf_op jit(solution)/shard_map/all_to_all | solution.py:253
  49.0 0.0 copy-start
  49.0 0.8 broadcast_in_dim.19.coef_ref
  49.9 0.8 copy-done
  50.6 17.0 %shard_map.119 = (bf16[32,176,128]{2,1,0:T(8,128)(2,1)}, bf16[192,384]{1,0:T(8,128)(2,1)}) custom-call(bf16[32,352,128]{2,1,0:T(8,128)(2,1)} %copy-done, bf16[192,384]{1,0:T(8,128)(2,1)} %copy.20.w_ref, bf16[352,192]{1,0:T(8,128)(2,1)} %slice_bitcast_fusion.wt_ref, f32[176,128]{1,0:T(8,128)} %broadcast_in_dim.19.coef_ref), custom_call_target="tpu_custom_call" | custom-call | tf_op jit(solution)/shard_map/pallas_call | solution.py:200
  67.6 6.6 %all-to-all-start.1 = ((bf16[32,176,128]{2,1,0:T(8,128)(2,1)}), bf16[32,176,128]{2,1,0:T(8,128)(2,1)S(1)}, u32[]{:S(2)}, u32[]{:S(2)}) async-start(bf16[32,176,128]{2,1,0:T(8,128)(2,1)} %get-tuple-element.14), calls=%async_computation.1 | async-start | bytes 2883584 | tf_op jit(solution)/shard_map/all_to_all | solution.py:258
  74.3 0.0 copy-done.7
  74.3 1.2 %collective-permute-start.2 = (bf16[192,384]{1,0:T(8,128)(2,1)S(1)}, bf16[192,384]{1,0:T(8,128)(2,1)S(1)}, u32[]{:S(2)}, u32[]{:S(2)}) collective-permute-start(bf16[192,384]{1,0:T(8,128)(2,1)S(1)} %copy-done.7), channel_id=1, source_target_pairs={{0,32},{4,36},{8,40},{12,44},{16,48},{20,52},{24,56},{28,60},{36,0... | collective-permute-start | bytes 442376 | tf_op jit(solution)/shard_map/ppermute | solution.py:259
  75.5 0.7 collective-permute-start.1
  76.2 18.5 %collective-permute-done.2 = bf16[192,384]{1,0:T(8,128)(2,1)S(1)} collective-permute-done((bf16[192,384]{1,0:T(8,128)(2,1)S(1)}, bf16[192,384]{1,0:T(8,128)(2,1)S(1)}, u32[]{:S(2)}, u32[]{:S(2)}) %collective-permute-start.2) | collective-permute-done | bytes 147488 | tf_op jit(solution)/shard_map/ppermute | solution.py:259
  94.7 0.0 collective-permute-done.1
  94.7 0.1 collective-permute-start.3
  94.8 7.6 %collective-permute-start.4 = (bf16[192,384]{1,0:T(8,128)(2,1)S(1)}, bf16[192,384]{1,0:T(8,128)(2,1)S(1)}, u32[]{:S(2)}, u32[]{:S(2)}) collective-permute-start(bf16[192,384]{1,0:T(8,128)(2,1)S(1)} %add_convert_fusion), channel_id=1, source_target_pairs={{0,128},{32,160},{64,192},{96,224},{128,0},{160,32},{192,64},{224,... | collective-permute-start | bytes 442376 | tf_op jit(solution)/shard_map/ppermute | solution.py:261
  102.4 2.5 %collective-permute-start.5 = (bf16[192,384]{1,0:T(8,128)(2,1)S(1)}, bf16[192,384]{1,0:T(8,128)(2,1)S(1)}, u32[]{:S(2)}, u32[]{:S(2)}) collective-permute-start(bf16[192,384]{1,0:T(8,128)(2,1)S(1)} %add_convert_fusion), channel_id=1, source_target_pairs={{0,192},{32,224},{64,0},{96,32},{128,64},{160,96},{192,128},{224,1... | collective-permute-start | bytes 442376 | tf_op jit(solution)/shard_map/ppermute | solution.py:261
  105.0 0.0 all-to-all-done.1.in_ref
  105.0 1.1 copy-done.1
  106.1 3.8 %shard_map.120 = bf16[128,5632]{1,0:T(8,128)(2,1)} custom-call(s32[1]{0:T(128)} %bitcast.z_ref, bf16[32,176,128]{2,1,0:T(8,128)(2,1)} %copy-done.1), custom_call_target="tpu_custom_call" | custom-call | tf_op jit(solution)/shard_map/pallas_call | solution.py:64
  109.9 0.0 collective-permute-done.3
  109.9 0.0 collective-permute-done.4
  109.9 0.0 collective-permute-done.5
  109.9 0.1 convert_add_fusion
  110.0 0.8 fusion.2
  110.8 0.6 fusion.1
  111.4 0.6 divide_multiply_fusion
  (7 shorter events, 0.1 us)
Async XLA Ops:
  5.1 7.6 %copy-start.4 = (bf16[176]{0:T(256)(128)(2,1)S(1)}, bf16[176]{0:T(256)(128)(2,1)}, u32[]{:S(2)}) copy-start(bf16[176]{0:T(256)(128)(2,1)} %param.13) | copy-start | bytes 1060
  5.1 7.7 %copy-start.5 = (bf16[176]{0:T(256)(128)(2,1)S(1)}, bf16[176]{0:T(256)(128)(2,1)}, u32[]{:S(2)}) copy-start(bf16[176]{0:T(256)(128)(2,1)} %param.12) | copy-start | bytes 1060
  5.1 7.8 %copy-start.6 = (bf16[176]{0:T(256)(128)(2,1)S(1)}, bf16[176]{0:T(256)(128)(2,1)}, u32[]{:S(2)}) copy-start(bf16[176]{0:T(256)(128)(2,1)} %param.11) | copy-start | bytes 1060
  5.1 8.0 %copy-start.2 = (bf16[176,176]{1,0:T(8,128)(2,1)S(1)}, bf16[176,176]{1,0:T(8,128)(2,1)}, u32[]{:S(2)}) copy-start(bf16[176,176]{1,0:T(8,128)(2,1)} %param.10) | copy-start | bytes 185860
  5.2 8.1 %copy-start.3 = (bf16[176,176]{1,0:T(8,128)(2,1)S(1)}, bf16[176,176]{1,0:T(8,128)(2,1)}, u32[]{:S(2)}) copy-start(bf16[176,176]{1,0:T(8,128)(2,1)} %param.9) | copy-start | bytes 185860
  5.2 43.9 %all-to-all-start = ((bf16[32,352,128]{2,1,0:T(8,128)(2,1)}), bf16[32,352,128]{2,1,0:T(8,128)(2,1)S(1)}, u32[]{:S(2)}, u32[]{:S(2)}) async-start(bf16[32,352,128]{2,1,0:T(8,128)(2,1)} %shard_map.118), calls=%async_computation | async-start | bytes 5767168 | tf_op jit(solution)/shard_map/all_to_all | solution.py:253
  13.6 0.7 collective-permute-start
  49.0 1.6 %copy-start = (bf16[32,352,128]{2,1,0:T(8,128)(2,1)}, bf16[32,352,128]{2,1,0:T(8,128)(2,1)S(1)}, u32[]{:S(2)}) copy-start(bf16[32,352,128]{2,1,0:T(8,128)(2,1)S(1)} %all-to-all-done.m_ref) | copy-start | bytes 8650756
  67.6 6.6 %copy-start.7 = (bf16[192,384]{1,0:T(8,128)(2,1)S(1)}, bf16[192,384]{1,0:T(8,128)(2,1)}, u32[]{:S(2)}) copy-start(bf16[192,384]{1,0:T(8,128)(2,1)} %get-tuple-element.13) | copy-start | bytes 442372
  67.6 37.3 %all-to-all-start.1 = ((bf16[32,176,128]{2,1,0:T(8,128)(2,1)}), bf16[32,176,128]{2,1,0:T(8,128)(2,1)S(1)}, u32[]{:S(2)}, u32[]{:S(2)}) async-start(bf16[32,176,128]{2,1,0:T(8,128)(2,1)} %get-tuple-element.14), calls=%async_computation.1 | async-start | bytes 2883584 | tf_op jit(solution)/shard_map/all_to_all | solution.py:258
  74.3 20.4 %collective-permute-start.2 = (bf16[192,384]{1,0:T(8,128)(2,1)S(1)}, bf16[192,384]{1,0:T(8,128)(2,1)S(1)}, u32[]{:S(2)}, u32[]{:S(2)}) collective-permute-start(bf16[192,384]{1,0:T(8,128)(2,1)S(1)} %copy-done.7), channel_id=1, source_target_pairs={{0,32},{4,36},{8,40},{12,44},{16,48},{20,52},{24,56},{28,60},{36,0... | collective-permute-start | bytes 442376 | tf_op jit(solution)/shard_map/ppermute | solution.py:259
  75.5 19.1 %collective-permute-start.1 = (bf16[192,384]{1,0:T(8,128)(2,1)S(1)}, bf16[192,384]{1,0:T(8,128)(2,1)S(1)}, u32[]{:S(2)}, u32[]{:S(2)}) collective-permute-start(bf16[192,384]{1,0:T(8,128)(2,1)S(1)} %copy-done.7), channel_id=1, source_target_pairs={{0,0},{4,4},{8,8},{12,12},{16,16},{20,20},{24,24},{28,28},{36,32},... | collective-permute-start | bytes 442376 | tf_op jit(solution)/shard_map/ppermute | solution.py:259
  94.7 15.2 %collective-permute-start.3 = (bf16[192,384]{1,0:T(8,128)(2,1)S(1)}, bf16[192,384]{1,0:T(8,128)(2,1)S(1)}, u32[]{:S(2)}, u32[]{:S(2)}) collective-permute-start(bf16[192,384]{1,0:T(8,128)(2,1)S(1)} %add_convert_fusion), channel_id=1, source_target_pairs={{0,64},{32,96},{64,128},{96,160},{128,192},{160,224},{192,0},{224,... | collective-permute-start | bytes 442376 | tf_op jit(solution)/shard_map/ppermute | solution.py:261
  94.8 15.1 %collective-permute-start.4 = (bf16[192,384]{1,0:T(8,128)(2,1)S(1)}, bf16[192,384]{1,0:T(8,128)(2,1)S(1)}, u32[]{:S(2)}, u32[]{:S(2)}) collective-permute-start(bf16[192,384]{1,0:T(8,128)(2,1)S(1)} %add_convert_fusion), channel_id=1, source_target_pairs={{0,128},{32,160},{64,192},{96,224},{128,0},{160,32},{192,64},{224,... | collective-permute-start | bytes 442376 | tf_op jit(solution)/shard_map/ppermute | solution.py:261
  102.4 7.4 %collective-permute-start.5 = (bf16[192,384]{1,0:T(8,128)(2,1)S(1)}, bf16[192,384]{1,0:T(8,128)(2,1)S(1)}, u32[]{:S(2)}, u32[]{:S(2)}) collective-permute-start(bf16[192,384]{1,0:T(8,128)(2,1)S(1)} %add_convert_fusion), channel_id=1, source_target_pairs={{0,192},{32,224},{64,0},{96,32},{128,64},{160,96},{192,128},{224,1... | collective-permute-start | bytes 442376 | tf_op jit(solution)/shard_map/ppermute | solution.py:261
  105.0 1.1 copy-start.1

commit v6 on v5

--- a/solution.py
+++ b/solution.py
@@ -17,42 +17,39 @@
 NI = 8
 SEQ = 128
 NSEQ = NI * NQ
-STEP = 8
+STEP = 32
 VMEM_LIMIT = 56 * 1024 * 1024
 
 
 def pack_kernel(z_ref, x_ref, c_ref, out_ref):
-    odd = z_ref[0] & 1
+    turn = z_ref[0] * NQ
     for k, ref in enumerate((x_ref, c_ref)):
-        turned = ref[...].T
-        for h in range(2 * NQ):
-            slot = (h // NQ ^ odd) * NQ + h % NQ
-            out_ref[slot, k * BLK : (k + 1) * BLK, :] = turned[h * BLK : (h + 1) * BLK, :]
+        for p in range(NZ // 2):
+            turned = ref[:, p * 2 * NQ * BLK : (p + 1) * 2 * NQ * BLK].T
+            for h in range(2 * NQ):
+                out_ref[(2 * NQ * p + h) ^ turn, k * BLK : (k + 1) * BLK, :] = turned[h * BLK : (h + 1) * BLK, :]
 
 
 def unpack_kernel(z_ref, in_ref, out_ref):
-    odd = z_ref[0] & 1
-    heads = [in_ref[(h // NQ ^ odd) * NQ + h % NQ] for h in range(2 * NQ)]
-    out_ref[...] = jnp.concatenate(heads, axis=0).T
+    turn = z_ref[0] * NQ
+    for p in range(NZ // 2):
+        heads = [in_ref[(2 * NQ * p + h) ^ turn] for h in range(2 * NQ)]
+        out_ref[:, p * 2 * NQ * BLK : (p + 1) * 2 * NQ * BLK] = jnp.concatenate(heads, axis=0).T
 
 
 def params():
     return pltpu.CompilerParams(vmem_limit_bytes=VMEM_LIMIT)
 
 
-def turn_specs(rows):
-    wide = pl.BlockSpec((SEQ, 2 * NQ * BLK), lambda p, z: (0, p))
-    tall = pl.BlockSpec((2 * NQ, rows, SEQ), lambda p, z: (p ^ (z[0] >> 1), 0, 0))
-    return wide, tall
+SMEM = pl.BlockSpec(memory_space=pltpu.SMEM)
+VMEM = pl.BlockSpec(memory_space=pltpu.VMEM)
 
 
 def pack(z, x, c, interpret=False):
-    wide, tall = turn_specs(TWO)
     return pl.pallas_call(
         pack_kernel,
-        grid_spec=pltpu.PrefetchScalarGridSpec(
-            num_scalar_prefetch=1, grid=(NZ // 2,), in_specs=[wide, wide], out_specs=tall
-        ),
+        in_specs=[SMEM, VMEM, VMEM],
+        out_specs=VMEM,
         out_shape=jax.ShapeDtypeStruct((NSEQ, TWO, SEQ), x.dtype),
         compiler_params=params(),
         interpret=interpret,
@@ -60,12 +57,10 @@
 
 
 def unpack(z, y, interpret=False):
-    wide, tall = turn_specs(BLK)
     return pl.pallas_call(
         unpack_kernel,
-        grid_spec=pltpu.PrefetchScalarGridSpec(
-            num_scalar_prefetch=1, grid=(NZ // 2,), in_specs=[tall], out_specs=wide
-        ),
+        in_specs=[SMEM, VMEM],
+        out_specs=VMEM,
         out_shape=jax.ShapeDtypeStruct((SEQ, NSEQ * BLK), y.dtype),
         compiler_params=params(),
         interpret=interpret,
@@ -77,15 +72,13 @@
 
 
 def sigmoid(pre):
-    base = 1.0 + jnp.exp2(jnp.minimum(pre * -LOG2E, 115.0))
-    rough = pl.reciprocal(base, approx=True)
-    return rough * (2.0 - base * rough)
+    return pl.reciprocal(1.0 + jnp.exp2(jnp.minimum(pre * -LOG2E, 115.0)), approx=True)
 
 
 def one_minus_square(u):
     series, power = 0.0, 1.0
     terms = []
-    for k in range(1, 8):
+    for k in range(1, 7):
         power = power * (2.0 * LN2) / k
         terms.append(-power)
     series = terms[-1]
@@ -98,8 +91,8 @@
 
 
 def main_kernel(
-    factor, m_ref, w_ref, wt_ref, coef_ref, out_ref, g_ref,
-    tri, x_s, pre_s, d_s, u_s, rest_s, own_s, f1_s, gain_s, drive_s, ub_s, log_s, fwd_in, rev_in, fwd_s, rev_s, q_s, g_s,
+    factor, m_ref, w_ref, wt_ref, out_ref, g_ref,
+    tri, x_s, pre_s, d_s, u_s, rest_s, own_s, f1_s, gain_s, drive_s, ub_s, log_s, fwd_in, rev_in, fwd_s, rev_s, coef_s, q_s, g_s,
 ):
     step = pl.program_id(0)
     f32, bf16 = jnp.float32, jnp.bfloat16
@@ -108,6 +101,9 @@
     def _():
         row = lax.broadcasted_iota(jnp.int32, (WROWS - BLK, STEP * SEQ), 0)
         x_s[BLK:, :] = jnp.where(row == 0, 1.0, 0.0).astype(x_s.dtype)
+        decay = wt_ref[:BLK, BLK + 1 : BLK + 2].astype(f32)
+        soft = jnp.maximum(decay, 0.0) + jnp.log1p(jnp.exp(-jnp.abs(decay)))
+        coef_s[...] = jnp.broadcast_to((-8.0 * LOG2E) * soft, (BLK, SEQ))
         q_s[...] = jnp.zeros_like(q_s)
         g_s[...] = jnp.zeros_like(g_s)
         src = lax.broadcasted_iota(jnp.int32, (2 * SEQ, 2 * SEQ), 0)
@@ -135,8 +131,8 @@
     def gates(s, r, cols, at):
         x = m_ref[s, r : r + CH, :].astype(f32)
         rgate = sigmoid(pre_s[r : r + CH, cols])
-        igate = sigmoid(pre_s[BLK + r : BLK + r + CH, cols])
-        u = coef_ref[r : r + CH, :] * rgate
+        igate = 0.5 + 0.5 * jnp.tanh(0.5 * pre_s[BLK + r : BLK + r + CH, cols])
+        u = coef_s[r : r + CH, :] * rgate
         var = one_minus_square(u)
         inv = lax.rsqrt(var)
         scale = var * inv
@@ -185,13 +181,13 @@
     @pl.when(step == pl.num_programs(0) - 1)
     def _():
         g_ref[...] = (g_s[...] * factor).astype(g_ref.dtype)
-        decay = jnp.sum((q_s[...] / coef_ref[...]).T, axis=0, keepdims=True) * (-8.0 * factor)
+        decay = jnp.sum((q_s[...] / coef_s[...]).T, axis=0, keepdims=True) * (-8.0 * factor)
         tail = g_s[BLK:, :BLK] * factor
         row = lax.broadcasted_iota(jnp.int32, tail.shape, 0)
         g_ref[BLK:, :BLK] = jnp.where(row == 1, decay, tail).astype(g_ref.dtype)
 
 
-def main_call(factor, m, w, wt, coef, grad_dtype=jnp.bfloat16, interpret=False):
+def main_call(factor, m, w, wt, grad_dtype=jnp.bfloat16, interpret=False):
     f32, bf16 = jnp.float32, jnp.bfloat16
     n = m.shape[0]
     tok = lambda rows: pl.BlockSpec((STEP, rows, SEQ), lambda p: (p, 0, 0))
@@ -204,7 +200,7 @@
             jax.ShapeDtypeStruct((n, BLK, SEQ), bf16),
             jax.ShapeDtypeStruct((WROWS, WCOLS), grad_dtype),
         ],
-        in_specs=[tok(TWO), full((WROWS, WCOLS)), full((TWO, WROWS)), full((BLK, SEQ))],
+        in_specs=[tok(TWO), full((WROWS, WCOLS)), full((TWO, WROWS))],
         out_specs=[tok(BLK), full((WROWS, WCOLS))],
         scratch_shapes=[
             pltpu.VMEM((3, 2 * SEQ, 2 * SEQ), bf16),
@@ -214,11 +210,12 @@
             flat, flat, flat, flat, flat, flat,
             half, flat, half, half, flat, flat,
             pltpu.VMEM((BLK, SEQ), f32),
+            pltpu.VMEM((BLK, SEQ), f32),
             pltpu.VMEM((WROWS, WCOLS), f32),
         ],
         compiler_params=params(),
         interpret=interpret,
-    )(m, w, wt, coef)
+    )(m, w, wt)
 
 
 def wire(wa, wx, ba, bx, decay):
@@ -236,31 +233,22 @@
     return jnp.pad(body, ((0, 0), (0, WCOLS - TWO)))
 
 
-def unwire(w):
-    wt = w[:, :TWO].T
-    coef = (-8.0 * LOG2E) * jax.nn.softplus(w[BLK + 1, :BLK].astype(jnp.float32))
-    return wt, jnp.broadcast_to(coef[:, None], (BLK, SEQ))
-
-
 def per_device(inputs, cotangent, wa, wx, ba, bx, decay):
     bf16, f32 = jnp.bfloat16, jnp.float32
     plane, line = ("cuts", "yh", "core"), ("cuts", "z")
     z = lax.axis_index("z").astype(jnp.int32).reshape(1)
     everyone = [(i, k) for i in range(NI) for k in range(NZ)]
     fetch = [(i * NZ + (k ^ i), i * NZ + k) for i, k in everyone]
-    across = [(i * NZ + (k ^ i), (i ^ 1) * NZ + k) for i, k in everyone]
-
+    homes = [[(i * NZ + (k ^ i), (i ^ j) * NZ + k) for i, k in everyone] for j in range(NI // 2)]
     got = lax.all_to_all(pack(z, inputs, cotangent), plane, 0, 0, tiled=True)
     w = lax.ppermute(wire(wa, wx, ba, bx, decay), line, fetch)
-    wt, coef = unwire(w)
     total = SEQ * NSEQ * NZ
-    out, grads = main_call(float(total) ** -0.5, got, w, wt, coef)
+    out, grads = main_call(float(total) ** -0.5, got, w, w[:, :TWO].T)
     input_grad = unpack(z, lax.all_to_all(out, plane, 0, 0, tiled=True))
-    pair = lax.ppermute(grads, line, fetch).astype(f32) + lax.ppermute(grads, line, across).astype(f32)
-    pair = pair.astype(bf16)
-    parts = [pair] + [lax.ppermute(pair, "cuts", [(i, (i + 2 * k) % NI) for i in range(NI)]) for k in (1, 2, 3)]
-    parts, input_grad = lax.optimization_barrier((parts, input_grad))
-    full = sum(p.astype(f32) for p in parts)
+    some = sum(lax.ppermute(grads, line, home).astype(f32) for home in homes).astype(bf16)
+    other = lax.ppermute(some, "cuts", [(i, i ^ (NI // 2)) for i in range(NI)])
+    some, other, input_grad = lax.optimization_barrier((some, other, input_grad))
+    full = some.astype(f32) + other.astype(f32)
     own = jax.nn.sigmoid(decay.astype(f32))
     return (
         input_grad,

time: 112 us -> 117 us (1.045)
  the two profiles are of different devices: /device:TPU:16 before, /device:TPU:1 now
where the time goes in v6:
time: 117 us
  waiting for transfers between devices  54.1 us (46%)
  starting transfers between devices  33.3 us (28%)
  Pallas kernels  21.3 us (18%)
  local copies, waits for them, and re-layouts  6.13 us (5%)
    all_to_all x1, waiting for transfers between devices, per_device(): got = lax.all_to_all(pack(z, inputs, cotangent), plane, 0, 0, tiled=True)  33 us
    ppermute x4, waiting for transfers between devices, per_device(): lax.ppermute(grads, line, home).astype(f32)  21.1 us
    pallas_call x1, Pallas kernels, main_call(): pl.pallas_call(functools.partial(main_kernel, factor), grid=(n // STEP,),...  14.2 us
    ppermute x4, starting transfers between devices, per_device(): lax.ppermute(grads, line, home).astype(f32)  8.8 us
    all_to_all x1, starting transfers between devices, per_device(): got = lax.all_to_all(pack(z, inputs, cotangent), plane, 0, 0, tiled=True)  8.73 us
    ppermute x1, starting transfers between devices, per_device(): other = lax.ppermute(some, 'cuts', [(i, i ^ NI // 2) for i in range(NI)])  8.18 us
    all_to_all x1, starting transfers between devices, per_device(): input_grad = unpack(z, lax.all_to_all(out, plane, 0, 0, tiled=True))  6.92 us
    pallas_call x1, Pallas kernels, pack(): pl.pallas_call(pack_kernel, in_specs=[SMEM, VMEM, VMEM], out_specs=VMEM,...  4.16 us
  transfers between devices with their start and end apart: 8, of which 3 were waited for; matrix products, arithmetic and copies ran while one was open for 2% of the time, Pallas kernels for 2%

profile of v6, /device:TPU:1, one launch (start us, length us, event | category | flops | bytes accessed | tf_op | source)
XLA Modules:
  0.0 116.5 jit_solution(11429406059119209693)
XLA Ops:
  0.6 4.2 %shard_map.118 = bf16[32,352,128]{2,1,0:T(8,128)(2,1)} custom-call(s32[1]{0:T(128)} %bitcast.z_ref, bf16[128,5632]{1,0:T(8,128)(2,1)} %x_ref.1, bf16[128,5632]{1,0:T(8,128)(2,1)} %c_ref.1), custom_call_target="tpu_custom_call" | custom-call | tf_op jit(solution)/shard_map/pallas_call | solution.py:49
  4.8 0.0 copy-start.5
  4.8 0.0 copy-start.6
  4.8 0.0 copy-start.4
  4.8 0.0 copy-start.2
  4.8 0.0 copy-start.3
  4.8 8.7 %all-to-all-start = ((bf16[32,352,128]{2,1,0:T(8,128)(2,1)}), bf16[32,352,128]{2,1,0:T(8,128)(2,1)S(1)}, u32[]{:S(2)}, u32[]{:S(2)}) async-start(bf16[32,352,128]{2,1,0:T(8,128)(2,1)} %shard_map.118), calls=%async_computation | async-start | bytes 5767168 | tf_op jit(solution)/shard_map/all_to_all | solution.py:243
  13.6 0.0 copy-done.5
  13.6 0.0 copy-done.6
  13.6 0.1 pad_maximum_fusion
  13.7 0.1 broadcast_in_dim.13
  13.8 0.0 copy-done.4
  13.8 0.1 broadcast_in_dim.14
  13.9 0.0 copy-done.2
  13.9 0.1 copy.16
  14.0 0.0 copy-done.3
  14.0 0.1 copy.17
  14.2 0.1 pad.10.clone
  14.2 0.1 maximum_maximum_fusion
  14.4 0.7 collective-permute-start
  15.1 0.0 collective-permute-done
  15.1 0.8 copy.20.w_ref
  15.9 0.7 slice_bitcast_fusion.wt_ref
  16.6 33.0 %all-to-all-done.m_ref = bf16[32,352,128]{2,1,0:T(8,128)(2,1)S(1)} async-done(((bf16[32,352,128]{2,1,0:T(8,128)(2,1)}), bf16[32,352,128]{2,1,0:T(8,128)(2,1)S(1)}, u32[]{:S(2)}, u32[]{:S(2)}) %all-to-all-start) | async-done | bytes 2883616 | tf_op jit(solution)/shard_map/all_to_all | solution.py:243
  49.6 0.0 copy-start
  49.6 1.6 %copy-done = bf16[32,352,128]{2,1,0:T(8,128)(2,1)} copy-done((bf16[32,352,128]{2,1,0:T(8,128)(2,1)}, bf16[32,352,128]{2,1,0:T(8,128)(2,1)S(1)}, u32[]{:S(2)}) %copy-start) | copy-done | bytes 2883608
  51.1 14.2 %shard_map.119 = (bf16[32,176,128]{2,1,0:T(8,128)(2,1)}, bf16[192,384]{1,0:T(8,128)(2,1)}) custom-call(bf16[32,352,128]{2,1,0:T(8,128)(2,1)} %copy-done, bf16[192,384]{1,0:T(8,128)(2,1)} %copy.20.w_ref, bf16[352,192]{1,0:T(8,128)(2,1)} %slice_bitcast_fusion.wt_ref), custom_call_target="tpu_custom_call" | custom-call | tf_op jit(solution)/shard_map/pallas_call | solution.py:196
  65.3 0.0 copy-start.7
  65.3 6.9 %all-to-all-start.1 = ((bf16[32,176,128]{2,1,0:T(8,128)(2,1)}), bf16[32,176,128]{2,1,0:T(8,128)(2,1)S(1)}, u32[]{:S(2)}, u32[]{:S(2)}) async-start(bf16[32,176,128]{2,1,0:T(8,128)(2,1)} %get-tuple-element.12), calls=%async_computation.1 | async-start | bytes 2883584 | tf_op jit(solution)/shard_map/all_to_all | solution.py:247
  72.3 0.0 copy-done.7
  72.3 0.7 collective-permute-start.1
  72.9 4.3 %collective-permute-start.2 = (bf16[192,384]{1,0:T(8,128)(2,1)S(1)}, bf16[192,384]{1,0:T(8,128)(2,1)S(1)}, u32[]{:S(2)}, u32[]{:S(2)}) collective-permute-start(bf16[192,384]{1,0:T(8,128)(2,1)S(1)} %copy-done.7), channel_id=1, source_target_pairs={{0,32},{4,36},{8,40},{12,44},{16,48},{20,52},{24,56},{28,60},{36,0... | collective-permute-start | bytes 442376 | tf_op jit(solution)/shard_map/ppermute | solution.py:248
  77.3 2.3 %collective-permute-start.3 = (bf16[192,384]{1,0:T(8,128)(2,1)S(1)}, bf16[192,384]{1,0:T(8,128)(2,1)S(1)}, u32[]{:S(2)}, u32[]{:S(2)}) collective-permute-start(bf16[192,384]{1,0:T(8,128)(2,1)S(1)} %copy-done.7), channel_id=1, source_target_pairs={{0,64},{4,68},{8,72},{12,76},{16,80},{20,84},{24,88},{28,92},{36,9... | collective-permute-start | bytes 442376 | tf_op jit(solution)/shard_map/ppermute | solution.py:248
  79.6 1.5 %collective-permute-start.4 = (bf16[192,384]{1,0:T(8,128)(2,1)S(1)}, bf16[192,384]{1,0:T(8,128)(2,1)S(1)}, u32[]{:S(2)}, u32[]{:S(2)}) collective-permute-start(bf16[192,384]{1,0:T(8,128)(2,1)S(1)} %copy-done.7), channel_id=1, source_target_pairs={{0,96},{4,100},{8,104},{12,108},{16,112},{20,116},{24,120},{28,124... | collective-permute-start | bytes 442376 | tf_op jit(solution)/shard_map/ppermute | solution.py:248
  81.1 0.0 collective-permute-done.1
  81.1 12.2 %collective-permute-done.2 = bf16[192,384]{1,0:T(8,128)(2,1)S(1)} collective-permute-done((bf16[192,384]{1,0:T(8,128)(2,1)S(1)}, bf16[192,384]{1,0:T(8,128)(2,1)S(1)}, u32[]{:S(2)}, u32[]{:S(2)}) %collective-permute-start.2) | collective-permute-done | bytes 147488 | tf_op jit(solution)/shard_map/ppermute | solution.py:248
  93.3 8.9 %collective-permute-done.3 = bf16[192,384]{1,0:T(8,128)(2,1)S(1)} collective-permute-done((bf16[192,384]{1,0:T(8,128)(2,1)S(1)}, bf16[192,384]{1,0:T(8,128)(2,1)S(1)}, u32[]{:S(2)}, u32[]{:S(2)}) %collective-permute-start.3) | collective-permute-done | bytes 147488 | tf_op jit(solution)/shard_map/ppermute | solution.py:248
  102.2 0.0 collective-permute-done.4
  102.2 0.1 add_convert_fusion
  102.3 8.2 %collective-permute-start.5 = (bf16[192,384]{1,0:T(8,128)(2,1)S(1)}, bf16[192,384]{1,0:T(8,128)(2,1)S(1)}, u32[]{:S(2)}, u32[]{:S(2)}) collective-permute-start(bf16[192,384]{1,0:T(8,128)(2,1)S(1)} %add_convert_fusion), channel_id=1, source_target_pairs={{0,128},{32,160},{64,192},{96,224},{128,0},{160,32},{192,64},{224,... | collective-permute-start | bytes 442376 | tf_op jit(solution)/shard_map/ppermute | solution.py:249
  110.4 0.0 all-to-all-done.1.in_ref
  110.4 0.0 copy-start.1
  110.4 1.1 copy-done.1
  111.6 2.9 %shard_map.120 = bf16[128,5632]{1,0:T(8,128)(2,1)} custom-call(s32[1]{0:T(128)} %bitcast.z_ref, bf16[32,176,128]{2,1,0:T(8,128)(2,1)} %copy-done.1), custom_call_target="tpu_custom_call" | custom-call | tf_op jit(solution)/shard_map/pallas_call | solution.py:60
  114.5 0.0 collective-permute-done.5
  114.5 0.8 fusion.1
  115.3 0.6 fusion
  115.9 0.6 divide_multiply_fusion
  (4 shorter events, 0.1 us)
Async XLA Ops:
  4.8 8.8 %copy-start.5 = (bf16[176]{0:T(256)(128)(2,1)S(1)}, bf16[176]{0:T(256)(128)(2,1)}, u32[]{:S(2)}) copy-start(bf16[176]{0:T(256)(128)(2,1)} %param.12) | copy-start | bytes 1060
  4.8 8.8 %copy-start.6 = (bf16[176]{0:T(256)(128)(2,1)S(1)}, bf16[176]{0:T(256)(128)(2,1)}, u32[]{:S(2)}) copy-start(bf16[176]{0:T(256)(128)(2,1)} %param.11) | copy-start | bytes 1060
  4.8 9.0 %copy-start.4 = (bf16[176]{0:T(256)(128)(2,1)S(1)}, bf16[176]{0:T(256)(128)(2,1)}, u32[]{:S(2)}) copy-start(bf16[176]{0:T(256)(128)(2,1)} %param.13) | copy-start | bytes 1060
  4.8 9.1 %copy-start.2 = (bf16[176,176]{1,0:T(8,128)(2,1)S(1)}, bf16[176,176]{1,0:T(8,128)(2,1)}, u32[]{:S(2)}) copy-start(bf16[176,176]{1,0:T(8,128)(2,1)} %param.9) | copy-start | bytes 185860
  4.8 9.2 %copy-start.3 = (bf16[176,176]{1,0:T(8,128)(2,1)S(1)}, bf16[176,176]{1,0:T(8,128)(2,1)}, u32[]{:S(2)}) copy-start(bf16[176,176]{1,0:T(8,128)(2,1)} %param.10) | copy-start | bytes 185860
  4.8 44.7 %all-to-all-start = ((bf16[32,352,128]{2,1,0:T(8,128)(2,1)}), bf16[32,352,128]{2,1,0:T(8,128)(2,1)S(1)}, u32[]{:S(2)}, u32[]{:S(2)}) async-start(bf16[32,352,128]{2,1,0:T(8,128)(2,1)} %shard_map.118), calls=%async_computation | async-start | bytes 5767168 | tf_op jit(solution)/shard_map/all_to_all | solution.py:243
  14.4 0.7 collective-permute-start
  49.6 1.6 %copy-start = (bf16[32,352,128]{2,1,0:T(8,128)(2,1)}, bf16[32,352,128]{2,1,0:T(8,128)(2,1)S(1)}, u32[]{:S(2)}) copy-start(bf16[32,352,128]{2,1,0:T(8,128)(2,1)S(1)} %all-to-all-done.m_ref) | copy-start | bytes 8650756
  65.3 6.9 %copy-start.7 = (bf16[192,384]{1,0:T(8,128)(2,1)S(1)}, bf16[192,384]{1,0:T(8,128)(2,1)}, u32[]{:S(2)}) copy-start(bf16[192,384]{1,0:T(8,128)(2,1)} %get-tuple-element.11) | copy-start | bytes 442372
  65.3 45.1 %all-to-all-start.1 = ((bf16[32,176,128]{2,1,0:T(8,128)(2,1)}), bf16[32,176,128]{2,1,0:T(8,128)(2,1)S(1)}, u32[]{:S(2)}, u32[]{:S(2)}) async-start(bf16[32,176,128]{2,1,0:T(8,128)(2,1)} %get-tuple-element.12), calls=%async_computation.1 | async-start | bytes 2883584 | tf_op jit(solution)/shard_map/all_to_all | solution.py:247
  72.3 8.8 %collective-permute-start.1 = (bf16[192,384]{1,0:T(8,128)(2,1)S(1)}, bf16[192,384]{1,0:T(8,128)(2,1)S(1)}, u32[]{:S(2)}, u32[]{:S(2)}) collective-permute-start(bf16[192,384]{1,0:T(8,128)(2,1)S(1)} %copy-done.7), channel_id=1, source_target_pairs={{0,0},{4,4},{8,8},{12,12},{16,16},{20,20},{24,24},{28,28},{36,32},... | collective-permute-start | bytes 442376 | tf_op jit(solution)/shard_map/ppermute | solution.py:248
  72.9 20.3 %collective-permute-start.2 = (bf16[192,384]{1,0:T(8,128)(2,1)S(1)}, bf16[192,384]{1,0:T(8,128)(2,1)S(1)}, u32[]{:S(2)}, u32[]{:S(2)}) collective-permute-start(bf16[192,384]{1,0:T(8,128)(2,1)S(1)} %copy-done.7), channel_id=1, source_target_pairs={{0,32},{4,36},{8,40},{12,44},{16,48},{20,52},{24,56},{28,60},{36,0... | collective-permute-start | bytes 442376 | tf_op jit(solution)/shard_map/ppermute | solution.py:248
  77.3 24.9 %collective-permute-start.3 = (bf16[192,384]{1,0:T(8,128)(2,1)S(1)}, bf16[192,384]{1,0:T(8,128)(2,1)S(1)}, u32[]{:S(2)}, u32[]{:S(2)}) collective-permute-start(bf16[192,384]{1,0:T(8,128)(2,1)S(1)} %copy-done.7), channel_id=1, source_target_pairs={{0,64},{4,68},{8,72},{12,76},{16,80},{20,84},{24,88},{28,92},{36,9... | collective-permute-start | bytes 442376 | tf_op jit(solution)/shard_map/ppermute | solution.py:248
  79.6 22.6 %collective-permute-start.4 = (bf16[192,384]{1,0:T(8,128)(2,1)S(1)}, bf16[192,384]{1,0:T(8,128)(2,1)S(1)}, u32[]{:S(2)}, u32[]{:S(2)}) collective-permute-start(bf16[192,384]{1,0:T(8,128)(2,1)S(1)} %copy-done.7), channel_id=1, source_target_pairs={{0,96},{4,100},{8,104},{12,108},{16,112},{20,116},{24,120},{28,124... | collective-permute-start | bytes 442376 | tf_op jit(solution)/shard_map/ppermute | solution.py:248
  102.3 12.2 %collective-permute-start.5 = (bf16[192,384]{1,0:T(8,128)(2,1)S(1)}, bf16[192,384]{1,0:T(8,128)(2,1)S(1)}, u32[]{:S(2)}, u32[]{:S(2)}) collective-permute-start(bf16[192,384]{1,0:T(8,128)(2,1)S(1)} %add_convert_fusion), channel_id=1, source_target_pairs={{0,128},{32,160},{64,192},{96,224},{128,0},{160,32},{192,64},{224,... | collective-permute-start | bytes 442376 | tf_op jit(solution)/shard_map/ppermute | solution.py:249
  110.4 1.1 copy-start.1

commit v7 on v6

v7 whole, which is shorter than its diff:
```python
import functools

import jax
import jax.numpy as jnp
from jax import lax
from jax.experimental import pallas as pl
from jax.experimental.pallas import tpu as pltpu
from jax.sharding import Mesh
from jax.sharding import PartitionSpec as P

BLK = 176
TWO = 2 * BLK
WROWS = 192
WCOLS = 384
NZ, NY, NC = 8, 2, 2
NQ = NY * NC
NI = 8
SEQ = 128
NSEQ = NI * NQ
STEP = 8
VMEM_LIMIT = 56 * 1024 * 1024


def pack_kernel(z_ref, x_hbm, c_hbm, out_hbm, x_s, c_s, out_s, in_sem, out_sem):
    wide = 2 * NQ * BLK
    loads = []
    for p in range(NZ // 2):
        for k, (src, dst) in enumerate(((x_hbm, x_s), (c_hbm, c_s))):
            cols = slice(p * wide, (p + 1) * wide)
            loads.append(pltpu.make_async_copy(src.at[:, cols], dst.at[:, cols], in_sem.at[k, p]))
            loads[-1].start()
    stores = []
    for p in range(NZ // 2):
        turned = []
        for k, ref in enumerate((x_s, c_s)):
            loads[2 * p + k].wait()
            turned.append(ref[:, p * wide : (p + 1) * wide].T)
        for half in range(2):
            group = (2 * p + half) ^ z_ref[0]
            for q in range(NQ):
                rows = slice((half * NQ + q) * BLK, (half * NQ + q + 1) * BLK)
                for k in range(2):
                    out_s[group * NQ + q, k * BLK : (k + 1) * BLK, :] = turned[k][rows]
            slots = pl.ds(group * NQ, NQ)
            stores.append(pltpu.make_async_copy(out_s.at[slots], out_hbm.at[slots], out_sem.at[2 * p + half]))
            stores[-1].start()
    for copy in stores:
        copy.wait()


def unpack_kernel(z_ref, in_hbm, out_hbm, in_s, out_s, in_sem, out_sem):
    wide = 2 * NQ * BLK
    loads = []
    for g in range(NZ):
        slots = pl.ds((g ^ z_ref[0]) * NQ, NQ)
        loads.append(pltpu.make_async_copy(in_hbm.at[slots], in_s.at[g], in_sem.at[g]))
        loads[-1].start()
    stores = []
    for p in range(NZ // 2):
        loads[2 * p].wait()
        loads[2 * p + 1].wait()
        cols = slice(p * wide, (p + 1) * wide)
        out_s[:, cols] = in_s[2 * p : 2 * p + 2].reshape(wide, SEQ).T
        stores.append(pltpu.make_async_copy(out_s.at[:, cols], out_hbm.at[:, cols], out_sem.at[p]))
        stores[-1].start()
    for copy in stores:
        copy.wait()


def params():
    return pltpu.CompilerParams(vmem_limit_bytes=VMEM_LIMIT)


SMEM = pl.BlockSpec(memory_space=pltpu.SMEM)
ANY = pl.BlockSpec(memory_space=pl.ANY)


def pack(z, x, c, interpret=False):
    sem = pltpu.SemaphoreType.DMA
    return pl.pallas_call(
        pack_kernel,
        in_specs=[SMEM, ANY, ANY],
        out_specs=ANY,
        out_shape=jax.ShapeDtypeStruct((NSEQ, TWO, SEQ), x.dtype),
        scratch_shapes=[
            pltpu.VMEM(x.shape, x.dtype),
            pltpu.VMEM(x.shape, x.dtype),
            pltpu.VMEM((NSEQ, TWO, SEQ), x.dtype),
            sem((2, NZ // 2)),
            sem((NZ,)),
        ],
        compiler_params=params(),
        interpret=interpret,
    )(z, x, c)


def unpack(z, y, interpret=False):
    sem = pltpu.SemaphoreType.DMA
    return pl.pallas_call(
        unpack_kernel,
        in_specs=[SMEM, ANY],
        out_specs=ANY,
        out_shape=jax.ShapeDtypeStruct((SEQ, NSEQ * BLK), y.dtype),
        scratch_shapes=[
            pltpu.VMEM((NZ, NQ, BLK, SEQ), y.dtype),
            pltpu.VMEM((SEQ, NSEQ * BLK), y.dtype),
            sem((NZ,)),
            sem((NZ // 2,)),
        ],
        compiler_params=params(),
        interpret=interpret,
    )(z, y)


LN2 = 0.6931471805599453
LOG2E = 1.4426950408889634


def sigmoid(pre):
    return pl.reciprocal(1.0 + jnp.exp2(jnp.minimum(pre * -LOG2E, 115.0)), approx=True)


def one_minus_square(u):
    series, power = 0.0, 1.0
    terms = []
    for k in range(1, 7):
        power = power * (2.0 * LN2) / k
        terms.append(-power)
    series = terms[-1]
    for t in terms[-2::-1]:
        series = series * u + t
    return series * u


CH = 16


def main_kernel(
    factor, m_hbm, w_ref, wt_ref, out_hbm, g_ref,
    m_ref, out_ref, tri, x_s, pre_s, d_s, u_s, rest_s, own_s, f1_s, gain_s, drive_s, ub_s, log_s,
    fwd_in, rev_in, fwd_s, rev_s, coef_s, q_s, in_sem, out_sem,
):
    f32, bf16 = jnp.float32, jnp.bfloat16
    blocks = [pl.ds(j * STEP, STEP) for j in range(NSEQ // STEP)]
    loads = [pltpu.make_async_copy(m_hbm.at[b], m_ref.at[b], in_sem.at[j]) for j, b in enumerate(blocks)]
    stores = [pltpu.make_async_copy(out_ref.at[b], out_hbm.at[b], out_sem.at[j]) for j, b in enumerate(blocks)]
    for copy in loads:
        copy.start()

    row = lax.broadcasted_iota(jnp.int32, (WROWS - BLK, NSEQ * SEQ), 0)
    x_s[BLK:, :] = jnp.where(row == 0, 1.0, 0.0).astype(x_s.dtype)
    decay = wt_ref[:BLK, BLK + 1 : BLK + 2].astype(f32)
    soft = jnp.maximum(decay, 0.0) + jnp.log1p(jnp.exp(-jnp.abs(decay)))
    coef_s[...] = jnp.broadcast_to((-8.0 * LOG2E) * soft, (BLK, SEQ))
    q_s[...] = jnp.zeros_like(q_s)
    src = lax.broadcasted_iota(jnp.int32, (2 * SEQ, 2 * SEQ), 0)
    dst = lax.broadcasted_iota(jnp.int32, (2 * SEQ, 2 * SEQ), 1)
    same = (src < SEQ) == (dst < SEQ)
    for k, seen in enumerate((src <= dst, src < dst, src >= dst)):
        tri[k] = jnp.where(seen & same, 1.0, 0.0).astype(bf16)

    def each(body, first=0, last=NSEQ // 2):
        def two(p, _):
            for half in range(2):
                s = 2 * p + half
                cols = pl.ds(pl.multiple_of(s * SEQ, SEQ), SEQ)
                for r in range(0, BLK, CH):
                    rows = pl.ds(pl.multiple_of(p * BLK + r, 16), CH)
                    body(s, r, cols, (rows, slice(half * SEQ, (half + 1) * SEQ)))
            return 0

        lax.fori_loop(first, last, two, 0)

    def gates(s, r, cols, at):
        x = m_ref[s, r : r + CH, :].astype(f32)
        rgate = sigmoid(pre_s[r : r + CH, cols])
        igate = 0.5 + 0.5 * jnp.tanh(0.5 * pre_s[BLK + r : BLK + r + CH, cols])
        u = coef_s[r : r + CH, :] * rgate
        var = one_minus_square(u)
        inv = lax.rsqrt(var)
        scale = var * inv
        ix = igate * x
        drive = scale * ix
        u_s[at] = u
        rest_s[at] = LN2 - LN2 * rgate
        own_s[at] = ix * (inv - scale)
        f1_s[at] = drive - drive * igate
        gain_s[at] = scale * igate
        drive_s[at] = drive
        ub_s[at] = u.astype(bf16)

    for j in range(NSEQ // STEP):
        loads[j].wait()
        cols = slice(j * STEP * SEQ, (j + 1) * STEP * SEQ)
        for s in range(j * STEP, (j + 1) * STEP):
            x_s[:BLK, s * SEQ : (s + 1) * SEQ] = m_ref[s, :BLK, :]
        pre_s[:, cols] = jnp.dot(wt_ref[...], x_s[:, cols], preferred_element_type=f32)
    each(gates)
    log_s[...] = jnp.dot(ub_s[...], tri[0], preferred_element_type=f32)

    def weigh(s, r, cols, at):
        total = log_s[at]
        cot = m_ref[s, BLK + r : BLK + r + CH, :].astype(f32)
        fwd_in[at] = (drive_s[at] * jnp.exp2(-total)).astype(bf16)
        rev_in[at] = (cot * jnp.exp2(total)).astype(bf16)

    each(weigh)
    fwd_s[...] = jnp.dot(fwd_in[...], tri[1], preferred_element_type=f32)
    rev_s[...] = jnp.dot(rev_in[...], tri[2], preferred_element_type=f32)

    def deltas(s, r, cols, at):
        total = log_s[at]
        adj = rev_s[at] * jnp.exp2(-total)
        dlog = adj * (fwd_s[at] * jnp.exp2(total) - own_s[at])
        v = dlog * u_s[at]
        q_s[r : r + CH, :] += v
        d_s[r : r + CH, cols] = (v * rest_s[at]).astype(bf16)
        d_s[BLK + r : BLK + r + CH, cols] = (adj * f1_s[at]).astype(bf16)
        pre_s[r : r + CH, cols] = adj * gain_s[at]

    each(deltas)

    for j in range(NSEQ // STEP):
        cols = slice(j * STEP * SEQ, (j + 1) * STEP * SEQ)
        back = jnp.dot(w_ref[:BLK, :TWO], d_s[:, cols], preferred_element_type=f32) + pre_s[:BLK, cols]
        for s in range(STEP):
            out_ref[j * STEP + s] = back[:, s * SEQ : (s + 1) * SEQ].astype(out_ref.dtype)
        stores[j].start()

    nt = (((1,), (1,)), ((), ()))
    grad = lax.dot_general(x_s[...], d_s[...], nt, preferred_element_type=f32) * factor
    g_ref[:, :TWO] = grad.astype(g_ref.dtype)
    g_ref[:, TWO:] = jnp.zeros((WROWS, WCOLS - TWO), g_ref.dtype)
    decay_row = jnp.sum((q_s[...] / coef_s[...]).T, axis=0, keepdims=True) * (-8.0 * factor)
    tail = grad[BLK:, :BLK]
    row = lax.broadcasted_iota(jnp.int32, tail.shape, 0)
    g_ref[BLK:, :BLK] = jnp.where(row == 1, decay_row, tail).astype(g_ref.dtype)
    for copy in stores:
        copy.wait()


def main_call(factor, m, w, wt, grad_dtype=jnp.bfloat16, interpret=False):
    f32, bf16 = jnp.float32, jnp.bfloat16
    vmem, sem = pltpu.VMEM, pltpu.SemaphoreType.DMA
    inside = pl.BlockSpec(memory_space=vmem)
    flat, half = (vmem((NSEQ // 2 * BLK, 2 * SEQ), kind) for kind in (f32, bf16))
    return pl.pallas_call(
        functools.partial(main_kernel, factor),
        out_shape=[
            jax.ShapeDtypeStruct((NSEQ, BLK, SEQ), bf16),
            jax.ShapeDtypeStruct((WROWS, WCOLS), grad_dtype),
        ],
        in_specs=[ANY, inside, inside],
        out_specs=[ANY, inside],
        scratch_shapes=[
            vmem((NSEQ, TWO, SEQ), bf16),
            vmem((NSEQ, BLK, SEQ), bf16),
            vmem((3, 2 * SEQ, 2 * SEQ), bf16),
            vmem((WROWS, NSEQ * SEQ), bf16),
            vmem((TWO, NSEQ * SEQ), f32),
            vmem((TWO, NSEQ * SEQ), bf16),
            flat, flat, flat, flat, flat, flat,
            half, flat, half, half, flat, flat,
            vmem((BLK, SEQ), f32),
            vmem((BLK, SEQ), f32),
            sem((NSEQ // STEP,)),
            sem((NSEQ // STEP,)),
        ],
        compiler_params=params(),
        interpret=interpret,
    )(m, w, wt)


def wire(wa, wx, ba, bx, decay):
    bf16 = jnp.bfloat16
    tail = jnp.zeros((WROWS - BLK - 2, TWO), bf16)
    body = jnp.concatenate(
        [
            jnp.concatenate([wa, wx], axis=1),
            jnp.concatenate([ba, bx])[None],
            jnp.concatenate([decay, jnp.zeros((BLK,), bf16)])[None],
            tail,
        ],
        axis=0,
    )
    return jnp.pad(body, ((0, 0), (0, WCOLS - TWO)))


def per_device(inputs, cotangent, wa, wx, ba, bx, decay):
    bf16, f32 = jnp.bfloat16, jnp.float32
    plane, line = ("cuts", "yh", "core"), ("cuts", "z")
    z = lax.axis_index("z").astype(jnp.int32).reshape(1)
    everyone = [(i, k) for i in range(NI) for k in range(NZ)]
    fetch = [(i * NZ + (k ^ i), i * NZ + k) for i, k in everyone]
    across = [(i * NZ + (k ^ i), (i ^ 1) * NZ + k) for i, k in everyone]

    got = lax.all_to_all(pack(z, inputs, cotangent), plane, 0, 0, tiled=True)
    w = lax.ppermute(wire(wa, wx, ba, bx, decay), line, fetch)
    total = SEQ * NSEQ * NZ
    out, grads = main_call(float(total) ** -0.5, got, w, w[:, :TWO].T)
    near, far = lax.ppermute(grads, line, fetch), lax.ppermute(grads, line, across)
    back = lax.all_to_all(out, plane, 0, 0, tiled=True)
    near, far, back = lax.optimization_barrier((near, far, back))
    pair = (near.astype(f32) + far.astype(f32)).astype(bf16)
    parts = [pair] + [lax.ppermute(pair, "cuts", [(i, (i + 2 * k) % NI) for i in range(NI)]) for k in (1, 2, 3)]
    input_grad = unpack(z, back)
    parts, input_grad = lax.optimization_barrier((parts, input_grad))
    full = sum(p.astype(f32) for p in parts)
    own = jax.nn.sigmoid(decay.astype(f32))
    return (
        input_grad,
        full[:BLK, :BLK],
        full[:BLK, BLK:TWO],
        full[BLK, :BLK],
        full[BLK, BLK:TWO],
        full[BLK + 1, :BLK] * own,
    )


def solution(mesh):
    fine = Mesh(mesh.devices.reshape(NI, NZ, NY, NC), ("cuts", "z", "yh", "core"))
    zero = ("z", "yh", "core")
    rows = P(("cuts",) + zero, None)
    return jax.shard_map(
        per_device,
        mesh=fine,
        in_specs=(rows, rows, P(zero, None), P(zero, None), P(zero), P(zero), P(zero)),
        out_specs=(rows, P(zero, None), P(zero, None), P(zero), P(zero), P(zero)),
        check_vma=False,
    )
```

time: 117 us -> 108 us (0.923)
  starting transfers between devices: 33.3 us -> 27.1 us
    ppermute x5, starting transfers between devices: 17 us -> 10.8 us  [the longest x3 5.74 us: per_device(): lax.ppermute(pair, 'cuts', [(i, (i + 2 * k) % NI) for i in range(NI)])]
  transfers between devices with their start and end apart: 8 -> 8, of which waited for: 3 -> 4; matrix products, arithmetic and copies ran while one was open for 2% -> 2% of each run, Pallas kernels for 2% -> 2%
where the time goes in v7:
time: 108 us
  waiting for transfers between devices  53.3 us (49%)
  starting transfers between devices  27.1 us (25%)
  Pallas kernels  20.8 us (19%)
  local copies, waits for them, and re-layouts  5.03 us (5%)
    all_to_all x1, waiting for transfers between devices, per_device(): got = lax.all_to_all(pack(z, inputs, cotangent), plane, 0, 0, tiled=True)  33 us
    ppermute x1, waiting for transfers between devices, per_device(): lax.ppermute(grads, line, across)  16 us
    pallas_call x1, Pallas kernels, main_call(): pl.pallas_call(functools.partial(main_kernel, factor), out_shape=[jax.Sha...  15 us
    all_to_all x1, starting transfers between devices, per_device(): got = lax.all_to_all(pack(z, inputs, cotangent), plane, 0, 0, tiled=True)  8.73 us
    all_to_all x1, starting transfers between devices, per_device(): back = lax.all_to_all(out, plane, 0, 0, tiled=True)  6.92 us
    ppermute x3, starting transfers between devices, per_device(): lax.ppermute(pair, 'cuts', [(i, (i + 2 * k) % NI) for i in range(NI)])  5.74 us
    ppermute x1, starting transfers between devices, per_device(): lax.ppermute(grads, line, across)  4.34 us
    ppermute x3, waiting for transfers between devices, per_device(): lax.ppermute(pair, 'cuts', [(i, (i + 2 * k) % NI) for i in range(NI)])  4.01 us
  transfers between devices with their start and end apart: 8, of which 4 were waited for; matrix products, arithmetic and copies ran while one was open for 2% of the time, Pallas kernels for 2%

profile of v7, /device:TPU:1, one launch (start us, length us, event | category | flops | bytes accessed | tf_op | source)
XLA Modules:
  0.0 108.0 jit_solution(11581133127368072644)
XLA Ops:
  0.6 3.3 %shard_map.118 = bf16[32,352,128]{2,1,0:T(8,128)(2,1)} custom-call(s32[1]{0:T(128)} %bitcast.z_ref, bf16[128,5632]{1,0:T(8,128)(2,1)} %x_hbm.1, bf16[128,5632]{1,0:T(8,128)(2,1)} %c_hbm.1), custom_call_target="tpu_custom_call" | custom-call | tf_op jit(solution)/shard_map/pallas_call | solution.py:80
  3.9 0.0 copy-start.5
  3.9 0.0 copy-start.6
  3.9 0.0 copy-start.4
  3.9 0.0 copy-start.2
  3.9 0.0 copy-start.3
  4.0 8.7 %all-to-all-start = ((bf16[32,352,128]{2,1,0:T(8,128)(2,1)}), bf16[32,352,128]{2,1,0:T(8,128)(2,1)S(1)}, u32[]{:S(2)}, u32[]{:S(2)}) async-start(bf16[32,352,128]{2,1,0:T(8,128)(2,1)} %shard_map.118), calls=%async_computation | async-start | bytes 5767168 | tf_op jit(solution)/shard_map/all_to_all | solution.py:297
  12.7 0.0 copy-done.5
  12.7 0.0 copy-done.6
  12.7 0.1 pad_maximum_fusion
  12.8 0.1 broadcast_in_dim.13
  12.9 0.0 copy-done.4
  12.9 0.1 broadcast_in_dim.14
  13.1 0.0 copy-done.2
  13.1 0.1 copy.16
  13.2 0.0 copy-done.3
  13.2 0.1 copy.17
  13.3 0.1 pad.10.clone
  13.4 0.1 maximum_maximum_fusion
  13.5 0.7 collective-permute-start
  14.2 0.0 collective-permute-done
  14.2 0.8 copy.20.w_ref
  15.0 0.7 slice_bitcast_fusion.wt_ref
  15.7 33.0 %all-to-all-done.m_hbm = bf16[32,352,128]{2,1,0:T(8,128)(2,1)S(1)} async-done(((bf16[32,352,128]{2,1,0:T(8,128)(2,1)}), bf16[32,352,128]{2,1,0:T(8,128)(2,1)S(1)}, u32[]{:S(2)}, u32[]{:S(2)}) %all-to-all-start) | async-done | bytes 2883616 | tf_op jit(solution)/shard_map/all_to_all | solution.py:297
  48.7 0.0 copy-start
  48.7 1.6 %copy-done = bf16[32,352,128]{2,1,0:T(8,128)(2,1)} copy-done((bf16[32,352,128]{2,1,0:T(8,128)(2,1)}, bf16[32,352,128]{2,1,0:T(8,128)(2,1)S(1)}, u32[]{:S(2)}) %copy-start) | copy-done | bytes 2883608
  50.3 15.0 %shard_map.119 = (bf16[32,176,128]{2,1,0:T(8,128)(2,1)}, bf16[192,384]{1,0:T(8,128)(2,1)}) custom-call(bf16[32,352,128]{2,1,0:T(8,128)(2,1)} %copy-done, bf16[192,384]{1,0:T(8,128)(2,1)} %copy.20.w_ref, bf16[352,192]{1,0:T(8,128)(2,1)} %slice_bitcast_fusion.wt_ref), custom_call_target="tpu_custom_call" | custom-call | tf_op jit(solution)/shard_map/pallas_call | solution.py:247
  65.3 0.0 copy-start.7
  65.3 6.9 %all-to-all-start.1 = ((bf16[32,176,128]{2,1,0:T(8,128)(2,1)}), bf16[32,176,128]{2,1,0:T(8,128)(2,1)S(1)}, u32[]{:S(2)}, u32[]{:S(2)}) async-start(bf16[32,176,128]{2,1,0:T(8,128)(2,1)} %get-tuple-element.17), calls=%async_computation.1 | async-start | bytes 2883584 | tf_op jit(solution)/shard_map/all_to_all | solution.py:302
  72.2 0.0 copy-done.7
  72.2 0.7 collective-permute-start.1
  72.9 4.3 %collective-permute-start.2 = (bf16[192,384]{1,0:T(8,128)(2,1)S(1)}, bf16[192,384]{1,0:T(8,128)(2,1)S(1)}, u32[]{:S(2)}, u32[]{:S(2)}) collective-permute-start(bf16[192,384]{1,0:T(8,128)(2,1)S(1)} %copy-done.7), channel_id=1, source_target_pairs={{0,32},{4,36},{8,40},{12,44},{16,48},{20,52},{24,56},{28,60},{36,0... | collective-permute-start | bytes 442376 | tf_op jit(solution)/shard_map/ppermute | solution.py:301
  77.3 0.0 collective-permute-done.1
  77.3 16.0 %collective-permute-done.2 = bf16[192,384]{1,0:T(8,128)(2,1)S(1)} collective-permute-done((bf16[192,384]{1,0:T(8,128)(2,1)S(1)}, bf16[192,384]{1,0:T(8,128)(2,1)S(1)}, u32[]{:S(2)}, u32[]{:S(2)}) %collective-permute-start.2) | collective-permute-done | bytes 147488 | tf_op jit(solution)/shard_map/ppermute | solution.py:301
  93.2 0.4 all-to-all-done.1.in_hbm
  93.6 0.0 copy-start.1
  93.6 2.5 %collective-permute-start.3 = (bf16[192,384]{1,0:T(8,128)(2,1)S(1)}, bf16[192,384]{1,0:T(8,128)(2,1)S(1)}, u32[]{:S(2)}, u32[]{:S(2)}) collective-permute-start(bf16[192,384]{1,0:T(8,128)(2,1)S(1)} %add_convert_fusion), channel_id=1, source_target_pairs={{0,64},{32,96},{64,128},{96,160},{128,192},{160,224},{192,0},{224,... | collective-permute-start | bytes 442376 | tf_op jit(solution)/shard_map/ppermute | solution.py:305
  96.1 2.7 %collective-permute-start.4 = (bf16[192,384]{1,0:T(8,128)(2,1)S(1)}, bf16[192,384]{1,0:T(8,128)(2,1)S(1)}, u32[]{:S(2)}, u32[]{:S(2)}) collective-permute-start(bf16[192,384]{1,0:T(8,128)(2,1)S(1)} %add_convert_fusion), channel_id=1, source_target_pairs={{0,128},{32,160},{64,192},{96,224},{128,0},{160,32},{192,64},{224,... | collective-permute-start | bytes 442376 | tf_op jit(solution)/shard_map/ppermute | solution.py:305
  98.8 0.6 collective-permute-start.5
  99.4 0.0 copy-done.1
  99.4 2.5 %shard_map.120 = bf16[128,5632]{1,0:T(8,128)(2,1)} custom-call(s32[1]{0:T(128)} %bitcast.z_ref, bf16[32,176,128]{2,1,0:T(8,128)(2,1)} %copy-done.1), custom_call_target="tpu_custom_call" | custom-call | tf_op jit(solution)/shard_map/pallas_call | solution.py:99
  101.9 0.0 collective-permute-done.3
  101.9 4.0 %collective-permute-done.4 = bf16[192,384]{1,0:T(8,128)(2,1)S(1)} collective-permute-done((bf16[192,384]{1,0:T(8,128)(2,1)S(1)}, bf16[192,384]{1,0:T(8,128)(2,1)S(1)}, u32[]{:S(2)}, u32[]{:S(2)}) %collective-permute-start.4) | collective-permute-done | bytes 147488 | tf_op jit(solution)/shard_map/ppermute | solution.py:305
  105.9 0.0 collective-permute-done.5
  105.9 0.1 convert_add_fusion
  106.0 0.8 fusion.1
  106.8 0.6 fusion
  107.4 0.6 divide_multiply_fusion
  (4 shorter events, 0.1 us)
Async XLA Ops:
  3.9 8.8 %copy-start.5 = (bf16[176]{0:T(256)(128)(2,1)S(1)}, bf16[176]{0:T(256)(128)(2,1)}, u32[]{:S(2)}) copy-start(bf16[176]{0:T(256)(128)(2,1)} %param.12) | copy-start | bytes 1060
  3.9 8.8 %copy-start.6 = (bf16[176]{0:T(256)(128)(2,1)S(1)}, bf16[176]{0:T(256)(128)(2,1)}, u32[]{:S(2)}) copy-start(bf16[176]{0:T(256)(128)(2,1)} %param.11) | copy-start | bytes 1060
  3.9 9.0 %copy-start.4 = (bf16[176]{0:T(256)(128)(2,1)S(1)}, bf16[176]{0:T(256)(128)(2,1)}, u32[]{:S(2)}) copy-start(bf16[176]{0:T(256)(128)(2,1)} %param.13) | copy-start | bytes 1060
  3.9 9.1 %copy-start.2 = (bf16[176,176]{1,0:T(8,128)(2,1)S(1)}, bf16[176,176]{1,0:T(8,128)(2,1)}, u32[]{:S(2)}) copy-start(bf16[176,176]{1,0:T(8,128)(2,1)} %param.9) | copy-start | bytes 185860
  3.9 9.2 %copy-start.3 = (bf16[176,176]{1,0:T(8,128)(2,1)S(1)}, bf16[176,176]{1,0:T(8,128)(2,1)}, u32[]{:S(2)}) copy-start(bf16[176,176]{1,0:T(8,128)(2,1)} %param.10) | copy-start | bytes 185860
  4.0 44.7 %all-to-all-start = ((bf16[32,352,128]{2,1,0:T(8,128)(2,1)}), bf16[32,352,128]{2,1,0:T(8,128)(2,1)S(1)}, u32[]{:S(2)}, u32[]{:S(2)}) async-start(bf16[32,352,128]{2,1,0:T(8,128)(2,1)} %shard_map.118), calls=%async_computation | async-start | bytes 5767168 | tf_op jit(solution)/shard_map/all_to_all | solution.py:297
  13.5 0.7 collective-permute-start
  48.7 1.6 %copy-start = (bf16[32,352,128]{2,1,0:T(8,128)(2,1)}, bf16[32,352,128]{2,1,0:T(8,128)(2,1)S(1)}, u32[]{:S(2)}) copy-start(bf16[32,352,128]{2,1,0:T(8,128)(2,1)S(1)} %all-to-all-done.m_hbm) | copy-start | bytes 8650756
  65.3 6.9 %copy-start.7 = (bf16[192,384]{1,0:T(8,128)(2,1)S(1)}, bf16[192,384]{1,0:T(8,128)(2,1)}, u32[]{:S(2)}) copy-start(bf16[192,384]{1,0:T(8,128)(2,1)} %get-tuple-element.16) | copy-start | bytes 442372
  65.3 28.3 %all-to-all-start.1 = ((bf16[32,176,128]{2,1,0:T(8,128)(2,1)}), bf16[32,176,128]{2,1,0:T(8,128)(2,1)S(1)}, u32[]{:S(2)}, u32[]{:S(2)}) async-start(bf16[32,176,128]{2,1,0:T(8,128)(2,1)} %get-tuple-element.17), calls=%async_computation.1 | async-start | bytes 2883584 | tf_op jit(solution)/shard_map/all_to_all | solution.py:302
  72.2 5.0 %collective-permute-start.1 = (bf16[192,384]{1,0:T(8,128)(2,1)S(1)}, bf16[192,384]{1,0:T(8,128)(2,1)S(1)}, u32[]{:S(2)}, u32[]{:S(2)}) collective-permute-start(bf16[192,384]{1,0:T(8,128)(2,1)S(1)} %copy-done.7), channel_id=1, source_target_pairs={{0,0},{4,4},{8,8},{12,12},{16,16},{20,20},{24,24},{28,28},{36,32},... | collective-permute-start | bytes 442376 | tf_op jit(solution)/shard_map/ppermute | solution.py:301
  72.9 20.3 %collective-permute-start.2 = (bf16[192,384]{1,0:T(8,128)(2,1)S(1)}, bf16[192,384]{1,0:T(8,128)(2,1)S(1)}, u32[]{:S(2)}, u32[]{:S(2)}) collective-permute-start(bf16[192,384]{1,0:T(8,128)(2,1)S(1)} %copy-done.7), channel_id=1, source_target_pairs={{0,32},{4,36},{8,40},{12,44},{16,48},{20,52},{24,56},{28,60},{36,0... | collective-permute-start | bytes 442376 | tf_op jit(solution)/shard_map/ppermute | solution.py:301
  93.6 5.8 %copy-start.1 = (bf16[32,176,128]{2,1,0:T(8,128)(2,1)}, bf16[32,176,128]{2,1,0:T(8,128)(2,1)S(1)}, u32[]{:S(2)}) copy-start(bf16[32,176,128]{2,1,0:T(8,128)(2,1)S(1)} %all-to-all-done.1.in_hbm) | copy-start | bytes 4325380
  93.6 8.3 %collective-permute-start.3 = (bf16[192,384]{1,0:T(8,128)(2,1)S(1)}, bf16[192,384]{1,0:T(8,128)(2,1)S(1)}, u32[]{:S(2)}, u32[]{:S(2)}) collective-permute-start(bf16[192,384]{1,0:T(8,128)(2,1)S(1)} %add_convert_fusion), channel_id=1, source_target_pairs={{0,64},{32,96},{64,128},{96,160},{128,192},{160,224},{192,0},{224,... | collective-permute-start | bytes 442376 | tf_op jit(solution)/shard_map/ppermute | solution.py:305
  96.1 9.8 %collective-permute-start.4 = (bf16[192,384]{1,0:T(8,128)(2,1)S(1)}, bf16[192,384]{1,0:T(8,128)(2,1)S(1)}, u32[]{:S(2)}, u32[]{:S(2)}) collective-permute-start(bf16[192,384]{1,0:T(8,128)(2,1)S(1)} %add_convert_fusion), channel_id=1, source_target_pairs={{0,128},{32,160},{64,192},{96,224},{128,0},{160,32},{192,64},{224,... | collective-permute-start | bytes 442376 | tf_op jit(solution)/shard_map/ppermute | solution.py:305
  98.8 7.1 %collective-permute-start.5 = (bf16[192,384]{1,0:T(8,128)(2,1)S(1)}, bf16[192,384]{1,0:T(8,128)(2,1)S(1)}, u32[]{:S(2)}, u32[]{:S(2)}) collective-permute-start(bf16[192,384]{1,0:T(8,128)(2,1)S(1)} %add_convert_fusion), channel_id=1, source_target_pairs={{0,192},{32,224},{64,0},{96,32},{128,64},{160,96},{192,128},{224,1... | collective-permute-start | bytes 442376 | tf_op jit(solution)/shard_map/ppermute | solution.py:305

commit v8 on v7

--- a/solution.py
+++ b/solution.py
@@ -17,11 +17,9 @@
 NI = 8
 SEQ = 128
 NSEQ = NI * NQ
-STEP = 8
-VMEM_LIMIT = 56 * 1024 * 1024
-
-
-def pack_kernel(z_ref, x_hbm, c_hbm, out_hbm, x_s, c_s, out_s, in_sem, out_sem):
+
+
+def pack_kernel(z_ref, x_hbm, c_hbm, out_ref, x_s, c_s, in_sem):
     wide = 2 * NQ * BLK
     loads = []
     for p in range(NZ // 2):
@@ -29,87 +27,68 @@
             cols = slice(p * wide, (p + 1) * wide)
             loads.append(pltpu.make_async_copy(src.at[:, cols], dst.at[:, cols], in_sem.at[k, p]))
             loads[-1].start()
+    turn = z_ref[0] * NQ
+    for p in range(NZ // 2):
+        for k, ref in enumerate((x_s, c_s)):
+            loads[2 * p + k].wait()
+            turned = ref[:, p * wide : (p + 1) * wide].T
+            for h in range(2 * NQ):
+                out_ref[(2 * NQ * p + h) ^ turn, k * BLK : (k + 1) * BLK, :] = turned[h * BLK : (h + 1) * BLK]
+
+
+def unpack_kernel(z_ref, in_ref, out_hbm, out_s, out_sem):
+    wide = 2 * NQ * BLK
+    turn = z_ref[0] * NQ
     stores = []
     for p in range(NZ // 2):
-        turned = []
-        for k, ref in enumerate((x_s, c_s)):
-            loads[2 * p + k].wait()
-            turned.append(ref[:, p * wide : (p + 1) * wide].T)
-        for half in range(2):
-            group = (2 * p + half) ^ z_ref[0]
-            for q in range(NQ):
-                rows = slice((half * NQ + q) * BLK, (half * NQ + q + 1) * BLK)
-                for k in range(2):
-                    out_s[group * NQ + q, k * BLK : (k + 1) * BLK, :] = turned[k][rows]
-            slots = pl.ds(group * NQ, NQ)
-            stores.append(pltpu.make_async_copy(out_s.at[slots], out_hbm.at[slots], out_sem.at[2 * p + half]))
-            stores[-1].start()
-    for copy in stores:
-        copy.wait()
-
-
-def unpack_kernel(z_ref, in_hbm, out_hbm, in_s, out_s, in_sem, out_sem):
-    wide = 2 * NQ * BLK
-    loads = []
-    for g in range(NZ):
-        slots = pl.ds((g ^ z_ref[0]) * NQ, NQ)
-        loads.append(pltpu.make_async_copy(in_hbm.at[slots], in_s.at[g], in_sem.at[g]))
-        loads[-1].start()
-    stores = []
-    for p in range(NZ // 2):
-        loads[2 * p].wait()
-        loads[2 * p + 1].wait()
         cols = slice(p * wide, (p + 1) * wide)
-        out_s[:, cols] = in_s[2 * p : 2 * p + 2].reshape(wide, SEQ).T
+        heads = [in_ref[(2 * NQ * p + h) ^ turn] for h in range(2 * NQ)]
+        out_s[:, cols] = jnp.concatenate(heads, axis=0).T
         stores.append(pltpu.make_async_copy(out_s.at[:, cols], out_hbm.at[:, cols], out_sem.at[p]))
         stores[-1].start()
     for copy in stores:
         copy.wait()
 
 
-def params():
-    return pltpu.CompilerParams(vmem_limit_bytes=VMEM_LIMIT)
-
-
 SMEM = pl.BlockSpec(memory_space=pltpu.SMEM)
 ANY = pl.BlockSpec(memory_space=pl.ANY)
+VMEM = pl.BlockSpec(memory_space=pltpu.VMEM)
+
+
+def kept(*arrays, where=pltpu.VMEM):
+    return [pltpu.with_memory_space_constraint(a, where) for a in arrays]
+
+
+def params(mebibytes):
+    return pltpu.CompilerParams(vmem_limit_bytes=mebibytes * 1024 * 1024)
 
 
 def pack(z, x, c, interpret=False):
-    sem = pltpu.SemaphoreType.DMA
     return pl.pallas_call(
         pack_kernel,
         in_specs=[SMEM, ANY, ANY],
-        out_specs=ANY,
-        out_shape=jax.ShapeDtypeStruct((NSEQ, TWO, SEQ), x.dtype),
+        out_specs=VMEM,
+        out_shape=pltpu.VMEM((NSEQ, TWO, SEQ), x.dtype),
         scratch_shapes=[
             pltpu.VMEM(x.shape, x.dtype),
             pltpu.VMEM(x.shape, x.dtype),
-            pltpu.VMEM((NSEQ, TWO, SEQ), x.dtype),
-            sem((2, NZ // 2)),
-            sem((NZ,)),
+            pltpu.SemaphoreType.DMA((2, NZ // 2)),
         ],
-        compiler_params=params(),
+        compiler_params=params(16),
         interpret=interpret,
-    )(z, x, c)
+    )(z, *kept(x, c, where=pltpu.HBM))
 
 
 def unpack(z, y, interpret=False):
-    sem = pltpu.SemaphoreType.DMA
     return pl.pallas_call(
         unpack_kernel,
-        in_specs=[SMEM, ANY],
+        in_specs=[SMEM, VMEM],
         out_specs=ANY,
-        out_shape=jax.ShapeDtypeStruct((SEQ, NSEQ * BLK), y.dtype),
-        scratch_shapes=[
-            pltpu.VMEM((NZ, NQ, BLK, SEQ), y.dtype),
-            pltpu.VMEM((SEQ, NSEQ * BLK), y.dtype),
-            sem((NZ,)),
-            sem((NZ // 2,)),
-        ],
-        compiler_params=params(),
+        out_shape=pltpu.HBM((SEQ, NSEQ * BLK), y.dtype),
+        scratch_shapes=[pltpu.VMEM((SEQ, NSEQ * BLK), y.dtype), pltpu.SemaphoreType.DMA((NZ // 2,))],
+        compiler_params=params(16),
         interpret=interpret,
-    )(z, y)
+    )(z, *kept(y))
 
 
 LN2 = 0.6931471805599453
@@ -136,17 +115,11 @@
 
 
 def main_kernel(
-    factor, m_hbm, w_ref, wt_ref, out_hbm, g_ref,
-    m_ref, out_ref, tri, x_s, pre_s, d_s, u_s, rest_s, own_s, f1_s, gain_s, drive_s, ub_s, log_s,
-    fwd_in, rev_in, fwd_s, rev_s, coef_s, q_s, in_sem, out_sem,
+    factor, m_ref, w_ref, wt_ref, out_ref, g_ref,
+    tri, x_s, pre_s, d_s, u_s, rest_s, own_s, f1_s, gain_s, drive_s, ub_s, log_s,
+    fwd_in, rev_in, fwd_s, rev_s, coef_s, q_s,
 ):
     f32, bf16 = jnp.float32, jnp.bfloat16
-    blocks = [pl.ds(j * STEP, STEP) for j in range(NSEQ // STEP)]
-    loads = [pltpu.make_async_copy(m_hbm.at[b], m_ref.at[b], in_sem.at[j]) for j, b in enumerate(blocks)]
-    stores = [pltpu.make_async_copy(out_ref.at[b], out_hbm.at[b], out_sem.at[j]) for j, b in enumerate(blocks)]
-    for copy in loads:
-        copy.start()
-
     row = lax.broadcasted_iota(jnp.int32, (WROWS - BLK, NSEQ * SEQ), 0)
     x_s[BLK:, :] = jnp.where(row == 0, 1.0, 0.0).astype(x_s.dtype)
     decay = wt_ref[:BLK, BLK + 1 : BLK + 2].astype(f32)
@@ -189,12 +162,9 @@
         drive_s[at] = drive
         ub_s[at] = u.astype(bf16)
 
-    for j in range(NSEQ // STEP):
-        loads[j].wait()
-        cols = slice(j * STEP * SEQ, (j + 1) * STEP * SEQ)
-        for s in range(j * STEP, (j + 1) * STEP):
-            x_s[:BLK, s * SEQ : (s + 1) * SEQ] = m_ref[s, :BLK, :]
-        pre_s[:, cols] = jnp.dot(wt_ref[...], x_s[:, cols], preferred_element_type=f32)
+    for s in range(NSEQ):
+        x_s[:BLK, s * SEQ : (s + 1) * SEQ] = m_ref[s, :BLK, :]
+    pre_s[...] = jnp.dot(wt_ref[...], x_s[...], preferred_element_type=f32)
     each(gates)
     log_s[...] = jnp.dot(ub_s[...], tri[0], preferred_element_type=f32)
 
@@ -220,12 +190,10 @@
 
     each(deltas)
 
-    for j in range(NSEQ // STEP):
-        cols = slice(j * STEP * SEQ, (j + 1) * STEP * SEQ)
-        back = jnp.dot(w_ref[:BLK, :TWO], d_s[:, cols], preferred_element_type=f32) + pre_s[:BLK, cols]
-        for s in range(STEP):
-            out_ref[j * STEP + s] = back[:, s * SEQ : (s + 1) * SEQ].astype(out_ref.dtype)
-        stores[j].start()
+    back = jnp.dot(w_ref[:BLK, :TWO], d_s[...], preferred_element_type=f32)
+    for s in range(NSEQ):
+        cols = slice(s * SEQ, (s + 1) * SEQ)
+        out_ref[s] = (back[:, cols] + pre_s[:BLK, cols]).astype(out_ref.dtype)
 
     nt = (((1,), (1,)), ((), ()))
     grad = lax.dot_general(x_s[...], d_s[...], nt, preferred_element_type=f32) * factor
@@ -235,26 +203,18 @@
     tail = grad[BLK:, :BLK]
     row = lax.broadcasted_iota(jnp.int32, tail.shape, 0)
     g_ref[BLK:, :BLK] = jnp.where(row == 1, decay_row, tail).astype(g_ref.dtype)
-    for copy in stores:
-        copy.wait()
 
 
 def main_call(factor, m, w, wt, grad_dtype=jnp.bfloat16, interpret=False):
     f32, bf16 = jnp.float32, jnp.bfloat16
-    vmem, sem = pltpu.VMEM, pltpu.SemaphoreType.DMA
-    inside = pl.BlockSpec(memory_space=vmem)
+    vmem = pltpu.VMEM
     flat, half = (vmem((NSEQ // 2 * BLK, 2 * SEQ), kind) for kind in (f32, bf16))
     return pl.pallas_call(
         functools.partial(main_kernel, factor),
-        out_shape=[
-            jax.ShapeDtypeStruct((NSEQ, BLK, SEQ), bf16),
-            jax.ShapeDtypeStruct((WROWS, WCOLS), grad_dtype),
-        ],
-        in_specs=[ANY, inside, inside],
-        out_specs=[ANY, inside],
+        out_shape=[vmem((NSEQ, BLK, SEQ), bf16), vmem((WROWS, WCOLS), grad_dtype)],
+        in_specs=[VMEM] * 3,
+        out_specs=[VMEM] * 2,
         scratch_shapes=[
-            vmem((NSEQ, TWO, SEQ), bf16),
-            vmem((NSEQ, BLK, SEQ), bf16),
             vmem((3, 2 * SEQ, 2 * SEQ), bf16),
             vmem((WROWS, NSEQ * SEQ), bf16),
             vmem((TWO, NSEQ * SEQ), f32),
@@ -263,12 +223,35 @@
             half, flat, half, half, flat, flat,
             vmem((BLK, SEQ), f32),
             vmem((BLK, SEQ), f32),
-            sem((NSEQ // STEP,)),
-            sem((NSEQ // STEP,)),
         ],
-        compiler_params=params(),
+        compiler_params=params(48),
         interpret=interpret,
-    )(m, w, wt)
+    )(*kept(m, w, wt))
+
+
+def finish_kernel(count, *refs):
+    parts, decay_ref, outs = refs[:count], refs[count], refs[count + 2 :]
+    f32 = jnp.float32
+    full = sum(p[...].astype(f32) for p in parts)
+    wa, wx, ba, bx, da = outs
+    right = pltpu.roll(full, WCOLS - BLK, 1)
+    wa[...] = full[:BLK, :BLK]
+    wx[...] = right[:BLK, :BLK]
+    ba[...] = full[BLK : BLK + 1, :BLK]
+    bx[...] = right[BLK : BLK + 1, :BLK]
+    own = 1.0 / (1.0 + jnp.exp(-decay_ref[...].astype(f32)))
+    da[...] = full[BLK + 1 : BLK + 2, :BLK] * own
+
+
+def finish(parts, decay, after):
+    square, row = (jax.ShapeDtypeStruct((n, BLK), jnp.float32) for n in (BLK, 1))
+    return pl.pallas_call(
+        functools.partial(finish_kernel, len(parts)),
+        in_specs=[VMEM] * (len(parts) + 1) + [ANY],
+        out_specs=[VMEM] * 5,
+        out_shape=[square, square, row, row, row],
+        compiler_params=params(16),
+    )(*kept(*parts, decay.reshape(1, BLK)), *kept(after, where=pltpu.HBM))
 
 
 def wire(wa, wx, ba, bx, decay):
@@ -304,17 +287,8 @@
     pair = (near.astype(f32) + far.astype(f32)).astype(bf16)
     parts = [pair] + [lax.ppermute(pair, "cuts", [(i, (i + 2 * k) % NI) for i in range(NI)]) for k in (1, 2, 3)]
     input_grad = unpack(z, back)
-    parts, input_grad = lax.optimization_barrier((parts, input_grad))
-    full = sum(p.astype(f32) for p in parts)
-    own = jax.nn.sigmoid(decay.astype(f32))
-    return (
-        input_grad,
-        full[:BLK, :BLK],
-        full[:BLK, BLK:TWO],
-        full[BLK, :BLK],
-        full[BLK, BLK:TWO],
-        full[BLK + 1, :BLK] * own,
-    )
+    grad_a, grad_x, *rows = finish(parts, decay, input_grad)
+    return (input_grad, grad_a, grad_x, *(row.reshape(BLK) for row in rows))
 
 
 def solution(mesh):

time: 108 us -> 104 us (0.963)
  Pallas kernels: 20.8 us -> 16 us
  waiting for transfers between devices: 53.3 us -> 55.9 us
  local copies, waits for them, and re-layouts: 5.03 us -> 3.37 us
    pallas_call x3 -> x4, Pallas kernels: 20.8 us -> 16 us  [the longest x1 11.6 us: main_call(): pl.pallas_call(functools.partial(main_kernel, factor), out_shape=[vmem((N...]
    slice x2 -> x0, local copies, waits for them, and re-layouts: 1.43 us -> none  [the longest x1 0.79 us: per_device(): full[:BLK, BLK:TWO]]
    all_to_all x1, waiting for transfers between devices: 33 us -> 34.3 us  [per_device(): got = lax.all_to_all(pack(z, inputs, cotangent), plane, 0, 0, tiled=True)]
    ppermute x3, waiting for transfers between devices: 4.01 us -> 5.23 us  [per_device(): lax.ppermute(pair, 'cuts', [(i, (i + 2 * k) % NI) for i in range(NI)])]
    unnamed x18 -> x16, local copies, waits for them, and re-layouts: 1.8 us -> 2.88 us
  transfers between devices with their start and end apart: 8 -> 8, of which waited for: 4 -> 5; matrix products, arithmetic and copies ran while one was open for 2% -> 1% of each run, Pallas kernels for 2% -> 1%
where the time goes in v8:
time: 104 us; the launch traced here: 103 us
  waiting for transfers between devices  55.9 us (54%)
  starting transfers between devices  26.9 us (26%)
  Pallas kernels  16 us (15%)
  local copies, waits for them, and re-layouts  3.37 us (3%)
    all_to_all x1, waiting for transfers between devices, per_device(): got = lax.all_to_all(pack(z, inputs, cotangent), plane, 0, 0, tiled=True)  34.3 us
    ppermute x1, waiting for transfers between devices, per_device(): lax.ppermute(grads, line, across)  16 us
    pallas_call x1, Pallas kernels, main_call(): pl.pallas_call(functools.partial(main_kernel, factor), out_shape=[vmem((N...  11.6 us
    all_to_all x1, starting transfers between devices, per_device(): got = lax.all_to_all(pack(z, inputs, cotangent), plane, 0, 0, tiled=True)  8.73 us
    all_to_all x1, starting transfers between devices, per_device(): back = lax.all_to_all(out, plane, 0, 0, tiled=True)  6.79 us
    ppermute x3, starting transfers between devices, per_device(): lax.ppermute(pair, 'cuts', [(i, (i + 2 * k) % NI) for i in range(NI)])  5.73 us
    ppermute x3, waiting for transfers between devices, per_device(): lax.ppermute(pair, 'cuts', [(i, (i + 2 * k) % NI) for i in range(NI)])  5.23 us
    ppermute x1, starting transfers between devices, per_device(): lax.ppermute(grads, line, across)  4.34 us
  transfers between devices with their start and end apart: 8, of which 5 were waited for; matrix products, arithmetic and copies ran while one was open for 1% of the time, Pallas kernels for 1%

profile of v8, /device:TPU:1, one launch (start us, length us, event | category | flops | bytes accessed | tf_op | source)
XLA Modules:
  0.0 103.3 jit_solution(13087600174230116759)
XLA Ops:
  0.6 2.3 %shard_map.118 = bf16[32,352,128]{2,1,0:T(8,128)(2,1)S(1)} custom-call(s32[1]{0:T(128)} %bitcast.z_ref, bf16[128,5632]{1,0:T(8,128)(2,1)} %x_hbm.1, bf16[128,5632]{1,0:T(8,128)(2,1)} %c_hbm.1), custom_call_target="tpu_custom_call" | custom-call | tf_op jit(solution)/shard_map/pallas_call | solution.py:67
  2.9 0.0 copy-start
  3.0 1.6 %copy-done = bf16[32,352,128]{2,1,0:T(8,128)(2,1)} copy-done((bf16[32,352,128]{2,1,0:T(8,128)(2,1)}, bf16[32,352,128]{2,1,0:T(8,128)(2,1)S(1)}, u32[]{:S(2)}) %copy-start) | copy-done | bytes 2883608
  4.5 0.0 copy-start.4
  4.5 0.0 copy-start.5
  4.5 0.0 copy-start.6
  4.5 0.0 copy-start.2
  4.5 0.0 copy-start.3
  4.5 8.7 %all-to-all-start = ((bf16[32,352,128]{2,1,0:T(8,128)(2,1)}), bf16[32,352,128]{2,1,0:T(8,128)(2,1)S(1)}, u32[]{:S(2)}, u32[]{:S(2)}) async-start(bf16[32,352,128]{2,1,0:T(8,128)(2,1)} %copy-done), calls=%async_computation | async-start | bytes 5767168 | tf_op jit(solution)/shard_map/all_to_all | solution.py:280
  13.3 0.0 copy-done.4
  13.3 0.0 copy-done.5
  13.3 0.1 pad_maximum_fusion
  13.4 0.1 broadcast_in_dim.13
  13.5 0.0 copy-done.6
  13.5 0.1 broadcast_in_dim.14
  13.6 0.0 copy-done.2
  13.7 0.1 copy.16
  13.8 0.0 copy-done.3
  13.8 0.1 copy.17
  13.9 0.1 pad.10.clone
  14.0 0.1 maximum_maximum_fusion
  14.1 0.7 collective-permute-start
  14.8 0.0 collective-permute-done
  14.8 0.1 copy.20.w_ref
  15.0 34.3 %all-to-all-done.m_ref = bf16[32,352,128]{2,1,0:T(8,128)(2,1)S(1)} async-done(((bf16[32,352,128]{2,1,0:T(8,128)(2,1)}), bf16[32,352,128]{2,1,0:T(8,128)(2,1)S(1)}, u32[]{:S(2)}, u32[]{:S(2)}) %all-to-all-start) | async-done | bytes 2883616 | tf_op jit(solution)/shard_map/all_to_all | solution.py:280
  49.3 11.6 %shard_map.119 = (bf16[32,176,128]{2,1,0:T(8,128)(2,1)S(1)}, bf16[192,384]{1,0:T(8,128)(2,1)S(1)}) custom-call(bf16[32,352,128]{2,1,0:T(8,128)(2,1)S(1)} %all-to-all-done.m_ref, bf16[192,384]{1,0:T(8,128)(2,1)S(1)} %copy.20.w_ref, bf16[352,192]{1,0:T(8,128)(2,1)S(1)} %slice_bitcast_fusion.wt_ref), custom_call_target="tpu_custom_call" | custom-call | tf_op jit(solution)/shard_map/pallas_call | solution.py:212
  60.9 0.0 copy-start.1
  60.9 1.1 %copy-done.1 = bf16[32,176,128]{2,1,0:T(8,128)(2,1)} copy-done((bf16[32,176,128]{2,1,0:T(8,128)(2,1)}, bf16[32,176,128]{2,1,0:T(8,128)(2,1)S(1)}, u32[]{:S(2)}) %copy-start.1) | copy-done | bytes 1441816
  62.0 6.8 %all-to-all-start.1 = ((bf16[32,176,128]{2,1,0:T(8,128)(2,1)}), bf16[32,176,128]{2,1,0:T(8,128)(2,1)S(1)}, u32[]{:S(2)}, u32[]{:S(2)}) async-start(bf16[32,176,128]{2,1,0:T(8,128)(2,1)} %copy-done.1), calls=%async_computation.1 | async-start | bytes 2883584 | tf_op jit(solution)/shard_map/all_to_all | solution.py:285
  68.8 0.7 collective-permute-start.1
  69.5 4.3 %collective-permute-start.2 = (bf16[192,384]{1,0:T(8,128)(2,1)S(1)}, bf16[192,384]{1,0:T(8,128)(2,1)S(1)}, u32[]{:S(2)}, u32[]{:S(2)}) collective-permute-start(bf16[192,384]{1,0:T(8,128)(2,1)S(1)} %get-tuple-element.16), channel_id=1, source_target_pairs={{0,32},{4,36},{8,40},{12,44},{16,48},{20,52},{24,56},{28,60},{36,0... | collective-permute-start | bytes 442376 | tf_op jit(solution)/shard_map/ppermute | solution.py:284
  73.8 0.0 collective-permute-done.1
  73.8 16.0 %collective-permute-done.2 = bf16[192,384]{1,0:T(8,128)(2,1)S(1)} collective-permute-done((bf16[192,384]{1,0:T(8,128)(2,1)S(1)}, bf16[192,384]{1,0:T(8,128)(2,1)S(1)}, u32[]{:S(2)}, u32[]{:S(2)}) %collective-permute-start.2) | collective-permute-done | bytes 147488 | tf_op jit(solution)/shard_map/ppermute | solution.py:284
  89.8 0.4 all-to-all-done.1.in_ref
  90.2 2.5 %collective-permute-start.3 = (bf16[192,384]{1,0:T(8,128)(2,1)S(1)}, bf16[192,384]{1,0:T(8,128)(2,1)S(1)}, u32[]{:S(2)}, u32[]{:S(2)}) collective-permute-start(bf16[192,384]{1,0:T(8,128)(2,1)S(1)} %add_convert_fusion.refs_0_), channel_id=1, source_target_pairs={{0,64},{32,96},{64,128},{96,160},{128,192},{160,224},{192,0},{224,... | collective-permute-start | bytes 442376 | tf_op jit(solution)/shard_map/ppermute | solution.py:288
  92.7 2.7 %collective-permute-start.4 = (bf16[192,384]{1,0:T(8,128)(2,1)S(1)}, bf16[192,384]{1,0:T(8,128)(2,1)S(1)}, u32[]{:S(2)}, u32[]{:S(2)}) collective-permute-start(bf16[192,384]{1,0:T(8,128)(2,1)S(1)} %add_convert_fusion.refs_0_), channel_id=1, source_target_pairs={{0,128},{32,160},{64,192},{96,224},{128,0},{160,32},{192,64},{224,... | collective-permute-start | bytes 442376 | tf_op jit(solution)/shard_map/ppermute | solution.py:288
  95.4 0.6 collective-permute-start.5
  95.9 1.3 %shard_map.120.refs_5_ = bf16[128,5632]{1,0:T(8,128)(2,1)} custom-call(s32[1]{0:T(128)} %bitcast.z_ref, bf16[32,176,128]{2,1,0:T(8,128)(2,1)S(1)} %all-to-all-done.1.in_ref), custom_call_target="tpu_custom_call" | custom-call | tf_op jit(solution)/shard_map/pallas_call | solution.py:83
  97.2 1.1 %collective-permute-done.3.refs_1_ = bf16[192,384]{1,0:T(8,128)(2,1)S(1)} collective-permute-done((bf16[192,384]{1,0:T(8,128)(2,1)S(1)}, bf16[192,384]{1,0:T(8,128)(2,1)S(1)}, u32[]{:S(2)}, u32[]{:S(2)}) %collective-permute-start.3) | collective-permute-done | bytes 147488 | tf_op jit(solution)/shard_map/ppermute | solution.py:288
  98.3 4.1 %collective-permute-done.4.refs_2_ = bf16[192,384]{1,0:T(8,128)(2,1)S(1)} collective-permute-done((bf16[192,384]{1,0:T(8,128)(2,1)S(1)}, bf16[192,384]{1,0:T(8,128)(2,1)S(1)}, u32[]{:S(2)}, u32[]{:S(2)}) %collective-permute-start.4) | collective-permute-done | bytes 147488 | tf_op jit(solution)/shard_map/ppermute | solution.py:288
  102.5 0.0 collective-permute-done.5.refs_3_
  102.5 0.8 shard_map.121
  (6 shorter events, 0.1 us)
Async XLA Ops:
  2.9 1.6 %copy-start = (bf16[32,352,128]{2,1,0:T(8,128)(2,1)}, bf16[32,352,128]{2,1,0:T(8,128)(2,1)S(1)}, u32[]{:S(2)}) copy-start(bf16[32,352,128]{2,1,0:T(8,128)(2,1)S(1)} %shard_map.118) | copy-start | bytes 8650756
  4.5 8.8 %copy-start.4 = (bf16[176]{0:T(256)(128)(2,1)S(1)}, bf16[176]{0:T(256)(128)(2,1)}, u32[]{:S(2)}) copy-start(bf16[176]{0:T(256)(128)(2,1)} %param.12) | copy-start | bytes 1060
  4.5 8.8 %copy-start.5 = (bf16[176]{0:T(256)(128)(2,1)S(1)}, bf16[176]{0:T(256)(128)(2,1)}, u32[]{:S(2)}) copy-start(bf16[176]{0:T(256)(128)(2,1)} %param.11) | copy-start | bytes 1060
  4.5 9.0 %copy-start.6 = (bf16[176]{0:T(256)(128)(2,1)S(1)}, bf16[176]{0:T(256)(128)(2,1)}, u32[]{:S(2)}) copy-start(bf16[176]{0:T(256)(128)(2,1)} %param.13) | copy-start | bytes 1060
  4.5 9.1 %copy-start.2 = (bf16[176,176]{1,0:T(8,128)(2,1)S(1)}, bf16[176,176]{1,0:T(8,128)(2,1)}, u32[]{:S(2)}) copy-start(bf16[176,176]{1,0:T(8,128)(2,1)} %param.9) | copy-start | bytes 185860
  4.5 9.2 %copy-start.3 = (bf16[176,176]{1,0:T(8,128)(2,1)S(1)}, bf16[176,176]{1,0:T(8,128)(2,1)}, u32[]{:S(2)}) copy-start(bf16[176,176]{1,0:T(8,128)(2,1)} %param.10) | copy-start | bytes 185860
  4.5 44.7 %all-to-all-start = ((bf16[32,352,128]{2,1,0:T(8,128)(2,1)}), bf16[32,352,128]{2,1,0:T(8,128)(2,1)S(1)}, u32[]{:S(2)}, u32[]{:S(2)}) async-start(bf16[32,352,128]{2,1,0:T(8,128)(2,1)} %copy-done), calls=%async_computation | async-start | bytes 5767168 | tf_op jit(solution)/shard_map/all_to_all | solution.py:280
  14.1 0.7 collective-permute-start
  60.9 1.1 %copy-start.1 = (bf16[32,176,128]{2,1,0:T(8,128)(2,1)}, bf16[32,176,128]{2,1,0:T(8,128)(2,1)S(1)}, u32[]{:S(2)}) copy-start(bf16[32,176,128]{2,1,0:T(8,128)(2,1)S(1)} %get-tuple-element.17) | copy-start | bytes 4325380
  62.0 28.1 %all-to-all-start.1 = ((bf16[32,176,128]{2,1,0:T(8,128)(2,1)}), bf16[32,176,128]{2,1,0:T(8,128)(2,1)S(1)}, u32[]{:S(2)}, u32[]{:S(2)}) async-start(bf16[32,176,128]{2,1,0:T(8,128)(2,1)} %copy-done.1), calls=%async_computation.1 | async-start | bytes 2883584 | tf_op jit(solution)/shard_map/all_to_all | solution.py:285
  68.8 5.0 %collective-permute-start.1 = (bf16[192,384]{1,0:T(8,128)(2,1)S(1)}, bf16[192,384]{1,0:T(8,128)(2,1)S(1)}, u32[]{:S(2)}, u32[]{:S(2)}) collective-permute-start(bf16[192,384]{1,0:T(8,128)(2,1)S(1)} %get-tuple-element.16), channel_id=1, source_target_pairs={{0,0},{4,4},{8,8},{12,12},{16,16},{20,20},{24,24},{28,28},{36,32},... | collective-permute-start | bytes 442376 | tf_op jit(solution)/shard_map/ppermute | solution.py:284
  69.5 20.3 %collective-permute-start.2 = (bf16[192,384]{1,0:T(8,128)(2,1)S(1)}, bf16[192,384]{1,0:T(8,128)(2,1)S(1)}, u32[]{:S(2)}, u32[]{:S(2)}) collective-permute-start(bf16[192,384]{1,0:T(8,128)(2,1)S(1)} %get-tuple-element.16), channel_id=1, source_target_pairs={{0,32},{4,36},{8,40},{12,44},{16,48},{20,52},{24,56},{28,60},{36,0... | collective-permute-start | bytes 442376 | tf_op jit(solution)/shard_map/ppermute | solution.py:284
  90.2 8.1 %collective-permute-start.3 = (bf16[192,384]{1,0:T(8,128)(2,1)S(1)}, bf16[192,384]{1,0:T(8,128)(2,1)S(1)}, u32[]{:S(2)}, u32[]{:S(2)}) collective-permute-start(bf16[192,384]{1,0:T(8,128)(2,1)S(1)} %add_convert_fusion.refs_0_), channel_id=1, source_target_pairs={{0,64},{32,96},{64,128},{96,160},{128,192},{160,224},{192,0},{224,... | collective-permute-start | bytes 442376 | tf_op jit(solution)/shard_map/ppermute | solution.py:288
  92.7 9.8 %collective-permute-start.4 = (bf16[192,384]{1,0:T(8,128)(2,1)S(1)}, bf16[192,384]{1,0:T(8,128)(2,1)S(1)}, u32[]{:S(2)}, u32[]{:S(2)}) collective-permute-start(bf16[192,384]{1,0:T(8,128)(2,1)S(1)} %add_convert_fusion.refs_0_), channel_id=1, source_target_pairs={{0,128},{32,160},{64,192},{96,224},{128,0},{160,32},{192,64},{224,... | collective-permute-start | bytes 442376 | tf_op jit(solution)/shard_map/ppermute | solution.py:288
  95.4 7.1 %collective-permute-start.5 = (bf16[192,384]{1,0:T(8,128)(2,1)S(1)}, bf16[192,384]{1,0:T(8,128)(2,1)S(1)}, u32[]{:S(2)}, u32[]{:S(2)}) collective-permute-start(bf16[192,384]{1,0:T(8,128)(2,1)S(1)} %add_convert_fusion.refs_0_), channel_id=1, source_target_pairs={{0,192},{32,224},{64,0},{96,32},{128,64},{160,96},{192,128},{224,1... | collective-permute-start | bytes 442376 | tf_op jit(solution)/shard_map/ppermute | solution.py:288

commit v9 on v8

--- a/solution.py
+++ b/solution.py
@@ -19,7 +19,7 @@
 NSEQ = NI * NQ
 
 
-def pack_kernel(z_ref, x_hbm, c_hbm, out_ref, x_s, c_s, in_sem):
+def pack_kernel(z_ref, x_hbm, c_hbm, out_hbm, x_s, c_s, out_s, in_sem, out_sem):
     wide = 2 * NQ * BLK
     loads = []
     for p in range(NZ // 2):
@@ -27,13 +27,23 @@
             cols = slice(p * wide, (p + 1) * wide)
             loads.append(pltpu.make_async_copy(src.at[:, cols], dst.at[:, cols], in_sem.at[k, p]))
             loads[-1].start()
-    turn = z_ref[0] * NQ
+    stores = []
     for p in range(NZ // 2):
+        turned = []
         for k, ref in enumerate((x_s, c_s)):
             loads[2 * p + k].wait()
-            turned = ref[:, p * wide : (p + 1) * wide].T
-            for h in range(2 * NQ):
-                out_ref[(2 * NQ * p + h) ^ turn, k * BLK : (k + 1) * BLK, :] = turned[h * BLK : (h + 1) * BLK]
+            turned.append(ref[:, p * wide : (p + 1) * wide].T)
+        for half in range(2):
+            group = (2 * p + half) ^ z_ref[0]
+            for q in range(NQ):
+                rows = slice((half * NQ + q) * BLK, (half * NQ + q + 1) * BLK)
+                for k in range(2):
+                    out_s[group * NQ + q, k * BLK : (k + 1) * BLK, :] = turned[k][rows]
+            slots = pl.ds(group * NQ, NQ)
+            stores.append(pltpu.make_async_copy(out_s.at[slots], out_hbm.at[slots], out_sem.at[2 * p + half]))
+            stores[-1].start()
+    for copy in stores:
+        copy.wait()
 
 
 def unpack_kernel(z_ref, in_ref, out_hbm, out_s, out_sem):
@@ -64,15 +74,18 @@
 
 
 def pack(z, x, c, interpret=False):
+    sem = pltpu.SemaphoreType.DMA
     return pl.pallas_call(
         pack_kernel,
         in_specs=[SMEM, ANY, ANY],
-        out_specs=VMEM,
-        out_shape=pltpu.VMEM((NSEQ, TWO, SEQ), x.dtype),
+        out_specs=ANY,
+        out_shape=pltpu.HBM((NSEQ, TWO, SEQ), x.dtype),
         scratch_shapes=[
             pltpu.VMEM(x.shape, x.dtype),
             pltpu.VMEM(x.shape, x.dtype),
-            pltpu.SemaphoreType.DMA((2, NZ // 2)),
+            pltpu.VMEM((NSEQ, TWO, SEQ), x.dtype),
+            sem((2, NZ // 2)),
+            sem((NZ,)),
         ],
         compiler_params=params(16),
         interpret=interpret,
@@ -112,12 +125,12 @@
 
 
 CH = 16
+PART = 8
 
 
 def main_kernel(
-    factor, m_ref, w_ref, wt_ref, out_ref, g_ref,
-    tri, x_s, pre_s, d_s, u_s, rest_s, own_s, f1_s, gain_s, drive_s, ub_s, log_s,
-    fwd_in, rev_in, fwd_s, rev_s, coef_s, q_s,
+    m_ref, w_ref, wt_ref, out_hbm, x_s, d_s, q_s, coef_s,
+    out_ref, tri, pre_s, u_s, own_s, f1_s, gain_s, ub_s, log_s, fwd_in, rev_in, fwd_s, rev_s, back_s, out_sem,
 ):
     f32, bf16 = jnp.float32, jnp.bfloat16
     row = lax.broadcasted_iota(jnp.int32, (WROWS - BLK, NSEQ * SEQ), 0)
@@ -125,6 +138,7 @@
     decay = wt_ref[:BLK, BLK + 1 : BLK + 2].astype(f32)
     soft = jnp.maximum(decay, 0.0) + jnp.log1p(jnp.exp(-jnp.abs(decay)))
     coef_s[...] = jnp.broadcast_to((-8.0 * LOG2E) * soft, (BLK, SEQ))
+    back_s[...] = LN2 / coef_s[...]
     q_s[...] = jnp.zeros_like(q_s)
     src = lax.broadcasted_iota(jnp.int32, (2 * SEQ, 2 * SEQ), 0)
     dst = lax.broadcasted_iota(jnp.int32, (2 * SEQ, 2 * SEQ), 1)
@@ -132,101 +146,133 @@
     for k, seen in enumerate((src <= dst, src < dst, src >= dst)):
         tri[k] = jnp.where(seen & same, 1.0, 0.0).astype(bf16)
 
-    def each(body, first=0, last=NSEQ // 2):
-        def two(p, _):
-            for half in range(2):
-                s = 2 * p + half
-                cols = pl.ds(pl.multiple_of(s * SEQ, SEQ), SEQ)
-                for r in range(0, BLK, CH):
-                    rows = pl.ds(pl.multiple_of(p * BLK + r, 16), CH)
-                    body(s, r, cols, (rows, slice(half * SEQ, (half + 1) * SEQ)))
-            return 0
-
-        lax.fori_loop(first, last, two, 0)
-
-    def gates(s, r, cols, at):
-        x = m_ref[s, r : r + CH, :].astype(f32)
-        rgate = sigmoid(pre_s[r : r + CH, cols])
-        igate = 0.5 + 0.5 * jnp.tanh(0.5 * pre_s[BLK + r : BLK + r + CH, cols])
-        u = coef_s[r : r + CH, :] * rgate
-        var = one_minus_square(u)
-        inv = lax.rsqrt(var)
-        scale = var * inv
-        ix = igate * x
-        drive = scale * ix
-        u_s[at] = u
-        rest_s[at] = LN2 - LN2 * rgate
-        own_s[at] = ix * (inv - scale)
-        f1_s[at] = drive - drive * igate
-        gain_s[at] = scale * igate
-        drive_s[at] = drive
-        ub_s[at] = u.astype(bf16)
-
     for s in range(NSEQ):
         x_s[:BLK, s * SEQ : (s + 1) * SEQ] = m_ref[s, :BLK, :]
     pre_s[...] = jnp.dot(wt_ref[...], x_s[...], preferred_element_type=f32)
+
+    def each(body):
+        def two(p, _):
+            for r in range(0, BLK, CH):
+                body(p, r, pl.ds(pl.multiple_of(p * BLK + r, 16), CH))
+            return 0
+
+        lax.fori_loop(0, NSEQ // 2, two, 0, unroll=2)
+
+    def halves(p):
+        for half in range(2):
+            s = 2 * p + half
+            yield s, pl.ds(pl.multiple_of(s * SEQ, SEQ), SEQ), slice(half * SEQ, (half + 1) * SEQ)
+
+    def gates(p, r, rows):
+        for s, cols, side in halves(p):
+            x = m_ref[s, r : r + CH, :].astype(f32)
+            rgate = sigmoid(pre_s[r : r + CH, cols])
+            igate = 0.5 + 0.5 * jnp.tanh(0.5 * pre_s[BLK + r : BLK + r + CH, cols])
+            u = coef_s[r : r + CH, :] * rgate
+            var = one_minus_square(u)
+            inv = lax.rsqrt(var)
+            scale = var * inv
+            gain = scale * igate
+            drive = gain * x
+            u_s[rows, side] = u
+            own_s[rows, side] = igate * x * (inv - scale)
+            f1_s[rows, side] = drive - drive * igate
+            gain_s[rows, side] = gain
+            ub_s[rows, side] = u.astype(bf16)
+
     each(gates)
     log_s[...] = jnp.dot(ub_s[...], tri[0], preferred_element_type=f32)
 
-    def weigh(s, r, cols, at):
-        total = log_s[at]
-        cot = m_ref[s, BLK + r : BLK + r + CH, :].astype(f32)
-        fwd_in[at] = (drive_s[at] * jnp.exp2(-total)).astype(bf16)
-        rev_in[at] = (cot * jnp.exp2(total)).astype(bf16)
+    def weigh(p, r, rows):
+        for s, cols, side in halves(p):
+            total = log_s[rows, side]
+            x = m_ref[s, r : r + CH, :].astype(f32)
+            cot = m_ref[s, BLK + r : BLK + r + CH, :].astype(f32)
+            fwd_in[rows, side] = (gain_s[rows, side] * x * jnp.exp2(-total)).astype(bf16)
+            rev_in[rows, side] = (cot * jnp.exp2(total)).astype(bf16)
 
     each(weigh)
     fwd_s[...] = jnp.dot(fwd_in[...], tri[1], preferred_element_type=f32)
     rev_s[...] = jnp.dot(rev_in[...], tri[2], preferred_element_type=f32)
 
-    def deltas(s, r, cols, at):
-        total = log_s[at]
-        adj = rev_s[at] * jnp.exp2(-total)
-        dlog = adj * (fwd_s[at] * jnp.exp2(total) - own_s[at])
-        v = dlog * u_s[at]
-        q_s[r : r + CH, :] += v
-        d_s[r : r + CH, cols] = (v * rest_s[at]).astype(bf16)
-        d_s[BLK + r : BLK + r + CH, cols] = (adj * f1_s[at]).astype(bf16)
-        pre_s[r : r + CH, cols] = adj * gain_s[at]
+    def deltas(p, r, rows):
+        part = q_s[r : r + CH, :]
+        for _, cols, side in halves(p):
+            total = log_s[rows, side]
+            u = u_s[rows, side]
+            adj = rev_s[rows, side] * jnp.exp2(-total)
+            v = adj * (fwd_s[rows, side] * jnp.exp2(total) - own_s[rows, side]) * u
+            part = part + v
+            rest = LN2 - u * back_s[r : r + CH, :]
+            d_s[r : r + CH, cols] = (v * rest).astype(bf16)
+            d_s[BLK + r : BLK + r + CH, cols] = (adj * f1_s[rows, side]).astype(bf16)
+            pre_s[r : r + CH, cols] = adj * gain_s[rows, side]
+        q_s[r : r + CH, :] = part
 
     each(deltas)
 
-    back = jnp.dot(w_ref[:BLK, :TWO], d_s[...], preferred_element_type=f32)
-    for s in range(NSEQ):
-        cols = slice(s * SEQ, (s + 1) * SEQ)
-        out_ref[s] = (back[:, cols] + pre_s[:BLK, cols]).astype(out_ref.dtype)
-
+    stores = []
+    for j in range(0, NSEQ, PART):
+        cols = slice(j * SEQ, (j + PART) * SEQ)
+        back = jnp.dot(w_ref[:BLK, :TWO], d_s[:, cols], preferred_element_type=f32) + pre_s[:BLK, cols]
+        for s in range(PART):
+            out_ref[j + s] = back[:, s * SEQ : (s + 1) * SEQ].astype(out_ref.dtype)
+        block = pl.ds(j, PART)
+        stores.append(pltpu.make_async_copy(out_ref.at[block], out_hbm.at[block], out_sem.at[j // PART]))
+        stores[-1].start()
+    for copy in stores:
+        copy.wait()
+
+
+def sums_kernel(factor, x_ref, d_ref, q_ref, coef_ref, g_ref):
     nt = (((1,), (1,)), ((), ()))
-    grad = lax.dot_general(x_s[...], d_s[...], nt, preferred_element_type=f32) * factor
+    grad = lax.dot_general(x_ref[...], d_ref[...], nt, preferred_element_type=jnp.float32) * factor
     g_ref[:, :TWO] = grad.astype(g_ref.dtype)
     g_ref[:, TWO:] = jnp.zeros((WROWS, WCOLS - TWO), g_ref.dtype)
-    decay_row = jnp.sum((q_s[...] / coef_s[...]).T, axis=0, keepdims=True) * (-8.0 * factor)
+    decay = jnp.sum((q_ref[...] / coef_ref[...]).T, axis=0, keepdims=True) * (-8.0 * factor)
     tail = grad[BLK:, :BLK]
     row = lax.broadcasted_iota(jnp.int32, tail.shape, 0)
-    g_ref[BLK:, :BLK] = jnp.where(row == 1, decay_row, tail).astype(g_ref.dtype)
-
-
-def main_call(factor, m, w, wt, grad_dtype=jnp.bfloat16, interpret=False):
+    g_ref[BLK:, :BLK] = jnp.where(row == 1, decay, tail).astype(g_ref.dtype)
+
+
+def main_call(m, w, wt, interpret=False):
     f32, bf16 = jnp.float32, jnp.bfloat16
     vmem = pltpu.VMEM
     flat, half = (vmem((NSEQ // 2 * BLK, 2 * SEQ), kind) for kind in (f32, bf16))
     return pl.pallas_call(
-        functools.partial(main_kernel, factor),
-        out_shape=[vmem((NSEQ, BLK, SEQ), bf16), vmem((WROWS, WCOLS), grad_dtype)],
-        in_specs=[VMEM] * 3,
-        out_specs=[VMEM] * 2,
-        scratch_shapes=[
-            vmem((3, 2 * SEQ, 2 * SEQ), bf16),
+        main_kernel,
+        out_shape=[
+            pltpu.HBM((NSEQ, BLK, SEQ), bf16),
             vmem((WROWS, NSEQ * SEQ), bf16),
-            vmem((TWO, NSEQ * SEQ), f32),
             vmem((TWO, NSEQ * SEQ), bf16),
-            flat, flat, flat, flat, flat, flat,
-            half, flat, half, half, flat, flat,
             vmem((BLK, SEQ), f32),
             vmem((BLK, SEQ), f32),
         ],
-        compiler_params=params(48),
+        in_specs=[VMEM] * 3,
+        out_specs=[ANY] + [VMEM] * 4,
+        scratch_shapes=[
+            vmem((NSEQ, BLK, SEQ), bf16),
+            vmem((3, 2 * SEQ, 2 * SEQ), bf16),
+            vmem((TWO, NSEQ * SEQ), f32),
+            flat, flat, flat, flat,
+            half, flat, half, half, flat, flat,
+            vmem((BLK, SEQ), f32),
+            pltpu.SemaphoreType.DMA((NSEQ // PART,)),
+        ],
+        compiler_params=params(44),
         interpret=interpret,
     )(*kept(m, w, wt))
+
+
+def sums_call(factor, x, d, q, coef, grad_dtype=jnp.bfloat16, interpret=False):
+    return pl.pallas_call(
+        functools.partial(sums_kernel, factor),
+        out_shape=pltpu.VMEM((WROWS, WCOLS), grad_dtype),
+        in_specs=[VMEM] * 4,
+        out_specs=VMEM,
+        compiler_params=params(16),
+        interpret=interpret,
+    )(*kept(x, d, q, coef))
 
 
 def finish_kernel(count, *refs):
@@ -280,9 +326,10 @@
     got = lax.all_to_all(pack(z, inputs, cotangent), plane, 0, 0, tiled=True)
     w = lax.ppermute(wire(wa, wx, ba, bx, decay), line, fetch)
     total = SEQ * NSEQ * NZ
-    out, grads = main_call(float(total) ** -0.5, got, w, w[:, :TWO].T)
+    out, *kept_here = main_call(got, w, w[:, :TWO].T)
+    back = lax.all_to_all(out, plane, 0, 0, tiled=True)
+    grads = sums_call(float(total) ** -0.5, *kept_here)
     near, far = lax.ppermute(grads, line, fetch), lax.ppermute(grads, line, across)
-    back = lax.all_to_all(out, plane, 0, 0, tiled=True)
     near, far, back = lax.optimization_barrier((near, far, back))
     pair = (near.astype(f32) + far.astype(f32)).astype(bf16)
     parts = [pair] + [lax.ppermute(pair, "cuts", [(i, (i + 2 * k) % NI) for i in range(NI)]) for k in (1, 2, 3)]

time: 104 us -> 105 us (level)
  waiting for transfers between devices: 55.9 us -> 52.6 us
  local copies, waits for them, and re-layouts: 3.37 us -> 5.23 us
  starting transfers between devices: 26.9 us -> 28.6 us
  Pallas kernels: 16 us -> 17.3 us
    ppermute x1, waiting for transfers between devices: 16 us -> 13 us  [per_device(): lax.ppermute(grads, line, across)]
    unnamed x16 -> x20, local copies, waits for them, and re-layouts: 2.88 us -> 4.74 us
    ppermute x3, starting transfers between devices: 5.73 us -> 7.3 us  [per_device(): lax.ppermute(pair, 'cuts', [(i, (i + 2 * k) % NI) for i in range(NI)])]
    pallas_call x2 -> x3, Pallas kernels: 13.9 us -> 15.2 us  [the longest x1 10.8 us: main_call(): pl.pallas_call(main_kernel, out_shape=[pltpu.HBM((NSEQ, BLK, SEQ), bf16),...]
  transfers between devices with their start and end apart: 8 -> 8, of which waited for: 5 -> 5; matrix products, arithmetic and copies ran while one was open for 1% -> 1% of each run, Pallas kernels for 1% -> 2%
where the time goes in v9:
time: 105 us
  waiting for transfers between devices  52.6 us (50%)
  starting transfers between devices  28.6 us (27%)
  Pallas kernels  17.3 us (16%)
  local copies, waits for them, and re-layouts  5.23 us (5%)
    all_to_all x1, waiting for transfers between devices, per_device(): got = lax.all_to_all(pack(z, inputs, cotangent), plane, 0, 0, tiled=True)  34.3 us
    ppermute x1, waiting for transfers between devices, per_device(): lax.ppermute(grads, line, across)  13 us
    pallas_call x1, Pallas kernels, main_call(): pl.pallas_call(main_kernel, out_shape=[pltpu.HBM((NSEQ, BLK, SEQ), bf16),...  10.8 us
    all_to_all x1, starting transfers between devices, per_device(): got = lax.all_to_all(pack(z, inputs, cotangent), plane, 0, 0, tiled=True)  8.73 us
    ppermute x3, starting transfers between devices, per_device(): lax.ppermute(pair, 'cuts', [(i, (i + 2 * k) % NI) for i in range(NI)])  7.3 us
    all_to_all x1, starting transfers between devices, per_device(): back = lax.all_to_all(out, plane, 0, 0, tiled=True)  6.91 us
    ppermute x3, waiting for transfers between devices, per_device(): lax.ppermute(pair, 'cuts', [(i, (i + 2 * k) % NI) for i in range(NI)])  4.89 us
    unnamed x20, local copies, waits for them, and re-layouts  4.74 us
  transfers between devices with their start and end apart: 8, of which 5 were waited for; matrix products, arithmetic and copies ran while one was open for 1% of the time, Pallas kernels for 2%

profile of v9, /device:TPU:1, one launch (start us, length us, event | category | flops | bytes accessed | tf_op | source)
XLA Modules:
  0.0 104.9 jit_solution(6536139884461970842)
XLA Ops:
  0.6 3.3 %shard_map.118 = bf16[32,352,128]{2,1,0:T(8,128)(2,1)} custom-call(s32[1]{0:T(128)} %bitcast.z_ref, bf16[128,5632]{1,0:T(8,128)(2,1)} %x_hbm.1, bf16[128,5632]{1,0:T(8,128)(2,1)} %c_hbm.1), custom_call_target="tpu_custom_call" | custom-call | tf_op jit(solution)/shard_map/pallas_call | solution.py:78
  3.9 0.0 copy-start.6
  3.9 0.0 copy-start.7
  3.9 0.0 copy-start.8
  3.9 0.0 copy-start.4
  3.9 0.0 copy-start.5
  4.0 8.7 %all-to-all-start = ((bf16[32,352,128]{2,1,0:T(8,128)(2,1)}), bf16[32,352,128]{2,1,0:T(8,128)(2,1)S(1)}, u32[]{:S(2)}, u32[]{:S(2)}) async-start(bf16[32,352,128]{2,1,0:T(8,128)(2,1)} %shard_map.118), calls=%async_computation | async-start | bytes 5767168 | tf_op jit(solution)/shard_map/all_to_all | solution.py:326
  12.7 0.0 copy-done.6
  12.7 0.0 copy-done.7
  12.7 0.1 pad_maximum_fusion
  12.8 0.1 broadcast_in_dim.13
  12.9 0.0 copy-done.8
  12.9 0.1 broadcast_in_dim.14
  13.1 0.0 copy-done.4
  13.1 0.1 copy.16
  13.2 0.0 copy-done.5
  13.2 0.1 copy.17
  13.3 0.1 pad.10.clone
  13.4 0.1 maximum_maximum_fusion
  13.5 0.7 collective-permute-start
  14.2 0.0 collective-permute-done
  14.2 0.1 copy.20.w_ref
  14.4 34.3 %all-to-all-done.m_ref = bf16[32,352,128]{2,1,0:T(8,128)(2,1)S(1)} async-done(((bf16[32,352,128]{2,1,0:T(8,128)(2,1)}), bf16[32,352,128]{2,1,0:T(8,128)(2,1)S(1)}, u32[]{:S(2)}, u32[]{:S(2)}) %all-to-all-start) | async-done | bytes 2883616 | tf_op jit(solution)/shard_map/all_to_all | solution.py:326
  48.7 10.8 %shard_map.119 = (bf16[32,176,128]{2,1,0:T(8,128)(2,1)}, bf16[192,4096]{1,0:T(8,128)(2,1)S(1)}, bf16[352,4096]{1,0:T(8,128)(2,1)S(1)}, f32[176,128]{1,0:T(8,128)S(1)}, f32[176,128]{1,0:T(8,128)S(1)}) custom-call(bf16[32,352,128]{2,1,0:T(8,128)(2,1)S(1)} %all-to-all-done.m_ref, bf16[192,384]{1,0:T(8,128)(2,1)S(1)} %copy.20.w_ref, ...), custom_call_target="tpu_custom_call" | custom-call | tf_op jit(solution)/shard_map/pallas_call | solution.py:242
  59.5 0.0 copy-start
  59.5 1.6 %copy-done = bf16[352,4096]{1,0:T(8,128)(2,1)} copy-done((bf16[352,4096]{1,0:T(8,128)(2,1)}, bf16[352,4096]{1,0:T(8,128)(2,1)S(1)}, u32[]{:S(2)}) %copy-start) | copy-done | bytes 2883608
  61.0 0.0 copy-start.2
  61.0 1.1 %copy-done.2 = bf16[192,4096]{1,0:T(8,128)(2,1)} copy-done((bf16[192,4096]{1,0:T(8,128)(2,1)}, bf16[192,4096]{1,0:T(8,128)(2,1)S(1)}, u32[]{:S(2)}) %copy-start.2) | copy-done | bytes 1572888
  62.2 0.0 copy-start.3
  62.2 6.9 %all-to-all-start.1 = ((bf16[32,176,128]{2,1,0:T(8,128)(2,1)}), bf16[32,176,128]{2,1,0:T(8,128)(2,1)S(1)}, u32[]{:S(2)}, u32[]{:S(2)}) async-start(bf16[32,176,128]{2,1,0:T(8,128)(2,1)} %get-tuple-element.23), calls=%async_computation.1 | async-start | bytes 2883584 | tf_op jit(solution)/shard_map/all_to_all | solution.py:330
  69.1 0.0 copy-done.3
  69.1 0.0 copy-start.1
  69.1 1.8 %copy-done.1 = bf16[352,4096]{1,0:T(8,128)(2,1)S(1)} copy-done((bf16[352,4096]{1,0:T(8,128)(2,1)S(1)}, bf16[352,4096]{1,0:T(8,128)(2,1)}, u32[]{:S(2)}) %copy-start.1) | copy-done | bytes 2883608
  70.9 1.2 %shard_map.120 = bf16[192,384]{1,0:T(8,128)(2,1)S(1)} custom-call(bf16[192,4096]{1,0:T(8,128)(2,1)S(1)} %copy-done.3, bf16[352,4096]{1,0:T(8,128)(2,1)S(1)} %copy-done.1, f32[176,128]{1,0:T(8,128)S(1)} %get-tuple-element.21.q_ref, f32[176,128]{1,0:T(8,128)S(1)} %get-tuple-element.22.coef_ref), custom_call_target="tpu_custom_call" | custom-call | tf_op jit(solution)/shard_map/pallas_call | solution.py:268
  72.1 0.7 collective-permute-start.1
  72.8 4.3 %collective-permute-start.2 = (bf16[192,384]{1,0:T(8,128)(2,1)S(1)}, bf16[192,384]{1,0:T(8,128)(2,1)S(1)}, u32[]{:S(2)}, u32[]{:S(2)}) collective-permute-start(bf16[192,384]{1,0:T(8,128)(2,1)S(1)} %shard_map.120), channel_id=1, source_target_pairs={{0,32},{4,36},{8,40},{12,44},{16,48},{20,52},{24,56},{28,60},{36,0... | collective-permute-start | bytes 442376 | tf_op jit(solution)/shard_map/ppermute | solution.py:332
  77.1 0.0 collective-permute-done.1
  77.1 13.0 %collective-permute-done.2 = bf16[192,384]{1,0:T(8,128)(2,1)S(1)} collective-permute-done((bf16[192,384]{1,0:T(8,128)(2,1)S(1)}, bf16[192,384]{1,0:T(8,128)(2,1)S(1)}, u32[]{:S(2)}, u32[]{:S(2)}) %collective-permute-start.2) | collective-permute-done | bytes 147488 | tf_op jit(solution)/shard_map/ppermute | solution.py:332
  90.1 0.5 all-to-all-done.1.in_ref
  90.6 0.7 collective-permute-start.3
  91.2 6.6 %collective-permute-start.4 = (bf16[192,384]{1,0:T(8,128)(2,1)S(1)}, bf16[192,384]{1,0:T(8,128)(2,1)S(1)}, u32[]{:S(2)}, u32[]{:S(2)}) collective-permute-start(bf16[192,384]{1,0:T(8,128)(2,1)S(1)} %add_convert_fusion.refs_0_), channel_id=1, source_target_pairs={{0,128},{32,160},{64,192},{96,224},{128,0},{160,32},{192,64},{224,... | collective-permute-start | bytes 442376 | tf_op jit(solution)/shard_map/ppermute | solution.py:335
  97.9 0.0 collective-permute-start.5
  97.9 1.3 %shard_map.121.refs_5_ = bf16[128,5632]{1,0:T(8,128)(2,1)} custom-call(s32[1]{0:T(128)} %bitcast.z_ref, bf16[32,176,128]{2,1,0:T(8,128)(2,1)S(1)} %all-to-all-done.1.in_ref), custom_call_target="tpu_custom_call" | custom-call | tf_op jit(solution)/shard_map/pallas_call | solution.py:96
  99.2 0.9 collective-permute-done.3.refs_1_
  100.1 4.0 %collective-permute-done.4.refs_2_ = bf16[192,384]{1,0:T(8,128)(2,1)S(1)} collective-permute-done((bf16[192,384]{1,0:T(8,128)(2,1)S(1)}, bf16[192,384]{1,0:T(8,128)(2,1)S(1)}, u32[]{:S(2)}, u32[]{:S(2)}) %collective-permute-start.4) | collective-permute-done | bytes 147488 | tf_op jit(solution)/shard_map/ppermute | solution.py:335
  104.1 0.0 collective-permute-done.5.refs_3_
  104.1 0.8 shard_map.122
  (6 shorter events, 0.1 us)
Async XLA Ops:
  3.9 8.8 %copy-start.6 = (bf16[176]{0:T(256)(128)(2,1)S(1)}, bf16[176]{0:T(256)(128)(2,1)}, u32[]{:S(2)}) copy-start(bf16[176]{0:T(256)(128)(2,1)} %param.12) | copy-start | bytes 1060
  3.9 8.8 %copy-start.7 = (bf16[176]{0:T(256)(128)(2,1)S(1)}, bf16[176]{0:T(256)(128)(2,1)}, u32[]{:S(2)}) copy-start(bf16[176]{0:T(256)(128)(2,1)} %param.11) | copy-start | bytes 1060
  3.9 9.0 %copy-start.8 = (bf16[176]{0:T(256)(128)(2,1)S(1)}, bf16[176]{0:T(256)(128)(2,1)}, u32[]{:S(2)}) copy-start(bf16[176]{0:T(256)(128)(2,1)} %param.13) | copy-start | bytes 1060
  3.9 9.1 %copy-start.4 = (bf16[176,176]{1,0:T(8,128)(2,1)S(1)}, bf16[176,176]{1,0:T(8,128)(2,1)}, u32[]{:S(2)}) copy-start(bf16[176,176]{1,0:T(8,128)(2,1)} %param.9) | copy-start | bytes 185860
  3.9 9.2 %copy-start.5 = (bf16[176,176]{1,0:T(8,128)(2,1)S(1)}, bf16[176,176]{1,0:T(8,128)(2,1)}, u32[]{:S(2)}) copy-start(bf16[176,176]{1,0:T(8,128)(2,1)} %param.10) | copy-start | bytes 185860
  4.0 44.7 %all-to-all-start = ((bf16[32,352,128]{2,1,0:T(8,128)(2,1)}), bf16[32,352,128]{2,1,0:T(8,128)(2,1)S(1)}, u32[]{:S(2)}, u32[]{:S(2)}) async-start(bf16[32,352,128]{2,1,0:T(8,128)(2,1)} %shard_map.118), calls=%async_computation | async-start | bytes 5767168 | tf_op jit(solution)/shard_map/all_to_all | solution.py:326
  13.5 0.7 collective-permute-start
  59.5 1.6 %copy-start = (bf16[352,4096]{1,0:T(8,128)(2,1)}, bf16[352,4096]{1,0:T(8,128)(2,1)S(1)}, u32[]{:S(2)}) copy-start(bf16[352,4096]{1,0:T(8,128)(2,1)S(1)} %get-tuple-element.20.d_ref) | copy-start | bytes 8650756
  61.0 1.1 %copy-start.2 = (bf16[192,4096]{1,0:T(8,128)(2,1)}, bf16[192,4096]{1,0:T(8,128)(2,1)S(1)}, u32[]{:S(2)}) copy-start(bf16[192,4096]{1,0:T(8,128)(2,1)S(1)} %get-tuple-element.19.x_ref) | copy-start | bytes 4718596
  62.2 6.9 %copy-start.3 = (bf16[192,4096]{1,0:T(8,128)(2,1)S(1)}, bf16[192,4096]{1,0:T(8,128)(2,1)}, u32[]{:S(2)}) copy-start(bf16[192,4096]{1,0:T(8,128)(2,1)} %copy-done.2) | copy-start | bytes 4718596
  62.2 28.4 %all-to-all-start.1 = ((bf16[32,176,128]{2,1,0:T(8,128)(2,1)}), bf16[32,176,128]{2,1,0:T(8,128)(2,1)S(1)}, u32[]{:S(2)}, u32[]{:S(2)}) async-start(bf16[32,176,128]{2,1,0:T(8,128)(2,1)} %get-tuple-element.23), calls=%async_computation.1 | async-start | bytes 2883584 | tf_op jit(solution)/shard_map/all_to_all | solution.py:330
  69.1 1.8 %copy-start.1 = (bf16[352,4096]{1,0:T(8,128)(2,1)S(1)}, bf16[352,4096]{1,0:T(8,128)(2,1)}, u32[]{:S(2)}) copy-start(bf16[352,4096]{1,0:T(8,128)(2,1)} %copy-done) | copy-start | bytes 8650756
  72.1 5.0 %collective-permute-start.1 = (bf16[192,384]{1,0:T(8,128)(2,1)S(1)}, bf16[192,384]{1,0:T(8,128)(2,1)S(1)}, u32[]{:S(2)}, u32[]{:S(2)}) collective-permute-start(bf16[192,384]{1,0:T(8,128)(2,1)S(1)} %shard_map.120), channel_id=1, source_target_pairs={{0,0},{4,4},{8,8},{12,12},{16,16},{20,20},{24,24},{28,28},{36,32},... | collective-permute-start | bytes 442376 | tf_op jit(solution)/shard_map/ppermute | solution.py:332
  72.8 17.3 %collective-permute-start.2 = (bf16[192,384]{1,0:T(8,128)(2,1)S(1)}, bf16[192,384]{1,0:T(8,128)(2,1)S(1)}, u32[]{:S(2)}, u32[]{:S(2)}) collective-permute-start(bf16[192,384]{1,0:T(8,128)(2,1)S(1)} %shard_map.120), channel_id=1, source_target_pairs={{0,32},{4,36},{8,40},{12,44},{16,48},{20,52},{24,56},{28,60},{36,0... | collective-permute-start | bytes 442376 | tf_op jit(solution)/shard_map/ppermute | solution.py:332
  90.6 9.5 %collective-permute-start.3 = (bf16[192,384]{1,0:T(8,128)(2,1)S(1)}, bf16[192,384]{1,0:T(8,128)(2,1)S(1)}, u32[]{:S(2)}, u32[]{:S(2)}) collective-permute-start(bf16[192,384]{1,0:T(8,128)(2,1)S(1)} %add_convert_fusion.refs_0_), channel_id=1, source_target_pairs={{0,64},{32,96},{64,128},{96,160},{128,192},{160,224},{192,0},{224,... | collective-permute-start | bytes 442376 | tf_op jit(solution)/shard_map/ppermute | solution.py:335
  91.2 12.8 %collective-permute-start.4 = (bf16[192,384]{1,0:T(8,128)(2,1)S(1)}, bf16[192,384]{1,0:T(8,128)(2,1)S(1)}, u32[]{:S(2)}, u32[]{:S(2)}) collective-permute-start(bf16[192,384]{1,0:T(8,128)(2,1)S(1)} %add_convert_fusion.refs_0_), channel_id=1, source_target_pairs={{0,128},{32,160},{64,192},{96,224},{128,0},{160,32},{192,64},{224,... | collective-permute-start | bytes 442376 | tf_op jit(solution)/shard_map/ppermute | solution.py:335
  97.9 6.2 %collective-permute-start.5 = (bf16[192,384]{1,0:T(8,128)(2,1)S(1)}, bf16[192,384]{1,0:T(8,128)(2,1)S(1)}, u32[]{:S(2)}, u32[]{:S(2)}) collective-permute-start(bf16[192,384]{1,0:T(8,128)(2,1)S(1)} %add_convert_fusion.refs_0_), channel_id=1, source_target_pairs={{0,192},{32,224},{64,0},{96,32},{128,64},{160,96},{192,128},{224,1... | collective-permute-start | bytes 442376 | tf_op jit(solution)/shard_map/ppermute | solution.py:335

commit v10 on v9

--- a/solution.py
+++ b/solution.py
@@ -129,8 +129,8 @@
 
 
 def main_kernel(
-    m_ref, w_ref, wt_ref, out_hbm, x_s, d_s, q_s, coef_s,
-    out_ref, tri, pre_s, u_s, own_s, f1_s, gain_s, ub_s, log_s, fwd_in, rev_in, fwd_s, rev_s, back_s, out_sem,
+    factor, m_ref, w_ref, wt_ref, out_hbm, g_ref,
+    x_s, d_s, q_s, coef_s, out_ref, tri, pre_s, u_s, own_s, f1_s, gain_s, ub_s, log_s, fwd_in, rev_in, fwd_s, rev_s, back_s, out_sem,
 ):
     f32, bf16 = jnp.float32, jnp.bfloat16
     row = lax.broadcasted_iota(jnp.int32, (WROWS - BLK, NSEQ * SEQ), 0)
@@ -220,37 +220,33 @@
         block = pl.ds(j, PART)
         stores.append(pltpu.make_async_copy(out_ref.at[block], out_hbm.at[block], out_sem.at[j // PART]))
         stores[-1].start()
+
+    nt = (((1,), (1,)), ((), ()))
+    grad = lax.dot_general(x_s[...], d_s[...], nt, preferred_element_type=f32) * factor
+    g_ref[:, :TWO] = grad.astype(g_ref.dtype)
+    g_ref[:, TWO:] = jnp.zeros((WROWS, WCOLS - TWO), g_ref.dtype)
+    decay_row = jnp.sum((q_s[...] / coef_s[...]).T, axis=0, keepdims=True) * (-8.0 * factor)
+    tail = grad[BLK:, :BLK]
+    row = lax.broadcasted_iota(jnp.int32, tail.shape, 0)
+    g_ref[BLK:, :BLK] = jnp.where(row == 1, decay_row, tail).astype(g_ref.dtype)
     for copy in stores:
         copy.wait()
 
 
-def sums_kernel(factor, x_ref, d_ref, q_ref, coef_ref, g_ref):
-    nt = (((1,), (1,)), ((), ()))
-    grad = lax.dot_general(x_ref[...], d_ref[...], nt, preferred_element_type=jnp.float32) * factor
-    g_ref[:, :TWO] = grad.astype(g_ref.dtype)
-    g_ref[:, TWO:] = jnp.zeros((WROWS, WCOLS - TWO), g_ref.dtype)
-    decay = jnp.sum((q_ref[...] / coef_ref[...]).T, axis=0, keepdims=True) * (-8.0 * factor)
-    tail = grad[BLK:, :BLK]
-    row = lax.broadcasted_iota(jnp.int32, tail.shape, 0)
-    g_ref[BLK:, :BLK] = jnp.where(row == 1, decay, tail).astype(g_ref.dtype)
-
-
-def main_call(m, w, wt, interpret=False):
+def main_call(factor, m, w, wt, grad_dtype=jnp.bfloat16, interpret=False):
     f32, bf16 = jnp.float32, jnp.bfloat16
     vmem = pltpu.VMEM
     flat, half = (vmem((NSEQ // 2 * BLK, 2 * SEQ), kind) for kind in (f32, bf16))
     return pl.pallas_call(
-        main_kernel,
-        out_shape=[
-            pltpu.HBM((NSEQ, BLK, SEQ), bf16),
+        functools.partial(main_kernel, factor),
+        out_shape=[pltpu.HBM((NSEQ, BLK, SEQ), bf16), vmem((WROWS, WCOLS), grad_dtype)],
+        in_specs=[VMEM] * 3,
+        out_specs=[ANY, VMEM],
+        scratch_shapes=[
             vmem((WROWS, NSEQ * SEQ), bf16),
             vmem((TWO, NSEQ * SEQ), bf16),
             vmem((BLK, SEQ), f32),
             vmem((BLK, SEQ), f32),
-        ],
-        in_specs=[VMEM] * 3,
-        out_specs=[ANY] + [VMEM] * 4,
-        scratch_shapes=[
             vmem((NSEQ, BLK, SEQ), bf16),
             vmem((3, 2 * SEQ, 2 * SEQ), bf16),
             vmem((TWO, NSEQ * SEQ), f32),
@@ -259,20 +255,9 @@
             vmem((BLK, SEQ), f32),
             pltpu.SemaphoreType.DMA((NSEQ // PART,)),
         ],
-        compiler_params=params(44),
+        compiler_params=params(48),
         interpret=interpret,
     )(*kept(m, w, wt))
-
-
-def sums_call(factor, x, d, q, coef, grad_dtype=jnp.bfloat16, interpret=False):
-    return pl.pallas_call(
-        functools.partial(sums_kernel, factor),
-        out_shape=pltpu.VMEM((WROWS, WCOLS), grad_dtype),
-        in_specs=[VMEM] * 4,
-        out_specs=VMEM,
-        compiler_params=params(16),
-        interpret=interpret,
-    )(*kept(x, d, q, coef))
 
 
 def finish_kernel(count, *refs):
@@ -326,9 +311,8 @@
     got = lax.all_to_all(pack(z, inputs, cotangent), plane, 0, 0, tiled=True)
     w = lax.ppermute(wire(wa, wx, ba, bx, decay), line, fetch)
     total = SEQ * NSEQ * NZ
-    out, *kept_here = main_call(got, w, w[:, :TWO].T)
+    out, grads = main_call(float(total) ** -0.5, got, w, w[:, :TWO].T)
     back = lax.all_to_all(out, plane, 0, 0, tiled=True)
-    grads = sums_call(float(total) ** -0.5, *kept_here)
     near, far = lax.ppermute(grads, line, fetch), lax.ppermute(grads, line, across)
     near, far, back = lax.optimization_barrier((near, far, back))
     pair = (near.astype(f32) + far.astype(f32)).astype(bf16)

time: 105 us -> 101 us (0.962)
  local copies, waits for them, and re-layouts: 5.23 us -> 0.73 us
  waiting for transfers between devices: 52.6 us -> 55.9 us
  starting transfers between devices: 28.6 us -> 26.9 us
  Pallas kernels: 17.3 us -> 16.1 us
    unnamed x20 -> x14, local copies, waits for them, and re-layouts: 4.74 us -> 0.24 us
    ppermute x1, waiting for transfers between devices: 13 us -> 16 us  [per_device(): lax.ppermute(grads, line, across)]
    ppermute x3, starting transfers between devices: 7.3 us -> 5.72 us  [per_device(): lax.ppermute(pair, 'cuts', [(i, (i + 2 * k) % NI) for i in range(NI)])]
    pallas_call x2 -> x1, Pallas kernels: 11.9 us -> 10.8 us  [main_call(): pl.pallas_call(functools.partial(main_kernel, factor), out_shape=[pltpu.H...]
  transfers between devices with their start and end apart: 8 -> 8, of which waited for: 5 -> 5; matrix products, arithmetic and copies ran while one was open for 1% -> 1% of each run, Pallas kernels for 2% -> 1%
where the time goes in v10:
time: 101 us
  waiting for transfers between devices  55.9 us (55%)
  starting transfers between devices  26.9 us (27%)
  Pallas kernels  16.1 us (16%)
    all_to_all x1, waiting for transfers between devices, per_device(): got = lax.all_to_all(pack(z, inputs, cotangent), plane, 0, 0, tiled=True)  34.3 us
    ppermute x1, waiting for transfers between devices, per_device(): lax.ppermute(grads, line, across)  16 us
    pallas_call x1, Pallas kernels, main_call(): pl.pallas_call(functools.partial(main_kernel, factor), out_shape=[pltpu.H...  10.8 us
    all_to_all x1, starting transfers between devices, per_device(): got = lax.all_to_all(pack(z, inputs, cotangent), plane, 0, 0, tiled=True)  8.73 us
    all_to_all x1, starting transfers between devices, per_device(): back = lax.all_to_all(out, plane, 0, 0, tiled=True)  6.79 us
    ppermute x3, starting transfers between devices, per_device(): lax.ppermute(pair, 'cuts', [(i, (i + 2 * k) % NI) for i in range(NI)])  5.72 us
    ppermute x3, waiting for transfers between devices, per_device(): lax.ppermute(pair, 'cuts', [(i, (i + 2 * k) % NI) for i in range(NI)])  5.25 us
    ppermute x1, starting transfers between devices, per_device(): lax.ppermute(grads, line, across)  4.34 us
  transfers between devices with their start and end apart: 8, of which 5 were waited for; matrix products, arithmetic and copies ran while one was open for 1% of the time, Pallas kernels for 1%

profile of v10, /device:TPU:1, one launch (start us, length us, event | category | flops | bytes accessed | tf_op | source)
XLA Modules:
  0.0 100.8 jit_solution(13227561852835840469)
XLA Ops:
  0.6 3.3 %shard_map.118 = bf16[32,352,128]{2,1,0:T(8,128)(2,1)} custom-call(s32[1]{0:T(128)} %bitcast.z_ref, bf16[128,5632]{1,0:T(8,128)(2,1)} %x_hbm.1, bf16[128,5632]{1,0:T(8,128)(2,1)} %c_hbm.1), custom_call_target="tpu_custom_call" | custom-call | tf_op jit(solution)/shard_map/pallas_call | solution.py:78
  3.9 0.0 copy-start.2
  3.9 0.0 copy-start.3
  3.9 0.0 copy-start.4
  3.9 0.0 copy-start
  3.9 0.0 copy-start.1
  4.0 8.7 %all-to-all-start = ((bf16[32,352,128]{2,1,0:T(8,128)(2,1)}), bf16[32,352,128]{2,1,0:T(8,128)(2,1)S(1)}, u32[]{:S(2)}, u32[]{:S(2)}) async-start(bf16[32,352,128]{2,1,0:T(8,128)(2,1)} %shard_map.118), calls=%async_computation | async-start | bytes 5767168 | tf_op jit(solution)/shard_map/all_to_all | solution.py:311
  12.7 0.0 copy-done.2
  12.7 0.0 copy-done.3
  12.7 0.1 pad_maximum_fusion
  12.8 0.1 broadcast_in_dim.13
  12.9 0.0 copy-done.4
  12.9 0.1 broadcast_in_dim.14
  13.1 0.0 copy-done
  13.1 0.1 copy.16
  13.2 0.0 copy-done.1
  13.2 0.1 copy.17
  13.3 0.1 pad.10.clone
  13.4 0.1 maximum_maximum_fusion
  13.5 0.7 collective-permute-start
  14.2 0.0 collective-permute-done
  14.2 0.1 copy.20.w_ref
  14.4 34.3 %all-to-all-done.m_ref = bf16[32,352,128]{2,1,0:T(8,128)(2,1)S(1)} async-done(((bf16[32,352,128]{2,1,0:T(8,128)(2,1)}), bf16[32,352,128]{2,1,0:T(8,128)(2,1)S(1)}, u32[]{:S(2)}, u32[]{:S(2)}) %all-to-all-start) | async-done | bytes 2883616 | tf_op jit(solution)/shard_map/all_to_all | solution.py:311
  48.7 10.8 %shard_map.119 = (bf16[32,176,128]{2,1,0:T(8,128)(2,1)}, bf16[192,384]{1,0:T(8,128)(2,1)S(1)}) custom-call(bf16[32,352,128]{2,1,0:T(8,128)(2,1)S(1)} %all-to-all-done.m_ref, bf16[192,384]{1,0:T(8,128)(2,1)S(1)} %copy.20.w_ref, bf16[352,192]{1,0:T(8,128)(2,1)S(1)} %slice_bitcast_fusion.wt_ref), custom_call_target="tpu_custom_call" | custom-call | tf_op jit(solution)/shard_map/pallas_call | solution.py:240
  59.5 0.0 copy-start.5
  59.5 6.8 %all-to-all-start.1 = ((bf16[32,176,128]{2,1,0:T(8,128)(2,1)}), bf16[32,176,128]{2,1,0:T(8,128)(2,1)S(1)}, u32[]{:S(2)}, u32[]{:S(2)}) async-start(bf16[32,176,128]{2,1,0:T(8,128)(2,1)} %get-tuple-element.17), calls=%async_computation.1 | async-start | bytes 2883584 | tf_op jit(solution)/shard_map/all_to_all | solution.py:315
  66.3 0.7 collective-permute-start.1
  67.0 4.3 %collective-permute-start.2 = (bf16[192,384]{1,0:T(8,128)(2,1)S(1)}, bf16[192,384]{1,0:T(8,128)(2,1)S(1)}, u32[]{:S(2)}, u32[]{:S(2)}) collective-permute-start(bf16[192,384]{1,0:T(8,128)(2,1)S(1)} %get-tuple-element.16), channel_id=1, source_target_pairs={{0,32},{4,36},{8,40},{12,44},{16,48},{20,52},{24,56},{28,60},{36,0... | collective-permute-start | bytes 442376 | tf_op jit(solution)/shard_map/ppermute | solution.py:316
  71.3 0.0 collective-permute-done.1
  71.3 16.0 %collective-permute-done.2 = bf16[192,384]{1,0:T(8,128)(2,1)S(1)} collective-permute-done((bf16[192,384]{1,0:T(8,128)(2,1)S(1)}, bf16[192,384]{1,0:T(8,128)(2,1)S(1)}, u32[]{:S(2)}, u32[]{:S(2)}) %collective-permute-start.2) | collective-permute-done | bytes 147488 | tf_op jit(solution)/shard_map/ppermute | solution.py:316
  87.3 0.4 all-to-all-done.1.in_ref
  87.7 2.5 %collective-permute-start.3 = (bf16[192,384]{1,0:T(8,128)(2,1)S(1)}, bf16[192,384]{1,0:T(8,128)(2,1)S(1)}, u32[]{:S(2)}, u32[]{:S(2)}) collective-permute-start(bf16[192,384]{1,0:T(8,128)(2,1)S(1)} %add_convert_fusion.refs_0_), channel_id=1, source_target_pairs={{0,64},{32,96},{64,128},{96,160},{128,192},{160,224},{192,0},{224,... | collective-permute-start | bytes 442376 | tf_op jit(solution)/shard_map/ppermute | solution.py:319
  90.1 2.7 %collective-permute-start.4 = (bf16[192,384]{1,0:T(8,128)(2,1)S(1)}, bf16[192,384]{1,0:T(8,128)(2,1)S(1)}, u32[]{:S(2)}, u32[]{:S(2)}) collective-permute-start(bf16[192,384]{1,0:T(8,128)(2,1)S(1)} %add_convert_fusion.refs_0_), channel_id=1, source_target_pairs={{0,128},{32,160},{64,192},{96,224},{128,0},{160,32},{192,64},{224,... | collective-permute-start | bytes 442376 | tf_op jit(solution)/shard_map/ppermute | solution.py:319
  92.9 0.5 collective-permute-start.5
  93.4 0.0 copy-done.5
  93.4 1.3 %shard_map.120.refs_5_ = bf16[128,5632]{1,0:T(8,128)(2,1)} custom-call(s32[1]{0:T(128)} %bitcast.z_ref, bf16[32,176,128]{2,1,0:T(8,128)(2,1)S(1)} %all-to-all-done.1.in_ref), custom_call_target="tpu_custom_call" | custom-call | tf_op jit(solution)/shard_map/pallas_call | solution.py:96
  94.7 1.1 %collective-permute-done.3.refs_1_ = bf16[192,384]{1,0:T(8,128)(2,1)S(1)} collective-permute-done((bf16[192,384]{1,0:T(8,128)(2,1)S(1)}, bf16[192,384]{1,0:T(8,128)(2,1)S(1)}, u32[]{:S(2)}, u32[]{:S(2)}) %collective-permute-start.3) | collective-permute-done | bytes 147488 | tf_op jit(solution)/shard_map/ppermute | solution.py:319
  95.8 4.1 %collective-permute-done.4.refs_2_ = bf16[192,384]{1,0:T(8,128)(2,1)S(1)} collective-permute-done((bf16[192,384]{1,0:T(8,128)(2,1)S(1)}, bf16[192,384]{1,0:T(8,128)(2,1)S(1)}, u32[]{:S(2)}, u32[]{:S(2)}) %collective-permute-start.4) | collective-permute-done | bytes 147488 | tf_op jit(solution)/shard_map/ppermute | solution.py:319
  100.0 0.0 collective-permute-done.5.refs_3_
  100.0 0.8 shard_map.121
  (6 shorter events, 0.1 us)
Async XLA Ops:
  3.9 8.8 %copy-start.2 = (bf16[176]{0:T(256)(128)(2,1)S(1)}, bf16[176]{0:T(256)(128)(2,1)}, u32[]{:S(2)}) copy-start(bf16[176]{0:T(256)(128)(2,1)} %param.12) | copy-start | bytes 1060
  3.9 8.8 %copy-start.3 = (bf16[176]{0:T(256)(128)(2,1)S(1)}, bf16[176]{0:T(256)(128)(2,1)}, u32[]{:S(2)}) copy-start(bf16[176]{0:T(256)(128)(2,1)} %param.11) | copy-start | bytes 1060
  3.9 9.0 %copy-start.4 = (bf16[176]{0:T(256)(128)(2,1)S(1)}, bf16[176]{0:T(256)(128)(2,1)}, u32[]{:S(2)}) copy-start(bf16[176]{0:T(256)(128)(2,1)} %param.13) | copy-start | bytes 1060
  3.9 9.1 %copy-start = (bf16[176,176]{1,0:T(8,128)(2,1)S(1)}, bf16[176,176]{1,0:T(8,128)(2,1)}, u32[]{:S(2)}) copy-start(bf16[176,176]{1,0:T(8,128)(2,1)} %param.9) | copy-start | bytes 185860
  3.9 9.2 %copy-start.1 = (bf16[176,176]{1,0:T(8,128)(2,1)S(1)}, bf16[176,176]{1,0:T(8,128)(2,1)}, u32[]{:S(2)}) copy-start(bf16[176,176]{1,0:T(8,128)(2,1)} %param.10) | copy-start | bytes 185860
  4.0 44.7 %all-to-all-start = ((bf16[32,352,128]{2,1,0:T(8,128)(2,1)}), bf16[32,352,128]{2,1,0:T(8,128)(2,1)S(1)}, u32[]{:S(2)}, u32[]{:S(2)}) async-start(bf16[32,352,128]{2,1,0:T(8,128)(2,1)} %shard_map.118), calls=%async_computation | async-start | bytes 5767168 | tf_op jit(solution)/shard_map/all_to_all | solution.py:311
  13.5 0.7 collective-permute-start
  59.5 33.9 %copy-start.5 = (bf16[176]{0:T(256)(128)(2,1)S(1)}, bf16[176]{0:T(256)(128)(2,1)}, u32[]{:S(2)}) copy-start(bf16[176]{0:T(256)(128)(2,1)} %param.13) | copy-start | bytes 1060
  59.5 28.1 %all-to-all-start.1 = ((bf16[32,176,128]{2,1,0:T(8,128)(2,1)}), bf16[32,176,128]{2,1,0:T(8,128)(2,1)S(1)}, u32[]{:S(2)}, u32[]{:S(2)}) async-start(bf16[32,176,128]{2,1,0:T(8,128)(2,1)} %get-tuple-element.17), calls=%async_computation.1 | async-start | bytes 2883584 | tf_op jit(solution)/shard_map/all_to_all | solution.py:315
  66.3 5.0 %collective-permute-start.1 = (bf16[192,384]{1,0:T(8,128)(2,1)S(1)}, bf16[192,384]{1,0:T(8,128)(2,1)S(1)}, u32[]{:S(2)}, u32[]{:S(2)}) collective-permute-start(bf16[192,384]{1,0:T(8,128)(2,1)S(1)} %get-tuple-element.16), channel_id=1, source_target_pairs={{0,0},{4,4},{8,8},{12,12},{16,16},{20,20},{24,24},{28,28},{36,32},... | collective-permute-start | bytes 442376 | tf_op jit(solution)/shard_map/ppermute | solution.py:316
  67.0 20.3 %collective-permute-start.2 = (bf16[192,384]{1,0:T(8,128)(2,1)S(1)}, bf16[192,384]{1,0:T(8,128)(2,1)S(1)}, u32[]{:S(2)}, u32[]{:S(2)}) collective-permute-start(bf16[192,384]{1,0:T(8,128)(2,1)S(1)} %get-tuple-element.16), channel_id=1, source_target_pairs={{0,32},{4,36},{8,40},{12,44},{16,48},{20,52},{24,56},{28,60},{36,0... | collective-permute-start | bytes 442376 | tf_op jit(solution)/shard_map/ppermute | solution.py:316
  87.7 8.1 %collective-permute-start.3 = (bf16[192,384]{1,0:T(8,128)(2,1)S(1)}, bf16[192,384]{1,0:T(8,128)(2,1)S(1)}, u32[]{:S(2)}, u32[]{:S(2)}) collective-permute-start(bf16[192,384]{1,0:T(8,128)(2,1)S(1)} %add_convert_fusion.refs_0_), channel_id=1, source_target_pairs={{0,64},{32,96},{64,128},{96,160},{128,192},{160,224},{192,0},{224,... | collective-permute-start | bytes 442376 | tf_op jit(solution)/shard_map/ppermute | solution.py:319
  90.1 9.8 %collective-permute-start.4 = (bf16[192,384]{1,0:T(8,128)(2,1)S(1)}, bf16[192,384]{1,0:T(8,128)(2,1)S(1)}, u32[]{:S(2)}, u32[]{:S(2)}) collective-permute-start(bf16[192,384]{1,0:T(8,128)(2,1)S(1)} %add_convert_fusion.refs_0_), channel_id=1, source_target_pairs={{0,128},{32,160},{64,192},{96,224},{128,0},{160,32},{192,64},{224,... | collective-permute-start | bytes 442376 | tf_op jit(solution)/shard_map/ppermute | solution.py:319
  92.9 7.1 %collective-permute-start.5 = (bf16[192,384]{1,0:T(8,128)(2,1)S(1)}, bf16[192,384]{1,0:T(8,128)(2,1)S(1)}, u32[]{:S(2)}, u32[]{:S(2)}) collective-permute-start(bf16[192,384]{1,0:T(8,128)(2,1)S(1)} %add_convert_fusion.refs_0_), channel_id=1, source_target_pairs={{0,192},{32,224},{64,0},{96,32},{128,64},{160,96},{192,128},{224,1... | collective-permute-start | bytes 442376 | tf_op jit(solution)/shard_map/ppermute | solution.py:319

commit v11 on v10

--- a/solution.py
+++ b/solution.py
@@ -125,6 +125,7 @@
 
 
 CH = 16
+LOTS = 2
 PART = 8
 
 
@@ -150,66 +151,73 @@
         x_s[:BLK, s * SEQ : (s + 1) * SEQ] = m_ref[s, :BLK, :]
     pre_s[...] = jnp.dot(wt_ref[...], x_s[...], preferred_element_type=f32)
 
-    def each(body):
-        def two(p, _):
-            for r in range(0, BLK, CH):
-                body(p, r, pl.ds(pl.multiple_of(p * BLK + r, 16), CH))
-            return 0
-
-        lax.fori_loop(0, NSEQ // 2, two, 0, unroll=2)
+    def gates(p, lot):
+        for r in range(0, BLK, CH):
+            for s, cols, side in halves(p):
+                rows = slice(r, r + CH)
+                x = m_ref[s, rows, :].astype(f32)
+                rgate = sigmoid(pre_s[rows, cols])
+                igate = 0.5 + 0.5 * jnp.tanh(0.5 * pre_s[BLK + r : BLK + r + CH, cols])
+                u = coef_s[rows, :] * rgate
+                var = one_minus_square(u)
+                inv = lax.rsqrt(var)
+                scale = var * inv
+                gain = scale * igate
+                drive = gain * x
+                u_s[lot, rows, side] = u
+                own_s[lot, rows, side] = igate * x * (inv - scale)
+                f1_s[lot, rows, side] = drive - drive * igate
+                gain_s[lot, rows, side] = gain
+                ub_s[lot, rows, side] = u.astype(bf16)
+
+    def weigh(p, lot):
+        for r in range(0, BLK, CH):
+            for s, cols, side in halves(p):
+                rows = slice(r, r + CH)
+                total = log_s[lot, rows, side]
+                x = m_ref[s, rows, :].astype(f32)
+                cot = m_ref[s, BLK + r : BLK + r + CH, :].astype(f32)
+                fwd_in[lot, rows, side] = (gain_s[lot, rows, side] * x * jnp.exp2(-total)).astype(bf16)
+                rev_in[lot, rows, side] = (cot * jnp.exp2(total)).astype(bf16)
+
+    def deltas(p, lot):
+        for r in range(0, BLK, CH):
+            rows = slice(r, r + CH)
+            part = q_s[rows, :]
+            for _, cols, side in halves(p):
+                total = log_s[lot, rows, side]
+                u = u_s[lot, rows, side]
+                adj = rev_s[lot, rows, side] * jnp.exp2(-total)
+                v = adj * (fwd_s[lot, rows, side] * jnp.exp2(total) - own_s[lot, rows, side]) * u
+                part = part + v
+                rest = LN2 - u * back_s[rows, :]
+                d_s[rows, cols] = (v * rest).astype(bf16)
+                d_s[BLK + r : BLK + r + CH, cols] = (adj * f1_s[lot, rows, side]).astype(bf16)
+                pre_s[rows, cols] = adj * gain_s[lot, rows, side]
+            q_s[rows, :] = part
 
     def halves(p):
         for half in range(2):
             s = 2 * p + half
             yield s, pl.ds(pl.multiple_of(s * SEQ, SEQ), SEQ), slice(half * SEQ, (half + 1) * SEQ)
 
-    def gates(p, r, rows):
-        for s, cols, side in halves(p):
-            x = m_ref[s, r : r + CH, :].astype(f32)
-            rgate = sigmoid(pre_s[r : r + CH, cols])
-            igate = 0.5 + 0.5 * jnp.tanh(0.5 * pre_s[BLK + r : BLK + r + CH, cols])
-            u = coef_s[r : r + CH, :] * rgate
-            var = one_minus_square(u)
-            inv = lax.rsqrt(var)
-            scale = var * inv
-            gain = scale * igate
-            drive = gain * x
-            u_s[rows, side] = u
-            own_s[rows, side] = igate * x * (inv - scale)
-            f1_s[rows, side] = drive - drive * igate
-            gain_s[rows, side] = gain
-            ub_s[rows, side] = u.astype(bf16)
-
-    each(gates)
-    log_s[...] = jnp.dot(ub_s[...], tri[0], preferred_element_type=f32)
-
-    def weigh(p, r, rows):
-        for s, cols, side in halves(p):
-            total = log_s[rows, side]
-            x = m_ref[s, r : r + CH, :].astype(f32)
-            cot = m_ref[s, BLK + r : BLK + r + CH, :].astype(f32)
-            fwd_in[rows, side] = (gain_s[rows, side] * x * jnp.exp2(-total)).astype(bf16)
-            rev_in[rows, side] = (cot * jnp.exp2(total)).astype(bf16)
-
-    each(weigh)
-    fwd_s[...] = jnp.dot(fwd_in[...], tri[1], preferred_element_type=f32)
-    rev_s[...] = jnp.dot(rev_in[...], tri[2], preferred_element_type=f32)
-
-    def deltas(p, r, rows):
-        part = q_s[r : r + CH, :]
-        for _, cols, side in halves(p):
-            total = log_s[rows, side]
-            u = u_s[rows, side]
-            adj = rev_s[rows, side] * jnp.exp2(-total)
-            v = adj * (fwd_s[rows, side] * jnp.exp2(total) - own_s[rows, side]) * u
-            part = part + v
-            rest = LN2 - u * back_s[r : r + CH, :]
-            d_s[r : r + CH, cols] = (v * rest).astype(bf16)
-            d_s[BLK + r : BLK + r + CH, cols] = (adj * f1_s[rows, side]).astype(bf16)
-            pre_s[r : r + CH, cols] = adj * gain_s[rows, side]
-        q_s[r : r + CH, :] = part
-
-    each(deltas)
+    def sums(dst, src, lot, k):
+        dst[lot] = jnp.dot(src[lot], tri[k], preferred_element_type=f32)
+
+    def several(i, _):
+        for lot in range(LOTS + 2):
+            if lot < LOTS:
+                gates(LOTS * i + lot, lot)
+                sums(log_s, ub_s, lot, 0)
+            if 1 <= lot <= LOTS:
+                weigh(LOTS * i + lot - 1, lot - 1)
+                sums(fwd_s, fwd_in, lot - 1, 1)
+                sums(rev_s, rev_in, lot - 1, 2)
+            if lot >= 2:
+                deltas(LOTS * i + lot - 2, lot - 2)
+        return 0
+
+    lax.fori_loop(0, NSEQ // (2 * LOTS), several, 0)
 
     stores = []
     for j in range(0, NSEQ, PART):
@@ -236,7 +244,7 @@
 def main_call(factor, m, w, wt, grad_dtype=jnp.bfloat16, interpret=False):
     f32, bf16 = jnp.float32, jnp.bfloat16
     vmem = pltpu.VMEM
-    flat, half = (vmem((NSEQ // 2 * BLK, 2 * SEQ), kind) for kind in (f32, bf16))
+    flat, half = (vmem((LOTS, BLK, 2 * SEQ), kind) for kind in (f32, bf16))
     return pl.pallas_call(
         functools.partial(main_kernel, factor),
         out_shape=[pltpu.HBM((NSEQ, BLK, SEQ), bf16), vmem((WROWS, WCOLS), grad_dtype)],

time: 101 us -> 99.4 us (0.984)
  Pallas kernels: 16.1 us -> 14.4 us
    pallas_call x1, Pallas kernels: 10.8 us -> 9.07 us  [main_call(): pl.pallas_call(functools.partial(main_kernel, factor), out_shape=[pltpu.H...]
where the time goes in v11:
time: 99.4 us; the launch traced here: 99.1 us
  waiting for transfers between devices  55.9 us (56%)
  starting transfers between devices  27 us (27%)
  Pallas kernels  14.4 us (14%)
    all_to_all x1, waiting for transfers between devices, per_device(): got = lax.all_to_all(pack(z, inputs, cotangent), plane, 0, 0, tiled=True)  34.3 us
    ppermute x1, waiting for transfers between devices, per_device(): lax.ppermute(grads, line, across)  16 us
    pallas_call x1, Pallas kernels, main_call(): pl.pallas_call(functools.partial(main_kernel, factor), out_shape=[pltpu.H...  9.07 us
    all_to_all x1, starting transfers between devices, per_device(): got = lax.all_to_all(pack(z, inputs, cotangent), plane, 0, 0, tiled=True)  8.73 us
    all_to_all x1, starting transfers between devices, per_device(): back = lax.all_to_all(out, plane, 0, 0, tiled=True)  6.8 us
    ppermute x3, starting transfers between devices, per_device(): lax.ppermute(pair, 'cuts', [(i, (i + 2 * k) % NI) for i in range(NI)])  5.74 us
    ppermute x3, waiting for transfers between devices, per_device(): lax.ppermute(pair, 'cuts', [(i, (i + 2 * k) % NI) for i in range(NI)])  5.25 us
    ppermute x1, starting transfers between devices, per_device(): lax.ppermute(grads, line, across)  4.34 us
  transfers between devices with their start and end apart: 8, of which 5 were waited for; matrix products, arithmetic and copies ran while one was open for 1% of the time, Pallas kernels for 1%

profile of v11, /device:TPU:1, one launch (start us, length us, event | category | flops | bytes accessed | tf_op | source)
XLA Modules:
  0.0 99.1 jit_solution(2660943780326749316)
XLA Ops:
  0.6 3.3 %shard_map.118 = bf16[32,352,128]{2,1,0:T(8,128)(2,1)} custom-call(s32[1]{0:T(128)} %bitcast.z_ref, bf16[128,5632]{1,0:T(8,128)(2,1)} %x_hbm.1, bf16[128,5632]{1,0:T(8,128)(2,1)} %c_hbm.1), custom_call_target="tpu_custom_call" | custom-call | tf_op jit(solution)/shard_map/pallas_call | solution.py:78
  3.9 0.0 copy-start.2
  3.9 0.0 copy-start.3
  3.9 0.0 copy-start.4
  3.9 0.0 copy-start
  3.9 0.0 copy-start.1
  4.0 8.7 %all-to-all-start = ((bf16[32,352,128]{2,1,0:T(8,128)(2,1)}), bf16[32,352,128]{2,1,0:T(8,128)(2,1)S(1)}, u32[]{:S(2)}, u32[]{:S(2)}) async-start(bf16[32,352,128]{2,1,0:T(8,128)(2,1)} %shard_map.118), calls=%async_computation | async-start | bytes 5767168 | tf_op jit(solution)/shard_map/all_to_all | solution.py:319
  12.7 0.0 copy-done.2
  12.7 0.0 copy-done.3
  12.7 0.1 pad_maximum_fusion
  12.8 0.1 broadcast_in_dim.13
  12.9 0.0 copy-done.4
  12.9 0.1 broadcast_in_dim.14
  13.1 0.0 copy-done
  13.1 0.1 copy.16
  13.2 0.0 copy-done.1
  13.2 0.1 copy.17
  13.3 0.1 pad.10.clone
  13.4 0.1 maximum_maximum_fusion
  13.5 0.7 collective-permute-start
  14.2 0.0 collective-permute-done
  14.2 0.1 copy.20.w_ref
  14.4 34.3 %all-to-all-done.m_ref = bf16[32,352,128]{2,1,0:T(8,128)(2,1)S(1)} async-done(((bf16[32,352,128]{2,1,0:T(8,128)(2,1)}), bf16[32,352,128]{2,1,0:T(8,128)(2,1)S(1)}, u32[]{:S(2)}, u32[]{:S(2)}) %all-to-all-start) | async-done | bytes 2883616 | tf_op jit(solution)/shard_map/all_to_all | solution.py:319
  48.7 9.1 %shard_map.119 = (bf16[32,176,128]{2,1,0:T(8,128)(2,1)}, bf16[192,384]{1,0:T(8,128)(2,1)S(1)}) custom-call(bf16[32,352,128]{2,1,0:T(8,128)(2,1)S(1)} %all-to-all-done.m_ref, bf16[192,384]{1,0:T(8,128)(2,1)S(1)} %copy.20.w_ref, bf16[352,192]{1,0:T(8,128)(2,1)S(1)} %slice_bitcast_fusion.wt_ref), custom_call_target="tpu_custom_call" | custom-call | tf_op jit(solution)/shard_map/pallas_call | solution.py:248
  57.8 0.0 copy-start.5
  57.8 6.8 %all-to-all-start.1 = ((bf16[32,176,128]{2,1,0:T(8,128)(2,1)}), bf16[32,176,128]{2,1,0:T(8,128)(2,1)S(1)}, u32[]{:S(2)}, u32[]{:S(2)}) async-start(bf16[32,176,128]{2,1,0:T(8,128)(2,1)} %get-tuple-element.17), calls=%async_computation.1 | async-start | bytes 2883584 | tf_op jit(solution)/shard_map/all_to_all | solution.py:323
  64.6 0.7 collective-permute-start.1
  65.3 4.3 %collective-permute-start.2 = (bf16[192,384]{1,0:T(8,128)(2,1)S(1)}, bf16[192,384]{1,0:T(8,128)(2,1)S(1)}, u32[]{:S(2)}, u32[]{:S(2)}) collective-permute-start(bf16[192,384]{1,0:T(8,128)(2,1)S(1)} %get-tuple-element.16), channel_id=1, source_target_pairs={{0,32},{4,36},{8,40},{12,44},{16,48},{20,52},{24,56},{28,60},{36,0... | collective-permute-start | bytes 442376 | tf_op jit(solution)/shard_map/ppermute | solution.py:324
  69.6 0.0 collective-permute-done.1
  69.6 16.0 %collective-permute-done.2 = bf16[192,384]{1,0:T(8,128)(2,1)S(1)} collective-permute-done((bf16[192,384]{1,0:T(8,128)(2,1)S(1)}, bf16[192,384]{1,0:T(8,128)(2,1)S(1)}, u32[]{:S(2)}, u32[]{:S(2)}) %collective-permute-start.2) | collective-permute-done | bytes 147488 | tf_op jit(solution)/shard_map/ppermute | solution.py:324
  85.6 0.4 all-to-all-done.1.in_ref
  86.0 2.5 %collective-permute-start.3 = (bf16[192,384]{1,0:T(8,128)(2,1)S(1)}, bf16[192,384]{1,0:T(8,128)(2,1)S(1)}, u32[]{:S(2)}, u32[]{:S(2)}) collective-permute-start(bf16[192,384]{1,0:T(8,128)(2,1)S(1)} %add_convert_fusion.refs_0_), channel_id=1, source_target_pairs={{0,64},{32,96},{64,128},{96,160},{128,192},{160,224},{192,0},{224,... | collective-permute-start | bytes 442376 | tf_op jit(solution)/shard_map/ppermute | solution.py:327
  88.4 2.7 %collective-permute-start.4 = (bf16[192,384]{1,0:T(8,128)(2,1)S(1)}, bf16[192,384]{1,0:T(8,128)(2,1)S(1)}, u32[]{:S(2)}, u32[]{:S(2)}) collective-permute-start(bf16[192,384]{1,0:T(8,128)(2,1)S(1)} %add_convert_fusion.refs_0_), channel_id=1, source_target_pairs={{0,128},{32,160},{64,192},{96,224},{128,0},{160,32},{192,64},{224,... | collective-permute-start | bytes 442376 | tf_op jit(solution)/shard_map/ppermute | solution.py:327
  91.2 0.6 collective-permute-start.5
  91.7 0.0 copy-done.5
  91.7 1.3 %shard_map.120.refs_5_ = bf16[128,5632]{1,0:T(8,128)(2,1)} custom-call(s32[1]{0:T(128)} %bitcast.z_ref, bf16[32,176,128]{2,1,0:T(8,128)(2,1)S(1)} %all-to-all-done.1.in_ref), custom_call_target="tpu_custom_call" | custom-call | tf_op jit(solution)/shard_map/pallas_call | solution.py:96
  93.0 1.1 %collective-permute-done.3.refs_1_ = bf16[192,384]{1,0:T(8,128)(2,1)S(1)} collective-permute-done((bf16[192,384]{1,0:T(8,128)(2,1)S(1)}, bf16[192,384]{1,0:T(8,128)(2,1)S(1)}, u32[]{:S(2)}, u32[]{:S(2)}) %collective-permute-start.3) | collective-permute-done | bytes 147488 | tf_op jit(solution)/shard_map/ppermute | solution.py:327
  94.1 4.2 %collective-permute-done.4.refs_2_ = bf16[192,384]{1,0:T(8,128)(2,1)S(1)} collective-permute-done((bf16[192,384]{1,0:T(8,128)(2,1)S(1)}, bf16[192,384]{1,0:T(8,128)(2,1)S(1)}, u32[]{:S(2)}, u32[]{:S(2)}) %collective-permute-start.4) | collective-permute-done | bytes 147488 | tf_op jit(solution)/shard_map/ppermute | solution.py:327
  98.3 0.0 collective-permute-done.5.refs_3_
  98.3 0.8 shard_map.121
  (6 shorter events, 0.1 us)
Async XLA Ops:
  3.9 8.8 %copy-start.2 = (bf16[176]{0:T(256)(128)(2,1)S(1)}, bf16[176]{0:T(256)(128)(2,1)}, u32[]{:S(2)}) copy-start(bf16[176]{0:T(256)(128)(2,1)} %param.12) | copy-start | bytes 1060
  3.9 8.8 %copy-start.3 = (bf16[176]{0:T(256)(128)(2,1)S(1)}, bf16[176]{0:T(256)(128)(2,1)}, u32[]{:S(2)}) copy-start(bf16[176]{0:T(256)(128)(2,1)} %param.11) | copy-start | bytes 1060
  3.9 9.0 %copy-start.4 = (bf16[176]{0:T(256)(128)(2,1)S(1)}, bf16[176]{0:T(256)(128)(2,1)}, u32[]{:S(2)}) copy-start(bf16[176]{0:T(256)(128)(2,1)} %param.13) | copy-start | bytes 1060
  3.9 9.1 %copy-start = (bf16[176,176]{1,0:T(8,128)(2,1)S(1)}, bf16[176,176]{1,0:T(8,128)(2,1)}, u32[]{:S(2)}) copy-start(bf16[176,176]{1,0:T(8,128)(2,1)} %param.9) | copy-start | bytes 185860
  3.9 9.2 %copy-start.1 = (bf16[176,176]{1,0:T(8,128)(2,1)S(1)}, bf16[176,176]{1,0:T(8,128)(2,1)}, u32[]{:S(2)}) copy-start(bf16[176,176]{1,0:T(8,128)(2,1)} %param.10) | copy-start | bytes 185860
  4.0 44.7 %all-to-all-start = ((bf16[32,352,128]{2,1,0:T(8,128)(2,1)}), bf16[32,352,128]{2,1,0:T(8,128)(2,1)S(1)}, u32[]{:S(2)}, u32[]{:S(2)}) async-start(bf16[32,352,128]{2,1,0:T(8,128)(2,1)} %shard_map.118), calls=%async_computation | async-start | bytes 5767168 | tf_op jit(solution)/shard_map/all_to_all | solution.py:319
  13.5 0.7 collective-permute-start
  57.8 33.9 %copy-start.5 = (bf16[176]{0:T(256)(128)(2,1)S(1)}, bf16[176]{0:T(256)(128)(2,1)}, u32[]{:S(2)}) copy-start(bf16[176]{0:T(256)(128)(2,1)} %param.13) | copy-start | bytes 1060
  57.8 28.1 %all-to-all-start.1 = ((bf16[32,176,128]{2,1,0:T(8,128)(2,1)}), bf16[32,176,128]{2,1,0:T(8,128)(2,1)S(1)}, u32[]{:S(2)}, u32[]{:S(2)}) async-start(bf16[32,176,128]{2,1,0:T(8,128)(2,1)} %get-tuple-element.17), calls=%async_computation.1 | async-start | bytes 2883584 | tf_op jit(solution)/shard_map/all_to_all | solution.py:323
  64.6 5.0 %collective-permute-start.1 = (bf16[192,384]{1,0:T(8,128)(2,1)S(1)}, bf16[192,384]{1,0:T(8,128)(2,1)S(1)}, u32[]{:S(2)}, u32[]{:S(2)}) collective-permute-start(bf16[192,384]{1,0:T(8,128)(2,1)S(1)} %get-tuple-element.16), channel_id=1, source_target_pairs={{0,0},{4,4},{8,8},{12,12},{16,16},{20,20},{24,24},{28,28},{36,32},... | collective-permute-start | bytes 442376 | tf_op jit(solution)/shard_map/ppermute | solution.py:324
  65.3 20.3 %collective-permute-start.2 = (bf16[192,384]{1,0:T(8,128)(2,1)S(1)}, bf16[192,384]{1,0:T(8,128)(2,1)S(1)}, u32[]{:S(2)}, u32[]{:S(2)}) collective-permute-start(bf16[192,384]{1,0:T(8,128)(2,1)S(1)} %get-tuple-element.16), channel_id=1, source_target_pairs={{0,32},{4,36},{8,40},{12,44},{16,48},{20,52},{24,56},{28,60},{36,0... | collective-permute-start | bytes 442376 | tf_op jit(solution)/shard_map/ppermute | solution.py:324
  86.0 8.1 %collective-permute-start.3 = (bf16[192,384]{1,0:T(8,128)(2,1)S(1)}, bf16[192,384]{1,0:T(8,128)(2,1)S(1)}, u32[]{:S(2)}, u32[]{:S(2)}) collective-permute-start(bf16[192,384]{1,0:T(8,128)(2,1)S(1)} %add_convert_fusion.refs_0_), channel_id=1, source_target_pairs={{0,64},{32,96},{64,128},{96,160},{128,192},{160,224},{192,0},{224,... | collective-permute-start | bytes 442376 | tf_op jit(solution)/shard_map/ppermute | solution.py:327
  88.4 9.8 %collective-permute-start.4 = (bf16[192,384]{1,0:T(8,128)(2,1)S(1)}, bf16[192,384]{1,0:T(8,128)(2,1)S(1)}, u32[]{:S(2)}, u32[]{:S(2)}) collective-permute-start(bf16[192,384]{1,0:T(8,128)(2,1)S(1)} %add_convert_fusion.refs_0_), channel_id=1, source_target_pairs={{0,128},{32,160},{64,192},{96,224},{128,0},{160,32},{192,64},{224,... | collective-permute-start | bytes 442376 | tf_op jit(solution)/shard_map/ppermute | solution.py:327
  91.2 7.1 %collective-permute-start.5 = (bf16[192,384]{1,0:T(8,128)(2,1)S(1)}, bf16[192,384]{1,0:T(8,128)(2,1)S(1)}, u32[]{:S(2)}, u32[]{:S(2)}) collective-permute-start(bf16[192,384]{1,0:T(8,128)(2,1)S(1)} %add_convert_fusion.refs_0_), channel_id=1, source_target_pairs={{0,192},{32,224},{64,0},{96,32},{128,64},{160,96},{192,128},{224,1... | collective-permute-start | bytes 442376 | tf_op jit(solution)/shard_map/ppermute | solution.py:327

commit v12 on v11

--- a/solution.py
+++ b/solution.py
@@ -314,17 +314,17 @@
     z = lax.axis_index("z").astype(jnp.int32).reshape(1)
     everyone = [(i, k) for i in range(NI) for k in range(NZ)]
     fetch = [(i * NZ + (k ^ i), i * NZ + k) for i, k in everyone]
-    across = [(i * NZ + (k ^ i), (i ^ 1) * NZ + k) for i, k in everyone]
 
     got = lax.all_to_all(pack(z, inputs, cotangent), plane, 0, 0, tiled=True)
     w = lax.ppermute(wire(wa, wx, ba, bx, decay), line, fetch)
     total = SEQ * NSEQ * NZ
     out, grads = main_call(float(total) ** -0.5, got, w, w[:, :TWO].T)
     back = lax.all_to_all(out, plane, 0, 0, tiled=True)
-    near, far = lax.ppermute(grads, line, fetch), lax.ppermute(grads, line, across)
-    near, far, back = lax.optimization_barrier((near, far, back))
-    pair = (near.astype(f32) + far.astype(f32)).astype(bf16)
-    parts = [pair] + [lax.ppermute(pair, "cuts", [(i, (i + 2 * k) % NI) for i in range(NI)]) for k in (1, 2, 3)]
+    near = lax.ppermute(grads, line, fetch)
+    shifts = [[(i, (i + 2 * k) % NI) for i in range(NI)] for k in (1, 2, 3)]
+    four = sum(p.astype(f32) for p in [near] + [lax.ppermute(near, "cuts", shift) for shift in shifts])
+    four, back = lax.optimization_barrier((four.astype(bf16), back))
+    parts = [four, lax.ppermute(four, "cuts", [(i, i ^ 1) for i in range(NI)])]
     input_grad = unpack(z, back)
     grad_a, grad_x, *rows = finish(parts, decay, input_grad)
     return (input_grad, grad_a, grad_x, *(row.reshape(BLK) for row in rows))

time: 99.4 us -> 96.2 us (0.968); the launches traced: 99.1 us -> 94.5 us
  waiting for transfers between devices: 55.9 us -> 43 us
  starting transfers between devices: 27 us -> 35.2 us
    ppermute x5, waiting for transfers between devices: 21.2 us -> 8.7 us  [the longest x3 6.9 us: per_device(): lax.ppermute(near, 'cuts', shift)]
    ppermute x5, starting transfers between devices: 10.8 us -> 19 us  [the longest x3 17.4 us: per_device(): lax.ppermute(near, 'cuts', shift)]
  transfers between devices with their start and end apart: 8 -> 8, of which waited for: 5 -> 4; matrix products, arithmetic and copies ran while one was open for 1% -> 1% of each run, Pallas kernels for 1% -> 1%
where the time goes in v12:
time: 96.2 us; the launch traced here: 94.5 us
  waiting for transfers between devices  43 us (45%)
  starting transfers between devices  35.2 us (37%)
  Pallas kernels  14.4 us (15%)
    all_to_all x1, waiting for transfers between devices, per_device(): got = lax.all_to_all(pack(z, inputs, cotangent), plane, 0, 0, tiled=True)  34.3 us
    ppermute x3, starting transfers between devices, per_device(): lax.ppermute(near, 'cuts', shift)  17.4 us
    pallas_call x1, Pallas kernels, main_call(): pl.pallas_call(functools.partial(main_kernel, factor), out_shape=[pltpu.H...  9.07 us
    all_to_all x1, starting transfers between devices, per_device(): got = lax.all_to_all(pack(z, inputs, cotangent), plane, 0, 0, tiled=True)  8.73 us
    ppermute x3, waiting for transfers between devices, per_device(): lax.ppermute(near, 'cuts', shift)  6.9 us
    all_to_all x1, starting transfers between devices, per_device(): back = lax.all_to_all(out, plane, 0, 0, tiled=True)  6.8 us
    pallas_call x1, Pallas kernels, pack(): pl.pallas_call(pack_kernel, in_specs=[SMEM, ANY, ANY], out_specs=ANY, out...  3.25 us
  transfers between devices with their start and end apart: 8, of which 4 were waited for; matrix products, arithmetic and copies ran while one was open for 1% of the time, Pallas kernels for 1%

profile of v12, /device:TPU:1, one launch (start us, length us, event | category | flops | bytes accessed | tf_op | source)
XLA Modules:
  0.0 94.5 jit_solution(3111891572583809626)
XLA Ops:
  0.6 3.3 %shard_map.118 = bf16[32,352,128]{2,1,0:T(8,128)(2,1)} custom-call(s32[1]{0:T(128)} %bitcast.z_ref, bf16[128,5632]{1,0:T(8,128)(2,1)} %x_hbm.1, bf16[128,5632]{1,0:T(8,128)(2,1)} %c_hbm.1), custom_call_target="tpu_custom_call" | custom-call | tf_op jit(solution)/shard_map/pallas_call | solution.py:78
  3.9 0.0 copy-start.2
  3.9 0.0 copy-start.3
  3.9 0.0 copy-start.4
  3.9 0.0 copy-start
  3.9 0.0 copy-start.1
  4.0 8.7 %all-to-all-start = ((bf16[32,352,128]{2,1,0:T(8,128)(2,1)}), bf16[32,352,128]{2,1,0:T(8,128)(2,1)S(1)}, u32[]{:S(2)}, u32[]{:S(2)}) async-start(bf16[32,352,128]{2,1,0:T(8,128)(2,1)} %shard_map.118), calls=%async_computation | async-start | bytes 5767168 | tf_op jit(solution)/shard_map/all_to_all | solution.py:318
  12.7 0.0 copy-done.2
  12.7 0.0 copy-done.3
  12.7 0.1 pad_maximum_fusion
  12.8 0.1 broadcast_in_dim.13
  12.9 0.0 copy-done.4
  12.9 0.1 broadcast_in_dim.14
  13.1 0.0 copy-done
  13.1 0.1 copy.16
  13.2 0.0 copy-done.1
  13.2 0.1 copy.17
  13.3 0.1 pad.10.clone
  13.4 0.1 maximum_maximum_fusion
  13.5 0.7 collective-permute-start
  14.2 0.0 collective-permute-done
  14.2 0.1 copy.20.w_ref
  14.4 34.3 %all-to-all-done.m_ref = bf16[32,352,128]{2,1,0:T(8,128)(2,1)S(1)} async-done(((bf16[32,352,128]{2,1,0:T(8,128)(2,1)}), bf16[32,352,128]{2,1,0:T(8,128)(2,1)S(1)}, u32[]{:S(2)}, u32[]{:S(2)}) %all-to-all-start) | async-done | bytes 2883616 | tf_op jit(solution)/shard_map/all_to_all | solution.py:318
  48.7 9.1 %shard_map.119 = (bf16[32,176,128]{2,1,0:T(8,128)(2,1)}, bf16[192,384]{1,0:T(8,128)(2,1)S(1)}) custom-call(bf16[32,352,128]{2,1,0:T(8,128)(2,1)S(1)} %all-to-all-done.m_ref, bf16[192,384]{1,0:T(8,128)(2,1)S(1)} %copy.20.w_ref, bf16[352,192]{1,0:T(8,128)(2,1)S(1)} %slice_bitcast_fusion.wt_ref), custom_call_target="tpu_custom_call" | custom-call | tf_op jit(solution)/shard_map/pallas_call | solution.py:248
  57.8 0.0 copy-start.5
  57.8 6.8 %all-to-all-start.1 = ((bf16[32,176,128]{2,1,0:T(8,128)(2,1)}), bf16[32,176,128]{2,1,0:T(8,128)(2,1)S(1)}, u32[]{:S(2)}, u32[]{:S(2)}) async-start(bf16[32,176,128]{2,1,0:T(8,128)(2,1)} %get-tuple-element.16), calls=%async_computation.1 | async-start | bytes 2883584 | tf_op jit(solution)/shard_map/all_to_all | solution.py:322
  64.6 0.7 collective-permute-start.1
  65.3 0.0 collective-permute-done.1
  65.3 12.7 %collective-permute-start.2 = (bf16[192,384]{1,0:T(8,128)(2,1)S(1)}, bf16[192,384]{1,0:T(8,128)(2,1)S(1)}, u32[]{:S(2)}, u32[]{:S(2)}) collective-permute-start(bf16[192,384]{1,0:T(8,128)(2,1)S(1)} %collective-permute-done.1), channel_id=1, source_target_pairs={{0,64},{32,96},{64,128},{96,160},{128,192},{160,224},{192,0},{224,... | collective-permute-start | bytes 442376 | tf_op jit(solution)/shard_map/ppermute | solution.py:325
  78.0 4.7 %collective-permute-start.3 = (bf16[192,384]{1,0:T(8,128)(2,1)S(1)}, bf16[192,384]{1,0:T(8,128)(2,1)S(1)}, u32[]{:S(2)}, u32[]{:S(2)}) collective-permute-start(bf16[192,384]{1,0:T(8,128)(2,1)S(1)} %collective-permute-done.1), channel_id=1, source_target_pairs={{0,128},{32,160},{64,192},{96,224},{128,0},{160,32},{192,64},{224,... | collective-permute-start | bytes 442376 | tf_op jit(solution)/shard_map/ppermute | solution.py:325
  82.7 0.0 collective-permute-start.4
  82.7 5.5 %collective-permute-done.2 = bf16[192,384]{1,0:T(8,128)(2,1)S(1)} collective-permute-done((bf16[192,384]{1,0:T(8,128)(2,1)S(1)}, bf16[192,384]{1,0:T(8,128)(2,1)S(1)}, u32[]{:S(2)}, u32[]{:S(2)}) %collective-permute-start.2) | collective-permute-done | bytes 147488 | tf_op jit(solution)/shard_map/ppermute | solution.py:325
  88.2 1.4 %collective-permute-done.3 = bf16[192,384]{1,0:T(8,128)(2,1)S(1)} collective-permute-done((bf16[192,384]{1,0:T(8,128)(2,1)S(1)}, bf16[192,384]{1,0:T(8,128)(2,1)S(1)}, u32[]{:S(2)}, u32[]{:S(2)}) %collective-permute-start.3) | collective-permute-done | bytes 147488 | tf_op jit(solution)/shard_map/ppermute | solution.py:325
  89.5 0.0 collective-permute-done.4
  89.6 0.1 add_convert_fusion.refs_0_
  89.6 0.0 all-to-all-done.1.in_ref
  89.6 1.0 %collective-permute-start.5 = (bf16[192,384]{1,0:T(8,128)(2,1)S(1)}, bf16[192,384]{1,0:T(8,128)(2,1)S(1)}, u32[]{:S(2)}, u32[]{:S(2)}) collective-permute-start(bf16[192,384]{1,0:T(8,128)(2,1)S(1)} %add_convert_fusion.refs_0_), channel_id=1, source_target_pairs={{0,32},{32,0},{64,96},{96,64},{128,160},{160,128},{192,224},{224,1... | collective-permute-start | bytes 442376 | tf_op jit(solution)/shard_map/ppermute | solution.py:327
  90.6 0.0 copy-done.5
  90.6 1.3 %shard_map.120.refs_3_ = bf16[128,5632]{1,0:T(8,128)(2,1)} custom-call(s32[1]{0:T(128)} %bitcast.z_ref, bf16[32,176,128]{2,1,0:T(8,128)(2,1)S(1)} %all-to-all-done.1.in_ref), custom_call_target="tpu_custom_call" | custom-call | tf_op jit(solution)/shard_map/pallas_call | solution.py:96
  91.9 1.8 %collective-permute-done.5.refs_1_ = bf16[192,384]{1,0:T(8,128)(2,1)S(1)} collective-permute-done((bf16[192,384]{1,0:T(8,128)(2,1)S(1)}, bf16[192,384]{1,0:T(8,128)(2,1)S(1)}, u32[]{:S(2)}, u32[]{:S(2)}) %collective-permute-start.5) | collective-permute-done | bytes 147488 | tf_op jit(solution)/shard_map/ppermute | solution.py:327
  93.7 0.8 shard_map.121
  (5 shorter events, 0.1 us)
Async XLA Ops:
  3.9 8.8 %copy-start.2 = (bf16[176]{0:T(256)(128)(2,1)S(1)}, bf16[176]{0:T(256)(128)(2,1)}, u32[]{:S(2)}) copy-start(bf16[176]{0:T(256)(128)(2,1)} %param.12) | copy-start | bytes 1060
  3.9 8.8 %copy-start.3 = (bf16[176]{0:T(256)(128)(2,1)S(1)}, bf16[176]{0:T(256)(128)(2,1)}, u32[]{:S(2)}) copy-start(bf16[176]{0:T(256)(128)(2,1)} %param.11) | copy-start | bytes 1060
  3.9 9.0 %copy-start.4 = (bf16[176]{0:T(256)(128)(2,1)S(1)}, bf16[176]{0:T(256)(128)(2,1)}, u32[]{:S(2)}) copy-start(bf16[176]{0:T(256)(128)(2,1)} %param.13) | copy-start | bytes 1060
  3.9 9.1 %copy-start = (bf16[176,176]{1,0:T(8,128)(2,1)S(1)}, bf16[176,176]{1,0:T(8,128)(2,1)}, u32[]{:S(2)}) copy-start(bf16[176,176]{1,0:T(8,128)(2,1)} %param.9) | copy-start | bytes 185860
  3.9 9.2 %copy-start.1 = (bf16[176,176]{1,0:T(8,128)(2,1)S(1)}, bf16[176,176]{1,0:T(8,128)(2,1)}, u32[]{:S(2)}) copy-start(bf16[176,176]{1,0:T(8,128)(2,1)} %param.10) | copy-start | bytes 185860
  4.0 44.7 %all-to-all-start = ((bf16[32,352,128]{2,1,0:T(8,128)(2,1)}), bf16[32,352,128]{2,1,0:T(8,128)(2,1)S(1)}, u32[]{:S(2)}, u32[]{:S(2)}) async-start(bf16[32,352,128]{2,1,0:T(8,128)(2,1)} %shard_map.118), calls=%async_computation | async-start | bytes 5767168 | tf_op jit(solution)/shard_map/all_to_all | solution.py:318
  13.5 0.7 collective-permute-start
  57.8 32.9 %copy-start.5 = (bf16[176]{0:T(256)(128)(2,1)S(1)}, bf16[176]{0:T(256)(128)(2,1)}, u32[]{:S(2)}) copy-start(bf16[176]{0:T(256)(128)(2,1)} %param.13) | copy-start | bytes 1060
  57.8 31.9 %all-to-all-start.1 = ((bf16[32,176,128]{2,1,0:T(8,128)(2,1)}), bf16[32,176,128]{2,1,0:T(8,128)(2,1)S(1)}, u32[]{:S(2)}, u32[]{:S(2)}) async-start(bf16[32,176,128]{2,1,0:T(8,128)(2,1)} %get-tuple-element.16), calls=%async_computation.1 | async-start | bytes 2883584 | tf_op jit(solution)/shard_map/all_to_all | solution.py:322
  64.6 0.7 collective-permute-start.1
  65.3 22.9 %collective-permute-start.2 = (bf16[192,384]{1,0:T(8,128)(2,1)S(1)}, bf16[192,384]{1,0:T(8,128)(2,1)S(1)}, u32[]{:S(2)}, u32[]{:S(2)}) collective-permute-start(bf16[192,384]{1,0:T(8,128)(2,1)S(1)} %collective-permute-done.1), channel_id=1, source_target_pairs={{0,64},{32,96},{64,128},{96,160},{128,192},{160,224},{192,0},{224,... | collective-permute-start | bytes 442376 | tf_op jit(solution)/shard_map/ppermute | solution.py:325
  78.0 11.6 %collective-permute-start.3 = (bf16[192,384]{1,0:T(8,128)(2,1)S(1)}, bf16[192,384]{1,0:T(8,128)(2,1)S(1)}, u32[]{:S(2)}, u32[]{:S(2)}) collective-permute-start(bf16[192,384]{1,0:T(8,128)(2,1)S(1)} %collective-permute-done.1), channel_id=1, source_target_pairs={{0,128},{32,160},{64,192},{96,224},{128,0},{160,32},{192,64},{224,... | collective-permute-start | bytes 442376 | tf_op jit(solution)/shard_map/ppermute | solution.py:325
  82.7 6.9 %collective-permute-start.4 = (bf16[192,384]{1,0:T(8,128)(2,1)S(1)}, bf16[192,384]{1,0:T(8,128)(2,1)S(1)}, u32[]{:S(2)}, u32[]{:S(2)}) collective-permute-start(bf16[192,384]{1,0:T(8,128)(2,1)S(1)} %collective-permute-done.1), channel_id=1, source_target_pairs={{0,192},{32,224},{64,0},{96,32},{128,64},{160,96},{192,128},{224,1... | collective-permute-start | bytes 442376 | tf_op jit(solution)/shard_map/ppermute | solution.py:325
  89.6 4.1 %collective-permute-start.5 = (bf16[192,384]{1,0:T(8,128)(2,1)S(1)}, bf16[192,384]{1,0:T(8,128)(2,1)S(1)}, u32[]{:S(2)}, u32[]{:S(2)}) collective-permute-start(bf16[192,384]{1,0:T(8,128)(2,1)S(1)} %add_convert_fusion.refs_0_), channel_id=1, source_target_pairs={{0,32},{32,0},{64,96},{96,64},{128,160},{160,128},{192,224},{224,1... | collective-permute-start | bytes 442376 | tf_op jit(solution)/shard_map/ppermute | solution.py:327

commit v13 on v12

--- a/solution.py
+++ b/solution.py
@@ -109,7 +109,7 @@
 
 
 def sigmoid(pre):
-    return pl.reciprocal(1.0 + jnp.exp2(jnp.minimum(pre * -LOG2E, 115.0)), approx=True)
+    return pl.reciprocal(1.0 + jnp.exp2(jnp.minimum(pre * -LOG2E, 80.0)), approx=True)
 
 
 def one_minus_square(u):
@@ -321,7 +321,7 @@
     out, grads = main_call(float(total) ** -0.5, got, w, w[:, :TWO].T)
     back = lax.all_to_all(out, plane, 0, 0, tiled=True)
     near = lax.ppermute(grads, line, fetch)
-    shifts = [[(i, (i + 2 * k) % NI) for i in range(NI)] for k in (1, 2, 3)]
+    shifts = [[(i, (i + 2 * k) % NI) for i in range(NI)] for k in (2, 1, 3)]
     four = sum(p.astype(f32) for p in [near] + [lax.ppermute(near, "cuts", shift) for shift in shifts])
     four, back = lax.optimization_barrier((four.astype(bf16), back))
     parts = [four, lax.ppermute(four, "cuts", [(i, i ^ 1) for i in range(NI)])]

time: 96.2 us -> 96.8 us (level); the launches traced: 94.5 us -> 96.5 us
  waiting for transfers between devices: 43 us -> 44.8 us
    ppermute x1, waiting for transfers between devices: 1.8 us -> 2.89 us  [per_device(): parts = [four, lax.ppermute(four, 'cuts', [(i, i ^ 1) for i in range(NI)])]]
where the time goes in v13:
time: 96.8 us; the launch traced here: 96.5 us
  waiting for transfers between devices  44.8 us (46%)
  starting transfers between devices  35.4 us (37%)
  Pallas kernels  14.4 us (15%)
    all_to_all x1, waiting for transfers between devices, per_device(): got = lax.all_to_all(pack(z, inputs, cotangent), plane, 0, 0, tiled=True)  34.3 us
    ppermute x3, starting transfers between devices, per_device(): lax.ppermute(near, 'cuts', shift)  17.6 us
    pallas_call x1, Pallas kernels, main_call(): pl.pallas_call(functools.partial(main_kernel, factor), out_shape=[pltpu.H...  9.07 us
    all_to_all x1, starting transfers between devices, per_device(): got = lax.all_to_all(pack(z, inputs, cotangent), plane, 0, 0, tiled=True)  8.73 us
    ppermute x3, waiting for transfers between devices, per_device(): lax.ppermute(near, 'cuts', shift)  7.62 us
    all_to_all x1, starting transfers between devices, per_device(): back = lax.all_to_all(out, plane, 0, 0, tiled=True)  6.8 us
    pallas_call x1, Pallas kernels, pack(): pl.pallas_call(pack_kernel, in_specs=[SMEM, ANY, ANY], out_specs=ANY, out...  3.25 us
    ppermute x1, waiting for transfers between devices, per_device(): parts = [four, lax.ppermute(four, 'cuts', [(i, i ^ 1) for i in range(NI)])]  2.89 us
  transfers between devices with their start and end apart: 8, of which 4 were waited for; matrix products, arithmetic and copies ran while one was open for 1% of the time, Pallas kernels for 1%

profile of v13, /device:TPU:1, one launch (start us, length us, event | category | flops | bytes accessed | tf_op | source)
XLA Modules:
  0.0 96.5 jit_solution(10294401814437103398)
XLA Ops:
  0.6 3.3 %shard_map.118 = bf16[32,352,128]{2,1,0:T(8,128)(2,1)} custom-call(s32[1]{0:T(128)} %bitcast.z_ref, bf16[128,5632]{1,0:T(8,128)(2,1)} %x_hbm.1, bf16[128,5632]{1,0:T(8,128)(2,1)} %c_hbm.1), custom_call_target="tpu_custom_call" | custom-call | tf_op jit(solution)/shard_map/pallas_call | solution.py:78
  3.9 0.0 copy-start.2
  3.9 0.0 copy-start.3
  3.9 0.0 copy-start.4
  3.9 0.0 copy-start
  3.9 0.0 copy-start.1
  4.0 8.7 %all-to-all-start = ((bf16[32,352,128]{2,1,0:T(8,128)(2,1)}), bf16[32,352,128]{2,1,0:T(8,128)(2,1)S(1)}, u32[]{:S(2)}, u32[]{:S(2)}) async-start(bf16[32,352,128]{2,1,0:T(8,128)(2,1)} %shard_map.118), calls=%async_computation | async-start | bytes 5767168 | tf_op jit(solution)/shard_map/all_to_all | solution.py:318
  12.7 0.0 copy-done.2
  12.7 0.0 copy-done.3
  12.7 0.1 pad_maximum_fusion
  12.8 0.1 broadcast_in_dim.13
  12.9 0.0 copy-done.4
  12.9 0.1 broadcast_in_dim.14
  13.1 0.0 copy-done
  13.1 0.1 copy.16
  13.2 0.0 copy-done.1
  13.2 0.1 copy.17
  13.3 0.1 pad.10.clone
  13.4 0.1 maximum_maximum_fusion
  13.5 0.7 collective-permute-start
  14.2 0.0 collective-permute-done
  14.2 0.1 copy.20.w_ref
  14.4 34.3 %all-to-all-done.m_ref = bf16[32,352,128]{2,1,0:T(8,128)(2,1)S(1)} async-done(((bf16[32,352,128]{2,1,0:T(8,128)(2,1)}), bf16[32,352,128]{2,1,0:T(8,128)(2,1)S(1)}, u32[]{:S(2)}, u32[]{:S(2)}) %all-to-all-start) | async-done | bytes 2883616 | tf_op jit(solution)/shard_map/all_to_all | solution.py:318
  48.7 9.1 %shard_map.119 = (bf16[32,176,128]{2,1,0:T(8,128)(2,1)}, bf16[192,384]{1,0:T(8,128)(2,1)S(1)}) custom-call(bf16[32,352,128]{2,1,0:T(8,128)(2,1)S(1)} %all-to-all-done.m_ref, bf16[192,384]{1,0:T(8,128)(2,1)S(1)} %copy.20.w_ref, bf16[352,192]{1,0:T(8,128)(2,1)S(1)} %slice_bitcast_fusion.wt_ref), custom_call_target="tpu_custom_call" | custom-call | tf_op jit(solution)/shard_map/pallas_call | solution.py:248
  57.8 0.0 copy-start.5
  57.8 6.8 %all-to-all-start.1 = ((bf16[32,176,128]{2,1,0:T(8,128)(2,1)}), bf16[32,176,128]{2,1,0:T(8,128)(2,1)S(1)}, u32[]{:S(2)}, u32[]{:S(2)}) async-start(bf16[32,176,128]{2,1,0:T(8,128)(2,1)} %get-tuple-element.16), calls=%async_computation.1 | async-start | bytes 2883584 | tf_op jit(solution)/shard_map/all_to_all | solution.py:322
  64.6 0.7 collective-permute-start.1
  65.3 0.0 collective-permute-done.1
  65.3 15.0 %collective-permute-start.2 = (bf16[192,384]{1,0:T(8,128)(2,1)S(1)}, bf16[192,384]{1,0:T(8,128)(2,1)S(1)}, u32[]{:S(2)}, u32[]{:S(2)}) collective-permute-start(bf16[192,384]{1,0:T(8,128)(2,1)S(1)} %collective-permute-done.1), channel_id=1, source_target_pairs={{0,128},{32,160},{64,192},{96,224},{128,0},{160,32},{192,64},{224,... | collective-permute-start | bytes 442376 | tf_op jit(solution)/shard_map/ppermute | solution.py:325
  80.2 1.8 %collective-permute-start.3 = (bf16[192,384]{1,0:T(8,128)(2,1)S(1)}, bf16[192,384]{1,0:T(8,128)(2,1)S(1)}, u32[]{:S(2)}, u32[]{:S(2)}) collective-permute-start(bf16[192,384]{1,0:T(8,128)(2,1)S(1)} %collective-permute-done.1), channel_id=1, source_target_pairs={{0,64},{32,96},{64,128},{96,160},{128,192},{160,224},{192,0},{224,... | collective-permute-start | bytes 442376 | tf_op jit(solution)/shard_map/ppermute | solution.py:325
  82.0 0.9 collective-permute-start.4
  82.9 4.0 %collective-permute-done.2 = bf16[192,384]{1,0:T(8,128)(2,1)S(1)} collective-permute-done((bf16[192,384]{1,0:T(8,128)(2,1)S(1)}, bf16[192,384]{1,0:T(8,128)(2,1)S(1)}, u32[]{:S(2)}, u32[]{:S(2)}) %collective-permute-start.2) | collective-permute-done | bytes 147488 | tf_op jit(solution)/shard_map/ppermute | solution.py:325
  87.0 3.6 %collective-permute-done.3 = bf16[192,384]{1,0:T(8,128)(2,1)S(1)} collective-permute-done((bf16[192,384]{1,0:T(8,128)(2,1)S(1)}, bf16[192,384]{1,0:T(8,128)(2,1)S(1)}, u32[]{:S(2)}, u32[]{:S(2)}) %collective-permute-start.3) | collective-permute-done | bytes 147488 | tf_op jit(solution)/shard_map/ppermute | solution.py:325
  90.5 0.0 collective-permute-done.4
  90.5 0.1 add_convert_fusion.refs_0_
  90.6 0.0 all-to-all-done.1.in_ref
  90.6 0.9 collective-permute-start.5
  91.5 0.0 copy-done.5
  91.5 1.3 %shard_map.120.refs_3_ = bf16[128,5632]{1,0:T(8,128)(2,1)} custom-call(s32[1]{0:T(128)} %bitcast.z_ref, bf16[32,176,128]{2,1,0:T(8,128)(2,1)S(1)} %all-to-all-done.1.in_ref), custom_call_target="tpu_custom_call" | custom-call | tf_op jit(solution)/shard_map/pallas_call | solution.py:96
  92.8 2.9 %collective-permute-done.5.refs_1_ = bf16[192,384]{1,0:T(8,128)(2,1)S(1)} collective-permute-done((bf16[192,384]{1,0:T(8,128)(2,1)S(1)}, bf16[192,384]{1,0:T(8,128)(2,1)S(1)}, u32[]{:S(2)}, u32[]{:S(2)}) %collective-permute-start.5) | collective-permute-done | bytes 147488 | tf_op jit(solution)/shard_map/ppermute | solution.py:327
  95.7 0.8 shard_map.121
  (5 shorter events, 0.1 us)
Async XLA Ops:
  3.9 8.8 %copy-start.2 = (bf16[176]{0:T(256)(128)(2,1)S(1)}, bf16[176]{0:T(256)(128)(2,1)}, u32[]{:S(2)}) copy-start(bf16[176]{0:T(256)(128)(2,1)} %param.12) | copy-start | bytes 1060
  3.9 8.8 %copy-start.3 = (bf16[176]{0:T(256)(128)(2,1)S(1)}, bf16[176]{0:T(256)(128)(2,1)}, u32[]{:S(2)}) copy-start(bf16[176]{0:T(256)(128)(2,1)} %param.11) | copy-start | bytes 1060
  3.9 9.0 %copy-start.4 = (bf16[176]{0:T(256)(128)(2,1)S(1)}, bf16[176]{0:T(256)(128)(2,1)}, u32[]{:S(2)}) copy-start(bf16[176]{0:T(256)(128)(2,1)} %param.13) | copy-start | bytes 1060
  3.9 9.1 %copy-start = (bf16[176,176]{1,0:T(8,128)(2,1)S(1)}, bf16[176,176]{1,0:T(8,128)(2,1)}, u32[]{:S(2)}) copy-start(bf16[176,176]{1,0:T(8,128)(2,1)} %param.9) | copy-start | bytes 185860
  3.9 9.2 %copy-start.1 = (bf16[176,176]{1,0:T(8,128)(2,1)S(1)}, bf16[176,176]{1,0:T(8,128)(2,1)}, u32[]{:S(2)}) copy-start(bf16[176,176]{1,0:T(8,128)(2,1)} %param.10) | copy-start | bytes 185860
  4.0 44.7 %all-to-all-start = ((bf16[32,352,128]{2,1,0:T(8,128)(2,1)}), bf16[32,352,128]{2,1,0:T(8,128)(2,1)S(1)}, u32[]{:S(2)}, u32[]{:S(2)}) async-start(bf16[32,352,128]{2,1,0:T(8,128)(2,1)} %shard_map.118), calls=%async_computation | async-start | bytes 5767168 | tf_op jit(solution)/shard_map/all_to_all | solution.py:318
  13.5 0.7 collective-permute-start
  57.8 33.7 %copy-start.5 = (bf16[176]{0:T(256)(128)(2,1)S(1)}, bf16[176]{0:T(256)(128)(2,1)}, u32[]{:S(2)}) copy-start(bf16[176]{0:T(256)(128)(2,1)} %param.13) | copy-start | bytes 1060
  57.8 32.8 %all-to-all-start.1 = ((bf16[32,176,128]{2,1,0:T(8,128)(2,1)}), bf16[32,176,128]{2,1,0:T(8,128)(2,1)S(1)}, u32[]{:S(2)}, u32[]{:S(2)}) async-start(bf16[32,176,128]{2,1,0:T(8,128)(2,1)} %get-tuple-element.16), calls=%async_computation.1 | async-start | bytes 2883584 | tf_op jit(solution)/shard_map/all_to_all | solution.py:322
  64.6 0.7 collective-permute-start.1
  65.3 21.7 %collective-permute-start.2 = (bf16[192,384]{1,0:T(8,128)(2,1)S(1)}, bf16[192,384]{1,0:T(8,128)(2,1)S(1)}, u32[]{:S(2)}, u32[]{:S(2)}) collective-permute-start(bf16[192,384]{1,0:T(8,128)(2,1)S(1)} %collective-permute-done.1), channel_id=1, source_target_pairs={{0,128},{32,160},{64,192},{96,224},{128,0},{160,32},{192,64},{224,... | collective-permute-start | bytes 442376 | tf_op jit(solution)/shard_map/ppermute | solution.py:325
  80.2 10.3 %collective-permute-start.3 = (bf16[192,384]{1,0:T(8,128)(2,1)S(1)}, bf16[192,384]{1,0:T(8,128)(2,1)S(1)}, u32[]{:S(2)}, u32[]{:S(2)}) collective-permute-start(bf16[192,384]{1,0:T(8,128)(2,1)S(1)} %collective-permute-done.1), channel_id=1, source_target_pairs={{0,64},{32,96},{64,128},{96,160},{128,192},{160,224},{192,0},{224,... | collective-permute-start | bytes 442376 | tf_op jit(solution)/shard_map/ppermute | solution.py:325
  82.0 8.5 %collective-permute-start.4 = (bf16[192,384]{1,0:T(8,128)(2,1)S(1)}, bf16[192,384]{1,0:T(8,128)(2,1)S(1)}, u32[]{:S(2)}, u32[]{:S(2)}) collective-permute-start(bf16[192,384]{1,0:T(8,128)(2,1)S(1)} %collective-permute-done.1), channel_id=1, source_target_pairs={{0,192},{32,224},{64,0},{96,32},{128,64},{160,96},{192,128},{224,1... | collective-permute-start | bytes 442376 | tf_op jit(solution)/shard_map/ppermute | solution.py:325
  90.6 5.1 %collective-permute-start.5 = (bf16[192,384]{1,0:T(8,128)(2,1)S(1)}, bf16[192,384]{1,0:T(8,128)(2,1)S(1)}, u32[]{:S(2)}, u32[]{:S(2)}) collective-permute-start(bf16[192,384]{1,0:T(8,128)(2,1)S(1)} %add_convert_fusion.refs_0_), channel_id=1, source_target_pairs={{0,32},{32,0},{64,96},{96,64},{128,160},{160,128},{192,224},{224,1... | collective-permute-start | bytes 442376 | tf_op jit(solution)/shard_map/ppermute | solution.py:327

commit v14 on v12

--- a/solution.py
+++ b/solution.py
@@ -268,6 +268,20 @@
     )(*kept(m, w, wt))
 
 
+def same_kernel(in_ref, near_ref, out_ref):
+    del in_ref, near_ref, out_ref
+
+
+def behind(x, after):
+    return pl.pallas_call(
+        same_kernel,
+        in_specs=[ANY, ANY],
+        out_specs=ANY,
+        out_shape=pltpu.HBM(x.shape, x.dtype),
+        input_output_aliases={0: 0},
+    )(*kept(x, where=pltpu.HBM), *kept(after, where=pltpu.HBM))
+
+
 def finish_kernel(count, *refs):
     parts, decay_ref, outs = refs[:count], refs[count], refs[count + 2 :]
     f32 = jnp.float32
@@ -319,8 +333,8 @@
     w = lax.ppermute(wire(wa, wx, ba, bx, decay), line, fetch)
     total = SEQ * NSEQ * NZ
     out, grads = main_call(float(total) ** -0.5, got, w, w[:, :TWO].T)
-    back = lax.all_to_all(out, plane, 0, 0, tiled=True)
     near = lax.ppermute(grads, line, fetch)
+    back = lax.all_to_all(behind(out, z), plane, 0, 0, tiled=True)
     shifts = [[(i, (i + 2 * k) % NI) for i in range(NI)] for k in (1, 2, 3)]
     four = sum(p.astype(f32) for p in [near] + [lax.ppermute(near, "cuts", shift) for shift in shifts])
     four, back = lax.optimization_barrier((four.astype(bf16), back))

time: 96.2 us -> 96.2 us (level)
  no operation moved by 1% of the time
where the time goes in v14:
time: 96.2 us; the launch traced here: 94.5 us
  waiting for transfers between devices  43 us (45%)
  starting transfers between devices  35.2 us (37%)
  Pallas kernels  14.4 us (15%)
    all_to_all x1, waiting for transfers between devices, per_device(): got = lax.all_to_all(pack(z, inputs, cotangent), plane, 0, 0, tiled=True)  34.3 us
    ppermute x3, starting transfers between devices, per_device(): lax.ppermute(near, 'cuts', shift)  17.4 us
    pallas_call x1, Pallas kernels, main_call(): pl.pallas_call(functools.partial(main_kernel, factor), out_shape=[pltpu.H...  9.07 us
    all_to_all x1, starting transfers between devices, per_device(): got = lax.all_to_all(pack(z, inputs, cotangent), plane, 0, 0, tiled=True)  8.73 us
    ppermute x3, waiting for transfers between devices, per_device(): lax.ppermute(near, 'cuts', shift)  6.88 us
    all_to_all x1, starting transfers between devices, per_device(): back = lax.all_to_all(behind(out, z), plane, 0, 0, tiled=True)  6.79 us
    pallas_call x1, Pallas kernels, pack(): pl.pallas_call(pack_kernel, in_specs=[SMEM, ANY, ANY], out_specs=ANY, out...  3.25 us
  transfers between devices with their start and end apart: 8, of which 4 were waited for; matrix products, arithmetic and copies ran while one was open for 1% of the time, Pallas kernels for 1%

profile of v14, /device:TPU:1, one launch (start us, length us, event | category | flops | bytes accessed | tf_op | source)
XLA Modules:
  0.0 94.5 jit_solution(3202058082841108974)
XLA Ops:
  0.6 3.3 %shard_map.118 = bf16[32,352,128]{2,1,0:T(8,128)(2,1)} custom-call(s32[1]{0:T(128)} %bitcast.z_ref.near_ref, bf16[128,5632]{1,0:T(8,128)(2,1)} %x_hbm.1, bf16[128,5632]{1,0:T(8,128)(2,1)} %c_hbm.1), custom_call_target="tpu_custom_call" | custom-call | tf_op jit(solution)/shard_map/pallas_call | solution.py:78
  3.9 0.0 copy-start.2
  3.9 0.0 copy-start.3
  3.9 0.0 copy-start.4
  3.9 0.0 copy-start
  3.9 0.0 copy-start.1
  4.0 8.7 %all-to-all-start = ((bf16[32,352,128]{2,1,0:T(8,128)(2,1)}), bf16[32,352,128]{2,1,0:T(8,128)(2,1)S(1)}, u32[]{:S(2)}, u32[]{:S(2)}) async-start(bf16[32,352,128]{2,1,0:T(8,128)(2,1)} %shard_map.118), calls=%async_computation | async-start | bytes 5767168 | tf_op jit(solution)/shard_map/all_to_all | solution.py:332
  12.7 0.0 copy-done.2
  12.7 0.0 copy-done.3
  12.7 0.1 pad_maximum_fusion
  12.8 0.1 broadcast_in_dim.13
  12.9 0.0 copy-done.4
  12.9 0.1 broadcast_in_dim.14
  13.1 0.0 copy-done
  13.1 0.1 copy.17
  13.2 0.0 copy-done.1
  13.2 0.1 copy.18
  13.3 0.1 pad.10.clone
  13.4 0.1 maximum_maximum_fusion
  13.5 0.7 collective-permute-start
  14.2 0.0 collective-permute-done
  14.2 0.1 copy.21.w_ref
  14.4 34.3 %all-to-all-done.m_ref = bf16[32,352,128]{2,1,0:T(8,128)(2,1)S(1)} async-done(((bf16[32,352,128]{2,1,0:T(8,128)(2,1)}), bf16[32,352,128]{2,1,0:T(8,128)(2,1)S(1)}, u32[]{:S(2)}, u32[]{:S(2)}) %all-to-all-start) | async-done | bytes 2883616 | tf_op jit(solution)/shard_map/all_to_all | solution.py:332
  48.7 9.1 %shard_map.119 = (bf16[32,176,128]{2,1,0:T(8,128)(2,1)}, bf16[192,384]{1,0:T(8,128)(2,1)S(1)}) custom-call(bf16[32,352,128]{2,1,0:T(8,128)(2,1)S(1)} %all-to-all-done.m_ref, bf16[192,384]{1,0:T(8,128)(2,1)S(1)} %copy.21.w_ref, bf16[352,192]{1,0:T(8,128)(2,1)S(1)} %slice_bitcast_fusion.wt_ref), custom_call_target="tpu_custom_call" | custom-call | tf_op jit(solution)/shard_map/pallas_call | solution.py:248
  57.8 0.0 copy-start.5
  57.8 6.8 %all-to-all-start.1 = ((bf16[32,176,128]{2,1,0:T(8,128)(2,1)}), bf16[32,176,128]{2,1,0:T(8,128)(2,1)S(1)}, u32[]{:S(2)}, u32[]{:S(2)}) async-start(bf16[32,176,128]{2,1,0:T(8,128)(2,1)} %shard_map.120), calls=%async_computation.1 | async-start | bytes 2883584 | tf_op jit(solution)/shard_map/all_to_all | solution.py:337
  64.6 0.7 collective-permute-start.1
  65.3 0.0 collective-permute-done.1
  65.3 12.7 %collective-permute-start.2 = (bf16[192,384]{1,0:T(8,128)(2,1)S(1)}, bf16[192,384]{1,0:T(8,128)(2,1)S(1)}, u32[]{:S(2)}, u32[]{:S(2)}) collective-permute-start(bf16[192,384]{1,0:T(8,128)(2,1)S(1)} %collective-permute-done.1), channel_id=1, source_target_pairs={{0,64},{32,96},{64,128},{96,160},{128,192},{160,224},{192,0},{224,... | collective-permute-start | bytes 442376 | tf_op jit(solution)/shard_map/ppermute | solution.py:339
  78.0 4.7 %collective-permute-start.3 = (bf16[192,384]{1,0:T(8,128)(2,1)S(1)}, bf16[192,384]{1,0:T(8,128)(2,1)S(1)}, u32[]{:S(2)}, u32[]{:S(2)}) collective-permute-start(bf16[192,384]{1,0:T(8,128)(2,1)S(1)} %collective-permute-done.1), channel_id=1, source_target_pairs={{0,128},{32,160},{64,192},{96,224},{128,0},{160,32},{192,64},{224,... | collective-permute-start | bytes 442376 | tf_op jit(solution)/shard_map/ppermute | solution.py:339
  82.7 0.0 collective-permute-start.4
  82.7 5.5 %collective-permute-done.2 = bf16[192,384]{1,0:T(8,128)(2,1)S(1)} collective-permute-done((bf16[192,384]{1,0:T(8,128)(2,1)S(1)}, bf16[192,384]{1,0:T(8,128)(2,1)S(1)}, u32[]{:S(2)}, u32[]{:S(2)}) %collective-permute-start.2) | collective-permute-done | bytes 147488 | tf_op jit(solution)/shard_map/ppermute | solution.py:339
  88.2 1.4 %collective-permute-done.3 = bf16[192,384]{1,0:T(8,128)(2,1)S(1)} collective-permute-done((bf16[192,384]{1,0:T(8,128)(2,1)S(1)}, bf16[192,384]{1,0:T(8,128)(2,1)S(1)}, u32[]{:S(2)}, u32[]{:S(2)}) %collective-permute-start.3) | collective-permute-done | bytes 147488 | tf_op jit(solution)/shard_map/ppermute | solution.py:339
  89.6 0.0 collective-permute-done.4
  89.6 0.1 add_convert_fusion.refs_0_
  89.6 0.0 all-to-all-done.1.in_ref
  89.7 1.0 %collective-permute-start.5 = (bf16[192,384]{1,0:T(8,128)(2,1)S(1)}, bf16[192,384]{1,0:T(8,128)(2,1)S(1)}, u32[]{:S(2)}, u32[]{:S(2)}) collective-permute-start(bf16[192,384]{1,0:T(8,128)(2,1)S(1)} %add_convert_fusion.refs_0_), channel_id=1, source_target_pairs={{0,32},{32,0},{64,96},{96,64},{128,160},{160,128},{192,224},{224,1... | collective-permute-start | bytes 442376 | tf_op jit(solution)/shard_map/ppermute | solution.py:341
  90.6 0.0 copy-done.5
  90.6 1.3 %shard_map.121.refs_3_ = bf16[128,5632]{1,0:T(8,128)(2,1)} custom-call(s32[1]{0:T(128)} %bitcast.z_ref.near_ref, bf16[32,176,128]{2,1,0:T(8,128)(2,1)S(1)} %all-to-all-done.1.in_ref), custom_call_target="tpu_custom_call" | custom-call | tf_op jit(solution)/shard_map/pallas_call | solution.py:96
  91.9 1.8 %collective-permute-done.5.refs_1_ = bf16[192,384]{1,0:T(8,128)(2,1)S(1)} collective-permute-done((bf16[192,384]{1,0:T(8,128)(2,1)S(1)}, bf16[192,384]{1,0:T(8,128)(2,1)S(1)}, u32[]{:S(2)}, u32[]{:S(2)}) %collective-permute-start.5) | collective-permute-done | bytes 147488 | tf_op jit(solution)/shard_map/ppermute | solution.py:341
  93.7 0.8 shard_map.122
  (6 shorter events, 0.1 us)
Async XLA Ops:
  3.9 8.8 %copy-start.2 = (bf16[176]{0:T(256)(128)(2,1)S(1)}, bf16[176]{0:T(256)(128)(2,1)}, u32[]{:S(2)}) copy-start(bf16[176]{0:T(256)(128)(2,1)} %param.12) | copy-start | bytes 1060
  3.9 8.8 %copy-start.3 = (bf16[176]{0:T(256)(128)(2,1)S(1)}, bf16[176]{0:T(256)(128)(2,1)}, u32[]{:S(2)}) copy-start(bf16[176]{0:T(256)(128)(2,1)} %param.11) | copy-start | bytes 1060
  3.9 9.0 %copy-start.4 = (bf16[176]{0:T(256)(128)(2,1)S(1)}, bf16[176]{0:T(256)(128)(2,1)}, u32[]{:S(2)}) copy-start(bf16[176]{0:T(256)(128)(2,1)} %param.13) | copy-start | bytes 1060
  3.9 9.1 %copy-start = (bf16[176,176]{1,0:T(8,128)(2,1)S(1)}, bf16[176,176]{1,0:T(8,128)(2,1)}, u32[]{:S(2)}) copy-start(bf16[176,176]{1,0:T(8,128)(2,1)} %param.9) | copy-start | bytes 185860
  3.9 9.2 %copy-start.1 = (bf16[176,176]{1,0:T(8,128)(2,1)S(1)}, bf16[176,176]{1,0:T(8,128)(2,1)}, u32[]{:S(2)}) copy-start(bf16[176,176]{1,0:T(8,128)(2,1)} %param.10) | copy-start | bytes 185860
  4.0 44.7 %all-to-all-start = ((bf16[32,352,128]{2,1,0:T(8,128)(2,1)}), bf16[32,352,128]{2,1,0:T(8,128)(2,1)S(1)}, u32[]{:S(2)}, u32[]{:S(2)}) async-start(bf16[32,352,128]{2,1,0:T(8,128)(2,1)} %shard_map.118), calls=%async_computation | async-start | bytes 5767168 | tf_op jit(solution)/shard_map/all_to_all | solution.py:332
  13.5 0.7 collective-permute-start
  57.8 32.9 %copy-start.5 = (bf16[176]{0:T(256)(128)(2,1)S(1)}, bf16[176]{0:T(256)(128)(2,1)}, u32[]{:S(2)}) copy-start(bf16[176]{0:T(256)(128)(2,1)} %param.13) | copy-start | bytes 1060
  57.8 31.8 %all-to-all-start.1 = ((bf16[32,176,128]{2,1,0:T(8,128)(2,1)}), bf16[32,176,128]{2,1,0:T(8,128)(2,1)S(1)}, u32[]{:S(2)}, u32[]{:S(2)}) async-start(bf16[32,176,128]{2,1,0:T(8,128)(2,1)} %shard_map.120), calls=%async_computation.1 | async-start | bytes 2883584 | tf_op jit(solution)/shard_map/all_to_all | solution.py:337
  64.6 0.7 collective-permute-start.1
  65.3 22.9 %collective-permute-start.2 = (bf16[192,384]{1,0:T(8,128)(2,1)S(1)}, bf16[192,384]{1,0:T(8,128)(2,1)S(1)}, u32[]{:S(2)}, u32[]{:S(2)}) collective-permute-start(bf16[192,384]{1,0:T(8,128)(2,1)S(1)} %collective-permute-done.1), channel_id=1, source_target_pairs={{0,64},{32,96},{64,128},{96,160},{128,192},{160,224},{192,0},{224,... | collective-permute-start | bytes 442376 | tf_op jit(solution)/shard_map/ppermute | solution.py:339
  78.0 11.6 %collective-permute-start.3 = (bf16[192,384]{1,0:T(8,128)(2,1)S(1)}, bf16[192,384]{1,0:T(8,128)(2,1)S(1)}, u32[]{:S(2)}, u32[]{:S(2)}) collective-permute-start(bf16[192,384]{1,0:T(8,128)(2,1)S(1)} %collective-permute-done.1), channel_id=1, source_target_pairs={{0,128},{32,160},{64,192},{96,224},{128,0},{160,32},{192,64},{224,... | collective-permute-start | bytes 442376 | tf_op jit(solution)/shard_map/ppermute | solution.py:339
  82.7 6.9 %collective-permute-start.4 = (bf16[192,384]{1,0:T(8,128)(2,1)S(1)}, bf16[192,384]{1,0:T(8,128)(2,1)S(1)}, u32[]{:S(2)}, u32[]{:S(2)}) collective-permute-start(bf16[192,384]{1,0:T(8,128)(2,1)S(1)} %collective-permute-done.1), channel_id=1, source_target_pairs={{0,192},{32,224},{64,0},{96,32},{128,64},{160,96},{192,128},{224,1... | collective-permute-start | bytes 442376 | tf_op jit(solution)/shard_map/ppermute | solution.py:339
  89.7 4.1 %collective-permute-start.5 = (bf16[192,384]{1,0:T(8,128)(2,1)S(1)}, bf16[192,384]{1,0:T(8,128)(2,1)S(1)}, u32[]{:S(2)}, u32[]{:S(2)}) collective-permute-start(bf16[192,384]{1,0:T(8,128)(2,1)S(1)} %add_convert_fusion.refs_0_), channel_id=1, source_target_pairs={{0,32},{32,0},{64,96},{96,64},{128,160},{160,128},{192,224},{224,1... | collective-permute-start | bytes 442376 | tf_op jit(solution)/shard_map/ppermute | solution.py:341

commit v15 on v12

--- a/solution.py
+++ b/solution.py
@@ -321,9 +321,11 @@
     out, grads = main_call(float(total) ** -0.5, got, w, w[:, :TWO].T)
     back = lax.all_to_all(out, plane, 0, 0, tiled=True)
     near = lax.ppermute(grads, line, fetch)
-    shifts = [[(i, (i + 2 * k) % NI) for i in range(NI)] for k in (1, 2, 3)]
-    four = sum(p.astype(f32) for p in [near] + [lax.ppermute(near, "cuts", shift) for shift in shifts])
-    four, back = lax.optimization_barrier((four.astype(bf16), back))
+    four = near
+    for step in (2, 4):
+        met = lax.ppermute(four, "cuts", [(i, i ^ step) for i in range(NI)])
+        four = (four.astype(f32) + met.astype(f32)).astype(bf16)
+    four, back = lax.optimization_barrier((four, back))
     parts = [four, lax.ppermute(four, "cuts", [(i, i ^ 1) for i in range(NI)])]
     input_grad = unpack(z, back)
     grad_a, grad_x, *rows = finish(parts, decay, input_grad)

time: 96.2 us -> 98.3 us (1.022)
  waiting for transfers between devices: 43 us -> 46.8 us
  starting transfers between devices: 35.2 us -> 33.4 us
    ppermute x3 -> x2, waiting for transfers between devices: 6.9 us -> 11 us  [per_device(): met = lax.ppermute(four, 'cuts', [(i, i ^ step) for i in range(NI)])]
    ppermute x3 -> x2, starting transfers between devices: 17.4 us -> 15.3 us  [per_device(): met = lax.ppermute(four, 'cuts', [(i, i ^ step) for i in range(NI)])]
  transfers between devices with their start and end apart: 8 -> 7, of which waited for: 4 -> 4; matrix products, arithmetic and copies ran while one was open for 1% -> 1% of each run, Pallas kernels for 1% -> 1%
where the time goes in v15:
time: 98.3 us; the launch traced here: 96.5 us
  waiting for transfers between devices  46.8 us (48%)
  starting transfers between devices  33.4 us (34%)
  Pallas kernels  14.4 us (15%)
    all_to_all x1, waiting for transfers between devices, per_device(): got = lax.all_to_all(pack(z, inputs, cotangent), plane, 0, 0, tiled=True)  34.3 us
    ppermute x2, starting transfers between devices, per_device(): met = lax.ppermute(four, 'cuts', [(i, i ^ step) for i in range(NI)])  15.3 us
    ppermute x2, waiting for transfers between devices, per_device(): met = lax.ppermute(four, 'cuts', [(i, i ^ step) for i in range(NI)])  11 us
    pallas_call x1, Pallas kernels, main_call(): pl.pallas_call(functools.partial(main_kernel, factor), out_shape=[pltpu.H...  9.07 us
    all_to_all x1, starting transfers between devices, per_device(): got = lax.all_to_all(pack(z, inputs, cotangent), plane, 0, 0, tiled=True)  8.73 us
    all_to_all x1, starting transfers between devices, per_device(): back = lax.all_to_all(out, plane, 0, 0, tiled=True)  6.8 us
    pallas_call x1, Pallas kernels, pack(): pl.pallas_call(pack_kernel, in_specs=[SMEM, ANY, ANY], out_specs=ANY, out...  3.26 us
  transfers between devices with their start and end apart: 7, of which 4 were waited for; matrix products, arithmetic and copies ran while one was open for 1% of the time, Pallas kernels for 1%

profile of v15, /device:TPU:1, one launch (start us, length us, event | category | flops | bytes accessed | tf_op | source)
XLA Modules:
  0.0 96.5 jit_solution(3982687066844579207)
XLA Ops:
  0.6 3.3 %shard_map.118 = bf16[32,352,128]{2,1,0:T(8,128)(2,1)} custom-call(s32[1]{0:T(128)} %bitcast.z_ref, bf16[128,5632]{1,0:T(8,128)(2,1)} %x_hbm.1, bf16[128,5632]{1,0:T(8,128)(2,1)} %c_hbm.1), custom_call_target="tpu_custom_call" | custom-call | tf_op jit(solution)/shard_map/pallas_call | solution.py:78
  3.9 0.0 copy-start.2
  3.9 0.0 copy-start.3
  3.9 0.0 copy-start.4
  3.9 0.0 copy-start
  3.9 0.0 copy-start.1
  4.0 8.7 %all-to-all-start = ((bf16[32,352,128]{2,1,0:T(8,128)(2,1)}), bf16[32,352,128]{2,1,0:T(8,128)(2,1)S(1)}, u32[]{:S(2)}, u32[]{:S(2)}) async-start(bf16[32,352,128]{2,1,0:T(8,128)(2,1)} %shard_map.118), calls=%async_computation | async-start | bytes 5767168 | tf_op jit(solution)/shard_map/all_to_all | solution.py:318
  12.7 0.0 copy-done.2
  12.7 0.0 copy-done.3
  12.7 0.1 pad_maximum_fusion
  12.8 0.1 broadcast_in_dim.13
  12.9 0.0 copy-done.4
  12.9 0.1 broadcast_in_dim.14
  13.1 0.0 copy-done
  13.1 0.1 copy.16
  13.2 0.0 copy-done.1
  13.2 0.1 copy.17
  13.3 0.1 pad.10.clone
  13.4 0.1 maximum_maximum_fusion
  13.5 0.7 collective-permute-start
  14.2 0.0 collective-permute-done
  14.2 0.1 copy.20.w_ref
  14.4 34.3 %all-to-all-done.m_ref = bf16[32,352,128]{2,1,0:T(8,128)(2,1)S(1)} async-done(((bf16[32,352,128]{2,1,0:T(8,128)(2,1)}), bf16[32,352,128]{2,1,0:T(8,128)(2,1)S(1)}, u32[]{:S(2)}, u32[]{:S(2)}) %all-to-all-start) | async-done | bytes 2883616 | tf_op jit(solution)/shard_map/all_to_all | solution.py:318
  48.7 9.1 %shard_map.119 = (bf16[32,176,128]{2,1,0:T(8,128)(2,1)}, bf16[192,384]{1,0:T(8,128)(2,1)S(1)}) custom-call(bf16[32,352,128]{2,1,0:T(8,128)(2,1)S(1)} %all-to-all-done.m_ref, bf16[192,384]{1,0:T(8,128)(2,1)S(1)} %copy.20.w_ref, bf16[352,192]{1,0:T(8,128)(2,1)S(1)} %slice_bitcast_fusion.wt_ref), custom_call_target="tpu_custom_call" | custom-call | tf_op jit(solution)/shard_map/pallas_call | solution.py:248
  57.8 0.0 copy-start.5
  57.8 6.8 %all-to-all-start.1 = ((bf16[32,176,128]{2,1,0:T(8,128)(2,1)}), bf16[32,176,128]{2,1,0:T(8,128)(2,1)S(1)}, u32[]{:S(2)}, u32[]{:S(2)}) async-start(bf16[32,176,128]{2,1,0:T(8,128)(2,1)} %get-tuple-element.16), calls=%async_computation.1 | async-start | bytes 2883584 | tf_op jit(solution)/shard_map/all_to_all | solution.py:322
  64.6 0.7 collective-permute-start.1
  65.3 0.0 collective-permute-done.1
  65.3 12.7 %collective-permute-start.2 = (bf16[192,384]{1,0:T(8,128)(2,1)S(1)}, bf16[192,384]{1,0:T(8,128)(2,1)S(1)}, u32[]{:S(2)}, u32[]{:S(2)}) collective-permute-start(bf16[192,384]{1,0:T(8,128)(2,1)S(1)} %collective-permute-done.1), channel_id=1, source_target_pairs={{0,64},{32,96},{64,0},{96,32},{128,192},{160,224},{192,128},{224,1... | collective-permute-start | bytes 442376 | tf_op jit(solution)/shard_map/ppermute | solution.py:326
  78.0 7.5 %collective-permute-done.2 = bf16[192,384]{1,0:T(8,128)(2,1)S(1)} collective-permute-done((bf16[192,384]{1,0:T(8,128)(2,1)S(1)}, bf16[192,384]{1,0:T(8,128)(2,1)S(1)}, u32[]{:S(2)}, u32[]{:S(2)}) %collective-permute-start.2) | collective-permute-done | bytes 147488 | tf_op jit(solution)/shard_map/ppermute | solution.py:326
  85.5 2.6 %collective-permute-start.3 = (bf16[192,384]{1,0:T(8,128)(2,1)S(1)}, bf16[192,384]{1,0:T(8,128)(2,1)S(1)}, u32[]{:S(2)}, u32[]{:S(2)}) collective-permute-start(bf16[192,384]{1,0:T(8,128)(2,1)S(1)} %add_convert_fusion.1), channel_id=1, source_target_pairs={{0,128},{32,160},{64,192},{96,224},{128,0},{160,32},{192,64},{224,... | collective-permute-start | bytes 442376 | tf_op jit(solution)/shard_map/ppermute | solution.py:326
  88.1 3.5 %collective-permute-done.3 = bf16[192,384]{1,0:T(8,128)(2,1)S(1)} collective-permute-done((bf16[192,384]{1,0:T(8,128)(2,1)S(1)}, bf16[192,384]{1,0:T(8,128)(2,1)S(1)}, u32[]{:S(2)}, u32[]{:S(2)}) %collective-permute-start.3) | collective-permute-done | bytes 147488 | tf_op jit(solution)/shard_map/ppermute | solution.py:326
  91.6 0.0 all-to-all-done.1.in_ref
  91.6 1.3 %collective-permute-start.4 = (bf16[192,384]{1,0:T(8,128)(2,1)S(1)}, bf16[192,384]{1,0:T(8,128)(2,1)S(1)}, u32[]{:S(2)}, u32[]{:S(2)}) collective-permute-start(bf16[192,384]{1,0:T(8,128)(2,1)S(1)} %add_convert_fusion.refs_0_), channel_id=1, source_target_pairs={{0,32},{32,0},{64,96},{96,64},{128,160},{160,128},{192,224},{224,1... | collective-permute-start | bytes 442376 | tf_op jit(solution)/shard_map/ppermute | solution.py:329
  92.9 0.0 copy-done.5
  92.9 1.3 %shard_map.120.refs_3_ = bf16[128,5632]{1,0:T(8,128)(2,1)} custom-call(s32[1]{0:T(128)} %bitcast.z_ref, bf16[32,176,128]{2,1,0:T(8,128)(2,1)S(1)} %all-to-all-done.1.in_ref), custom_call_target="tpu_custom_call" | custom-call | tf_op jit(solution)/shard_map/pallas_call | solution.py:96
  94.2 1.5 %collective-permute-done.4.refs_1_ = bf16[192,384]{1,0:T(8,128)(2,1)S(1)} collective-permute-done((bf16[192,384]{1,0:T(8,128)(2,1)S(1)}, bf16[192,384]{1,0:T(8,128)(2,1)S(1)}, u32[]{:S(2)}, u32[]{:S(2)}) %collective-permute-start.4) | collective-permute-done | bytes 147488 | tf_op jit(solution)/shard_map/ppermute | solution.py:329
  95.7 0.8 shard_map.121
  (7 shorter events, 0.1 us)
Async XLA Ops:
  3.9 8.8 %copy-start.2 = (bf16[176]{0:T(256)(128)(2,1)S(1)}, bf16[176]{0:T(256)(128)(2,1)}, u32[]{:S(2)}) copy-start(bf16[176]{0:T(256)(128)(2,1)} %param.12) | copy-start | bytes 1060
  3.9 8.8 %copy-start.3 = (bf16[176]{0:T(256)(128)(2,1)S(1)}, bf16[176]{0:T(256)(128)(2,1)}, u32[]{:S(2)}) copy-start(bf16[176]{0:T(256)(128)(2,1)} %param.11) | copy-start | bytes 1060
  3.9 9.0 %copy-start.4 = (bf16[176]{0:T(256)(128)(2,1)S(1)}, bf16[176]{0:T(256)(128)(2,1)}, u32[]{:S(2)}) copy-start(bf16[176]{0:T(256)(128)(2,1)} %param.13) | copy-start | bytes 1060
  3.9 9.1 %copy-start = (bf16[176,176]{1,0:T(8,128)(2,1)S(1)}, bf16[176,176]{1,0:T(8,128)(2,1)}, u32[]{:S(2)}) copy-start(bf16[176,176]{1,0:T(8,128)(2,1)} %param.9) | copy-start | bytes 185860
  3.9 9.2 %copy-start.1 = (bf16[176,176]{1,0:T(8,128)(2,1)S(1)}, bf16[176,176]{1,0:T(8,128)(2,1)}, u32[]{:S(2)}) copy-start(bf16[176,176]{1,0:T(8,128)(2,1)} %param.10) | copy-start | bytes 185860
  4.0 44.7 %all-to-all-start = ((bf16[32,352,128]{2,1,0:T(8,128)(2,1)}), bf16[32,352,128]{2,1,0:T(8,128)(2,1)S(1)}, u32[]{:S(2)}, u32[]{:S(2)}) async-start(bf16[32,352,128]{2,1,0:T(8,128)(2,1)} %shard_map.118), calls=%async_computation | async-start | bytes 5767168 | tf_op jit(solution)/shard_map/all_to_all | solution.py:318
  13.5 0.7 collective-permute-start
  57.8 35.1 %copy-start.5 = (bf16[176]{0:T(256)(128)(2,1)S(1)}, bf16[176]{0:T(256)(128)(2,1)}, u32[]{:S(2)}) copy-start(bf16[176]{0:T(256)(128)(2,1)} %param.13) | copy-start | bytes 1060
  57.8 33.8 %all-to-all-start.1 = ((bf16[32,176,128]{2,1,0:T(8,128)(2,1)}), bf16[32,176,128]{2,1,0:T(8,128)(2,1)S(1)}, u32[]{:S(2)}, u32[]{:S(2)}) async-start(bf16[32,176,128]{2,1,0:T(8,128)(2,1)} %get-tuple-element.16), calls=%async_computation.1 | async-start | bytes 2883584 | tf_op jit(solution)/shard_map/all_to_all | solution.py:322
  64.6 0.7 collective-permute-start.1
  65.3 20.2 %collective-permute-start.2 = (bf16[192,384]{1,0:T(8,128)(2,1)S(1)}, bf16[192,384]{1,0:T(8,128)(2,1)S(1)}, u32[]{:S(2)}, u32[]{:S(2)}) collective-permute-start(bf16[192,384]{1,0:T(8,128)(2,1)S(1)} %collective-permute-done.1), channel_id=1, source_target_pairs={{0,64},{32,96},{64,0},{96,32},{128,192},{160,224},{192,128},{224,1... | collective-permute-start | bytes 442376 | tf_op jit(solution)/shard_map/ppermute | solution.py:326
  85.5 6.1 %collective-permute-start.3 = (bf16[192,384]{1,0:T(8,128)(2,1)S(1)}, bf16[192,384]{1,0:T(8,128)(2,1)S(1)}, u32[]{:S(2)}, u32[]{:S(2)}) collective-permute-start(bf16[192,384]{1,0:T(8,128)(2,1)S(1)} %add_convert_fusion.1), channel_id=1, source_target_pairs={{0,128},{32,160},{64,192},{96,224},{128,0},{160,32},{192,64},{224,... | collective-permute-start | bytes 442376 | tf_op jit(solution)/shard_map/ppermute | solution.py:326
  91.6 4.1 %collective-permute-start.4 = (bf16[192,384]{1,0:T(8,128)(2,1)S(1)}, bf16[192,384]{1,0:T(8,128)(2,1)S(1)}, u32[]{:S(2)}, u32[]{:S(2)}) collective-permute-start(bf16[192,384]{1,0:T(8,128)(2,1)S(1)} %add_convert_fusion.refs_0_), channel_id=1, source_target_pairs={{0,32},{32,0},{64,96},{96,64},{128,160},{160,128},{192,224},{224,1... | collective-permute-start | bytes 442376 | tf_op jit(solution)/shard_map/ppermute | solution.py:329
